TPU v7x, 128 devices: a whole 4x4x4 slice. The times are simulated.
128 devices in a mesh: row: 8 (over z_hi, y), col: 16 (over x, z_lo, core).
Axes of the slice: x: 4, y: 4, z: 4 (z_hi: 2, z_lo: 2; z = z_hi * 2 + z_lo), core: 2. Of those that a mesh axis runs over, the one named last changes fastest.
Arguments:
- object_tile: float32 [2, 2048, 4096], P(None, 'row', 'col'), may hold values from -6 to 6
- probe: float32 [2, 2, 256, 256], replicated, may hold values from -6 to 6
- amplitudes: float32 [8, 16, 4, 256, 256], P('row', 'col'), may hold values from 0 to 15
- offsets: int32 [8, 16, 4, 2], P('row', 'col'), may hold values from 0 to 256
Outputs:
- object_update: float32 [2, 2048, 4096], P(None, 'row', 'col')
- probe_update: float32 [2, 2, 256, 256], replicated
- position_step: float32 [8, 16, 4, 2], P('row', 'col')
- relative_error: float32 [1], replicated
All inputs are finite; a program needn't handle non-finite values.
Results may differ from a plain program's by a relative error of at most 0.00021.
Values sent between devices are 32-bit elements; how exact they have to be, the bound alone decides.
No kernel may reach another device: no remote copies, remote signals or barrier semaphores. Data moves between devices by JAX's collectives and lax.ppermute only.
A program may use at most 128 MiB of HBM per device.

v0:
```python
import jax
import jax.numpy as jnp
import ml_dtypes
import numpy as np
from jax import lax
from jax.experimental import pallas as pl
from jax.experimental.pallas import tpu as pltpu
from jax.sharding import PartitionSpec as P

intensity_floor = 0.1
object_damping = 1.0
small_value = 1e-06

SIZE = 256
HALF = 128
CHUNK = 32
BF = jnp.bfloat16
F32 = jnp.float32
AXES = ("row", "col")
VMEM_LIMIT = 56 * 2**20


def transform_matrices():
    n = np.arange(HALF)[:, None]
    q = np.arange(HALF)[None, :]
    out = []
    for odd in (0, 1):
        angle = -2.0 * np.pi * ((n * (2 * q + odd)) % SIZE) / SIZE
        re, im = np.cos(angle) / 16.0, np.sin(angle) / 16.0
        out.append(np.block([[re, im], [-im, re]]))
    return out


def split_np(matrix):
    high = matrix.astype(ml_dtypes.bfloat16)
    low = (matrix - high.astype(np.float64)).astype(ml_dtypes.bfloat16)
    return high, low


def constants():
    right_f, left_f, right_i, left_i = [], [], [], []
    for matrix in transform_matrices():
        high, low = split_np(matrix)
        right_f.append(np.concatenate([high, high, low], 0))
        left_f.append(np.concatenate([high.T, low.T, high.T], 1))
        right_i.append(np.concatenate([high.T, high.T, low.T], 0))
        left_i.append(np.concatenate([high, low, high], 1))
    return [np.stack(x) for x in (right_f, left_f, right_i, left_i)]


def permutation():
    order = np.concatenate([np.arange(0, SIZE, 2), np.arange(1, SIZE, 2)])
    onehot = np.zeros((SIZE, SIZE), np.float32)
    onehot[order, np.arange(SIZE)] = 1.0
    columns = np.concatenate([onehot] * 3, 0).astype(ml_dtypes.bfloat16)
    rows = np.concatenate([onehot.T] * 3, 1).astype(ml_dtypes.bfloat16)
    return columns, rows


def split2(value):
    high = value.astype(BF)
    return high, (value - high.astype(F32)).astype(BF)


def split3(value):
    high = value.astype(BF)
    rest = value - high.astype(F32)
    middle = rest.astype(BF)
    return high, middle, (rest - middle.astype(F32)).astype(BF)


def dot(a, b):
    return jnp.dot(a, b, preferred_element_type=F32)


def lane_index(rows):
    return lax.broadcasted_iota(jnp.int32, (rows, HALF), 1)


def spread(first, second, shift, lanes):
    a = pltpu.roll(first, shift, 1)
    b = pltpu.roll(second, shift, 1)
    wrapped = lanes < shift
    return jnp.where(wrapped, 0.0, a), jnp.where(wrapped, a, b), jnp.where(wrapped, b, 0.0)


def gather_lanes(blocks, shift, lanes):
    back = jnp.where(shift == 0, 0, HALF - shift)
    a, b, c = [pltpu.roll(x, back, 1) for x in blocks]
    inside = lanes < HALF - shift
    return jnp.where(inside, a, b), jnp.where(inside, b, c)


def fold8(value):
    return jnp.sum(value.reshape(-1, 8, HALF), axis=0)


def prepare_kernel(starts, probe, measured, cols, rows, center, left, right, permuted, power, accum):
    accum[...] = jnp.zeros_like(accum)
    for i in range(0, SIZE, CHUNK):
        part = pl.ds(i, CHUNK)
        total = probe[0, 0, part] ** 2 + probe[0, 1, part] ** 2
        power[part] = total + probe[1, 0, part] ** 2 + probe[1, 1, part] ** 2
    lanes = lane_index(CHUNK)
    for j in range(measured.shape[0]):
        row, col = starts[j, 0], starts[j, 1]
        base, shift = col // HALF, lax.rem(col, HALF)
        for i in range(0, SIZE, CHUNK):
            part = pl.ds(i, CHUNK)
            moved = spread(power[part, :HALF], power[part, HALF:], shift, lanes)
            where = pl.ds(row + i, CHUNK)
            for b in range(3):
                accum[base + b, where, :] += moved[b]
    center[:, :HALF] = accum[1]
    center[:, HALF:] = accum[2]
    left[...] = accum[0]
    right[...] = accum[3]
    for j in range(measured.shape[0]):
        moved = dot(jnp.concatenate(split3(measured[j]), 1), cols[...])
        permuted[j] = dot(rows[...], jnp.concatenate(split3(moved), 0))


def main_kernel(
    starts, core, own, up, down, left, right, left_corner, right_corner, probe, power, measured,
    right_f, left_f, right_i, left_i,
    grad_center, grad_left, grad_right, keep, send, steps,
    tile, patch, grad, totals, xs, zs, gs, ys, back, sums,
):
    step = pl.program_id(0)
    modes = probe.shape[0]
    lanes = lane_index(CHUNK)

    @pl.when(step == 0)
    def _():
        for p in range(2):
            tile[p, 0, 0:128] = left_corner[0, p]
            tile[p, 0, 128:384] = left[p]
            tile[p, 0, 384:512] = left_corner[1, p]
            tile[p, 3, 0:128] = right_corner[0, p]
            tile[p, 3, 128:384] = right[p]
            tile[p, 3, 384:512] = right_corner[1, p]
            for b in range(2):
                span = slice(b * HALF, (b + 1) * HALF)
                tile[p, 1 + b, 0:128] = up[p, :, span]
                tile[p, 1 + b, 128:384] = own[p, :, span]
                tile[p, 1 + b, 384:512] = down[p, :, span]
            tile[p, 4] = jnp.zeros((2 * SIZE, HALF), F32)
        grad[...] = jnp.zeros_like(grad)
        totals[...] = jnp.zeros_like(totals)
        sums[...] = jnp.zeros_like(sums)
        patch[:, :, 0:8, :] = jnp.zeros((2, 2, 8, HALF), F32)
        patch[:, :, 264:272, :] = jnp.zeros((2, 2, 8, HALF), F32)

    row, col = starts[step, 0], starts[step, 1]
    base, shift = col // HALF, lax.rem(col, HALF)

    for i in range(0, SIZE, CHUNK):
        part = pl.ds(i, CHUNK)
        where = pl.ds(row + i, CHUNK)
        obj = []
        for p in range(2):
            blocks = [tile[p, base + b, where, :] for b in range(3)]
            obj.append(gather_lanes(blocks, shift, lanes))
            for b in range(2):
                patch[p, b, pl.ds(8 + i, CHUNK), :] = obj[p][b]
        for m in range(modes):
            wave = []
            for b in range(2):
                span = slice(b * HALF, (b + 1) * HALF)
                pr, pi = probe[m, 0, part, span], probe[m, 1, part, span]
                wave.append((pr * obj[0][b] - pi * obj[1][b], pr * obj[1][b] + pi * obj[0][b]))
            for odd in range(2):
                sign = 1.0 - 2.0 * odd
                for p in range(2):
                    high, low = split2(wave[0][p] + sign * wave[1][p])
                    at = pl.ds(m * SIZE + i, CHUNK)
                    xs[odd, at, p * HALF : (p + 1) * HALF] = high
                    xs[odd, at, SIZE + p * HALF : SIZE + (p + 1) * HALF] = low
                    xs[odd, at, 2 * SIZE + p * HALF : 2 * SIZE + (p + 1) * HALF] = high

    for odd in range(2):
        ys[odd] = dot(xs[odd], right_f[odd])

    for m in range(modes):
        for odd in range(2):
            lane_span = slice(odd * HALF, (odd + 1) * HALF)
            for i in range(0, HALF, CHUNK):
                top = ys[odd, pl.ds(m * SIZE + i, CHUNK), :]
                bottom = ys[odd, pl.ds(m * SIZE + HALF + i, CHUNK), :]
                for odd_row in range(2):
                    high, low = split2(top + bottom if odd_row == 0 else top - bottom)
                    for p in range(2):
                        span = slice(p * HALF, (p + 1) * HALF)
                        at = p * HALF + i
                        zs[m, odd_row, pl.ds(at, CHUNK), lane_span] = high[:, span]
                        zs[m, odd_row, pl.ds(SIZE + at, CHUNK), lane_span] = high[:, span]
                        zs[m, odd_row, pl.ds(2 * SIZE + at, CHUNK), lane_span] = low[:, span]

    error = jnp.zeros((8, HALF), F32)
    energy = jnp.zeros((8, HALF), F32)
    for odd_row in range(2):
        far = [dot(left_f[odd_row], zs[m, odd_row]) for m in range(modes)]
        for i in range(0, HALF, CHUNK):
            parts = [(f[i : i + CHUNK], f[HALF + i : HALF + i + CHUNK]) for f in far]
            intensity = parts[0][0] ** 2 + parts[0][1] ** 2 + (parts[1][0] ** 2 + parts[1][1] ** 2)
            intensity = jnp.maximum(intensity, intensity_floor)
            inverse = lax.rsqrt(intensity)
            modulus = intensity * inverse
            amplitude = measured[0, pl.ds(odd_row * HALF + i, CHUNK), :]
            factor = 1.0 - amplitude * inverse
            misfit = (modulus - amplitude) ** 2
            strength = amplitude**2
            error = error + fold8(misfit[:, :HALF]) + fold8(misfit[:, HALF:])
            energy = energy + fold8(strength[:, :HALF]) + fold8(strength[:, HALF:])
            for m in range(modes):
                for p in range(2):
                    high, low = split2(parts[m][p] * factor)
                    at = p * HALF + i
                    gs[m, odd_row, pl.ds(at, CHUNK), :] = high
                    gs[m, odd_row, pl.ds(SIZE + at, CHUNK), :] = high
                    gs[m, odd_row, pl.ds(2 * SIZE + at, CHUNK), :] = low
    sums[0] += error
    sums[1] += energy

    for m in range(modes):
        even = dot(left_i[0], gs[m, 0])
        odds = dot(left_i[1], gs[m, 1])
        for i in range(0, HALF, CHUNK):
            for p in range(2):
                a, b = even[p * HALF + i : p * HALF + i + CHUNK], odds[p * HALF + i : p * HALF + i + CHUNK]
                for bottom in range(2):
                    high, low = split2(a - b if bottom else a + b)
                    at = pl.ds(m * SIZE + bottom * HALF + i, CHUNK)
                    for odd in range(2):
                        span = slice(odd * HALF, (odd + 1) * HALF)
                        xs[odd, at, p * HALF : (p + 1) * HALF] = high[:, span]
                        xs[odd, at, SIZE + p * HALF : SIZE + (p + 1) * HALF] = low[:, span]
                        xs[odd, at, 2 * SIZE + p * HALF : 2 * SIZE + (p + 1) * HALF] = high[:, span]

    for odd in range(2):
        back[odd] = dot(xs[odd], right_i[odd])

    parts = [jnp.zeros((8, HALF), F32) for _ in range(4)]
    for i in range(0, SIZE, CHUNK):
        part = pl.ds(i, CHUNK)
        obj = [[patch[p, b, pl.ds(8 + i, CHUNK), :] for b in range(2)] for p in range(2)]
        grads = [[0.0, 0.0], [0.0, 0.0]]
        for m in range(modes):
            at = pl.ds(m * SIZE + i, CHUNK)
            for b in range(2):
                span = slice(b * HALF, (b + 1) * HALF)
                br, bi = [
                    back[0, at, p * HALF : (p + 1) * HALF] + (1.0 - 2.0 * b) * back[1, at, p * HALF : (p + 1) * HALF]
                    for p in range(2)
                ]
                pr, pi = probe[m, 0, part, span], probe[m, 1, part, span]
                grads[0][b] = grads[0][b] + (pr * br + pi * bi)
                grads[1][b] = grads[1][b] + (pr * bi - pi * br)
                totals[b, 2 * m, part, :] += obj[0][b] * br + obj[1][b] * bi
                totals[b, 2 * m + 1, part, :] += obj[0][b] * bi - obj[1][b] * br
        for b in range(2):
            totals[b, 4, part, :] += obj[0][b] ** 2 + obj[1][b] ** 2
        where = pl.ds(row + i, CHUNK)
        for p in range(2):
            moved = spread(grads[p][0], grads[p][1], shift, lanes)
            for b in range(3):
                grad[p, base + b, where, :] += moved[b]
        first, last = lanes == 0, lanes == HALF - 1
        slopes = [[None, None], [None, None]]
        for p in range(2):
            before = [pltpu.roll(obj[p][b], 1, 1) for b in range(2)]
            after = [pltpu.roll(obj[p][b], HALF - 1, 1) for b in range(2)]
            slopes[p][0] = jnp.where(last, after[1], after[0]) - jnp.where(first, 0.0, before[0])
            slopes[p][1] = jnp.where(last, 0.0, after[1]) - jnp.where(first, before[0], before[1])
        for b in range(2):
            strength = power[part, b * HALF : (b + 1) * HALF]
            rows = [
                patch[p, b, pl.ds(9 + i, CHUNK), :] - patch[p, b, pl.ds(7 + i, CHUNK), :] for p in range(2)
            ]
            for d, slope in enumerate((rows, [slopes[0][b], slopes[1][b]])):
                parts[2 * d] = parts[2 * d] + fold8(grads[0][b] * slope[0] + grads[1][b] * slope[1])
                parts[2 * d + 1] = parts[2 * d + 1] + fold8(strength * (slope[0] ** 2 + slope[1] ** 2))

    for d in range(2):
        numerator = 0.5 * jnp.sum(parts[2 * d], keepdims=True)
        denominator = 0.25 * jnp.sum(parts[2 * d + 1], keepdims=True) + small_value
        steps[pl.ds(2 * step + d, 1), :] = jnp.broadcast_to(-numerator / denominator, (1, HALF))

    @pl.when(step == pl.num_programs(0) - 1)
    def _():
        for p in range(2):
            grad_left[p] = grad[p, 0]
            grad_right[p] = grad[p, 3]
            grad_center[p, :, :HALF] = grad[p, 1]
            grad_center[p, :, HALF:] = grad[p, 2]
        k = core[0]
        scalar = jnp.where(
            lax.broadcasted_iota(jnp.int32, (1, 4, HALF), 2) == 0,
            jnp.sum(sums[0]),
            jnp.sum(sums[1]),
        )
        for out, block in ((keep, k), (send, 1 - k)):
            for c in range(5):
                out[:, 4 * c : 4 * c + 4, :] = totals[block, c].reshape(64, 4, HALF)
            out[:, 20:24, :] = jnp.broadcast_to(scalar, (64, 4, HALF))


def whole(*shape):
    return pl.BlockSpec(shape, lambda *_: (0,) * len(shape))


def prepare(starts, probe, measured):
    count = measured.shape[0]
    cols, rows = permutation()
    shapes = [(2 * SIZE, SIZE), (2 * SIZE, HALF), (2 * SIZE, HALF), (count, SIZE, SIZE), (SIZE, SIZE)]
    return pl.pallas_call(
        prepare_kernel,
        out_shape=[jax.ShapeDtypeStruct(s, F32) for s in shapes],
        grid_spec=pltpu.PrefetchScalarGridSpec(
            num_scalar_prefetch=1,
            grid=(),
            in_specs=[whole(*x.shape) for x in (probe, measured, cols, rows)],
            out_specs=[whole(*s) for s in shapes],
            scratch_shapes=[pltpu.VMEM((5, 2 * SIZE, HALF), F32)],
        ),
        compiler_params=pltpu.CompilerParams(vmem_limit_bytes=VMEM_LIMIT),
        cost_estimate=pl.CostEstimate(flops=1 << 30, bytes_accessed=5 << 20, transcendentals=0),
    )(starts, probe, measured, jnp.asarray(cols), jnp.asarray(rows))


def compute(starts, core, own, halo, probe, power, measured):
    mats = [jnp.asarray(x) for x in constants()]
    arrays = [own, *halo, probe, power]
    count = measured.shape[0]
    shapes = [
        (2, 2 * SIZE, SIZE), (2, 2 * SIZE, HALF), (2, 2 * SIZE, HALF), (64, 24, HALF), (64, 24, HALF), (2 * count, HALF),
    ]
    return pl.pallas_call(
        main_kernel,
        out_shape=[jax.ShapeDtypeStruct(s, F32) for s in shapes],
        grid_spec=pltpu.PrefetchScalarGridSpec(
            num_scalar_prefetch=2,
            grid=(count,),
            in_specs=[whole(*x.shape) for x in arrays]
            + [pl.BlockSpec((1, SIZE, SIZE), lambda i, *_: (i, 0, 0))]
            + [whole(*x.shape) for x in mats],
            out_specs=[whole(*s) for s in shapes],
            scratch_shapes=[
                pltpu.VMEM((2, 5, 2 * SIZE, HALF), F32),
                pltpu.VMEM((2, 2, SIZE + 16, HALF), F32),
                pltpu.VMEM((2, 5, 2 * SIZE, HALF), F32),
                pltpu.VMEM((2, 5, SIZE, HALF), F32),
                pltpu.VMEM((2, 2 * SIZE, 3 * SIZE), BF),
                pltpu.VMEM((2, 2, 3 * SIZE, SIZE), BF),
                pltpu.VMEM((2, 2, 3 * SIZE, SIZE), BF),
                pltpu.VMEM((2, 2 * SIZE, SIZE), F32),
                pltpu.VMEM((2, 2 * SIZE, SIZE), F32),
                pltpu.VMEM((2, 8, HALF), F32),
            ],
        ),
        compiler_params=pltpu.CompilerParams(vmem_limit_bytes=VMEM_LIMIT),
        cost_estimate=pl.CostEstimate(flops=13 << 30, bytes_accessed=8 << 20, transcendentals=1 << 18),
    )(starts, core, *arrays, measured, *mats)


def neighbours(axis):
    up = [(i, i + 1) for i in range(lax.axis_size(axis) - 1)]
    return up, [(j, i) for i, j in up]


def local(object_tile, probe, amplitudes, offsets):
    starts = offsets[0, 0]
    measured = amplitudes[0, 0]
    row_up, row_down = neighbours("row")
    col_up, col_down = neighbours("col")
    col_index = lax.axis_index("col")
    core = lax.rem(col_index, 2)

    with jax.named_scope("object_halo"):
        up = lax.ppermute(object_tile[:, HALF:], "row", row_up)
        down = lax.ppermute(object_tile[:, :HALF], "row", row_down)
        left = lax.ppermute(object_tile[:, :, HALF:], "col", col_up)
        right = lax.ppermute(object_tile[:, :, :HALF], "col", col_down)
    center, light_left, light_right, permuted, power = prepare(starts, probe, measured)
    with jax.named_scope("object_corners"):
        left_corner = lax.ppermute(jnp.stack([up[:, :, HALF:], down[:, :, HALF:]]), "col", col_up)
        right_corner = lax.ppermute(jnp.stack([up[:, :, :HALF], down[:, :, :HALF]]), "col", col_down)

    halo = [up, down, left, right, left_corner, right_corner]
    grad_center, grad_left, grad_right, keep, send, steps = compute(
        starts, core.reshape(1), object_tile, halo, probe, power, permuted
    )

    with jax.named_scope("gradient_columns"):
        strip_left = jnp.concatenate([grad_left, light_left[None]], 0)
        strip_right = jnp.concatenate([grad_right, light_right[None]], 0)
        from_left = lax.ppermute(strip_right, "col", col_up)
        from_right = lax.ppermute(strip_left, "col", col_down)

    with jax.named_scope("probe_reduce"):
        devices = lax.axis_size("row") * lax.axis_size("col")
        partners = [(i, i ^ 1) for i in range(devices)]
        groups = [[i for i in range(devices) if i % 2 == k] for k in range(2)]
        chunk = keep + lax.ppermute(send, AXES, partners)
        chunk = lax.all_to_all(chunk, AXES, 0, 0, axis_index_groups=groups, tiled=True)
        total = jnp.sum(chunk, axis=0)
        quotient = total[:16].reshape(4, 4, HALF) / total[16:20]
        relative_error = (total[20, 0] / total[20, 1]).reshape(1)

    with jax.named_scope("gradient_rows"):
        fields = jnp.concatenate([grad_center, center[None]], 0)
        fields = fields + jnp.concatenate([from_left, from_right], 2)
        from_above = lax.ppermute(fields[:, SIZE + HALF :], "row", row_up)
        from_below = lax.ppermute(fields[:, :HALF], "row", row_down)

    with jax.named_scope("probe_gather"):
        spread_out = jnp.broadcast_to(quotient.reshape(1, 16, HALF), (devices // 2, 16, HALF))
        gathered = lax.all_to_all(spread_out, AXES, 0, 0, axis_index_groups=groups, tiled=True)
        other = lax.ppermute(gathered, AXES, partners)
        first = jnp.where(core == 0, gathered, other)
        second = jnp.where(core == 0, other, gathered)
        both = jnp.stack([first, second], 0).reshape(2, 64, 4, 4, HALF)
        probe_update = both.transpose(2, 1, 3, 0, 4).reshape(2, 2, SIZE, SIZE)

    with jax.named_scope("object_update"):
        combined = fields[:, HALF : HALF + SIZE] + jnp.concatenate([from_above, from_below], 1)
        object_update = combined[:2] / (combined[2:] + object_damping)

    position_step = steps[:, 0].reshape(1, 1, -1, 2)
    return (object_update, probe_update, position_step, relative_error)


def solution(mesh):
    in_specs = (
        P(None, "row", "col"),
        P(),
        P("row", "col", None, None, None),
        P("row", "col", None, None),
    )
    out_specs = (P(None, "row", "col"), P(), P("row", "col", None, None), P())
    return jax.shard_map(local, mesh=mesh, in_specs=in_specs, out_specs=out_specs, check_vma=False)
```

profile of v0, /device:TPU:1, one launch (start us, length us, event | category | flops | bytes accessed | tf_op | source)
XLA Modules:
  0.0 127.5 jit_solution(15323214604707453444)
XLA Ops:
  0.6 1.1 fusion.2
  1.7 4.0 %collective-permute-start = (f32[2,128,256]{2,1,0:T(8,128)S(1)}, f32[2,128,256]{2,1,0:T(8,128)S(1)}, u32[]{:S(2)}, u32[]{:S(2)}) collective-permute-start(f32[2,128,256]{2,1,0:T(8,128)S(1)} %get-tuple-element.49), channel_id=1, source_target_pairs={{0,16},{16,32},{32,48},{48,64},{64,80},{80,96},{96,112},{1,17},{17... | collective-permute-start | bytes 786440 | tf_op jit(solution)/shard_map/object_halo/ppermute | solution.py:380
  5.8 0.0 copy-start.9
  5.8 1.3 %collective-permute-start.1 = (f32[2,128,256]{2,1,0:T(8,128)S(1)}, f32[2,128,256]{2,1,0:T(8,128)S(1)}, u32[]{:S(2)}, u32[]{:S(2)}) collective-permute-start(f32[2,128,256]{2,1,0:T(8,128)S(1)} %get-tuple-element.48), channel_id=1, source_target_pairs={{16,0},{32,16},{48,32},{64,48},{80,64},{96,80},{112,96},{17,1},{33... | collective-permute-start | bytes 786440 | tf_op jit(solution)/shard_map/object_halo/ppermute | solution.py:381
  7.1 1.1 fusion.1
  8.1 4.4 %collective-permute-start.2 = (f32[2,256,128]{2,1,0:T(8,128)S(1)}, f32[2,256,128]{2,1,0:T(8,128)S(1)}, u32[]{:S(2)}, u32[]{:S(2)}) collective-permute-start(f32[2,256,128]{2,1,0:T(8,128)S(1)} %get-tuple-element.47), channel_id=1, source_target_pairs={{0,1},{1,2},{2,3},{3,4},{4,5},{5,6},{6,7},{7,8},{8,9},{9,10},{10,1... | collective-permute-start | bytes 786440 | tf_op jit(solution)/shard_map/object_halo/ppermute | solution.py:382
  12.5 1.9 %collective-permute-start.3 = (f32[2,256,128]{2,1,0:T(8,128)S(1)}, f32[2,256,128]{2,1,0:T(8,128)S(1)}, u32[]{:S(2)}, u32[]{:S(2)}) collective-permute-start(f32[2,256,128]{2,1,0:T(8,128)S(1)} %get-tuple-element.46), channel_id=1, source_target_pairs={{1,0},{2,1},{3,2},{4,3},{5,4},{6,5},{7,6},{8,7},{9,8},{10,9},{11,1... | collective-permute-start | bytes 786440 | tf_op jit(solution)/shard_map/object_halo/ppermute | solution.py:383
  14.5 0.0 collective-permute-done.up
  14.5 0.0 copy-start.4
  14.5 0.0 collective-permute-done.1.down
  14.5 0.0 copy-start.5
  14.6 5.3 %collective-permute-start.4 = (f32[2,2,128,128]{3,2,1,0:T(8,128)S(1)}, f32[2,2,128,128]{3,2,1,0:T(8,128)S(1)}, u32[]{:S(2)}, u32[]{:S(2)}) collective-permute-start(f32[2,2,128,128]{3,2,1,0:T(8,128)S(1)} %pad_maximum_fusion.2), channel_id=1, source_target_pairs={{0,1},{1,2},{2,3},{3,4},{4,5},{5,6},{6,7},{7,8},{8,9},{9,10},{10,1... | collective-permute-start | bytes 786440 | tf_op jit(solution)/shard_map/object_corners/ppermute | solution.py:386
  19.9 1.9 %collective-permute-start.5 = (f32[2,2,128,128]{3,2,1,0:T(8,128)S(1)}, f32[2,2,128,128]{3,2,1,0:T(8,128)S(1)}, u32[]{:S(2)}, u32[]{:S(2)}) collective-permute-start(f32[2,2,128,128]{3,2,1,0:T(8,128)S(1)} %pad_maximum_fusion.3), channel_id=1, source_target_pairs={{1,0},{2,1},{3,2},{4,3},{5,4},{6,5},{7,6},{8,7},{9,8},{10,9},{11,1... | collective-permute-start | bytes 786440 | tf_op jit(solution)/shard_map/object_corners/ppermute | solution.py:387
  21.8 0.0 copy-done.9
  21.8 0.6 copy.25.starts
  22.5 5.0 %shard_map.129 = (f32[512,256]{1,0:T(8,128)}, f32[512,128]{1,0:T(8,128)}, f32[512,128]{1,0:T(8,128)}, f32[4,256,256]{2,1,0:T(8,128)}, f32[256,256]{1,0:T(8,128)}) custom-call(s32[4,2]{1,0:T(4,128)} %copy.25.starts, f32[2,2,256,256]{3,2,1,0:T(8,128)} %probe.3, f32[4,256,256]{2,1,0:T(8,128)} %bitcast.30, bf16[768,256]{1,0:T(8,128)(2,1)} %constant.26.clone.cols, ...), custom_call_target="tpu_custom_call" | custom-call | flops 1073741824 | bytes 5242880 | tf_op jit(solution)/shard_map/pallas_call | solution.py:316
  27.5 0.0 copy-done.4
  27.5 0.0 copy-done.5
  27.5 0.0 collective-permute-done.2.left
  27.5 0.0 collective-permute-done.3.right
  27.5 0.0 collective-permute-done.4.left_corner
  27.6 0.0 collective-permute-done.5.right_corner
  27.6 0.6 copy-done.10
  28.2 0.1 copy-done.11
  28.3 0.1 copy-done.12
  28.4 0.1 copy-done.13
  28.5 19.7 %shard_map.130 = (f32[2,512,256]{2,1,0:T(8,128)}, f32[2,512,128]{2,1,0:T(8,128)}, f32[2,512,128]{2,1,0:T(8,128)}, f32[64,24,128]{2,1,0:T(8,128)}, f32[64,24,128]{2,1,0:T(8,128)}, /*index=5*/f32[8,128]{1,0:T(8,128)}) custom-call(s32[4,2]{1,0:T(4,128)} %copy.25.starts, s32[1]{0:T(128)} %bitcast.1.core, f32[2,256,256]{2,1,0:T(8,128)} %own.1, ...), custom_call_target="tpu_custom_call" | custom-call | flops 13958643712 | bytes 8388608 | tf_op jit(solution)/shard_map/pallas_call | solution.py:338
  48.3 0.1 collective-permute-start.10
  48.4 2.1 %pad_maximum_fusion = f32[3,512,128]{2,1,0:T(8,128)} fusion(f32[1,512,128]{2,1,0:T(8,128)S(1)} %bitcast.27, f32[2,512,128]{2,1,0:T(8,128)} %get-tuple-element.19), kind=kLoop, calls=%fused_computation.3 | loop fusion | flops 196608 | bytes 1572864 | tf_op jit(solution)/shard_map/gradient_columns/concatenate | solution.py:396
  50.5 4.1 %collective-permute-start.6 = (f32[3,512,128]{2,1,0:T(8,128)}, f32[3,512,128]{2,1,0:T(8,128)S(1)}, u32[]{:S(2)}, u32[]{:S(2)}) collective-permute-start(f32[3,512,128]{2,1,0:T(8,128)} %pad_maximum_fusion), channel_id=1, source_target_pairs={{0,1},{1,2},{2,3},{3,4},{4,5},{5,6},{6,7},{7,8},{8,9},{9,10},{10,1... | collective-permute-start | bytes 2359304 | tf_op jit(solution)/shard_map/gradient_columns/ppermute | solution.py:397
  54.6 0.0 copy-done.3
  54.6 0.0 copy-done.6
  54.6 0.9 pad_maximum_fusion.1
  55.6 1.9 %collective-permute-start.7 = (f32[3,512,128]{2,1,0:T(8,128)}, f32[3,512,128]{2,1,0:T(8,128)}, u32[]{:S(2)}, u32[]{:S(2)}) collective-permute-start(f32[3,512,128]{2,1,0:T(8,128)} %pad_maximum_fusion.1), channel_id=1, source_target_pairs={{1,0},{2,1},{3,2},{4,3},{5,4},{6,5},{7,6},{8,7},{9,8},{10,9},{11,1... | collective-permute-start | bytes 2359304 | tf_op jit(solution)/shard_map/gradient_columns/ppermute | solution.py:398
  57.5 0.0 collective-permute-done.10
  57.5 0.0 copy-start.1
  57.5 1.0 add.19
  58.5 15.2 %all-to-all-start = ((f32[64,24,128]{2,1,0:T(8,128)}), f32[64,24,128]{2,1,0:T(8,128)S(1)}, u32[]{:S(2)}, u32[]{:S(2)}) async-start(f32[64,24,128]{2,1,0:T(8,128)} %add.19), calls=%async_computation | async-start | bytes 1572864 | tf_op jit(solution)/shard_map/probe_reduce/all_to_all | solution.py:405
  73.8 0.0 collective-permute-done.6
  73.8 0.0 collective-permute-done.7
  73.8 2.0 %maximum_add_fusion.2 = (f32[3,128,256]{2,1,0:T(8,128)}, f32[3,128,256]{2,1,0:T(8,128)}) fusion(f32[1,512,256]{2,1,0:T(8,128)S(1)} %bitcast.22, f32[2,512,256]{2,1,0:T(8,128)S(1)} %copy-done, f32[3,512,128]{2,1,0:T(8,128)} %collective-permute-done.7, f32[3,512,128]{2,1,0:T(8,128)S(1)} %collective-permute-done.6), kind=kLoop, calls=%fused_computation.7 | loop fusion | flops 589824 | bytes 3932160 | tf_op jit(solution)/shard_map/gradient_rows/slice | solution.py:413
  75.8 3.1 %collective-permute-start.8 = (f32[3,128,256]{2,1,0:T(8,128)}, f32[3,128,256]{2,1,0:T(8,128)S(1)}, u32[]{:S(2)}, u32[]{:S(2)}) collective-permute-start(f32[3,128,256]{2,1,0:T(8,128)} %get-tuple-element.42), channel_id=1, source_target_pairs={{0,16},{16,32},{32,48},{48,64},{64,80},{80,96},{96,112},{1,17},{17... | collective-permute-start | bytes 1179656 | tf_op jit(solution)/shard_map/gradient_rows/ppermute | solution.py:413
  78.9 1.3 %collective-permute-start.9 = (f32[3,128,256]{2,1,0:T(8,128)}, f32[3,128,256]{2,1,0:T(8,128)}, u32[]{:S(2)}, u32[]{:S(2)}) collective-permute-start(f32[3,128,256]{2,1,0:T(8,128)} %get-tuple-element.43), channel_id=1, source_target_pairs={{16,0},{32,16},{48,32},{64,48},{80,64},{96,80},{112,96},{17,1},{33... | collective-permute-start | bytes 1179656 | tf_op jit(solution)/shard_map/gradient_rows/ppermute | solution.py:414
  80.2 7.4 %all-to-all-done = f32[64,24,128]{2,1,0:T(8,128)S(1)} async-done(((f32[64,24,128]{2,1,0:T(8,128)}), f32[64,24,128]{2,1,0:T(8,128)S(1)}, u32[]{:S(2)}, u32[]{:S(2)}) %all-to-all-start) | async-done | bytes 786464 | tf_op jit(solution)/shard_map/probe_reduce/all_to_all | solution.py:405
  87.5 0.1 reduce_sum.9
  87.6 0.8 broadcast_in_dim.18
  88.5 18.1 %all-to-all-start.1 = ((f32[64,16,128]{2,1,0:T(8,128)}), f32[64,16,128]{2,1,0:T(8,128)S(1)}, u32[]{:S(2)}, u32[]{:S(2)}) async-start(f32[64,16,128]{2,1,0:T(8,128)} %broadcast_in_dim.18), calls=%async_computation.1 | async-start | bytes 1048576 | tf_op jit(solution)/shard_map/probe_gather/all_to_all | solution.py:418
  106.5 0.1 slice_reduce_fusion
  106.7 0.1 reshape_squeeze.3
  106.7 0.7 copy.30
  107.4 1.3 %maximum_add_fusion = f32[3,512,256]{2,1,0:T(8,128)S(1)} fusion(f32[1,512,256]{2,1,0:T(8,128)S(1)} %bitcast.23, f32[2,512,256]{2,1,0:T(8,128)S(1)} %copy-done, f32[3,512,128]{2,1,0:T(8,128)} %collective-permute-done.7, f32[3,512,128]{2,1,0:T(8,128)S(1)} %collective-permute-done.6), kind=kLoop, calls=%fused_computation | loop fusion | flops 1179648 | bytes 4718592 | tf_op jit(solution)/shard_map/gradient_rows/add | solution.py:412
  108.7 0.0 collective-permute-done.8
  108.7 0.0 collective-permute-done.9
  108.7 1.1 slice_add_fusion
  109.8 8.7 %all-to-all-done.1 = f32[64,16,128]{2,1,0:T(8,128)S(1)} async-done(((f32[64,16,128]{2,1,0:T(8,128)}), f32[64,16,128]{2,1,0:T(8,128)S(1)}, u32[]{:S(2)}, u32[]{:S(2)}) %all-to-all-start.1) | async-done | bytes 524320 | tf_op jit(solution)/shard_map/probe_gather/all_to_all | solution.py:418
  118.5 0.2 copy.27
  118.7 2.0 %collective-permute-start.11 = (f32[64,16,128]{2,0,1:T(8,128)S(1)}, f32[64,16,128]{2,0,1:T(8,128)S(1)}, u32[]{:S(2)}, u32[]{:S(2)}) collective-permute-start(f32[64,16,128]{2,0,1:T(8,128)S(1)} %copy.27), channel_id=1, source_target_pairs={{0,1},{1,0},{2,3},{3,2},{4,5},{5,4},{6,7},{7,6},{8,9},{9,8},{10,11... | collective-permute-start | bytes 1572872 | tf_op jit(solution)/shard_map/probe_gather/ppermute | solution.py:419
  120.7 0.8 slice_divide_fusion
  121.6 0.6 fusion.3
  123.5 0.0 collective-permute-done.11
  123.5 0.2 broadcast_select_fusion.1
  123.7 0.1 maximum_bitcast_fusion
  123.8 0.8 copy.29
  124.6 1.8 %reshape.35 = f32[2,2,256,256]{3,2,1,0:T(8,128)} reshape(f32[4,64,4,2,128]{4,3,2,1,0:T(2,128)S(1)} %copy.29) | data formatting | bytes 2097152 | tf_op jit(solution)/shard_map/probe_gather/reshape | solution.py:423
  (23 shorter events, 0.1 us)
Async XLA Ops:
  1.7 12.8 %collective-permute-start = (f32[2,128,256]{2,1,0:T(8,128)S(1)}, f32[2,128,256]{2,1,0:T(8,128)S(1)}, u32[]{:S(2)}, u32[]{:S(2)}) collective-permute-start(f32[2,128,256]{2,1,0:T(8,128)S(1)} %get-tuple-element.49), channel_id=1, source_target_pairs={{0,16},{16,32},{32,48},{48,64},{64,80},{80,96},{96,112},{1,17},{17... | collective-permute-start | bytes 786440 | tf_op jit(solution)/shard_map/object_halo/ppermute | solution.py:380
  5.8 16.1 %copy-start.9 = (s32[1,1,4,2]{2,3,1,0:T(2,128)S(1)}, s32[1,1,4,2]{2,3,1,0:T(2,128)}, u32[]{:S(2)}) copy-start(s32[1,1,4,2]{2,3,1,0:T(2,128)} %param.13) | copy-start | bytes 100
  5.8 8.8 %collective-permute-start.1 = (f32[2,128,256]{2,1,0:T(8,128)S(1)}, f32[2,128,256]{2,1,0:T(8,128)S(1)}, u32[]{:S(2)}, u32[]{:S(2)}) collective-permute-start(f32[2,128,256]{2,1,0:T(8,128)S(1)} %get-tuple-element.48), channel_id=1, source_target_pairs={{16,0},{32,16},{48,32},{64,48},{80,64},{96,80},{112,96},{17,1},{33... | collective-permute-start | bytes 786440 | tf_op jit(solution)/shard_map/object_halo/ppermute | solution.py:381
  8.1 19.4 %collective-permute-start.2 = (f32[2,256,128]{2,1,0:T(8,128)S(1)}, f32[2,256,128]{2,1,0:T(8,128)S(1)}, u32[]{:S(2)}, u32[]{:S(2)}) collective-permute-start(f32[2,256,128]{2,1,0:T(8,128)S(1)} %get-tuple-element.47), channel_id=1, source_target_pairs={{0,1},{1,2},{2,3},{3,4},{4,5},{5,6},{6,7},{7,8},{8,9},{9,10},{10,1... | collective-permute-start | bytes 786440 | tf_op jit(solution)/shard_map/object_halo/ppermute | solution.py:382
  12.5 15.0 %collective-permute-start.3 = (f32[2,256,128]{2,1,0:T(8,128)S(1)}, f32[2,256,128]{2,1,0:T(8,128)S(1)}, u32[]{:S(2)}, u32[]{:S(2)}) collective-permute-start(f32[2,256,128]{2,1,0:T(8,128)S(1)} %get-tuple-element.46), channel_id=1, source_target_pairs={{1,0},{2,1},{3,2},{4,3},{5,4},{6,5},{7,6},{8,7},{9,8},{10,9},{11,1... | collective-permute-start | bytes 786440 | tf_op jit(solution)/shard_map/object_halo/ppermute | solution.py:383
  14.5 13.0 %copy-start.4 = (f32[2,128,256]{2,1,0:T(8,128)}, f32[2,128,256]{2,1,0:T(8,128)S(1)}, u32[]{:S(2)}) copy-start(f32[2,128,256]{2,1,0:T(8,128)S(1)} %collective-permute-done.up) | copy-start | bytes 786436
  14.5 13.0 %copy-start.5 = (f32[2,128,256]{2,1,0:T(8,128)}, f32[2,128,256]{2,1,0:T(8,128)S(1)}, u32[]{:S(2)}) copy-start(f32[2,128,256]{2,1,0:T(8,128)S(1)} %collective-permute-done.1.down) | copy-start | bytes 786436
  14.6 13.0 %collective-permute-start.4 = (f32[2,2,128,128]{3,2,1,0:T(8,128)S(1)}, f32[2,2,128,128]{3,2,1,0:T(8,128)S(1)}, u32[]{:S(2)}, u32[]{:S(2)}) collective-permute-start(f32[2,2,128,128]{3,2,1,0:T(8,128)S(1)} %pad_maximum_fusion.2), channel_id=1, source_target_pairs={{0,1},{1,2},{2,3},{3,4},{4,5},{5,6},{6,7},{7,8},{8,9},{9,10},{10,1... | collective-permute-start | bytes 786440 | tf_op jit(solution)/shard_map/object_corners/ppermute | solution.py:386
  19.9 7.7 %collective-permute-start.5 = (f32[2,2,128,128]{3,2,1,0:T(8,128)S(1)}, f32[2,2,128,128]{3,2,1,0:T(8,128)S(1)}, u32[]{:S(2)}, u32[]{:S(2)}) collective-permute-start(f32[2,2,128,128]{3,2,1,0:T(8,128)S(1)} %pad_maximum_fusion.3), channel_id=1, source_target_pairs={{1,0},{2,1},{3,2},{4,3},{5,4},{6,5},{7,6},{8,7},{9,8},{10,9},{11,1... | collective-permute-start | bytes 786440 | tf_op jit(solution)/shard_map/object_corners/ppermute | solution.py:387
  27.5 0.7 copy-start.10
  27.5 0.8 copy-start.11
  27.6 0.9 copy-start.12
  27.6 0.9 copy-start.13
  28.5 19.9 %copy-start.7 = (f32[512,128]{1,0:T(8,128)S(1)}, f32[512,128]{1,0:T(8,128)}, u32[]{:S(2)}) copy-start(f32[512,128]{1,0:T(8,128)} %get-tuple-element.20) | copy-start | bytes 786436
  48.3 6.3 %copy-start.3 = (f32[2,512,128]{2,1,0:T(8,128)S(1)}, f32[2,512,128]{2,1,0:T(8,128)}, u32[]{:S(2)}) copy-start(f32[2,512,128]{2,1,0:T(8,128)} %get-tuple-element.21) | copy-start | bytes 1572868
  48.3 6.4 %copy-start.6 = (f32[512,128]{1,0:T(8,128)S(1)}, f32[512,128]{1,0:T(8,128)}, u32[]{:S(2)}) copy-start(f32[512,128]{1,0:T(8,128)} %get-tuple-element.22) | copy-start | bytes 786436
  48.3 9.2 %collective-permute-start.10 = (f32[64,24,128]{2,1,0:T(8,128)}, f32[64,24,128]{2,1,0:T(8,128)S(1)}, u32[]{:S(2)}, u32[]{:S(2)}) collective-permute-start(f32[64,24,128]{2,1,0:T(8,128)} %get-tuple-element.24), channel_id=1, source_target_pairs={{0,1},{1,0},{2,3},{3,2},{4,5},{5,4},{6,7},{7,6},{8,9},{9,8},{10,11... | collective-permute-start | bytes 2359304 | tf_op jit(solution)/shard_map/probe_reduce/ppermute | solution.py:404
  48.4 9.1 %copy-start.2 = (f32[64,24,128]{2,1,0:T(8,128)S(1)}, f32[64,24,128]{2,1,0:T(8,128)}, u32[]{:S(2)}) copy-start(f32[64,24,128]{2,1,0:T(8,128)} %get-tuple-element.23) | copy-start | bytes 2359300
  50.5 23.3 %collective-permute-start.6 = (f32[3,512,128]{2,1,0:T(8,128)}, f32[3,512,128]{2,1,0:T(8,128)S(1)}, u32[]{:S(2)}, u32[]{:S(2)}) collective-permute-start(f32[3,512,128]{2,1,0:T(8,128)} %pad_maximum_fusion), channel_id=1, source_target_pairs={{0,1},{1,2},{2,3},{3,4},{4,5},{5,6},{6,7},{7,8},{8,9},{9,10},{10,1... | collective-permute-start | bytes 2359304 | tf_op jit(solution)/shard_map/gradient_columns/ppermute | solution.py:397
  55.6 18.2 %collective-permute-start.7 = (f32[3,512,128]{2,1,0:T(8,128)}, f32[3,512,128]{2,1,0:T(8,128)}, u32[]{:S(2)}, u32[]{:S(2)}) collective-permute-start(f32[3,512,128]{2,1,0:T(8,128)} %pad_maximum_fusion.1), channel_id=1, source_target_pairs={{1,0},{2,1},{3,2},{4,3},{5,4},{6,5},{7,6},{8,7},{9,8},{10,9},{11,1... | collective-permute-start | bytes 2359304 | tf_op jit(solution)/shard_map/gradient_columns/ppermute | solution.py:398
  57.5 16.3 %copy-start = (f32[2,512,256]{2,1,0:T(8,128)S(1)}, f32[2,512,256]{2,1,0:T(8,128)}, u32[]{:S(2)}) copy-start(f32[2,512,256]{2,1,0:T(8,128)} %get-tuple-element.17) | copy-start | bytes 3145732
  57.5 16.3 %copy-start.1 = (f32[512,256]{1,0:T(8,128)S(1)}, f32[512,256]{1,0:T(8,128)}, u32[]{:S(2)}) copy-start(f32[512,256]{1,0:T(8,128)} %get-tuple-element.18) | copy-start | bytes 1572868
  58.5 29.0 %all-to-all-start = ((f32[64,24,128]{2,1,0:T(8,128)}), f32[64,24,128]{2,1,0:T(8,128)S(1)}, u32[]{:S(2)}, u32[]{:S(2)}) async-start(f32[64,24,128]{2,1,0:T(8,128)} %add.19), calls=%async_computation | async-start | bytes 1572864 | tf_op jit(solution)/shard_map/probe_reduce/all_to_all | solution.py:405
  75.8 30.7 %copy-start.8 = (f32[8,128]{1,0:T(8,128)S(1)}, f32[8,128]{1,0:T(8,128)}, u32[]{:S(2)}) copy-start(f32[8,128]{1,0:T(8,128)} %get-tuple-element.25) | copy-start | bytes 12292
  75.8 32.9 %collective-permute-start.8 = (f32[3,128,256]{2,1,0:T(8,128)}, f32[3,128,256]{2,1,0:T(8,128)S(1)}, u32[]{:S(2)}, u32[]{:S(2)}) collective-permute-start(f32[3,128,256]{2,1,0:T(8,128)} %get-tuple-element.42), channel_id=1, source_target_pairs={{0,16},{16,32},{32,48},{48,64},{64,80},{80,96},{96,112},{1,17},{17... | collective-permute-start | bytes 1179656 | tf_op jit(solution)/shard_map/gradient_rows/ppermute | solution.py:413
  78.9 29.8 %collective-permute-start.9 = (f32[3,128,256]{2,1,0:T(8,128)}, f32[3,128,256]{2,1,0:T(8,128)}, u32[]{:S(2)}, u32[]{:S(2)}) collective-permute-start(f32[3,128,256]{2,1,0:T(8,128)} %get-tuple-element.43), channel_id=1, source_target_pairs={{16,0},{32,16},{48,32},{64,48},{80,64},{96,80},{112,96},{17,1},{33... | collective-permute-start | bytes 1179656 | tf_op jit(solution)/shard_map/gradient_rows/ppermute | solution.py:414
  88.5 30.0 %all-to-all-start.1 = ((f32[64,16,128]{2,1,0:T(8,128)}), f32[64,16,128]{2,1,0:T(8,128)S(1)}, u32[]{:S(2)}, u32[]{:S(2)}) async-start(f32[64,16,128]{2,1,0:T(8,128)} %broadcast_in_dim.18), calls=%async_computation.1 | async-start | bytes 1048576 | tf_op jit(solution)/shard_map/probe_gather/all_to_all | solution.py:418
  118.7 4.8 %collective-permute-start.11 = (f32[64,16,128]{2,0,1:T(8,128)S(1)}, f32[64,16,128]{2,0,1:T(8,128)S(1)}, u32[]{:S(2)}, u32[]{:S(2)}) collective-permute-start(f32[64,16,128]{2,0,1:T(8,128)S(1)} %copy.27), channel_id=1, source_target_pairs={{0,1},{1,0},{2,3},{3,2},{4,5},{5,4},{6,7},{7,6},{8,9},{9,8},{10,11... | collective-permute-start | bytes 1572872 | tf_op jit(solution)/shard_map/probe_gather/ppermute | solution.py:419
where the time goes:
time: 128 us
  starting transfers between devices  64.7 us (51%)
  Pallas kernels  24.8 us (19%)
  waiting for transfers between devices  16.1 us (13%)
  other arithmetic  9.61 us (8%)
  local copies, waits for them, and re-layouts  8.85 us (7%)
  between operations  3.55 us (3%)
    pallas_call x1, Pallas kernels, compute(): pl.pallas_call(main_kernel, out_shape=[jax.ShapeDtypeStruct(s, F32) for s...  19.7 us
    all_to_all x1, starting transfers between devices, local(): lax.all_to_all(spread_out, AXES, 0, 0, axis_index_groups=groups, tiled=True)  18.1 us
    all_to_all x1, starting transfers between devices, local(): lax.all_to_all(chunk, AXES, 0, 0, axis_index_groups=groups, tiled=True)  15.2 us
    all_to_all x1, waiting for transfers between devices, local(): lax.all_to_all(spread_out, AXES, 0, 0, axis_index_groups=groups, tiled=True)  8.66 us
    all_to_all x1, waiting for transfers between devices, local(): lax.all_to_all(chunk, AXES, 0, 0, axis_index_groups=groups, tiled=True)  7.36 us
    ppermute x1, starting transfers between devices, local(): lax.ppermute(jnp.stack([up[:, :, HALF:], down[:, :, HALF:]]), 'col', col_up)  5.28 us
    pallas_call x1, Pallas kernels, prepare(): pl.pallas_call(prepare_kernel, out_shape=[jax.ShapeDtypeStruct(s, F32) fo...  5.03 us
    ppermute x1, starting transfers between devices, local(): left = lax.ppermute(object_tile[:, :, HALF:], 'col', col_up)  4.39 us
  transfers between devices with their start and end apart: 14, of which 2 were waited for; matrix products, arithmetic and copies ran while one was open for 10% of the time, Pallas kernels for 4%

commit v1 on v0

v1 whole, which is shorter than its diff:
```python
import jax
import jax.numpy as jnp
import ml_dtypes
import numpy as np
from jax import lax
from jax.experimental import pallas as pl
from jax.experimental.pallas import tpu as pltpu
from jax.sharding import PartitionSpec as P

intensity_floor = 0.1
object_damping = 1.0
small_value = 1e-06

SIZE = 256
HALF = 128
CHUNK = 32
UNIT = 88
BF = jnp.bfloat16
F32 = jnp.float32
AXES = ("row", "col")
VMEM_LIMIT = 56 * 2**20


def transform_matrices():
    n = np.arange(HALF)[:, None]
    q = np.arange(HALF)[None, :]
    out = []
    for odd in (0, 1):
        angle = -2.0 * np.pi * ((n * (2 * q + odd)) % SIZE) / SIZE
        re, im = np.cos(angle) / 16.0, np.sin(angle) / 16.0
        out.append(np.block([[re, im], [-im, re]]))
    return out


def split_np(matrix):
    high = matrix.astype(ml_dtypes.bfloat16)
    low = (matrix - high.astype(np.float64)).astype(ml_dtypes.bfloat16)
    return high, low


def constants():
    right_f, left_f, right_i, left_i = [], [], [], []
    for matrix in transform_matrices():
        high, low = split_np(matrix)
        right_f.append(np.concatenate([high, high, low], 0))
        left_f.append(np.concatenate([high.T, low.T, high.T], 1))
        right_i.append(np.concatenate([high.T, high.T, low.T], 0))
        left_i.append(np.concatenate([high, low, high], 1))
    return [np.stack(x) for x in (right_f, left_f, right_i, left_i)]


def permutation():
    order = np.concatenate([np.arange(0, SIZE, 2), np.arange(1, SIZE, 2)])
    onehot = np.zeros((SIZE, SIZE), np.float32)
    onehot[order, np.arange(SIZE)] = 1.0
    columns = np.concatenate([onehot] * 3, 0).astype(ml_dtypes.bfloat16)
    rows = np.concatenate([onehot.T] * 3, 1).astype(ml_dtypes.bfloat16)
    return columns, rows


def split2(value):
    high = value.astype(BF)
    return high, (value - high.astype(F32)).astype(BF)


def split3(value):
    high = value.astype(BF)
    rest = value - high.astype(F32)
    middle = rest.astype(BF)
    return high, middle, (rest - middle.astype(F32)).astype(BF)


def dot(a, b):
    return jnp.dot(a, b, preferred_element_type=F32)


def lane_index(rows):
    return lax.broadcasted_iota(jnp.int32, (rows, HALF), 1)


def spread(first, second, shift, lanes):
    a = pltpu.roll(first, shift, 1)
    b = pltpu.roll(second, shift, 1)
    wrapped = lanes < shift
    return jnp.where(wrapped, 0.0, a), jnp.where(wrapped, a, b), jnp.where(wrapped, b, 0.0)


def gather_lanes(blocks, shift, lanes):
    back = jnp.where(shift == 0, 0, HALF - shift)
    a, b, c = [pltpu.roll(x, back, 1) for x in blocks]
    inside = lanes < HALF - shift
    return jnp.where(inside, a, b), jnp.where(inside, b, c)


def fold8(value):
    return jnp.sum(value.reshape(-1, 8, HALF), axis=0)


def prepare_kernel(measured, cols, rows, permuted):
    for j in range(measured.shape[0]):
        moved = dot(jnp.concatenate(split3(measured[j]), 1), cols[...])
        permuted[j] = dot(rows[...], jnp.concatenate(split3(moved), 0))


def transform_kernel(
    starts, place, own, up, down, left, right, up_corner, down_corner, probe, measured,
    right_f, left_f, right_i, left_i,
    keep, send, object_part, patch,
    tile, totals, xs, zs, gs, ys, back, sums,
):
    step = pl.program_id(0)
    modes = probe.shape[0]
    lanes = lane_index(CHUNK)

    @pl.when(step == 0)
    def _():
        for p in range(2):
            for side, (strip, at) in enumerate(((left, 0), (right, 3))):
                tile[p, at, 0:128] = up_corner[side, p]
                tile[p, at, 128:384] = strip[p]
                tile[p, at, 384:512] = down_corner[side, p]
            for b in range(2):
                span = slice(b * HALF, (b + 1) * HALF)
                tile[p, 1 + b, 0:128] = up[p, :, span]
                tile[p, 1 + b, 128:384] = own[p, :, span]
                tile[p, 1 + b, 384:512] = down[p, :, span]
            tile[p, 4] = jnp.zeros((2 * SIZE, HALF), F32)
        totals[...] = jnp.zeros_like(totals)
        sums[...] = jnp.zeros_like(sums)

    row, col = starts[step, 0], starts[step, 1]
    base, shift = col // HALF, lax.rem(col, HALF)

    for i in range(0, SIZE, CHUNK):
        part = pl.ds(i, CHUNK)
        where = pl.ds(row + i, CHUNK)
        obj = []
        for p in range(2):
            blocks = [tile[p, base + b, where, :] for b in range(3)]
            obj.append(gather_lanes(blocks, shift, lanes))
            for b in range(2):
                patch[0, p, b, part, :] = obj[p][b]
        for m in range(modes):
            wave = []
            for b in range(2):
                span = slice(b * HALF, (b + 1) * HALF)
                pr, pi = probe[m, 0, part, span], probe[m, 1, part, span]
                wave.append((pr * obj[0][b] - pi * obj[1][b], pr * obj[1][b] + pi * obj[0][b]))
            for odd in range(2):
                for p in range(2):
                    high, low = split2(wave[0][p] - wave[1][p] if odd else wave[0][p] + wave[1][p])
                    at = pl.ds(m * SIZE + i, CHUNK)
                    xs[odd, at, p * HALF : (p + 1) * HALF] = high
                    xs[odd, at, SIZE + p * HALF : SIZE + (p + 1) * HALF] = low
                    xs[odd, at, 2 * SIZE + p * HALF : 2 * SIZE + (p + 1) * HALF] = high

    for odd in range(2):
        ys[odd] = dot(xs[odd], right_f[odd])

    for m in range(modes):
        for odd in range(2):
            lane_span = slice(odd * HALF, (odd + 1) * HALF)
            for i in range(0, HALF, CHUNK):
                top = ys[odd, pl.ds(m * SIZE + i, CHUNK), :]
                bottom = ys[odd, pl.ds(m * SIZE + HALF + i, CHUNK), :]
                for odd_row in range(2):
                    high, low = split2(top - bottom if odd_row else top + bottom)
                    for p in range(2):
                        span = slice(p * HALF, (p + 1) * HALF)
                        at = p * HALF + i
                        zs[m, odd_row, pl.ds(at, CHUNK), lane_span] = high[:, span]
                        zs[m, odd_row, pl.ds(SIZE + at, CHUNK), lane_span] = high[:, span]
                        zs[m, odd_row, pl.ds(2 * SIZE + at, CHUNK), lane_span] = low[:, span]

    error = jnp.zeros((8, HALF), F32)
    energy = jnp.zeros((8, HALF), F32)
    for odd_row in range(2):
        far = [dot(left_f[odd_row], zs[m, odd_row]) for m in range(modes)]
        for i in range(0, HALF, CHUNK):
            parts = [(f[i : i + CHUNK], f[HALF + i : HALF + i + CHUNK]) for f in far]
            intensity = parts[0][0] ** 2 + parts[0][1] ** 2 + (parts[1][0] ** 2 + parts[1][1] ** 2)
            intensity = jnp.maximum(intensity, intensity_floor)
            inverse = lax.rsqrt(intensity)
            modulus = intensity * inverse
            amplitude = measured[0, pl.ds(odd_row * HALF + i, CHUNK), :]
            factor = 1.0 - amplitude * inverse
            misfit = (modulus - amplitude) ** 2
            strength = amplitude**2
            error = error + fold8(misfit[:, :HALF]) + fold8(misfit[:, HALF:])
            energy = energy + fold8(strength[:, :HALF]) + fold8(strength[:, HALF:])
            for m in range(modes):
                for p in range(2):
                    high, low = split2(parts[m][p] * factor)
                    at = p * HALF + i
                    gs[m, odd_row, pl.ds(at, CHUNK), :] = high
                    gs[m, odd_row, pl.ds(SIZE + at, CHUNK), :] = high
                    gs[m, odd_row, pl.ds(2 * SIZE + at, CHUNK), :] = low
    sums[0] += error
    sums[1] += energy

    for m in range(modes):
        even = dot(left_i[0], gs[m, 0])
        odds = dot(left_i[1], gs[m, 1])
        for i in range(0, HALF, CHUNK):
            for p in range(2):
                a, b = even[p * HALF + i : p * HALF + i + CHUNK], odds[p * HALF + i : p * HALF + i + CHUNK]
                for bottom in range(2):
                    high, low = split2(a - b if bottom else a + b)
                    at = pl.ds(m * SIZE + bottom * HALF + i, CHUNK)
                    for odd in range(2):
                        span = slice(odd * HALF, (odd + 1) * HALF)
                        xs[odd, at, p * HALF : (p + 1) * HALF] = high[:, span]
                        xs[odd, at, SIZE + p * HALF : SIZE + (p + 1) * HALF] = low[:, span]
                        xs[odd, at, 2 * SIZE + p * HALF : 2 * SIZE + (p + 1) * HALF] = high[:, span]

    for odd in range(2):
        back[odd] = dot(xs[odd], right_i[odd])

    for i in range(0, SIZE, CHUNK):
        part = pl.ds(i, CHUNK)
        for b in range(2):
            re, im = patch[0, 0, b, part, :], patch[0, 1, b, part, :]
            span = slice(b * HALF, (b + 1) * HALF)
            grad_re, grad_im = 0.0, 0.0
            for m in range(modes):
                at = pl.ds(m * SIZE + i, CHUNK)
                even = [back[0, at, p * HALF : (p + 1) * HALF] for p in range(2)]
                odds = [back[1, at, p * HALF : (p + 1) * HALF] for p in range(2)]
                br, bi = [x - y if b else x + y for x, y in zip(even, odds)]
                pr, pi = probe[m, 0, part, span], probe[m, 1, part, span]
                grad_re = grad_re + (pr * br + pi * bi)
                grad_im = grad_im + (pr * bi - pi * br)
                totals[b, 2 * m, part, :] += re * br + im * bi
                totals[b, 2 * m + 1, part, :] += re * bi - im * br
            object_part[0, 0, b, part, :] = grad_re
            object_part[0, 1, b, part, :] = grad_im
            totals[b, 4, part, :] += re**2 + im**2

    @pl.when(step == pl.num_programs(0) - 1)
    def _():
        core, x, y = place[0], place[1], place[2]
        scalar = jnp.where(lax.broadcasted_iota(jnp.int32, (8, HALF), 1) == 0, jnp.sum(sums[0]), jnp.sum(sums[1]))
        for out, block in ((keep, core), (send, 1 - core)):
            for ry in range(4):
                for rx in range(4):
                    unit = 4 * lax.rem(y + ry, 4) + lax.rem(x + rx, 4)
                    at = UNIT * (4 * ry + rx)
                    for c in range(5):
                        source = pl.ds(pl.multiple_of(16 * unit, 16), 16)
                        out[at + 16 * c : at + 16 * c + 16, :] = totals[block, c, source, :]
                    out[at + 80 : at + 88, :] = scalar


def place_kernel(starts, object_part, patch, probe, center, left, right, steps, padded, power, accum):
    step = pl.program_id(0)
    lanes = lane_index(CHUNK)

    @pl.when(step == 0)
    def _():
        accum[...] = jnp.zeros_like(accum)
        padded[:, :, 0:8, :] = jnp.zeros((2, 2, 8, HALF), F32)
        padded[:, :, 264:272, :] = jnp.zeros((2, 2, 8, HALF), F32)
        for i in range(0, SIZE, CHUNK):
            part = pl.ds(i, CHUNK)
            total = probe[0, 0, part] ** 2 + probe[0, 1, part] ** 2
            power[part] = total + probe[1, 0, part] ** 2 + probe[1, 1, part] ** 2

    row, col = starts[step, 0], starts[step, 1]
    base, shift = col // HALF, lax.rem(col, HALF)
    for p in range(2):
        for b in range(2):
            padded[p, b, 8:264] = patch[0, p, b]

    first, last = lanes == 0, lanes == HALF - 1
    parts = [jnp.zeros((8, HALF), F32) for _ in range(4)]
    for i in range(0, SIZE, CHUNK):
        part = pl.ds(i, CHUNK)
        where = pl.ds(row + i, CHUNK)
        grads = [[object_part[0, p, b, part, :] for b in range(2)] for p in range(2)]
        strength = [power[part, :HALF], power[part, HALF:]]
        for p, pair in enumerate(grads + [strength]):
            moved = spread(pair[0], pair[1], shift, lanes)
            for b in range(3):
                accum[p, base + b, where, :] += moved[b]
        columns = []
        for p in range(2):
            obj = [patch[0, p, b, part, :] for b in range(2)]
            before = [pltpu.roll(x, 1, 1) for x in obj]
            after = [pltpu.roll(x, HALF - 1, 1) for x in obj]
            columns.append(
                (
                    jnp.where(last, after[1], after[0]) - jnp.where(first, 0.0, before[0]),
                    jnp.where(last, 0.0, after[1]) - jnp.where(first, before[0], before[1]),
                )
            )
        for b in range(2):
            rows = [padded[p, b, pl.ds(9 + i, CHUNK), :] - padded[p, b, pl.ds(7 + i, CHUNK), :] for p in range(2)]
            for d, slope in enumerate((rows, [columns[0][b], columns[1][b]])):
                parts[2 * d] = parts[2 * d] + fold8(grads[0][b] * slope[0] + grads[1][b] * slope[1])
                parts[2 * d + 1] = parts[2 * d + 1] + fold8(strength[b] * (slope[0] ** 2 + slope[1] ** 2))

    for d in range(2):
        numerator = 0.5 * jnp.sum(parts[2 * d], keepdims=True)
        denominator = 0.25 * jnp.sum(parts[2 * d + 1], keepdims=True) + small_value
        steps[pl.ds(2 * step + d, 1), :] = jnp.broadcast_to(-numerator / denominator, (1, HALF))

    @pl.when(step == pl.num_programs(0) - 1)
    def _():
        for p in range(3):
            left[p] = accum[p, 0]
            right[p] = accum[p, 3]
            center[p, :, :HALF] = accum[p, 1]
            center[p, :, HALF:] = accum[p, 2]


def assemble_kernel(place, mine, other, out):
    core, x, y = place[0], place[1], place[2]

    def write(source, block):
        for sy in range(4):
            for sx in range(4):
                unit = 4 * lax.rem(y + 4 - sy, 4) + lax.rem(x + 4 - sx, 4)
                target = pl.ds(pl.multiple_of(16 * unit, 16), 16)
                for c in range(4):
                    at = 64 * (4 * sy + sx) + 16 * c
                    out[c, target, block * HALF : (block + 1) * HALF] = source[at : at + 16, :]

    @pl.when(core == 0)
    def _():
        write(mine, 0)
        write(other, 1)

    @pl.when(core == 1)
    def _():
        write(mine, 1)
        write(other, 0)


def whole(*shape):
    return pl.BlockSpec(shape, lambda *_: (0,) * len(shape))


def stepped(*shape):
    return pl.BlockSpec((1, *shape), lambda i, *_: (i,) + (0,) * len(shape))


def shaped(shapes):
    return [jax.ShapeDtypeStruct(s, F32) for s in shapes]


def params():
    return pltpu.CompilerParams(vmem_limit_bytes=VMEM_LIMIT)


def cost(flops, size):
    return pl.CostEstimate(flops=flops, bytes_accessed=size, transcendentals=0)


def prepare(measured):
    cols, rows = permutation()
    return pl.pallas_call(
        prepare_kernel,
        out_shape=jax.ShapeDtypeStruct(measured.shape, F32),
        compiler_params=params(),
        cost_estimate=cost(1 << 30, 3 << 20),
    )(measured, jnp.asarray(cols), jnp.asarray(rows))


def transforms(starts, place, own, halo, probe, measured):
    mats = [jnp.asarray(x) for x in constants()]
    arrays = [own, *halo, probe]
    count = measured.shape[0]
    halves = (16 * UNIT, HALF)
    fields = (2, 2, SIZE, HALF)
    return pl.pallas_call(
        transform_kernel,
        out_shape=shaped([halves, halves, (count, *fields), (count, *fields)]),
        grid_spec=pltpu.PrefetchScalarGridSpec(
            num_scalar_prefetch=2,
            grid=(count,),
            in_specs=[whole(*x.shape) for x in arrays] + [stepped(SIZE, SIZE)] + [whole(*x.shape) for x in mats],
            out_specs=[whole(*halves), whole(*halves), stepped(*fields), stepped(*fields)],
            scratch_shapes=[
                pltpu.VMEM((2, 5, 2 * SIZE, HALF), F32),
                pltpu.VMEM((2, 5, SIZE, HALF), F32),
                pltpu.VMEM((2, 2 * SIZE, 3 * SIZE), BF),
                pltpu.VMEM((2, 2, 3 * SIZE, SIZE), BF),
                pltpu.VMEM((2, 2, 3 * SIZE, SIZE), BF),
                pltpu.VMEM((2, 2 * SIZE, SIZE), F32),
                pltpu.VMEM((2, 2 * SIZE, SIZE), F32),
                pltpu.VMEM((2, 8, HALF), F32),
            ],
        ),
        compiler_params=params(),
        cost_estimate=cost(13 << 30, 12 << 20),
    )(starts, place, *arrays, measured, *mats)


def place_parts(starts, object_part, patch, probe):
    count = patch.shape[0]
    fields = (2, 2, SIZE, HALF)
    shapes = [(3, 2 * SIZE, SIZE), (3, 2 * SIZE, HALF), (3, 2 * SIZE, HALF), (2 * count, HALF)]
    return pl.pallas_call(
        place_kernel,
        out_shape=shaped(shapes),
        grid_spec=pltpu.PrefetchScalarGridSpec(
            num_scalar_prefetch=1,
            grid=(count,),
            in_specs=[stepped(*fields), stepped(*fields), whole(*probe.shape)],
            out_specs=[whole(*s) for s in shapes],
            scratch_shapes=[
                pltpu.VMEM((2, 2, SIZE + 16, HALF), F32),
                pltpu.VMEM((SIZE, SIZE), F32),
                pltpu.VMEM((3, 5, 2 * SIZE, HALF), F32),
            ],
        ),
        compiler_params=params(),
        cost_estimate=cost(5 << 30, 8 << 20),
    )(starts, object_part, patch, probe)


def assemble(place, mine, other):
    shape = (4, SIZE, SIZE)
    return pl.pallas_call(
        assemble_kernel,
        out_shape=jax.ShapeDtypeStruct(shape, F32),
        grid_spec=pltpu.PrefetchScalarGridSpec(
            num_scalar_prefetch=1,
            grid=(),
            in_specs=[whole(*mine.shape), whole(*other.shape)],
            out_specs=whole(*shape),
        ),
        compiler_params=params(),
        cost_estimate=cost(1 << 20, 2 << 20),
    )(place, mine, other)


def neighbours(axis):
    up = [(i, i + 1) for i in range(lax.axis_size(axis) - 1)]
    return up, [(j, i) for i, j in up]


def chips(index):
    row, col = divmod(index, 16)
    return [col // 4, row % 4, 2 * (row // 4) + col // 2 % 2, col % 2]


def device(x, y, z, core):
    return (4 * (z // 2) + y) * 16 + 4 * x + 2 * (z % 2) + core


def along(value, dim, distance):
    pairs = []
    for source in range(lax.axis_size("row") * lax.axis_size("col")):
        target = chips(source)
        target[dim] = (target[dim] + distance) % (2 if dim == 3 else 4)
        pairs.append((source, device(*target)))
    return lax.ppermute(value, AXES, pairs)


def others(pieces, dim):
    return [pieces[0]] + [along(pieces[d], dim, d) for d in (1, 2, 3)]


def total_of(values):
    return (values[0] + values[1]) + (values[2] + values[3])


def local(object_tile, probe, amplitudes, offsets):
    starts = offsets[0, 0]
    measured = amplitudes[0, 0]
    row_up, row_down = neighbours("row")
    col_up, col_down = neighbours("col")
    row_index, col_index = lax.axis_index("row"), lax.axis_index("col")
    place = jnp.stack([lax.rem(col_index, 2), lax.div(col_index, 4), lax.rem(row_index, 4)])

    with jax.named_scope("object_halo"):
        left = lax.ppermute(object_tile[:, :, HALF:], "col", col_up)
        right = lax.ppermute(object_tile[:, :, :HALF], "col", col_down)
        up = lax.ppermute(object_tile[:, HALF:], "row", row_up)
        down = lax.ppermute(object_tile[:, :HALF], "row", row_down)
    permuted = prepare(measured)
    with jax.named_scope("object_corners"):
        left, right, permuted = lax.optimization_barrier((left, right, permuted))
        up_corner = lax.ppermute(jnp.stack([left[:, HALF:], right[:, HALF:]]), "row", row_up)
        down_corner = lax.ppermute(jnp.stack([left[:, :HALF], right[:, :HALF]]), "row", row_down)

    halo = [up, down, left, right, up_corner, down_corner]
    keep, send, object_part, patch = transforms(starts, place, object_tile, halo, probe, permuted)

    with jax.named_scope("probe_reduce"):
        chunk = keep + along(send, 3, 1)
        chunk, object_part = lax.optimization_barrier((chunk, object_part))
        chunk = total_of(others(jnp.split(chunk, 4), 1))

    parts = place_parts(starts, object_part, patch, probe)
    chunk, (center, grad_left, grad_right, steps) = lax.optimization_barrier((chunk, parts))

    with jax.named_scope("gradient_columns"):
        from_left = lax.ppermute(grad_right, "col", col_up)
        from_right = lax.ppermute(grad_left, "col", col_down)

    with jax.named_scope("probe_sum"):
        chunk = total_of(others(jnp.split(chunk, 4), 0))
        chunk = total_of([chunk] + [along(chunk, 2, d) for d in (1, 2, 3)])
        quotient = (chunk[:64].reshape(4, 16, HALF) / chunk[64:80]).reshape(64, HALF)
        relative_error = (chunk[80, 0] / chunk[80, 1]).reshape(1)

    with jax.named_scope("gradient_rows"):
        fields = center + jnp.concatenate([from_left, from_right], 2)
        quotient, fields = lax.optimization_barrier((quotient, fields))
        from_above = lax.ppermute(fields[:, SIZE + HALF :], "row", row_up)
        from_below = lax.ppermute(fields[:, :HALF], "row", row_down)

    with jax.named_scope("probe_gather"):
        quotient = jnp.concatenate(others([quotient] * 4, 0))
        quotient = jnp.concatenate(others([quotient] * 4, 1))

    with jax.named_scope("object_update"):
        combined = fields[:, HALF : HALF + SIZE] + jnp.concatenate([from_above, from_below], 1)
        object_update = combined[:2] / (combined[2:] + object_damping)
        quotient, object_update = lax.optimization_barrier((quotient, object_update))

    probe_update = assemble(place, quotient, along(quotient, 3, 1)).reshape(probe.shape)
    position_step = steps[:, 0].reshape(1, 1, -1, 2)
    return (object_update, probe_update, position_step, relative_error)


def solution(mesh):
    in_specs = (
        P(None, "row", "col"),
        P(),
        P("row", "col", None, None, None),
        P("row", "col", None, None),
    )
    out_specs = (P(None, "row", "col"), P(), P("row", "col", None, None), P())
    return jax.shard_map(local, mesh=mesh, in_specs=in_specs, out_specs=out_specs, check_vma=False)
```

time: 128 us -> 138 us (1.078)
  the two profiles are of different devices: /device:TPU:1 before, /device:TPU:25 now
where the time goes in v1:
time: 138 us
  starting transfers between devices  57.8 us (42%)
  waiting for transfers between devices  35.2 us (26%)
  Pallas kernels  32 us (23%)
  local copies, waits for them, and re-layouts  5.98 us (4%)
  between operations  3.51 us (3%)
  other arithmetic  3.04 us (2%)
    ppermute x17, starting transfers between devices, along(): return lax.ppermute(value, AXES, pairs)  25.1 us
    ppermute x17, waiting for transfers between devices, along(): return lax.ppermute(value, AXES, pairs)  23.3 us
    pallas_call x1, Pallas kernels, transforms(): pl.pallas_call(transform_kernel, out_shape=shaped([halves, halves, (count...  17.6 us
    pallas_call x1, Pallas kernels, place_parts(): pl.pallas_call(place_kernel, out_shape=shaped(shapes), grid_spec=pltpu.Pr...  7.85 us
    ppermute x1, starting transfers between devices, local(): up = lax.ppermute(object_tile[:, HALF:], 'row', row_up)  6.52 us
    ppermute x1, waiting for transfers between devices, local(): lax.ppermute(jnp.stack([left[:, :HALF], right[:, :HALF]]), 'row', row_down)  5.57 us
    ppermute x1, starting transfers between devices, local(): from_left = lax.ppermute(grad_right, 'col', col_up)  4.33 us
    ppermute x1, starting transfers between devices, local(): from_above = lax.ppermute(fields[:, SIZE + HALF:], 'row', row_up)  4.31 us
  transfers between devices with their start and end apart: 27, of which 12 were waited for; matrix products, arithmetic and copies ran while one was open for 3% of the time, Pallas kernels for 8%

profile of v1, /device:TPU:25, one launch (start us, length us, event | category | flops | bytes accessed | tf_op | source)
XLA Modules:
  0.0 137.5 jit_solution(2053845621634100156)
XLA Ops:
  0.6 1.1 fusion.3
  1.7 2.6 %collective-permute-start.3 = (f32[2,256,128]{2,1,0:T(8,128)S(1)}, f32[2,256,128]{2,1,0:T(8,128)S(1)}, u32[]{:S(2)}, u32[]{:S(2)}) collective-permute-start(f32[2,256,128]{2,1,0:T(8,128)S(1)} %get-tuple-element.61), channel_id=1, source_target_pairs={{1,0},{2,1},{3,2},{4,3},{5,4},{6,5},{7,6},{8,7},{9,8},{10,9},{11,1... | collective-permute-start | bytes 786440 | tf_op jit(solution)/shard_map/object_halo/ppermute | solution.py:479
  4.3 3.4 %collective-permute-start.2 = (f32[2,256,128]{2,1,0:T(8,128)S(1)}, f32[2,256,128]{2,1,0:T(8,128)S(1)}, u32[]{:S(2)}, u32[]{:S(2)}) collective-permute-start(f32[2,256,128]{2,1,0:T(8,128)S(1)} %get-tuple-element.62), channel_id=1, source_target_pairs={{0,1},{1,2},{2,3},{3,4},{4,5},{5,6},{6,7},{7,8},{8,9},{9,10},{10,1... | collective-permute-start | bytes 786440 | tf_op jit(solution)/shard_map/object_halo/ppermute | solution.py:478
  7.7 1.1 fusion.4
  8.8 2.4 %collective-permute-start.1 = (f32[2,128,256]{2,1,0:T(8,128)S(1)}, f32[2,128,256]{2,1,0:T(8,128)S(1)}, u32[]{:S(2)}, u32[]{:S(2)}) collective-permute-start(f32[2,128,256]{2,1,0:T(8,128)S(1)} %get-tuple-element.63), channel_id=1, source_target_pairs={{16,0},{32,16},{48,32},{64,48},{80,64},{96,80},{112,96},{17,1},{33... | collective-permute-start | bytes 786440 | tf_op jit(solution)/shard_map/object_halo/ppermute | solution.py:481
  11.2 6.5 %collective-permute-start = (f32[2,128,256]{2,1,0:T(8,128)S(1)}, f32[2,128,256]{2,1,0:T(8,128)S(1)}, u32[]{:S(2)}, u32[]{:S(2)}) collective-permute-start(f32[2,128,256]{2,1,0:T(8,128)S(1)} %get-tuple-element.64), channel_id=1, source_target_pairs={{0,16},{16,32},{32,48},{48,64},{64,80},{80,96},{96,112},{1,17},{17... | collective-permute-start | bytes 786440 | tf_op jit(solution)/shard_map/object_halo/ppermute | solution.py:480
  17.7 3.7 %shard_map.129.measured = f32[4,256,256]{2,1,0:T(8,128)} custom-call(f32[4,256,256]{2,1,0:T(8,128)} %bitcast.21, bf16[768,256]{1,0:T(8,128)(2,1)} %constant.35.clone.cols, bf16[256,768]{1,0:T(8,128)(2,1)} %constant.36.clone.rows), custom_call_target="tpu_custom_call" | custom-call | flops 1073741824 | bytes 3145728 | tf_op jit(solution)/shard_map/pallas_call | solution.py:361
  21.5 1.9 %collective-permute-start.4 = (f32[2,2,128,128]{3,2,1,0:T(8,128)S(1)}, f32[2,2,128,128]{3,2,1,0:T(8,128)S(1)}, u32[]{:S(2)}, u32[]{:S(2)}) collective-permute-start(f32[2,2,128,128]{3,2,1,0:T(8,128)S(1)} %pad_maximum_fusion), channel_id=1, source_target_pairs={{0,16},{16,32},{32,48},{48,64},{64,80},{80,96},{96,112},{1,17},{17... | collective-permute-start | bytes 786440 | tf_op jit(solution)/shard_map/object_corners/ppermute | solution.py:485
  23.5 3.4 %collective-permute-start.5 = (f32[2,2,128,128]{3,2,1,0:T(8,128)S(1)}, f32[2,2,128,128]{3,2,1,0:T(8,128)S(1)}, u32[]{:S(2)}, u32[]{:S(2)}) collective-permute-start(f32[2,2,128,128]{3,2,1,0:T(8,128)S(1)} %pad_maximum_fusion.1), channel_id=1, source_target_pairs={{16,0},{32,16},{48,32},{64,48},{80,64},{96,80},{112,96},{17,1},{33... | collective-permute-start | bytes 786440 | tf_op jit(solution)/shard_map/object_corners/ppermute | solution.py:486
  26.9 0.7 copy.17.starts
  27.5 0.6 pad_add_fusion.place
  28.1 0.0 copy-start.8
  28.2 3.6 %collective-permute-done.4.up_corner = f32[2,2,128,128]{3,2,1,0:T(8,128)S(1)} collective-permute-done((f32[2,2,128,128]{3,2,1,0:T(8,128)S(1)}, f32[2,2,128,128]{3,2,1,0:T(8,128)S(1)}, u32[]{:S(2)}, u32[]{:S(2)}) %collective-permute-start.4) | collective-permute-done | bytes 262176 | tf_op jit(solution)/shard_map/object_corners/ppermute | solution.py:485
  31.7 5.6 %collective-permute-done.5.down_corner = f32[2,2,128,128]{3,2,1,0:T(8,128)S(1)} collective-permute-done((f32[2,2,128,128]{3,2,1,0:T(8,128)S(1)}, f32[2,2,128,128]{3,2,1,0:T(8,128)S(1)}, u32[]{:S(2)}, u32[]{:S(2)}) %collective-permute-start.5) | collective-permute-done | bytes 262176 | tf_op jit(solution)/shard_map/object_corners/ppermute | solution.py:486
  37.3 0.7 copy-done.10
  38.0 17.6 %shard_map.130 = (f32[1408,128]{1,0:T(8,128)}, f32[1408,128]{1,0:T(8,128)}, f32[4,2,2,256,128]{4,3,2,1,0:T(8,128)}, f32[4,2,2,256,128]{4,3,2,1,0:T(8,128)}) custom-call(s32[4,2]{1,0:T(4,128)} %copy.17.starts, s32[3]{0:T(128)} %pad_add_fusion.place, f32[2,256,256]{2,1,0:T(8,128)} %own.1, f32[2,128,256]{2,1,0:T(8,128)} %copy-done.8, f32[2,128,256]{2,1,0:T(8,128)} %copy-done.7, ...), custom_call_target="tpu_custom_call" | custom-call | flops 13958643712 | bytes 12582912 | tf_op jit(solution)/shard_map/pallas_call | solution.py:375
  55.6 0.4 collective-permute-start.6
  56.0 2.0 %collective-permute-done.6 = f32[1408,128]{1,0:T(8,128)S(1)} collective-permute-done((f32[1408,128]{1,0:T(8,128)}, f32[1408,128]{1,0:T(8,128)S(1)}, u32[]{:S(2)}, u32[]{:S(2)}) %collective-permute-start.6) | collective-permute-done | bytes 720928 | tf_op jit(solution)/shard_map/probe_reduce/ppermute | solution.py:458
  58.1 1.2 add.42
  59.3 0.1 collective-permute-start.7
  59.4 1.5 %collective-permute-start.9 = (f32[352,128]{1,0:T(8,128)S(1)}, f32[352,128]{1,0:T(8,128)S(1)}, u32[]{:S(2)}, u32[]{:S(2)}) collective-permute-start(f32[352,128]{1,0:T(8,128)S(1)} %get-tuple-element.59), channel_id=1, source_target_pairs={{0,48},{1,49},{2,50},{3,51},{4,52},{5,53},{6,54},{7,55},{8,56},{9,... | collective-permute-start | bytes 540680 | tf_op jit(solution)/shard_map/probe_reduce/ppermute | solution.py:458
  60.8 0.0 collective-permute-start.8
  60.8 7.8 %shard_map.131 = (f32[3,512,256]{2,1,0:T(8,128)}, f32[3,512,128]{2,1,0:T(8,128)}, f32[3,512,128]{2,1,0:T(8,128)}, f32[8,128]{1,0:T(8,128)}) custom-call(s32[4,2]{1,0:T(4,128)} %copy.17.starts, f32[4,2,2,256,128]{4,3,2,1,0:T(8,128)} %get-tuple-element.33.object_part, f32[4,2,2,256,128]{4,3,2,1,0:T(8,128)} %get-tuple-element.34.patch, f32[2,2,256,256]{3,2,1,0:T(8,128)} %probe.3), custom_call_target="tpu_custom_call" | custom-call | flops 5368709120 | bytes 8388608 | tf_op jit(solution)/shard_map/pallas_call | solution.py:403
  68.7 1.6 %collective-permute-done.9 = f32[352,128]{1,0:T(8,128)S(1)} collective-permute-done((f32[352,128]{1,0:T(8,128)S(1)}, f32[352,128]{1,0:T(8,128)S(1)}, u32[]{:S(2)}, u32[]{:S(2)}) %collective-permute-start.9) | collective-permute-done | bytes 180256 | tf_op jit(solution)/shard_map/probe_reduce/ppermute | solution.py:458
  70.3 0.0 collective-permute-done.8
  70.3 4.3 %collective-permute-start.16 = (f32[3,512,128]{2,1,0:T(8,128)}, f32[3,512,128]{2,1,0:T(8,128)S(1)}, u32[]{:S(2)}, u32[]{:S(2)}) collective-permute-start(f32[3,512,128]{2,1,0:T(8,128)} %get-tuple-element.41), channel_id=1, source_target_pairs={{0,1},{1,2},{2,3},{3,4},{4,5},{5,6},{6,7},{7,8},{8,9},{9,10},{10,1... | collective-permute-start | bytes 2359304 | tf_op jit(solution)/shard_map/gradient_columns/ppermute | solution.py:500
  74.7 1.9 %collective-permute-start.17 = (f32[3,512,128]{2,1,0:T(8,128)}, f32[3,512,128]{2,1,0:T(8,128)S(1)}, u32[]{:S(2)}, u32[]{:S(2)}) collective-permute-start(f32[3,512,128]{2,1,0:T(8,128)} %get-tuple-element.42), channel_id=1, source_target_pairs={{1,0},{2,1},{3,2},{4,3},{5,4},{6,5},{7,6},{8,7},{9,8},{10,9},{11,1... | collective-permute-start | bytes 2359304 | tf_op jit(solution)/shard_map/gradient_columns/ppermute | solution.py:501
  76.6 1.3 collective-permute-start.10
  77.9 1.5 %collective-permute-start.12 = (f32[88,128]{1,0:T(8,128)S(1)}, f32[88,128]{1,0:T(8,128)S(1)}, u32[]{:S(2)}, u32[]{:S(2)}) collective-permute-start(f32[88,128]{1,0:T(8,128)S(1)} %get-tuple-element.70), channel_id=1, source_target_pairs={{0,12},{1,13},{2,14},{3,15},{4,0},{5,1},{6,2},{7,3},{8,4},{9,5},{1... | collective-permute-start | bytes 135176 | tf_op jit(solution)/shard_map/probe_sum/ppermute | solution.py:458
  79.4 1.5 %collective-permute-start.11 = (f32[88,128]{1,0:T(8,128)S(1)}, f32[88,128]{1,0:T(8,128)S(1)}, u32[]{:S(2)}, u32[]{:S(2)}) collective-permute-start(f32[88,128]{1,0:T(8,128)S(1)} %get-tuple-element.71), channel_id=1, source_target_pairs={{0,8},{1,9},{2,10},{3,11},{4,12},{5,13},{6,14},{7,15},{8,0},{9,1},... | collective-permute-start | bytes 135176 | tf_op jit(solution)/shard_map/probe_sum/ppermute | solution.py:458
  80.9 0.0 collective-permute-done.10
  80.9 0.1 collective-permute-done.12
  81.0 3.2 %collective-permute-done.11 = f32[88,128]{1,0:T(8,128)S(1)} collective-permute-done((f32[88,128]{1,0:T(8,128)S(1)}, f32[88,128]{1,0:T(8,128)S(1)}, u32[]{:S(2)}, u32[]{:S(2)}) %collective-permute-start.11) | collective-permute-done | bytes 45088 | tf_op jit(solution)/shard_map/probe_sum/ppermute | solution.py:458
  84.2 3.9 %collective-permute-start.15 = (f32[88,128]{1,0:T(8,128)S(1)}, f32[88,128]{1,0:T(8,128)S(1)}, u32[]{:S(2)}, u32[]{:S(2)}) collective-permute-start(f32[88,128]{1,0:T(8,128)S(1)} %add_add_fusion.2), channel_id=1, source_target_pairs={{0,66},{1,67},{2,0},{3,1},{4,70},{5,71},{6,4},{7,5},{8,74},{9,75},... | collective-permute-start | bytes 135176 | tf_op jit(solution)/shard_map/probe_sum/ppermute | solution.py:458
  88.1 3.5 %collective-permute-start.14 = (f32[88,128]{1,0:T(8,128)S(1)}, f32[88,128]{1,0:T(8,128)S(1)}, u32[]{:S(2)}, u32[]{:S(2)}) collective-permute-start(f32[88,128]{1,0:T(8,128)S(1)} %add_add_fusion.2), channel_id=1, source_target_pairs={{0,64},{1,65},{2,66},{3,67},{4,68},{5,69},{6,70},{7,71},{8,72},{9,... | collective-permute-start | bytes 135176 | tf_op jit(solution)/shard_map/probe_sum/ppermute | solution.py:458
  91.6 0.0 collective-permute-start.13
  91.6 0.0 collective-permute-done.15
  91.6 1.8 %collective-permute-done.14 = f32[88,128]{1,0:T(8,128)S(1)} collective-permute-done((f32[88,128]{1,0:T(8,128)S(1)}, f32[88,128]{1,0:T(8,128)S(1)}, u32[]{:S(2)}, u32[]{:S(2)}) %collective-permute-start.14) | collective-permute-done | bytes 45088 | tf_op jit(solution)/shard_map/probe_sum/ppermute | solution.py:458
  93.5 2.7 %collective-permute-done.13 = f32[88,128]{1,0:T(8,128)S(1)} collective-permute-done((f32[88,128]{1,0:T(8,128)S(1)}, f32[88,128]{1,0:T(8,128)S(1)}, u32[]{:S(2)}, u32[]{:S(2)}) %collective-permute-start.13) | collective-permute-done | bytes 45088 | tf_op jit(solution)/shard_map/probe_sum/ppermute | solution.py:458
  96.3 0.0 collective-permute-done.16
  96.3 0.0 collective-permute-done.17
  96.3 0.2 maximum_add_fusion
  96.5 1.0 collective-permute-start.20
  97.4 0.6 collective-permute-start.19
  98.1 0.8 collective-permute-start.18
  98.8 3.2 %collective-permute-done.18 = f32[64,128]{1,0:T(8,128)S(1)} collective-permute-done((f32[64,128]{1,0:T(8,128)S(1)}, f32[64,128]{1,0:T(8,128)S(1)}, u32[]{:S(2)}, u32[]{:S(2)}) %collective-permute-start.18) | collective-permute-done | bytes 32800 | tf_op jit(solution)/shard_map/probe_gather/ppermute | solution.py:458
  102.1 1.2 collective-permute-start.21
  103.2 0.1 fusion.1
  103.3 4.3 %collective-permute-start.24 = (f32[3,128,256]{2,1,0:T(8,128)S(1)}, f32[3,128,256]{2,1,0:T(8,128)S(1)}, u32[]{:S(2)}, u32[]{:S(2)}) collective-permute-start(f32[3,128,256]{2,1,0:T(8,128)S(1)} %get-tuple-element.56), channel_id=1, source_target_pairs={{0,16},{16,32},{32,48},{48,64},{64,80},{80,96},{96,112},{1,17},{17... | collective-permute-start | bytes 1179656 | tf_op jit(solution)/shard_map/gradient_rows/ppermute | solution.py:512
  107.6 1.9 %collective-permute-start.25 = (f32[3,128,256]{2,1,0:T(8,128)S(1)}, f32[3,128,256]{2,1,0:T(8,128)S(1)}, u32[]{:S(2)}, u32[]{:S(2)}) collective-permute-start(f32[3,128,256]{2,1,0:T(8,128)S(1)} %get-tuple-element.57), channel_id=1, source_target_pairs={{16,0},{32,16},{48,32},{64,48},{80,64},{96,80},{112,96},{17,1},{33... | collective-permute-start | bytes 1179656 | tf_op jit(solution)/shard_map/gradient_rows/ppermute | solution.py:513
  109.5 0.1 collective-permute-start.22
  109.6 0.1 collective-permute-start.23
  109.8 6.4 %collective-permute-done.22 = f32[256,128]{1,0:T(8,128)S(1)} collective-permute-done((f32[256,128]{1,0:T(8,128)S(1)}, f32[256,128]{1,0:T(8,128)S(1)}, u32[]{:S(2)}, u32[]{:S(2)}) %collective-permute-start.22) | collective-permute-done | bytes 131104 | tf_op jit(solution)/shard_map/probe_gather/ppermute | solution.py:458
  116.1 2.3 %collective-permute-done.23 = f32[256,128]{1,0:T(8,128)S(1)} collective-permute-done((f32[256,128]{1,0:T(8,128)S(1)}, f32[256,128]{1,0:T(8,128)S(1)}, u32[]{:S(2)}, u32[]{:S(2)}) %collective-permute-start.23) | collective-permute-done | bytes 131104 | tf_op jit(solution)/shard_map/probe_gather/ppermute | solution.py:458
  118.4 2.7 %collective-permute-done.25 = f32[3,128,256]{2,1,0:T(8,128)S(1)} collective-permute-done((f32[3,128,256]{2,1,0:T(8,128)S(1)}, f32[3,128,256]{2,1,0:T(8,128)S(1)}, u32[]{:S(2)}, u32[]{:S(2)}) %collective-permute-start.25) | collective-permute-done | bytes 393248 | tf_op jit(solution)/shard_map/gradient_rows/ppermute | solution.py:513
  121.2 0.1 maximum_add_fusion.1
  121.3 0.8 slice_divide_fusion
  122.1 7.7 %collective-permute-start.26 = (f32[1024,128]{1,0:T(8,128)S(1)}, f32[1024,128]{1,0:T(8,128)S(1)}, u32[]{:S(2)}, u32[]{:S(2)}) collective-permute-start(f32[1024,128]{1,0:T(8,128)S(1)} %constant_dynamic-update-slice_fusion.4.mine), channel_id=1, source_target_pairs={{0,1},{1,0},{2,3},{3,2},{4,5},{5,4},{6,7},{7,6},{8,9},{9,8},{10,11... | collective-permute-start | bytes 1572872 | tf_op jit(solution)/shard_map/ppermute | solution.py:458
  129.9 0.1 slice_reduce_fusion
  130.0 0.1 reshape_squeeze.3
  130.1 0.7 copy.19
  130.7 0.6 fusion.6
  132.7 0.8 copy-done.2
  133.5 2.9 %shard_map.132 = f32[4,256,256]{2,1,0:T(8,128)} custom-call(s32[3]{0:T(128)} %pad_add_fusion.place, f32[1024,128]{1,0:T(8,128)} %copy-done.1, f32[1024,128]{1,0:T(8,128)} %copy-done.2), custom_call_target="tpu_custom_call" | custom-call | flops 1048576 | bytes 2097152 | tf_op jit(solution)/shard_map/pallas_call | solution.py:424
  (47 shorter events, 0.3 us)
Async XLA Ops:
  1.7 19.7 %collective-permute-start.3 = (f32[2,256,128]{2,1,0:T(8,128)S(1)}, f32[2,256,128]{2,1,0:T(8,128)S(1)}, u32[]{:S(2)}, u32[]{:S(2)}) collective-permute-start(f32[2,256,128]{2,1,0:T(8,128)S(1)} %get-tuple-element.61), channel_id=1, source_target_pairs={{1,0},{2,1},{3,2},{4,3},{5,4},{6,5},{7,6},{8,7},{9,8},{10,9},{11,1... | collective-permute-start | bytes 786440 | tf_op jit(solution)/shard_map/object_halo/ppermute | solution.py:479
  4.3 17.1 %collective-permute-start.2 = (f32[2,256,128]{2,1,0:T(8,128)S(1)}, f32[2,256,128]{2,1,0:T(8,128)S(1)}, u32[]{:S(2)}, u32[]{:S(2)}) collective-permute-start(f32[2,256,128]{2,1,0:T(8,128)S(1)} %get-tuple-element.62), channel_id=1, source_target_pairs={{0,1},{1,2},{2,3},{3,4},{4,5},{5,6},{6,7},{7,8},{8,9},{9,10},{10,1... | collective-permute-start | bytes 786440 | tf_op jit(solution)/shard_map/object_halo/ppermute | solution.py:478
  8.8 19.3 %collective-permute-start.1 = (f32[2,128,256]{2,1,0:T(8,128)S(1)}, f32[2,128,256]{2,1,0:T(8,128)S(1)}, u32[]{:S(2)}, u32[]{:S(2)}) collective-permute-start(f32[2,128,256]{2,1,0:T(8,128)S(1)} %get-tuple-element.63), channel_id=1, source_target_pairs={{16,0},{32,16},{48,32},{64,48},{80,64},{96,80},{112,96},{17,1},{33... | collective-permute-start | bytes 786440 | tf_op jit(solution)/shard_map/object_halo/ppermute | solution.py:481
  11.2 16.9 %collective-permute-start = (f32[2,128,256]{2,1,0:T(8,128)S(1)}, f32[2,128,256]{2,1,0:T(8,128)S(1)}, u32[]{:S(2)}, u32[]{:S(2)}) collective-permute-start(f32[2,128,256]{2,1,0:T(8,128)S(1)} %get-tuple-element.64), channel_id=1, source_target_pairs={{0,16},{16,32},{32,48},{48,64},{64,80},{80,96},{96,112},{1,17},{17... | collective-permute-start | bytes 786440 | tf_op jit(solution)/shard_map/object_halo/ppermute | solution.py:480
  21.4 5.4 %copy-start.6 = (s32[1,1,4,2]{2,3,1,0:T(2,128)S(1)}, s32[1,1,4,2]{2,3,1,0:T(2,128)}, u32[]{:S(2)}) copy-start(s32[1,1,4,2]{2,3,1,0:T(2,128)} %param.13) | copy-start | bytes 100
  21.4 15.9 %copy-start.3 = (f32[2,256,128]{2,1,0:T(8,128)}, f32[2,256,128]{2,1,0:T(8,128)S(1)}, u32[]{:S(2)}) copy-start(f32[2,256,128]{2,1,0:T(8,128)S(1)} %collective-permute-done.3.right) | copy-start | bytes 786436
  21.4 15.9 %copy-start.4 = (f32[2,256,128]{2,1,0:T(8,128)}, f32[2,256,128]{2,1,0:T(8,128)S(1)}, u32[]{:S(2)}) copy-start(f32[2,256,128]{2,1,0:T(8,128)S(1)} %collective-permute-done.2.left) | copy-start | bytes 786436
  21.5 10.2 %collective-permute-start.4 = (f32[2,2,128,128]{3,2,1,0:T(8,128)S(1)}, f32[2,2,128,128]{3,2,1,0:T(8,128)S(1)}, u32[]{:S(2)}, u32[]{:S(2)}) collective-permute-start(f32[2,2,128,128]{3,2,1,0:T(8,128)S(1)} %pad_maximum_fusion), channel_id=1, source_target_pairs={{0,16},{16,32},{32,48},{48,64},{64,80},{80,96},{96,112},{1,17},{17... | collective-permute-start | bytes 786440 | tf_op jit(solution)/shard_map/object_corners/ppermute | solution.py:485
  23.5 13.8 %collective-permute-start.5 = (f32[2,2,128,128]{3,2,1,0:T(8,128)S(1)}, f32[2,2,128,128]{3,2,1,0:T(8,128)S(1)}, u32[]{:S(2)}, u32[]{:S(2)}) collective-permute-start(f32[2,2,128,128]{3,2,1,0:T(8,128)S(1)} %pad_maximum_fusion.1), channel_id=1, source_target_pairs={{16,0},{32,16},{48,32},{64,48},{80,64},{96,80},{112,96},{17,1},{33... | collective-permute-start | bytes 786440 | tf_op jit(solution)/shard_map/object_corners/ppermute | solution.py:486
  28.1 9.2 %copy-start.7 = (f32[2,128,256]{2,1,0:T(8,128)}, f32[2,128,256]{2,1,0:T(8,128)S(1)}, u32[]{:S(2)}) copy-start(f32[2,128,256]{2,1,0:T(8,128)S(1)} %collective-permute-done.1.down) | copy-start | bytes 786436
  28.1 9.2 %copy-start.8 = (f32[2,128,256]{2,1,0:T(8,128)}, f32[2,128,256]{2,1,0:T(8,128)S(1)}, u32[]{:S(2)}) copy-start(f32[2,128,256]{2,1,0:T(8,128)S(1)} %collective-permute-done.up) | copy-start | bytes 786436
  31.7 5.6 %copy-start.9 = (f32[2,2,128,128]{3,2,1,0:T(8,128)}, f32[2,2,128,128]{3,2,1,0:T(8,128)S(1)}, u32[]{:S(2)}) copy-start(f32[2,2,128,128]{3,2,1,0:T(8,128)S(1)} %collective-permute-done.4.up_corner) | copy-start | bytes 786436
  37.3 0.7 copy-start.10
  55.6 2.5 %collective-permute-start.6 = (f32[1408,128]{1,0:T(8,128)}, f32[1408,128]{1,0:T(8,128)S(1)}, u32[]{:S(2)}, u32[]{:S(2)}) collective-permute-start(f32[1408,128]{1,0:T(8,128)} %get-tuple-element.30), channel_id=1, source_target_pairs={{0,1},{1,0},{2,3},{3,2},{4,5},{5,4},{6,7},{7,6},{8,9},{9,8},{10,11... | collective-permute-start | bytes 2162696 | tf_op jit(solution)/shard_map/probe_reduce/ppermute | solution.py:458
  59.3 9.4 %collective-permute-start.7 = (f32[352,128]{1,0:T(8,128)S(1)}, f32[352,128]{1,0:T(8,128)S(1)}, u32[]{:S(2)}, u32[]{:S(2)}) collective-permute-start(f32[352,128]{1,0:T(8,128)S(1)} %get-tuple-element.58), channel_id=1, source_target_pairs={{0,16},{1,17},{2,18},{3,19},{4,20},{5,21},{6,22},{7,23},{8,24},{9,... | collective-permute-start | bytes 540680 | tf_op jit(solution)/shard_map/probe_reduce/ppermute | solution.py:458
  59.4 10.9 %collective-permute-start.9 = (f32[352,128]{1,0:T(8,128)S(1)}, f32[352,128]{1,0:T(8,128)S(1)}, u32[]{:S(2)}, u32[]{:S(2)}) collective-permute-start(f32[352,128]{1,0:T(8,128)S(1)} %get-tuple-element.59), channel_id=1, source_target_pairs={{0,48},{1,49},{2,50},{3,51},{4,52},{5,53},{6,54},{7,55},{8,56},{9,... | collective-permute-start | bytes 540680 | tf_op jit(solution)/shard_map/probe_reduce/ppermute | solution.py:458
  60.8 9.5 %collective-permute-start.8 = (f32[352,128]{1,0:T(8,128)S(1)}, f32[352,128]{1,0:T(8,128)S(1)}, u32[]{:S(2)}, u32[]{:S(2)}) collective-permute-start(f32[352,128]{1,0:T(8,128)S(1)} %get-tuple-element.60), channel_id=1, source_target_pairs={{0,32},{1,33},{2,34},{3,35},{4,36},{5,37},{6,38},{7,39},{8,40},{9,... | collective-permute-start | bytes 540680 | tf_op jit(solution)/shard_map/probe_reduce/ppermute | solution.py:458
  68.7 27.6 %copy-start = (f32[3,512,256]{2,1,0:T(8,128)S(1)}, f32[3,512,256]{2,1,0:T(8,128)}, u32[]{:S(2)}) copy-start(f32[3,512,256]{2,1,0:T(8,128)} %get-tuple-element.40) | copy-start | bytes 4718596
  70.3 25.9 %collective-permute-start.16 = (f32[3,512,128]{2,1,0:T(8,128)}, f32[3,512,128]{2,1,0:T(8,128)S(1)}, u32[]{:S(2)}, u32[]{:S(2)}) collective-permute-start(f32[3,512,128]{2,1,0:T(8,128)} %get-tuple-element.41), channel_id=1, source_target_pairs={{0,1},{1,2},{2,3},{3,4},{4,5},{5,6},{6,7},{7,8},{8,9},{9,10},{10,1... | collective-permute-start | bytes 2359304 | tf_op jit(solution)/shard_map/gradient_columns/ppermute | solution.py:500
  74.7 21.6 %collective-permute-start.17 = (f32[3,512,128]{2,1,0:T(8,128)}, f32[3,512,128]{2,1,0:T(8,128)S(1)}, u32[]{:S(2)}, u32[]{:S(2)}) collective-permute-start(f32[3,512,128]{2,1,0:T(8,128)} %get-tuple-element.42), channel_id=1, source_target_pairs={{1,0},{2,1},{3,2},{4,3},{5,4},{6,5},{7,6},{8,7},{9,8},{10,9},{11,1... | collective-permute-start | bytes 2359304 | tf_op jit(solution)/shard_map/gradient_columns/ppermute | solution.py:501
  76.6 4.3 %collective-permute-start.10 = (f32[88,128]{1,0:T(8,128)S(1)}, f32[88,128]{1,0:T(8,128)S(1)}, u32[]{:S(2)}, u32[]{:S(2)}) collective-permute-start(f32[88,128]{1,0:T(8,128)S(1)} %get-tuple-element.69), channel_id=1, source_target_pairs={{0,4},{1,5},{2,6},{3,7},{4,8},{5,9},{6,10},{7,11},{8,12},{9,13},{1... | collective-permute-start | bytes 135176 | tf_op jit(solution)/shard_map/probe_sum/ppermute | solution.py:458
  77.9 3.1 %collective-permute-start.12 = (f32[88,128]{1,0:T(8,128)S(1)}, f32[88,128]{1,0:T(8,128)S(1)}, u32[]{:S(2)}, u32[]{:S(2)}) collective-permute-start(f32[88,128]{1,0:T(8,128)S(1)} %get-tuple-element.70), channel_id=1, source_target_pairs={{0,12},{1,13},{2,14},{3,15},{4,0},{5,1},{6,2},{7,3},{8,4},{9,5},{1... | collective-permute-start | bytes 135176 | tf_op jit(solution)/shard_map/probe_sum/ppermute | solution.py:458
  79.4 4.8 %collective-permute-start.11 = (f32[88,128]{1,0:T(8,128)S(1)}, f32[88,128]{1,0:T(8,128)S(1)}, u32[]{:S(2)}, u32[]{:S(2)}) collective-permute-start(f32[88,128]{1,0:T(8,128)S(1)} %get-tuple-element.71), channel_id=1, source_target_pairs={{0,8},{1,9},{2,10},{3,11},{4,12},{5,13},{6,14},{7,15},{8,0},{9,1},... | collective-permute-start | bytes 135176 | tf_op jit(solution)/shard_map/probe_sum/ppermute | solution.py:458
  84.2 7.4 %collective-permute-start.15 = (f32[88,128]{1,0:T(8,128)S(1)}, f32[88,128]{1,0:T(8,128)S(1)}, u32[]{:S(2)}, u32[]{:S(2)}) collective-permute-start(f32[88,128]{1,0:T(8,128)S(1)} %add_add_fusion.2), channel_id=1, source_target_pairs={{0,66},{1,67},{2,0},{3,1},{4,70},{5,71},{6,4},{7,5},{8,74},{9,75},... | collective-permute-start | bytes 135176 | tf_op jit(solution)/shard_map/probe_sum/ppermute | solution.py:458
  88.1 5.4 %collective-permute-start.14 = (f32[88,128]{1,0:T(8,128)S(1)}, f32[88,128]{1,0:T(8,128)S(1)}, u32[]{:S(2)}, u32[]{:S(2)}) collective-permute-start(f32[88,128]{1,0:T(8,128)S(1)} %add_add_fusion.2), channel_id=1, source_target_pairs={{0,64},{1,65},{2,66},{3,67},{4,68},{5,69},{6,70},{7,71},{8,72},{9,... | collective-permute-start | bytes 135176 | tf_op jit(solution)/shard_map/probe_sum/ppermute | solution.py:458
  91.6 4.6 %collective-permute-start.13 = (f32[88,128]{1,0:T(8,128)S(1)}, f32[88,128]{1,0:T(8,128)S(1)}, u32[]{:S(2)}, u32[]{:S(2)}) collective-permute-start(f32[88,128]{1,0:T(8,128)S(1)} %add_add_fusion.2), channel_id=1, source_target_pairs={{0,2},{1,3},{2,64},{3,65},{4,6},{5,7},{6,68},{7,69},{8,10},{9,11},... | collective-permute-start | bytes 135176 | tf_op jit(solution)/shard_map/probe_sum/ppermute | solution.py:458
  96.5 5.6 %collective-permute-start.20 = (f32[64,128]{1,0:T(8,128)S(1)}, f32[64,128]{1,0:T(8,128)S(1)}, u32[]{:S(2)}, u32[]{:S(2)}) collective-permute-start(f32[64,128]{1,0:T(8,128)S(1)} %slice_divide_fusion.1), channel_id=1, source_target_pairs={{0,12},{1,13},{2,14},{3,15},{4,0},{5,1},{6,2},{7,3},{8,4},{9,5},{1... | collective-permute-start | bytes 98312 | tf_op jit(solution)/shard_map/probe_gather/ppermute | solution.py:458
  97.4 4.6 %collective-permute-start.19 = (f32[64,128]{1,0:T(8,128)S(1)}, f32[64,128]{1,0:T(8,128)S(1)}, u32[]{:S(2)}, u32[]{:S(2)}) collective-permute-start(f32[64,128]{1,0:T(8,128)S(1)} %slice_divide_fusion.1), channel_id=1, source_target_pairs={{0,8},{1,9},{2,10},{3,11},{4,12},{5,13},{6,14},{7,15},{8,0},{9,1},... | collective-permute-start | bytes 98312 | tf_op jit(solution)/shard_map/probe_gather/ppermute | solution.py:458
  98.1 4.0 %collective-permute-start.18 = (f32[64,128]{1,0:T(8,128)S(1)}, f32[64,128]{1,0:T(8,128)S(1)}, u32[]{:S(2)}, u32[]{:S(2)}) collective-permute-start(f32[64,128]{1,0:T(8,128)S(1)} %slice_divide_fusion.1), channel_id=1, source_target_pairs={{0,4},{1,5},{2,6},{3,7},{4,8},{5,9},{6,10},{7,11},{8,12},{9,13},{1... | collective-permute-start | bytes 98312 | tf_op jit(solution)/shard_map/probe_gather/ppermute | solution.py:458
  102.1 7.6 %collective-permute-start.21 = (f32[256,128]{1,0:T(8,128)S(1)}, f32[256,128]{1,0:T(8,128)S(1)}, u32[]{:S(2)}, u32[]{:S(2)}) collective-permute-start(f32[256,128]{1,0:T(8,128)S(1)} %get-tuple-element.74), channel_id=1, source_target_pairs={{0,16},{1,17},{2,18},{3,19},{4,20},{5,21},{6,22},{7,23},{8,24},{9,... | collective-permute-start | bytes 393224 | tf_op jit(solution)/shard_map/probe_gather/ppermute | solution.py:458
  103.3 15.1 %collective-permute-start.24 = (f32[3,128,256]{2,1,0:T(8,128)S(1)}, f32[3,128,256]{2,1,0:T(8,128)S(1)}, u32[]{:S(2)}, u32[]{:S(2)}) collective-permute-start(f32[3,128,256]{2,1,0:T(8,128)S(1)} %get-tuple-element.56), channel_id=1, source_target_pairs={{0,16},{16,32},{32,48},{48,64},{64,80},{80,96},{96,112},{1,17},{17... | collective-permute-start | bytes 1179656 | tf_op jit(solution)/shard_map/gradient_rows/ppermute | solution.py:512
  107.6 13.5 %collective-permute-start.25 = (f32[3,128,256]{2,1,0:T(8,128)S(1)}, f32[3,128,256]{2,1,0:T(8,128)S(1)}, u32[]{:S(2)}, u32[]{:S(2)}) collective-permute-start(f32[3,128,256]{2,1,0:T(8,128)S(1)} %get-tuple-element.57), channel_id=1, source_target_pairs={{16,0},{32,16},{48,32},{64,48},{80,64},{96,80},{112,96},{17,1},{33... | collective-permute-start | bytes 1179656 | tf_op jit(solution)/shard_map/gradient_rows/ppermute | solution.py:513
  109.5 6.6 %collective-permute-start.22 = (f32[256,128]{1,0:T(8,128)S(1)}, f32[256,128]{1,0:T(8,128)S(1)}, u32[]{:S(2)}, u32[]{:S(2)}) collective-permute-start(f32[256,128]{1,0:T(8,128)S(1)} %get-tuple-element.74), channel_id=1, source_target_pairs={{0,32},{1,33},{2,34},{3,35},{4,36},{5,37},{6,38},{7,39},{8,40},{9,... | collective-permute-start | bytes 393224 | tf_op jit(solution)/shard_map/probe_gather/ppermute | solution.py:458
  109.6 8.7 %collective-permute-start.23 = (f32[256,128]{1,0:T(8,128)S(1)}, f32[256,128]{1,0:T(8,128)S(1)}, u32[]{:S(2)}, u32[]{:S(2)}) collective-permute-start(f32[256,128]{1,0:T(8,128)S(1)} %get-tuple-element.74), channel_id=1, source_target_pairs={{0,48},{1,49},{2,50},{3,51},{4,52},{5,53},{6,54},{7,55},{8,56},{9,... | collective-permute-start | bytes 393224 | tf_op jit(solution)/shard_map/probe_gather/ppermute | solution.py:458
  118.4 3.7 %copy-start.1 = (f32[1024,128]{1,0:T(8,128)}, f32[1024,128]{1,0:T(8,128)S(1)}, u32[]{:S(2)}) copy-start(f32[1024,128]{1,0:T(8,128)S(1)} %constant_dynamic-update-slice_fusion.4.mine) | copy-start | bytes 1572868
  118.4 11.4 %copy-start.5 = (f32[8,128]{1,0:T(8,128)S(1)}, f32[8,128]{1,0:T(8,128)}, u32[]{:S(2)}) copy-start(f32[8,128]{1,0:T(8,128)} %get-tuple-element.47) | copy-start | bytes 12292
  122.1 10.5 %collective-permute-start.26 = (f32[1024,128]{1,0:T(8,128)S(1)}, f32[1024,128]{1,0:T(8,128)S(1)}, u32[]{:S(2)}, u32[]{:S(2)}) collective-permute-start(f32[1024,128]{1,0:T(8,128)S(1)} %constant_dynamic-update-slice_fusion.4.mine), channel_id=1, source_target_pairs={{0,1},{1,0},{2,3},{3,2},{4,5},{5,4},{6,7},{7,6},{8,9},{9,8},{10,11... | collective-permute-start | bytes 1572872 | tf_op jit(solution)/shard_map/ppermute | solution.py:458
  132.6 0.8 copy-start.2

commit v2 on v1

--- a/solution.py
+++ b/solution.py
@@ -14,7 +14,6 @@
 SIZE = 256
 HALF = 128
 CHUNK = 32
-UNIT = 88
 BF = jnp.bfloat16
 F32 = jnp.float32
 AXES = ("row", "col")
@@ -102,8 +101,40 @@
         permuted[j] = dot(rows[...], jnp.concatenate(split3(moved), 0))
 
 
+def pack_kernel(starts, place, own, even, odd, cross, same):
+    row_odd, core = place[0], place[1]
+    lanes = lane_index(8)
+    offsets = jnp.zeros((8, HALF), F32)
+    for j in range(starts.shape[0]):
+        for d in range(2):
+            offsets = jnp.where(lanes == 2 * j + d, (starts[j, d] + 1).astype(F32), offsets)
+    at = pl.multiple_of(HALF * row_odd, HALF)
+    for p in range(2):
+        even[p, :HALF] = own[p, pl.ds(HALF - at, HALF), :]
+        odd[p, :HALF] = own[p, pl.ds(at, HALF), :]
+        for b in range(2):
+            for out in (even, odd):
+                out[p, HALF:, b * HALF : (b + 1) * HALF] = offsets
+        for out in (cross, same):
+            out[p, SIZE:] = offsets
+
+    for k in range(2):
+
+        @pl.when(core == k)
+        def _(k=k):
+            for p in range(2):
+                cross[p, :SIZE] = own[p, :, k * HALF : (k + 1) * HALF]
+                same[p, :SIZE] = own[p, :, (1 - k) * HALF : (2 - k) * HALF]
+
+
+def sides(place):
+    even_row = pl.multiple_of(3 * HALF * (1 - place[0]), HALF)
+    odd_row = pl.multiple_of(3 * HALF * place[0], HALF)
+    return even_row, odd_row, 3 * place[1], 3 - 3 * place[1]
+
+
 def transform_kernel(
-    starts, place, own, up, down, left, right, up_corner, down_corner, probe, measured,
+    starts, place, own, even_strip, odd_strip, cross, same, cross_corner, same_corner, probe, measured,
     right_f, left_f, right_i, left_i,
     keep, send, object_part, patch,
     tile, totals, xs, zs, gs, ys, back, sums,
@@ -114,16 +145,17 @@
 
     @pl.when(step == 0)
     def _():
+        even_row, odd_row, cross_block, same_block = sides(place)
         for p in range(2):
-            for side, (strip, at) in enumerate(((left, 0), (right, 3))):
-                tile[p, at, 0:128] = up_corner[side, p]
-                tile[p, at, 128:384] = strip[p]
-                tile[p, at, 384:512] = down_corner[side, p]
+            for block, strip, corner in ((cross_block, cross, cross_corner), (same_block, same, same_corner)):
+                tile[p, block, 128:384] = strip[p, :SIZE]
+                tile[p, block, pl.ds(even_row, HALF)] = corner[0, p, :HALF]
+                tile[p, block, pl.ds(odd_row, HALF)] = corner[1, p, :HALF]
             for b in range(2):
                 span = slice(b * HALF, (b + 1) * HALF)
-                tile[p, 1 + b, 0:128] = up[p, :, span]
                 tile[p, 1 + b, 128:384] = own[p, :, span]
-                tile[p, 1 + b, 384:512] = down[p, :, span]
+                tile[p, 1 + b, pl.ds(even_row, HALF)] = even_strip[p, :HALF, span]
+                tile[p, 1 + b, pl.ds(odd_row, HALF)] = odd_strip[p, :HALF, span]
             tile[p, 4] = jnp.zeros((2 * SIZE, HALF), F32)
         totals[...] = jnp.zeros_like(totals)
         sums[...] = jnp.zeros_like(sums)
@@ -238,20 +270,19 @@
 
     @pl.when(step == pl.num_programs(0) - 1)
     def _():
-        core, x, y = place[0], place[1], place[2]
-        scalar = jnp.where(lax.broadcasted_iota(jnp.int32, (8, HALF), 1) == 0, jnp.sum(sums[0]), jnp.sum(sums[1]))
+        core = place[1]
+        scalar = jnp.where(lax.broadcasted_iota(jnp.int32, (1, 4, HALF), 2) == 0, jnp.sum(sums[0]), jnp.sum(sums[1]))
         for out, block in ((keep, core), (send, 1 - core)):
-            for ry in range(4):
-                for rx in range(4):
-                    unit = 4 * lax.rem(y + ry, 4) + lax.rem(x + rx, 4)
-                    at = UNIT * (4 * ry + rx)
-                    for c in range(5):
-                        source = pl.ds(pl.multiple_of(16 * unit, 16), 16)
-                        out[at + 16 * c : at + 16 * c + 16, :] = totals[block, c, source, :]
-                    out[at + 80 : at + 88, :] = scalar
-
-
-def place_kernel(starts, object_part, patch, probe, center, left, right, steps, padded, power, accum):
+            for c in range(5):
+                out[:, 4 * c : 4 * c + 4, :] = totals[block, c].reshape(64, 4, HALF)
+            out[:, 20:24, :] = jnp.broadcast_to(scalar, (64, 4, HALF))
+
+
+def place_kernel(
+    starts, place, object_part, patch, probe,
+    center, even, odd, cross, same, cross_corner, same_corner, steps,
+    padded, power, accum,
+):
     step = pl.program_id(0)
     lanes = lane_index(CHUNK)
 
@@ -262,8 +293,7 @@
         padded[:, :, 264:272, :] = jnp.zeros((2, 2, 8, HALF), F32)
         for i in range(0, SIZE, CHUNK):
             part = pl.ds(i, CHUNK)
-            total = probe[0, 0, part] ** 2 + probe[0, 1, part] ** 2
-            power[part] = total + probe[1, 0, part] ** 2 + probe[1, 1, part] ** 2
+            power[part] = probe_power(probe, part)
 
     row, col = starts[step, 0], starts[step, 1]
     base, shift = col // HALF, lax.rem(col, HALF)
@@ -278,7 +308,7 @@
         where = pl.ds(row + i, CHUNK)
         grads = [[object_part[0, p, b, part, :] for b in range(2)] for p in range(2)]
         strength = [power[part, :HALF], power[part, HALF:]]
-        for p, pair in enumerate(grads + [strength]):
+        for p, pair in enumerate(grads):
             moved = spread(pair[0], pair[1], shift, lanes)
             for b in range(3):
                 accum[p, base + b, where, :] += moved[b]
@@ -306,31 +336,104 @@
 
     @pl.when(step == pl.num_programs(0) - 1)
     def _():
-        for p in range(3):
-            left[p] = accum[p, 0]
-            right[p] = accum[p, 3]
-            center[p, :, :HALF] = accum[p, 1]
-            center[p, :, HALF:] = accum[p, 2]
+        even_row, odd_row, cross_block, same_block = sides(place)
+        for p in range(2):
+            for b in range(2):
+                span = slice(b * HALF, (b + 1) * HALF)
+                center[p, :, span] = accum[p, 1 + b, 128:384]
+                even[p, :, span] = accum[p, 1 + b, pl.ds(even_row, HALF)]
+                odd[p, :, span] = accum[p, 1 + b, pl.ds(odd_row, HALF)]
+            for block, strip, corner in ((cross_block, cross, cross_corner), (same_block, same, same_corner)):
+                strip[p] = accum[p, block, 128:384]
+                corner[0, p] = accum[p, block, pl.ds(even_row, HALF)]
+                corner[1, p] = accum[p, block, pl.ds(odd_row, HALF)]
+
+
+def probe_power(probe, part):
+    return (probe[0, 0, part] ** 2 + probe[0, 1, part] ** 2) + (probe[1, 0, part] ** 2 + probe[1, 1, part] ** 2)
+
+
+def light_kernel(starts, around, place, probe, light, power, accum):
+    accum[...] = jnp.zeros_like(accum)
+    for i in range(0, SIZE, CHUNK):
+        part = pl.ds(i, CHUNK)
+        total = probe_power(probe, part)
+        power[0, part] = total[:, :HALF]
+        power[1, part] = total[:, HALF:]
+    lanes = lane_index(CHUNK)
+    even, cross = 1 - 2 * place[0], 2 * place[1] - 1
+    neighbours = [(even, None), (-even, None), (None, cross), (None, -cross)]
+    neighbours += [(even, cross), (-even, cross), (even, -cross), (-even, -cross)]
+
+    def add(row, col, down, right):
+        rows, source_row, row = (SIZE, 0, row + HALF) if down is None else (
+            HALF, pl.multiple_of(jnp.where(down < 0, HALF, 0), HALF), row + jnp.where(down < 0, 0, 3 * HALF)
+        )
+        if right is None:
+            col = col + HALF
+        else:
+            source = jnp.where(right < 0, 1, 0)
+            col = col + jnp.where(right < 0, 0, 3 * HALF)
+        base, shift = col // HALF, lax.rem(col, HALF)
+        for i in range(0, rows, CHUNK):
+            part = pl.ds(source_row + i, CHUNK)
+            where = pl.ds(row + i, CHUNK)
+            if right is None:
+                moved = spread(power[0, part], power[1, part], shift, lanes)
+            else:
+                rolled = pltpu.roll(power[source, part], shift, 1)
+                moved = jnp.where(lanes < shift, 0.0, rolled), jnp.where(lanes < shift, rolled, 0.0)
+            for b, value in enumerate(moved):
+                accum[base + b, where, :] += value
+
+    for j in range(starts.shape[0]):
+        add(starts[j, 0], starts[j, 1], None, None)
+    for n, (down, right) in enumerate(neighbours):
+        for j in range(starts.shape[0]):
+            row, col = around[n, 2 * j] - 1, around[n, 2 * j + 1] - 1
+            near = row >= 0
+            if down is not None:
+                near = near & jnp.where(down < 0, row > HALF, row < HALF)
+            if right is not None:
+                near = near & jnp.where(right < 0, col > HALF, col < HALF)
+
+            @pl.when(near)
+            def _(row=row, col=col, down=down, right=right):
+                add(row, col, down, right)
+
+    light[:, :HALF] = accum[2, 256:512]
+    light[:, HALF:] = accum[3, 256:512]
+
+
+def update_kernel(place, center, even, odd, cross, same, light, out, total):
+    for p in range(2):
+        total[p] = center[p]
+    even_half = pl.ds(pl.multiple_of(HALF * (1 - place[0]), HALF), HALF)
+    odd_half = pl.ds(pl.multiple_of(HALF * place[0], HALF), HALF)
+    for p in range(2):
+        total[p, even_half, :] += even[p]
+        total[p, odd_half, :] += odd[p]
+    swapped = place[1] == 1
+    for i in range(0, SIZE, CHUNK):
+        part = pl.ds(i, CHUNK)
+        scale = 1.0 / (light[part] + object_damping)
+        for p in range(2):
+            a, b = cross[p, part], same[p, part]
+            out[p, part, :HALF] = (total[p, part, :HALF] + jnp.where(swapped, b, a)) * scale[:, :HALF]
+            out[p, part, HALF:] = (total[p, part, HALF:] + jnp.where(swapped, a, b)) * scale[:, HALF:]
 
 
 def assemble_kernel(place, mine, other, out):
-    core, x, y = place[0], place[1], place[2]
-
     def write(source, block):
-        for sy in range(4):
-            for sx in range(4):
-                unit = 4 * lax.rem(y + 4 - sy, 4) + lax.rem(x + 4 - sx, 4)
-                target = pl.ds(pl.multiple_of(16 * unit, 16), 16)
-                for c in range(4):
-                    at = 64 * (4 * sy + sx) + 16 * c
-                    out[c, target, block * HALF : (block + 1) * HALF] = source[at : at + 16, :]
-
-    @pl.when(core == 0)
+        for c in range(4):
+            out[c, :, block * HALF : (block + 1) * HALF] = source[:, 4 * c : 4 * c + 4, :].reshape(SIZE, HALF)
+
+    @pl.when(place[1] == 0)
     def _():
         write(mine, 0)
         write(other, 1)
 
-    @pl.when(core == 1)
+    @pl.when(place[1] == 1)
     def _():
         write(mine, 1)
         write(other, 0)
@@ -356,21 +459,41 @@
     return pl.CostEstimate(flops=flops, bytes_accessed=size, transcendentals=0)
 
 
+def simple(kernel, scalars, arrays, shapes, scratch, flops, size):
+    single = not isinstance(shapes, list)
+    outs = [shapes] if single else shapes
+    call = pl.pallas_call(
+        kernel,
+        out_shape=shaped(outs)[0] if single else shaped(outs),
+        grid_spec=pltpu.PrefetchScalarGridSpec(
+            num_scalar_prefetch=len(scalars),
+            grid=(),
+            in_specs=[whole(*x.shape) for x in arrays],
+            out_specs=whole(*shapes) if single else [whole(*s) for s in outs],
+            scratch_shapes=[pltpu.VMEM(s, F32) for s in scratch],
+        ),
+        compiler_params=params(),
+        cost_estimate=cost(flops, size),
+    )
+    return call(*scalars, *arrays)
+
+
+def pack(starts, place, own):
+    rows, columns = (2, HALF + 8, SIZE), (2, SIZE + 8, HALF)
+    return simple(pack_kernel, [starts, place], [own], [rows, rows, columns, columns], [], 1 << 10, 2 << 20)
+
+
 def prepare(measured):
     cols, rows = permutation()
-    return pl.pallas_call(
-        prepare_kernel,
-        out_shape=jax.ShapeDtypeStruct(measured.shape, F32),
-        compiler_params=params(),
-        cost_estimate=cost(1 << 30, 3 << 20),
-    )(measured, jnp.asarray(cols), jnp.asarray(rows))
+    arrays = [measured, jnp.asarray(cols), jnp.asarray(rows)]
+    return simple(prepare_kernel, [], arrays, measured.shape, [], 1 << 30, 3 << 20)
 
 
 def transforms(starts, place, own, halo, probe, measured):
     mats = [jnp.asarray(x) for x in constants()]
     arrays = [own, *halo, probe]
     count = measured.shape[0]
-    halves = (16 * UNIT, HALF)
+    halves = (64, 24, HALF)
     fields = (2, 2, SIZE, HALF)
     return pl.pallas_call(
         transform_kernel,
@@ -396,132 +519,123 @@
     )(starts, place, *arrays, measured, *mats)
 
 
-def place_parts(starts, object_part, patch, probe):
+def place_parts(starts, place, object_part, patch, probe):
     count = patch.shape[0]
     fields = (2, 2, SIZE, HALF)
-    shapes = [(3, 2 * SIZE, SIZE), (3, 2 * SIZE, HALF), (3, 2 * SIZE, HALF), (2 * count, HALF)]
+    rows, columns, corners = (2, HALF, SIZE), (2, SIZE, HALF), (2, 2, HALF, HALF)
+    shapes = [(2, SIZE, SIZE), rows, rows, columns, columns, corners, corners, (2 * count, HALF)]
     return pl.pallas_call(
         place_kernel,
         out_shape=shaped(shapes),
         grid_spec=pltpu.PrefetchScalarGridSpec(
-            num_scalar_prefetch=1,
+            num_scalar_prefetch=2,
             grid=(count,),
             in_specs=[stepped(*fields), stepped(*fields), whole(*probe.shape)],
             out_specs=[whole(*s) for s in shapes],
             scratch_shapes=[
                 pltpu.VMEM((2, 2, SIZE + 16, HALF), F32),
                 pltpu.VMEM((SIZE, SIZE), F32),
-                pltpu.VMEM((3, 5, 2 * SIZE, HALF), F32),
+                pltpu.VMEM((2, 5, 2 * SIZE, HALF), F32),
             ],
         ),
         compiler_params=params(),
         cost_estimate=cost(5 << 30, 8 << 20),
-    )(starts, object_part, patch, probe)
+    )(starts, place, object_part, patch, probe)
+
+
+def illuminate(starts, around, place, probe):
+    scratch = [(2, SIZE, HALF), (7, 3 * SIZE, HALF)]
+    return simple(light_kernel, [starts, around, place], [probe], (SIZE, SIZE), scratch, 2 << 30, 4 << 20)
+
+
+def update(place, arrays):
+    shape = arrays[0].shape
+    return simple(update_kernel, [place], arrays, shape, [shape], 1 << 20, 3 << 20)
 
 
 def assemble(place, mine, other):
-    shape = (4, SIZE, SIZE)
-    return pl.pallas_call(
-        assemble_kernel,
-        out_shape=jax.ShapeDtypeStruct(shape, F32),
-        grid_spec=pltpu.PrefetchScalarGridSpec(
-            num_scalar_prefetch=1,
-            grid=(),
-            in_specs=[whole(*mine.shape), whole(*other.shape)],
-            out_specs=whole(*shape),
-        ),
-        compiler_params=params(),
-        cost_estimate=cost(1 << 20, 2 << 20),
-    )(place, mine, other)
-
-
-def neighbours(axis):
-    up = [(i, i + 1) for i in range(lax.axis_size(axis) - 1)]
-    return up, [(j, i) for i, j in up]
-
-
-def chips(index):
-    row, col = divmod(index, 16)
-    return [col // 4, row % 4, 2 * (row // 4) + col // 2 % 2, col % 2]
-
-
-def device(x, y, z, core):
-    return (4 * (z // 2) + y) * 16 + 4 * x + 2 * (z % 2) + core
-
-
-def along(value, dim, distance):
+    return simple(assemble_kernel, [place], [mine, other], (4, SIZE, SIZE), [], 1 << 20, 2 << 20)
+
+
+def pairs_from(first, count):
     pairs = []
-    for source in range(lax.axis_size("row") * lax.axis_size("col")):
-        target = chips(source)
-        target[dim] = (target[dim] + distance) % (2 if dim == 3 else 4)
-        pairs.append((source, device(*target)))
-    return lax.ppermute(value, AXES, pairs)
-
-
-def others(pieces, dim):
-    return [pieces[0]] + [along(pieces[d], dim, d) for d in (1, 2, 3)]
-
-
-def total_of(values):
-    return (values[0] + values[1]) + (values[2] + values[3])
+    for i in range(first, count - 1, 2):
+        pairs += [(i, i + 1), (i + 1, i)]
+    return pairs
+
+
+def swap_rows(value, first):
+    return lax.ppermute(value, "row", pairs_from(first, lax.axis_size("row")))
+
+
+def swap_columns(value, first):
+    return lax.ppermute(value, "col", pairs_from(first, lax.axis_size("col")))
+
+
+def half_lanes(value, first):
+    return jnp.where(first, value[..., :HALF], value[..., HALF:])
 
 
 def local(object_tile, probe, amplitudes, offsets):
     starts = offsets[0, 0]
     measured = amplitudes[0, 0]
-    row_up, row_down = neighbours("row")
-    col_up, col_down = neighbours("col")
-    row_index, col_index = lax.axis_index("row"), lax.axis_index("col")
-    place = jnp.stack([lax.rem(col_index, 2), lax.div(col_index, 4), lax.rem(row_index, 4)])
+    core = lax.rem(lax.axis_index("col"), 2)
+    place = jnp.stack([lax.rem(lax.axis_index("row"), 2), core])
+    devices = lax.axis_size("row") * lax.axis_size("col")
+    groups = [[i for i in range(devices) if i % 2 == k] for k in range(2)]
 
     with jax.named_scope("object_halo"):
-        left = lax.ppermute(object_tile[:, :, HALF:], "col", col_up)
-        right = lax.ppermute(object_tile[:, :, :HALF], "col", col_down)
-        up = lax.ppermute(object_tile[:, HALF:], "row", row_up)
-        down = lax.ppermute(object_tile[:, :HALF], "row", row_down)
+        even, odd, cross, same = pack(starts, place, object_tile)
+        even = swap_rows(even, 0)
+        odd = swap_rows(odd, 1)
+        cross = swap_columns(cross, 1)
+        same = swap_columns(same, 0)
     permuted = prepare(measured)
     with jax.named_scope("object_corners"):
-        left, right, permuted = lax.optimization_barrier((left, right, permuted))
-        up_corner = lax.ppermute(jnp.stack([left[:, HALF:], right[:, HALF:]]), "row", row_up)
-        down_corner = lax.ppermute(jnp.stack([left[:, :HALF], right[:, :HALF]]), "row", row_down)
-
-    halo = [up, down, left, right, up_corner, down_corner]
+        rows, permuted = lax.optimization_barrier((jnp.stack([even, odd]), permuted))
+        cross_corner = swap_columns(half_lanes(rows, core == 0), 1)
+        same_corner = swap_columns(half_lanes(rows, core == 1), 0)
+
+    halo = [even, odd, cross, same, cross_corner, same_corner]
     keep, send, object_part, patch = transforms(starts, place, object_tile, halo, probe, permuted)
 
     with jax.named_scope("probe_reduce"):
-        chunk = keep + along(send, 3, 1)
-        chunk, object_part = lax.optimization_barrier((chunk, object_part))
-        chunk = total_of(others(jnp.split(chunk, 4), 1))
-
-    parts = place_parts(starts, object_part, patch, probe)
-    chunk, (center, grad_left, grad_right, steps) = lax.optimization_barrier((chunk, parts))
-
-    with jax.named_scope("gradient_columns"):
-        from_left = lax.ppermute(grad_right, "col", col_up)
-        from_right = lax.ppermute(grad_left, "col", col_down)
+        chunk = keep + swap_columns(send, 0)
+        around = [x[0, -8:-7, :8] for x in halo[:4]]
+        around += [x[n, 0, -8:-7, :8] for x in halo[4:] for n in range(2)]
+        around = jnp.concatenate(around, 0).astype(jnp.int32)
+        chunk, object_part, around = lax.optimization_barrier((chunk, object_part, around))
+        chunk = lax.all_to_all(chunk, AXES, 0, 0, axis_index_groups=groups, tiled=True)
+
+    parts = place_parts(starts, place, object_part, patch, probe)
+    light = illuminate(starts, around, place, probe)
+    chunk, parts, light = lax.optimization_barrier((chunk, parts, light))
+    center, even, odd, cross, same, cross_corner, same_corner, steps = parts
+
+    with jax.named_scope("gradient_corners"):
+        cross_corner = swap_columns(cross_corner, 1)
+        same_corner = swap_columns(same_corner, 0)
 
     with jax.named_scope("probe_sum"):
-        chunk = total_of(others(jnp.split(chunk, 4), 0))
-        chunk = total_of([chunk] + [along(chunk, 2, d) for d in (1, 2, 3)])
-        quotient = (chunk[:64].reshape(4, 16, HALF) / chunk[64:80]).reshape(64, HALF)
-        relative_error = (chunk[80, 0] / chunk[80, 1]).reshape(1)
+        total = jnp.sum(chunk, axis=0)
+        quotient = total[:16].reshape(4, 4, HALF) / total[16:20]
+        relative_error = (total[20, 0] / total[20, 1]).reshape(1)
 
     with jax.named_scope("gradient_rows"):
-        fields = center + jnp.concatenate([from_left, from_right], 2)
-        quotient, fields = lax.optimization_barrier((quotient, fields))
-        from_above = lax.ppermute(fields[:, SIZE + HALF :], "row", row_up)
-        from_below = lax.ppermute(fields[:, :HALF], "row", row_down)
+        first = jnp.where(core == 0, cross_corner, same_corner)
+        second = jnp.where(core == 0, same_corner, cross_corner)
+        added = jnp.concatenate([first, second], -1)
+        even = swap_rows(even + added[0], 0)
+        odd = swap_rows(odd + added[1], 1)
+        cross = swap_columns(cross, 1)
+        same = swap_columns(same, 0)
 
     with jax.named_scope("probe_gather"):
-        quotient = jnp.concatenate(others([quotient] * 4, 0))
-        quotient = jnp.concatenate(others([quotient] * 4, 1))
-
-    with jax.named_scope("object_update"):
-        combined = fields[:, HALF : HALF + SIZE] + jnp.concatenate([from_above, from_below], 1)
-        object_update = combined[:2] / (combined[2:] + object_damping)
-        quotient, object_update = lax.optimization_barrier((quotient, object_update))
-
-    probe_update = assemble(place, quotient, along(quotient, 3, 1)).reshape(probe.shape)
+        spread_out = jnp.broadcast_to(quotient.reshape(1, 16, HALF), (devices // 2, 16, HALF))
+        gathered = lax.all_to_all(spread_out, AXES, 0, 0, axis_index_groups=groups, tiled=True)
+        probe_update = assemble(place, gathered, swap_columns(gathered, 0)).reshape(probe.shape)
+
+    object_update = update(place, [center, even, odd, cross, same, light])
     position_step = steps[:, 0].reshape(1, 1, -1, 2)
     return (object_update, probe_update, position_step, relative_error)
 

time: 138 us -> 129 us (0.935)
  waiting for transfers between devices: 35.2 us -> 20.1 us
  Pallas kernels: 32 us -> 42.1 us
  starting transfers between devices: 57.8 us -> 48.7 us
  local copies, waits for them, and re-layouts: 5.98 us -> 9.38 us
    ppermute x27 -> x14, starting transfers between devices: 57.8 us -> 29.6 us  [the longest x10 16.8 us: swap_columns(): return lax.ppermute(value, 'col', pairs_from(first, lax.axis_size('col')))]
    ppermute x27 -> x14, waiting for transfers between devices: 35.2 us -> 13.2 us  [the longest x10 8.38 us: swap_columns(): return lax.ppermute(value, 'col', pairs_from(first, lax.axis_size('col')))]
    all_to_all x0 -> x2, starting transfers between devices: none -> 19.1 us  [the longest x1 11.6 us: local(): lax.all_to_all(chunk, AXES, 0, 0, axis_index_groups=groups, tiled=True)]
    pallas_call x2 -> x5, Pallas kernels: 6.62 us -> 17.2 us  [simple(): return call(*scalars, *arrays)]
    all_to_all x0 -> x2, waiting for transfers between devices: none -> 6.81 us  [the longest x1 4.42 us: local(): lax.all_to_all(spread_out, AXES, 0, 0, axis_index_groups=groups, tiled=True)]
    squeeze x0 -> x6, local copies, waits for them, and re-layouts: none -> 2.78 us  [the longest x2 1.4 us: local(): around += [x[n, 0, -8:-7, :8] for x in halo[4:] for n in range(2)]]
    slice x5 -> x2, local copies, waits for them, and re-layouts: 2.78 us -> 0.59 us  [the longest x1 0.58 us: local(): relative_error = (total[20, 0] / total[20, 1]).reshape(1)]
    unnamed x28 -> x37, local copies, waits for them, and re-layouts: 2.24 us -> 3.61 us
  transfers between devices with their start and end apart: 27 -> 16, of which waited for: 12 -> 6; matrix products, arithmetic and copies ran while one was open for 3% -> 4% of each run, Pallas kernels for 8% -> 15%
where the time goes in v2:
time: 129 us; the launch traced here: 127 us
  starting transfers between devices  48.7 us (38%)
  Pallas kernels  42.1 us (33%)
  waiting for transfers between devices  20.1 us (16%)
  local copies, waits for them, and re-layouts  9.38 us (7%)
  other arithmetic  3.59 us (3%)
  between operations  3.44 us (3%)
    pallas_call x1, Pallas kernels, transforms(): pl.pallas_call(transform_kernel, out_shape=shaped([halves, halves, (count...  17.7 us
    pallas_call x5, Pallas kernels, simple(): return call(*scalars, *arrays)  17.2 us
    ppermute x10, starting transfers between devices, swap_columns(): return lax.ppermute(value, 'col', pairs_from(first, lax.axis_size('col')))  16.8 us
    ppermute x4, starting transfers between devices, swap_rows(): return lax.ppermute(value, 'row', pairs_from(first, lax.axis_size('row')))  12.8 us
    all_to_all x1, starting transfers between devices, local(): lax.all_to_all(chunk, AXES, 0, 0, axis_index_groups=groups, tiled=True)  11.6 us
    ppermute x10, waiting for transfers between devices, swap_columns(): return lax.ppermute(value, 'col', pairs_from(first, lax.axis_size('col')))  8.38 us
    all_to_all x1, starting transfers between devices, local(): lax.all_to_all(spread_out, AXES, 0, 0, axis_index_groups=groups, tiled=True)  7.47 us
    pallas_call x1, Pallas kernels, place_parts(): pl.pallas_call(place_kernel, out_shape=shaped(shapes), grid_spec=pltpu.Pr...  7.18 us
  transfers between devices with their start and end apart: 16, of which 6 were waited for; matrix products, arithmetic and copies ran while one was open for 4% of the time, Pallas kernels for 15%

profile of v2, /device:TPU:25, one launch (start us, length us, event | category | flops | bytes accessed | tf_op | source)
XLA Modules:
  0.0 127.3 jit_solution(18121818095762842170)
XLA Ops:
  0.6 1.3 %copy.20.starts = s32[4,2]{1,0:T(4,128)} copy(s32[4,2]{0,1:T(2,128)} %bitcast.37) | data formatting | bytes 64 | tf_op jit(solution)/shard_map/squeeze | solution.py:580
  2.0 0.6 pad_add_fusion.place
  2.6 2.8 %object_halo.1 = (f32[2,136,256]{2,1,0:T(8,128)}, f32[2,136,256]{2,1,0:T(8,128)}, f32[2,264,128]{2,1,0:T(8,128)}, f32[2,264,128]{2,1,0:T(8,128)}) custom-call(s32[4,2]{1,0:T(4,128)} %copy.20.starts, s32[2]{0:T(128)} %pad_add_fusion.place, f32[2,256,256]{2,1,0:T(8,128)} %own.3), custom_call_target="tpu_custom_call" | custom-call | flops 1024 | bytes 2097152 | tf_op jit(solution)/shard_map/object_halo/pallas_call | solution.py:478
  5.4 0.5 collective-permute-start
  5.8 6.0 %collective-permute-start.1 = (f32[2,136,256]{2,1,0:T(8,128)}, f32[2,136,256]{2,1,0:T(8,128)S(1)}, u32[]{:S(2)}, u32[]{:S(2)}) collective-permute-start(f32[2,136,256]{2,1,0:T(8,128)} %get-tuple-element.36), channel_id=1, source_target_pairs={{16,32},{32,16},{48,64},{64,48},{80,96},{96,80},{17,33},{33,17},{4... | collective-permute-start | bytes 835592 | tf_op jit(solution)/shard_map/object_halo/ppermute | solution.py:568
  11.8 3.8 %collective-permute-start.2 = (f32[2,264,128]{2,1,0:T(8,128)}, f32[2,264,128]{2,1,0:T(8,128)S(1)}, u32[]{:S(2)}, u32[]{:S(2)}) collective-permute-start(f32[2,264,128]{2,1,0:T(8,128)} %get-tuple-element.37), channel_id=1, source_target_pairs={{1,2},{2,1},{3,4},{4,3},{5,6},{6,5},{7,8},{8,7},{9,10},{10,9},{11,... | collective-permute-start | bytes 811016 | tf_op jit(solution)/shard_map/object_halo/ppermute | solution.py:572
  15.6 0.1 collective-permute-start.3
  15.7 3.7 %shard_map.129.measured = f32[4,256,256]{2,1,0:T(8,128)} custom-call(f32[4,256,256]{2,1,0:T(8,128)} %bitcast.38, bf16[768,256]{1,0:T(8,128)(2,1)} %constant.32.clone.cols, bf16[256,768]{1,0:T(8,128)(2,1)} %constant.33.clone.rows), custom_call_target="tpu_custom_call" | custom-call | flops 1073741824 | bytes 3145728 | tf_op jit(solution)/shard_map/pallas_call | solution.py:478
  19.4 0.0 collective-permute-done.even_strip
  19.4 1.0 collective-permute-done.1.odd_strip
  20.5 3.7 %collective-permute-start.4 = (f32[2,2,136,128]{3,2,1,0:T(8,128)S(1)}, f32[2,2,136,128]{3,2,1,0:T(8,128)S(1)}, u32[]{:S(2)}, u32[]{:S(2)}) collective-permute-start(f32[2,2,136,128]{3,2,1,0:T(8,128)S(1)} %get-tuple-element.75), channel_id=1, source_target_pairs={{1,2},{2,1},{3,4},{4,3},{5,6},{6,5},{7,8},{8,7},{9,10},{10,9},{11,... | collective-permute-start | bytes 835592 | tf_op jit(solution)/shard_map/object_corners/ppermute | solution.py:572
  24.3 0.1 collective-permute-start.5
  24.4 0.0 collective-permute-done.2.cross
  24.4 0.0 collective-permute-done.3.same
  24.4 0.0 copy-start.14
  24.4 6.3 %collective-permute-done.4.cross_corner = f32[2,2,136,128]{3,2,1,0:T(8,128)S(1)} collective-permute-done((f32[2,2,136,128]{3,2,1,0:T(8,128)S(1)}, f32[2,2,136,128]{3,2,1,0:T(8,128)S(1)}, u32[]{:S(2)}, u32[]{:S(2)}) %collective-permute-start.4) | collective-permute-done | bytes 278560 | tf_op jit(solution)/shard_map/object_corners/ppermute | solution.py:572
  30.7 0.0 collective-permute-done.5.same_corner
  30.7 0.0 copy-done.2
  30.8 0.7 copy-done.11
  31.4 0.7 copy-done.12
  32.1 17.7 %shard_map.130 = (f32[64,24,128]{2,1,0:T(8,128)}, f32[64,24,128]{2,1,0:T(8,128)}, f32[4,2,2,256,128]{4,3,2,1,0:T(8,128)}, f32[4,2,2,256,128]{4,3,2,1,0:T(8,128)}) custom-call(s32[4,2]{1,0:T(4,128)} %copy.20.starts, s32[2]{0:T(128)} %pad_add_fusion.place, f32[2,256,256]{2,1,0:T(8,128)} %own.3, f32[2,136,256]{2,1,0:T(8,128)} %copy-done.2, ...), custom_call_target="tpu_custom_call" | custom-call | flops 13958643712 | bytes 12582912 | tf_op jit(solution)/shard_map/pallas_call | solution.py:498
  49.8 0.0 collective-permute-start.6
  49.9 0.7 slice_bitcast_fusion.7
  50.6 0.7 slice_bitcast_fusion.6
  51.3 0.7 slice_bitcast_fusion.2
  52.0 0.7 slice_bitcast_fusion
  52.7 0.6 convert_element_type.3.around
  53.3 0.0 collective-permute-done.6
  53.3 2.1 %add.9 = f32[64,24,128]{2,1,0:T(8,128)} add(f32[64,24,128]{2,1,0:T(8,128)} %get-tuple-element.41, f32[64,24,128]{2,1,0:T(8,128)S(1)} %collective-permute-done.6) | non-fusion elementwise | flops 196608 | bytes 2359296 | tf_op jit(solution)/shard_map/probe_reduce/add | solution.py:603
  55.4 11.6 %all-to-all-start = ((f32[64,24,128]{2,1,0:T(8,128)}), f32[64,24,128]{2,1,0:T(8,128)S(1)}, u32[]{:S(2)}, u32[]{:S(2)}) async-start(f32[64,24,128]{2,1,0:T(8,128)} %add.9), calls=%async_computation | async-start | bytes 1572864 | tf_op jit(solution)/shard_map/probe_reduce/all_to_all | solution.py:608
  67.0 4.8 %shard_map.132.light = f32[256,256]{1,0:T(8,128)} custom-call(s32[4,2]{1,0:T(4,128)} %copy.20.starts, s32[8,8]{1,0:T(8,128)} %convert_element_type.3.around, s32[2]{0:T(128)} %pad_add_fusion.place, f32[2,2,256,256]{3,2,1,0:T(8,128)} %probe.5), custom_call_target="tpu_custom_call" | custom-call | flops 2147483648 | bytes 4194304 | tf_op jit(solution)/shard_map/pallas_call | solution.py:478
  71.8 7.2 %shard_map.131 = (f32[2,256,256]{2,1,0:T(8,128)}, f32[2,128,256]{2,1,0:T(8,128)}, f32[2,128,256]{2,1,0:T(8,128)}, f32[2,256,128]{2,1,0:T(8,128)}, f32[2,256,128]...) custom-call(s32[4,2]{1,0:T(4,128)} %copy.20.starts, ...), custom_call_target="tpu_custom_call" | custom-call | flops 5368709120 | bytes 8388608 | tf_op jit(solution)/shard_map/pallas_call | solution.py:527
  79.0 2.4 %all-to-all-done = f32[64,24,128]{2,1,0:T(8,128)S(1)} async-done(((f32[64,24,128]{2,1,0:T(8,128)}), f32[64,24,128]{2,1,0:T(8,128)S(1)}, u32[]{:S(2)}, u32[]{:S(2)}) %all-to-all-start) | async-done | bytes 786464 | tf_op jit(solution)/shard_map/probe_reduce/all_to_all | solution.py:608
  81.4 0.1 reduce_sum.9
  81.5 0.8 broadcast_in_dim.2
  82.4 7.5 %all-to-all-start.1 = ((f32[64,16,128]{2,1,0:T(8,128)}), f32[64,16,128]{2,1,0:T(8,128)S(1)}, u32[]{:S(2)}, u32[]{:S(2)}) async-start(f32[64,16,128]{2,1,0:T(8,128)} %broadcast_in_dim.2), calls=%async_computation.1 | async-start | bytes 1048576 | tf_op jit(solution)/shard_map/probe_gather/all_to_all | solution.py:635
  89.8 1.3 collective-permute-start.8
  91.1 3.0 %collective-permute-start.7 = (f32[2,2,128,128]{3,2,1,0:T(8,128)S(1)}, f32[2,2,128,128]{3,2,1,0:T(8,128)S(1)}, u32[]{:S(2)}, u32[]{:S(2)}) collective-permute-start(f32[2,2,128,128]{3,2,1,0:T(8,128)S(1)} %copy-done.17), channel_id=1, source_target_pairs={{1,2},{2,1},{3,4},{4,3},{5,6},{6,5},{7,8},{8,7},{9,10},{10,9},{11,... | collective-permute-start | bytes 786440 | tf_op jit(solution)/shard_map/gradient_corners/ppermute | solution.py:572
  94.1 2.5 %collective-permute-start.11 = (f32[2,256,128]{2,1,0:T(8,128)S(1)}, f32[2,256,128]{2,1,0:T(8,128)S(1)}, u32[]{:S(2)}, u32[]{:S(2)}) collective-permute-start(f32[2,256,128]{2,1,0:T(8,128)S(1)} %copy-done.16), channel_id=1, source_target_pairs={{1,2},{2,1},{3,4},{4,3},{5,6},{6,5},{7,8},{8,7},{9,10},{10,9},{11,... | collective-permute-start | bytes 786440 | tf_op jit(solution)/shard_map/gradient_rows/ppermute | solution.py:572
  96.7 0.0 copy-done.15
  96.7 0.1 collective-permute-start.12
  96.8 4.4 %all-to-all-done.1.mine = f32[64,16,128]{2,1,0:T(8,128)S(1)} async-done(((f32[64,16,128]{2,1,0:T(8,128)}), f32[64,16,128]{2,1,0:T(8,128)S(1)}, u32[]{:S(2)}, u32[]{:S(2)}) %all-to-all-start.1) | async-done | bytes 524320 | tf_op jit(solution)/shard_map/probe_gather/all_to_all | solution.py:635
  101.2 2.2 %collective-permute-start.13 = (f32[64,16,128]{2,1,0:T(8,128)S(1)}, f32[64,16,128]{2,1,0:T(8,128)S(1)}, u32[]{:S(2)}, u32[]{:S(2)}) collective-permute-start(f32[64,16,128]{2,1,0:T(8,128)S(1)} %all-to-all-done.1.mine), channel_id=1, source_target_pairs={{0,1},{1,0},{2,3},{3,2},{4,5},{5,4},{6,7},{7,6},{8,9},{9,8},{10,11... | collective-permute-start | bytes 1572872 | tf_op jit(solution)/shard_map/probe_gather/ppermute | solution.py:572
  103.4 0.0 collective-permute-done.8
  103.4 2.1 %collective-permute-done.7 = f32[2,2,128,128]{3,2,1,0:T(8,128)S(1)} collective-permute-done((f32[2,2,128,128]{3,2,1,0:T(8,128)S(1)}, f32[2,2,128,128]{3,2,1,0:T(8,128)S(1)}, u32[]{:S(2)}, u32[]{:S(2)}) %collective-permute-start.7) | collective-permute-done | bytes 262176 | tf_op jit(solution)/shard_map/gradient_corners/ppermute | solution.py:572
  105.5 0.1 fusion.4
  105.6 0.6 collective-permute-start.9
  106.2 5.7 %collective-permute-start.10 = (f32[2,128,256]{2,1,0:T(8,128)S(1)}, f32[2,128,256]{2,1,0:T(8,128)S(1)}, u32[]{:S(2)}, u32[]{:S(2)}) collective-permute-start(f32[2,128,256]{2,1,0:T(8,128)S(1)} %get-tuple-element.76), channel_id=1, source_target_pairs={{16,32},{32,16},{48,64},{64,48},{80,96},{96,80},{17,33},{33,17},{4... | collective-permute-start | bytes 786440 | tf_op jit(solution)/shard_map/gradient_rows/ppermute | solution.py:568
  112.0 0.1 slice_reduce_fusion
  112.1 0.1 reshape_squeeze.3
  112.2 0.7 copy.23
  112.8 0.6 fusion.5
  114.7 0.0 collective-permute-done.11.cross
  114.8 0.0 collective-permute-done.12.same
  114.8 0.0 copy-start.5
  114.8 0.0 collective-permute-done.9.even
  114.8 0.0 copy-start.6
  114.8 3.9 %collective-permute-done.10.odd = f32[2,128,256]{2,1,0:T(8,128)S(1)} collective-permute-done((f32[2,128,256]{2,1,0:T(8,128)S(1)}, f32[2,128,256]{2,1,0:T(8,128)S(1)}, u32[]{:S(2)}, u32[]{:S(2)}) %collective-permute-start.10) | collective-permute-done | bytes 262176 | tf_op jit(solution)/shard_map/gradient_rows/ppermute | solution.py:568
  118.7 0.0 copy-done.5
  118.7 0.7 copy-done.7
  119.4 3.0 %shard_map.133 = f32[2,256,256]{2,1,0:T(8,128)} custom-call(s32[2]{0:T(128)} %pad_add_fusion.place, f32[2,256,256]{2,1,0:T(8,128)} %get-tuple-element.56.center, f32[2,128,256]{2,1,0:T(8,128)} %copy-done.6, f32[2,128,256]{2,1,0:T(8,128)} %copy-done.7, f32[2,256,128]{2,1,0:T(8,128)} %copy-done.4, f32[2,256,128]{2,1,0:T(8,128)} %copy-done.5, ...), custom_call_target="tpu_custom_call" | custom-call | flops 1048576 | bytes 3145728 | tf_op jit(solution)/shard_map/pallas_call | solution.py:478
  122.4 0.0 collective-permute-done.13.other
  122.4 0.8 copy-done.1
  123.2 2.9 %probe_gather.1 = f32[4,256,256]{2,1,0:T(8,128)} custom-call(s32[2]{0:T(128)} %pad_add_fusion.place, f32[64,16,128]{2,1,0:T(8,128)} %copy-done, f32[64,16,128]{2,1,0:T(8,128)} %copy-done.1), custom_call_target="tpu_custom_call" | custom-call | flops 1048576 | bytes 2097152 | tf_op jit(solution)/shard_map/probe_gather/pallas_call | solution.py:478
  (35 shorter events, 0.2 us)
Async XLA Ops:
  5.4 14.0 %collective-permute-start = (f32[2,136,256]{2,1,0:T(8,128)}, f32[2,136,256]{2,1,0:T(8,128)S(1)}, u32[]{:S(2)}, u32[]{:S(2)}) collective-permute-start(f32[2,136,256]{2,1,0:T(8,128)} %get-tuple-element.35), channel_id=1, source_target_pairs={{0,16},{16,0},{32,48},{48,32},{64,80},{80,64},{96,112},{112,96},{1... | collective-permute-start | bytes 835592 | tf_op jit(solution)/shard_map/object_halo/ppermute | solution.py:568
  5.8 14.6 %collective-permute-start.1 = (f32[2,136,256]{2,1,0:T(8,128)}, f32[2,136,256]{2,1,0:T(8,128)S(1)}, u32[]{:S(2)}, u32[]{:S(2)}) collective-permute-start(f32[2,136,256]{2,1,0:T(8,128)} %get-tuple-element.36), channel_id=1, source_target_pairs={{16,32},{32,16},{48,64},{64,48},{80,96},{96,80},{17,33},{33,17},{4... | collective-permute-start | bytes 835592 | tf_op jit(solution)/shard_map/object_halo/ppermute | solution.py:568
  11.8 12.6 %collective-permute-start.2 = (f32[2,264,128]{2,1,0:T(8,128)}, f32[2,264,128]{2,1,0:T(8,128)S(1)}, u32[]{:S(2)}, u32[]{:S(2)}) collective-permute-start(f32[2,264,128]{2,1,0:T(8,128)} %get-tuple-element.37), channel_id=1, source_target_pairs={{1,2},{2,1},{3,4},{4,3},{5,6},{6,5},{7,8},{8,7},{9,10},{10,9},{11,... | collective-permute-start | bytes 811016 | tf_op jit(solution)/shard_map/object_halo/ppermute | solution.py:572
  15.6 8.8 %collective-permute-start.3 = (f32[2,264,128]{2,1,0:T(8,128)}, f32[2,264,128]{2,1,0:T(8,128)S(1)}, u32[]{:S(2)}, u32[]{:S(2)}) collective-permute-start(f32[2,264,128]{2,1,0:T(8,128)} %get-tuple-element.38), channel_id=1, source_target_pairs={{0,1},{1,0},{2,3},{3,2},{4,5},{5,4},{6,7},{7,6},{8,9},{9,8},{10,11... | collective-permute-start | bytes 811016 | tf_op jit(solution)/shard_map/object_halo/ppermute | solution.py:572
  19.4 11.3 %copy-start.2 = (f32[2,136,256]{2,1,0:T(8,128)}, f32[2,136,256]{2,1,0:T(8,128)S(1)}, u32[]{:S(2)}) copy-start(f32[2,136,256]{2,1,0:T(8,128)S(1)} %collective-permute-done.even_strip) | copy-start | bytes 835588
  20.4 10.3 %copy-start.3 = (f32[2,136,256]{2,1,0:T(8,128)}, f32[2,136,256]{2,1,0:T(8,128)S(1)}, u32[]{:S(2)}) copy-start(f32[2,136,256]{2,1,0:T(8,128)S(1)} %collective-permute-done.1.odd_strip) | copy-start | bytes 835588
  20.5 10.2 %collective-permute-start.4 = (f32[2,2,136,128]{3,2,1,0:T(8,128)S(1)}, f32[2,2,136,128]{3,2,1,0:T(8,128)S(1)}, u32[]{:S(2)}, u32[]{:S(2)}) collective-permute-start(f32[2,2,136,128]{3,2,1,0:T(8,128)S(1)} %get-tuple-element.75), channel_id=1, source_target_pairs={{1,2},{2,1},{3,4},{4,3},{5,6},{6,5},{7,8},{8,7},{9,10},{10,9},{11,... | collective-permute-start | bytes 835592 | tf_op jit(solution)/shard_map/object_corners/ppermute | solution.py:572
  24.3 6.5 %collective-permute-start.5 = (f32[2,2,136,128]{3,2,1,0:T(8,128)S(1)}, f32[2,2,136,128]{3,2,1,0:T(8,128)S(1)}, u32[]{:S(2)}, u32[]{:S(2)}) collective-permute-start(f32[2,2,136,128]{3,2,1,0:T(8,128)S(1)} %get-tuple-element.74), channel_id=1, source_target_pairs={{0,1},{1,0},{2,3},{3,2},{4,5},{5,4},{6,7},{7,6},{8,9},{9,8},{10,11... | collective-permute-start | bytes 835592 | tf_op jit(solution)/shard_map/object_corners/ppermute | solution.py:572
  24.4 6.3 %copy-start.13 = (f32[2,264,128]{2,1,0:T(8,128)}, f32[2,264,128]{2,1,0:T(8,128)S(1)}, u32[]{:S(2)}) copy-start(f32[2,264,128]{2,1,0:T(8,128)S(1)} %collective-permute-done.2.cross) | copy-start | bytes 811012
  24.4 6.3 %copy-start.14 = (f32[2,264,128]{2,1,0:T(8,128)}, f32[2,264,128]{2,1,0:T(8,128)S(1)}, u32[]{:S(2)}) copy-start(f32[2,264,128]{2,1,0:T(8,128)S(1)} %collective-permute-done.3.same) | copy-start | bytes 811012
  30.7 0.7 copy-start.11
  31.4 0.7 copy-start.12
  49.8 3.5 %collective-permute-start.6 = (f32[64,24,128]{2,1,0:T(8,128)}, f32[64,24,128]{2,1,0:T(8,128)S(1)}, u32[]{:S(2)}, u32[]{:S(2)}) collective-permute-start(f32[64,24,128]{2,1,0:T(8,128)} %get-tuple-element.42), channel_id=1, source_target_pairs={{0,1},{1,0},{2,3},{3,2},{4,5},{5,4},{6,7},{7,6},{8,9},{9,8},{10,11... | collective-permute-start | bytes 2359304 | tf_op jit(solution)/shard_map/probe_reduce/ppermute | solution.py:572
  55.4 26.0 %all-to-all-start = ((f32[64,24,128]{2,1,0:T(8,128)}), f32[64,24,128]{2,1,0:T(8,128)S(1)}, u32[]{:S(2)}, u32[]{:S(2)}) async-start(f32[64,24,128]{2,1,0:T(8,128)} %add.9), calls=%async_computation | async-start | bytes 1572864 | tf_op jit(solution)/shard_map/probe_reduce/all_to_all | solution.py:608
  79.0 12.1 %copy-start.17 = (f32[2,2,128,128]{3,2,1,0:T(8,128)S(1)}, f32[2,2,128,128]{3,2,1,0:T(8,128)}, u32[]{:S(2)}) copy-start(f32[2,2,128,128]{3,2,1,0:T(8,128)} %get-tuple-element.58) | copy-start | bytes 786436
  79.0 15.1 %copy-start.16 = (f32[2,256,128]{2,1,0:T(8,128)S(1)}, f32[2,256,128]{2,1,0:T(8,128)}, u32[]{:S(2)}) copy-start(f32[2,256,128]{2,1,0:T(8,128)} %get-tuple-element.61) | copy-start | bytes 786436
  79.0 17.7 %copy-start.15 = (f32[2,256,128]{2,1,0:T(8,128)S(1)}, f32[2,256,128]{2,1,0:T(8,128)}, u32[]{:S(2)}) copy-start(f32[2,256,128]{2,1,0:T(8,128)} %get-tuple-element.62) | copy-start | bytes 786436
  79.0 26.5 %copy-start.8 = (f32[2,128,256]{2,1,0:T(8,128)S(1)}, f32[2,128,256]{2,1,0:T(8,128)}, u32[]{:S(2)}) copy-start(f32[2,128,256]{2,1,0:T(8,128)} %get-tuple-element.57) | copy-start | bytes 786436
  79.0 26.5 %copy-start.9 = (f32[2,128,256]{2,1,0:T(8,128)S(1)}, f32[2,128,256]{2,1,0:T(8,128)}, u32[]{:S(2)}) copy-start(f32[2,128,256]{2,1,0:T(8,128)} %get-tuple-element.60) | copy-start | bytes 786436
  81.5 30.4 %copy-start.10 = (f32[8,128]{1,0:T(8,128)S(1)}, f32[8,128]{1,0:T(8,128)}, u32[]{:S(2)}) copy-start(f32[8,128]{1,0:T(8,128)} %get-tuple-element.65) | copy-start | bytes 12292
  82.4 18.8 %all-to-all-start.1 = ((f32[64,16,128]{2,1,0:T(8,128)}), f32[64,16,128]{2,1,0:T(8,128)S(1)}, u32[]{:S(2)}, u32[]{:S(2)}) async-start(f32[64,16,128]{2,1,0:T(8,128)} %broadcast_in_dim.2), calls=%async_computation.1 | async-start | bytes 1048576 | tf_op jit(solution)/shard_map/probe_gather/all_to_all | solution.py:635
  89.8 13.6 %collective-permute-start.8 = (f32[2,2,128,128]{3,2,1,0:T(8,128)}, f32[2,2,128,128]{3,2,1,0:T(8,128)S(1)}, u32[]{:S(2)}, u32[]{:S(2)}) collective-permute-start(f32[2,2,128,128]{3,2,1,0:T(8,128)} %get-tuple-element.59), channel_id=1, source_target_pairs={{0,1},{1,0},{2,3},{3,2},{4,5},{5,4},{6,7},{7,6},{8,9},{9,8},{10,11... | collective-permute-start | bytes 786440 | tf_op jit(solution)/shard_map/gradient_corners/ppermute | solution.py:572
  91.1 14.4 %collective-permute-start.7 = (f32[2,2,128,128]{3,2,1,0:T(8,128)S(1)}, f32[2,2,128,128]{3,2,1,0:T(8,128)S(1)}, u32[]{:S(2)}, u32[]{:S(2)}) collective-permute-start(f32[2,2,128,128]{3,2,1,0:T(8,128)S(1)} %copy-done.17), channel_id=1, source_target_pairs={{1,2},{2,1},{3,4},{4,3},{5,6},{6,5},{7,8},{8,7},{9,10},{10,9},{11,... | collective-permute-start | bytes 786440 | tf_op jit(solution)/shard_map/gradient_corners/ppermute | solution.py:572
  94.1 20.6 %collective-permute-start.11 = (f32[2,256,128]{2,1,0:T(8,128)S(1)}, f32[2,256,128]{2,1,0:T(8,128)S(1)}, u32[]{:S(2)}, u32[]{:S(2)}) collective-permute-start(f32[2,256,128]{2,1,0:T(8,128)S(1)} %copy-done.16), channel_id=1, source_target_pairs={{1,2},{2,1},{3,4},{4,3},{5,6},{6,5},{7,8},{8,7},{9,10},{10,9},{11,... | collective-permute-start | bytes 786440 | tf_op jit(solution)/shard_map/gradient_rows/ppermute | solution.py:572
  96.7 18.1 %collective-permute-start.12 = (f32[2,256,128]{2,1,0:T(8,128)S(1)}, f32[2,256,128]{2,1,0:T(8,128)S(1)}, u32[]{:S(2)}, u32[]{:S(2)}) collective-permute-start(f32[2,256,128]{2,1,0:T(8,128)S(1)} %copy-done.15), channel_id=1, source_target_pairs={{0,1},{1,0},{2,3},{3,2},{4,5},{5,4},{6,7},{7,6},{8,9},{9,8},{10,11... | collective-permute-start | bytes 786440 | tf_op jit(solution)/shard_map/gradient_rows/ppermute | solution.py:572
  101.2 21.2 %copy-start = (f32[64,16,128]{2,1,0:T(8,128)}, f32[64,16,128]{2,1,0:T(8,128)S(1)}, u32[]{:S(2)}) copy-start(f32[64,16,128]{2,1,0:T(8,128)S(1)} %all-to-all-done.1.mine) | copy-start | bytes 1572868
  101.2 21.2 %collective-permute-start.13 = (f32[64,16,128]{2,1,0:T(8,128)S(1)}, f32[64,16,128]{2,1,0:T(8,128)S(1)}, u32[]{:S(2)}, u32[]{:S(2)}) collective-permute-start(f32[64,16,128]{2,1,0:T(8,128)S(1)} %all-to-all-done.1.mine), channel_id=1, source_target_pairs={{0,1},{1,0},{2,3},{3,2},{4,5},{5,4},{6,7},{7,6},{8,9},{9,8},{10,11... | collective-permute-start | bytes 1572872 | tf_op jit(solution)/shard_map/probe_gather/ppermute | solution.py:572
  105.6 9.2 %collective-permute-start.9 = (f32[2,128,256]{2,1,0:T(8,128)S(1)}, f32[2,128,256]{2,1,0:T(8,128)S(1)}, u32[]{:S(2)}, u32[]{:S(2)}) collective-permute-start(f32[2,128,256]{2,1,0:T(8,128)S(1)} %get-tuple-element.77), channel_id=1, source_target_pairs={{0,16},{16,0},{32,48},{48,32},{64,80},{80,64},{96,112},{112,96},{1... | collective-permute-start | bytes 786440 | tf_op jit(solution)/shard_map/gradient_rows/ppermute | solution.py:568
  106.2 12.5 %collective-permute-start.10 = (f32[2,128,256]{2,1,0:T(8,128)S(1)}, f32[2,128,256]{2,1,0:T(8,128)S(1)}, u32[]{:S(2)}, u32[]{:S(2)}) collective-permute-start(f32[2,128,256]{2,1,0:T(8,128)S(1)} %get-tuple-element.76), channel_id=1, source_target_pairs={{16,32},{32,16},{48,64},{64,48},{80,96},{96,80},{17,33},{33,17},{4... | collective-permute-start | bytes 786440 | tf_op jit(solution)/shard_map/gradient_rows/ppermute | solution.py:568
  114.8 3.9 %copy-start.4 = (f32[2,256,128]{2,1,0:T(8,128)}, f32[2,256,128]{2,1,0:T(8,128)S(1)}, u32[]{:S(2)}) copy-start(f32[2,256,128]{2,1,0:T(8,128)S(1)} %collective-permute-done.11.cross) | copy-start | bytes 786436
  114.8 3.9 %copy-start.5 = (f32[2,256,128]{2,1,0:T(8,128)}, f32[2,256,128]{2,1,0:T(8,128)S(1)}, u32[]{:S(2)}) copy-start(f32[2,256,128]{2,1,0:T(8,128)S(1)} %collective-permute-done.12.same) | copy-start | bytes 786436
  114.8 3.9 %copy-start.6 = (f32[2,128,256]{2,1,0:T(8,128)}, f32[2,128,256]{2,1,0:T(8,128)S(1)}, u32[]{:S(2)}) copy-start(f32[2,128,256]{2,1,0:T(8,128)S(1)} %collective-permute-done.9.even) | copy-start | bytes 786436
  118.7 0.7 copy-start.7
  122.4 0.8 copy-start.1

commit v3 on v2

--- a/solution.py
+++ b/solution.py
@@ -17,7 +17,7 @@
 BF = jnp.bfloat16
 F32 = jnp.float32
 AXES = ("row", "col")
-VMEM_LIMIT = 56 * 2**20
+VMEM_LIMIT = 32 * 2**20
 
 
 def transform_matrices():
@@ -38,14 +38,7 @@
 
 
 def constants():
-    right_f, left_f, right_i, left_i = [], [], [], []
-    for matrix in transform_matrices():
-        high, low = split_np(matrix)
-        right_f.append(np.concatenate([high, high, low], 0))
-        left_f.append(np.concatenate([high.T, low.T, high.T], 1))
-        right_i.append(np.concatenate([high.T, high.T, low.T], 0))
-        left_i.append(np.concatenate([high, low, high], 1))
-    return [np.stack(x) for x in (right_f, left_f, right_i, left_i)]
+    return np.stack([np.stack([np.stack(split_np(x)) for x in (m, m.T)]) for m in transform_matrices()])
 
 
 def permutation():
@@ -101,66 +94,92 @@
         permuted[j] = dot(rows[...], jnp.concatenate(split3(moved), 0))
 
 
-def pack_kernel(starts, place, own, even, odd, cross, same):
-    row_odd, core = place[0], place[1]
+def place_of():
+    return lax.rem(lax.axis_index("row"), 2), lax.rem(lax.axis_index("col"), 2)
+
+
+def run_all(copies):
+    for copy in copies:
+        copy.start()
+    for copy in copies:
+        copy.wait()
+
+
+def pack_kernel(starts, own, even, odd, cross, same, offsets, sems):
+    row_odd, core = place_of()
     lanes = lane_index(8)
-    offsets = jnp.zeros((8, HALF), F32)
-    for j in range(starts.shape[0]):
+    value = jnp.zeros((8, HALF), F32)
+    for j in range(starts.shape[1]):
         for d in range(2):
-            offsets = jnp.where(lanes == 2 * j + d, (starts[j, d] + 1).astype(F32), offsets)
-    at = pl.multiple_of(HALF * row_odd, HALF)
+            value = jnp.where(lanes == 2 * j + d, (starts[d, j] + 1).astype(F32), value)
     for p in range(2):
-        even[p, :HALF] = own[p, pl.ds(HALF - at, HALF), :]
-        odd[p, :HALF] = own[p, pl.ds(at, HALF), :]
-        for b in range(2):
-            for out in (even, odd):
-                out[p, HALF:, b * HALF : (b + 1) * HALF] = offsets
-        for out in (cross, same):
-            out[p, SIZE:] = offsets
-
-    for k in range(2):
-
-        @pl.when(core == k)
-        def _(k=k):
-            for p in range(2):
-                cross[p, :SIZE] = own[p, :, k * HALF : (k + 1) * HALF]
-                same[p, :SIZE] = own[p, :, (1 - k) * HALF : (2 - k) * HALF]
-
-
-def sides(place):
-    even_row = pl.multiple_of(3 * HALF * (1 - place[0]), HALF)
-    odd_row = pl.multiple_of(3 * HALF * place[0], HALF)
-    return even_row, odd_row, 3 * place[1], 3 - 3 * place[1]
+        offsets[p, :, :HALF] = value
+        offsets[p, :, HALF:] = value
+    top = pl.ds(pl.multiple_of(HALF * row_odd, HALF), HALF)
+    bottom = pl.ds(pl.multiple_of(HALF * (1 - row_odd), HALF), HALF)
+    near = pl.ds(pl.multiple_of(HALF * core, HALF), HALF)
+    far = pl.ds(pl.multiple_of(HALF * (1 - core), HALF), HALF)
+    moves = [
+        (own.at[:, top, :], odd.at[:, :HALF, :]),
+        (own.at[:, bottom, :], even.at[:, :HALF, :]),
+        (own.at[:, :, near], cross.at[:, :SIZE, :]),
+        (own.at[:, :, far], same.at[:, :SIZE, :]),
+        (offsets, odd.at[:, HALF:, :]),
+        (offsets, even.at[:, HALF:, :]),
+        (offsets.at[:, :, :HALF], cross.at[:, SIZE:, :]),
+        (offsets.at[:, :, :HALF], same.at[:, SIZE:, :]),
+    ]
+    run_all([pltpu.make_async_copy(x, y, sems.at[n]) for n, (x, y) in enumerate(moves)])
+
+
+def sides():
+    row_odd, core = place_of()
+    even_rows = pl.ds(pl.multiple_of(3 * HALF * (1 - row_odd), HALF), HALF)
+    odd_rows = pl.ds(pl.multiple_of(3 * HALF * row_odd, HALF), HALF)
+    return even_rows, odd_rows, 3 * core, 3 - 3 * core
 
 
 def transform_kernel(
-    starts, place, own, even_strip, odd_strip, cross, same, cross_corner, same_corner, probe, measured,
-    right_f, left_f, right_i, left_i,
-    keep, send, object_part, patch,
-    tile, totals, xs, zs, gs, ys, back, sums,
+    starts, own, even_strip, odd_strip, cross, same, cross_corner, same_corner, probe_in, matrices, measured,
+    keep, send, object_part, patch, around,
+    tile, probe, mats, offsets, totals, xs, zs, gs, ys, back, sums, sems,
 ):
     step = pl.program_id(0)
     modes = probe.shape[0]
     lanes = lane_index(CHUNK)
+    late = pltpu.make_async_copy(matrices, mats, sems.at[0])
 
     @pl.when(step == 0)
     def _():
-        even_row, odd_row, cross_block, same_block = sides(place)
-        for p in range(2):
-            for block, strip, corner in ((cross_block, cross, cross_corner), (same_block, same, same_corner)):
-                tile[p, block, 128:384] = strip[p, :SIZE]
-                tile[p, block, pl.ds(even_row, HALF)] = corner[0, p, :HALF]
-                tile[p, block, pl.ds(odd_row, HALF)] = corner[1, p, :HALF]
-            for b in range(2):
-                span = slice(b * HALF, (b + 1) * HALF)
-                tile[p, 1 + b, 128:384] = own[p, :, span]
-                tile[p, 1 + b, pl.ds(even_row, HALF)] = even_strip[p, :HALF, span]
-                tile[p, 1 + b, pl.ds(odd_row, HALF)] = odd_strip[p, :HALF, span]
-            tile[p, 4] = jnp.zeros((2 * SIZE, HALF), F32)
+        late.start()
+        even_rows, odd_rows, cross_block, same_block = sides()
+        center = pl.ds(HALF, SIZE)
+        moves = [(probe_in, probe)]
+        for block, strip, corner in ((cross_block, cross, cross_corner), (same_block, same, same_corner)):
+            moves.append((strip.at[:, :SIZE, :], tile.at[:, block, center, :]))
+            moves.append((corner.at[0, :, :HALF, :], tile.at[:, block, even_rows, :]))
+            moves.append((corner.at[1, :, :HALF, :], tile.at[:, block, odd_rows, :]))
+        for b in range(2):
+            span = pl.ds(b * HALF, HALF)
+            moves.append((own.at[:, :, span], tile.at[:, 1 + b, center, :]))
+            moves.append((even_strip.at[:, :HALF, span], tile.at[:, 1 + b, even_rows, :]))
+            moves.append((odd_strip.at[:, :HALF, span], tile.at[:, 1 + b, odd_rows, :]))
+        strips = [x.at[0] for x in (even_strip, odd_strip, cross, same)]
+        strips += [x.at[n, 0] for x in (cross_corner, same_corner) for n in range(2)]
+        for n, strip in enumerate(strips):
+            moves.append((strip.at[pl.ds(strip.shape[0] - 8, 8), pl.ds(0, HALF)], offsets.at[n]))
+        copies = [pltpu.make_async_copy(x, y, sems.at[1 + n]) for n, (x, y) in enumerate(moves)]
+        for copy in copies:
+            copy.start()
+        tile[:, 4] = jnp.zeros((2, 2 * SIZE, HALF), F32)
         totals[...] = jnp.zeros_like(totals)
         sums[...] = jnp.zeros_like(sums)
-
-    row, col = starts[step, 0], starts[step, 1]
+        for copy in copies:
+            copy.wait()
+        for n in range(8):
+            around[pl.ds(n, 1), :] = offsets[n, :1, :].astype(jnp.int32)
+
+    row, col = starts[0, step], starts[1, step]
     base, shift = col // HALF, lax.rem(col, HALF)
 
     for i in range(0, SIZE, CHUNK):
@@ -186,8 +205,20 @@
                     xs[odd, at, SIZE + p * HALF : SIZE + (p + 1) * HALF] = low
                     xs[odd, at, 2 * SIZE + p * HALF : 2 * SIZE + (p + 1) * HALF] = high
 
+    @pl.when(step == 0)
+    def _():
+        late.wait()
+
+    def right(odd, transposed):
+        high, low = mats[odd, transposed, 0], mats[odd, transposed, 1]
+        return jnp.concatenate([high, high, low], 0)
+
+    def left(odd, transposed):
+        high, low = mats[odd, transposed, 0], mats[odd, transposed, 1]
+        return jnp.concatenate([high, low, high], 1)
+
     for odd in range(2):
-        ys[odd] = dot(xs[odd], right_f[odd])
+        ys[odd] = dot(xs[odd], right(odd, 0))
 
     for m in range(modes):
         for odd in range(2):
@@ -207,7 +238,7 @@
     error = jnp.zeros((8, HALF), F32)
     energy = jnp.zeros((8, HALF), F32)
     for odd_row in range(2):
-        far = [dot(left_f[odd_row], zs[m, odd_row]) for m in range(modes)]
+        far = [dot(left(odd_row, 1), zs[m, odd_row]) for m in range(modes)]
         for i in range(0, HALF, CHUNK):
             parts = [(f[i : i + CHUNK], f[HALF + i : HALF + i + CHUNK]) for f in far]
             intensity = parts[0][0] ** 2 + parts[0][1] ** 2 + (parts[1][0] ** 2 + parts[1][1] ** 2)
@@ -231,8 +262,8 @@
     sums[1] += energy
 
     for m in range(modes):
-        even = dot(left_i[0], gs[m, 0])
-        odds = dot(left_i[1], gs[m, 1])
+        even = dot(left(0, 0), gs[m, 0])
+        odds = dot(left(1, 0), gs[m, 1])
         for i in range(0, HALF, CHUNK):
             for p in range(2):
                 a, b = even[p * HALF + i : p * HALF + i + CHUNK], odds[p * HALF + i : p * HALF + i + CHUNK]
@@ -246,7 +277,7 @@
                         xs[odd, at, 2 * SIZE + p * HALF : 2 * SIZE + (p + 1) * HALF] = high[:, span]
 
     for odd in range(2):
-        back[odd] = dot(xs[odd], right_i[odd])
+        back[odd] = dot(xs[odd], right(odd, 1))
 
     for i in range(0, SIZE, CHUNK):
         part = pl.ds(i, CHUNK)
@@ -270,7 +301,7 @@
 
     @pl.when(step == pl.num_programs(0) - 1)
     def _():
-        core = place[1]
+        core = place_of()[1]
         scalar = jnp.where(lax.broadcasted_iota(jnp.int32, (1, 4, HALF), 2) == 0, jnp.sum(sums[0]), jnp.sum(sums[1]))
         for out, block in ((keep, core), (send, 1 - core)):
             for c in range(5):
@@ -279,7 +310,7 @@
 
 
 def place_kernel(
-    starts, place, object_part, patch, probe,
+    starts, object_part, patch, probe,
     center, even, odd, cross, same, cross_corner, same_corner, steps,
     padded, power, accum,
 ):
@@ -295,7 +326,7 @@
             part = pl.ds(i, CHUNK)
             power[part] = probe_power(probe, part)
 
-    row, col = starts[step, 0], starts[step, 1]
+    row, col = starts[0, step], starts[1, step]
     base, shift = col // HALF, lax.rem(col, HALF)
     for p in range(2):
         for b in range(2):
@@ -336,24 +367,24 @@
 
     @pl.when(step == pl.num_programs(0) - 1)
     def _():
-        even_row, odd_row, cross_block, same_block = sides(place)
+        even_rows, odd_rows, cross_block, same_block = sides()
         for p in range(2):
             for b in range(2):
                 span = slice(b * HALF, (b + 1) * HALF)
                 center[p, :, span] = accum[p, 1 + b, 128:384]
-                even[p, :, span] = accum[p, 1 + b, pl.ds(even_row, HALF)]
-                odd[p, :, span] = accum[p, 1 + b, pl.ds(odd_row, HALF)]
+                even[p, :, span] = accum[p, 1 + b, even_rows]
+                odd[p, :, span] = accum[p, 1 + b, odd_rows]
             for block, strip, corner in ((cross_block, cross, cross_corner), (same_block, same, same_corner)):
                 strip[p] = accum[p, block, 128:384]
-                corner[0, p] = accum[p, block, pl.ds(even_row, HALF)]
-                corner[1, p] = accum[p, block, pl.ds(odd_row, HALF)]
+                corner[0, p] = accum[p, block, even_rows]
+                corner[1, p] = accum[p, block, odd_rows]
 
 
 def probe_power(probe, part):
     return (probe[0, 0, part] ** 2 + probe[0, 1, part] ** 2) + (probe[1, 0, part] ** 2 + probe[1, 1, part] ** 2)
 
 
-def light_kernel(starts, around, place, probe, light, power, accum):
+def light_kernel(starts, around, probe, light, power, accum):
     accum[...] = jnp.zeros_like(accum)
     for i in range(0, SIZE, CHUNK):
         part = pl.ds(i, CHUNK)
@@ -361,7 +392,8 @@
         power[0, part] = total[:, :HALF]
         power[1, part] = total[:, HALF:]
     lanes = lane_index(CHUNK)
-    even, cross = 1 - 2 * place[0], 2 * place[1] - 1
+    row_odd, core = place_of()
+    even, cross = 1 - 2 * row_odd, 2 * core - 1
     neighbours = [(even, None), (-even, None), (None, cross), (None, -cross)]
     neighbours += [(even, cross), (-even, cross), (even, -cross), (-even, -cross)]
 
@@ -386,10 +418,11 @@
             for b, value in enumerate(moved):
                 accum[base + b, where, :] += value
 
-    for j in range(starts.shape[0]):
-        add(starts[j, 0], starts[j, 1], None, None)
+    count = starts.shape[1]
+    for j in range(count):
+        add(starts[0, j], starts[1, j], None, None)
     for n, (down, right) in enumerate(neighbours):
-        for j in range(starts.shape[0]):
+        for j in range(count):
             row, col = around[n, 2 * j] - 1, around[n, 2 * j + 1] - 1
             near = row >= 0
             if down is not None:
@@ -405,15 +438,16 @@
     light[:, HALF:] = accum[3, 256:512]
 
 
-def update_kernel(place, center, even, odd, cross, same, light, out, total):
+def update_kernel(center, even, odd, cross, same, light, out, total):
     for p in range(2):
         total[p] = center[p]
-    even_half = pl.ds(pl.multiple_of(HALF * (1 - place[0]), HALF), HALF)
-    odd_half = pl.ds(pl.multiple_of(HALF * place[0], HALF), HALF)
+    row_odd, core = place_of()
+    even_half = pl.ds(pl.multiple_of(HALF * (1 - row_odd), HALF), HALF)
+    odd_half = pl.ds(pl.multiple_of(HALF * row_odd, HALF), HALF)
     for p in range(2):
         total[p, even_half, :] += even[p]
         total[p, odd_half, :] += odd[p]
-    swapped = place[1] == 1
+    swapped = core == 1
     for i in range(0, SIZE, CHUNK):
         part = pl.ds(i, CHUNK)
         scale = 1.0 / (light[part] + object_damping)
@@ -423,17 +457,19 @@
             out[p, part, HALF:] = (total[p, part, HALF:] + jnp.where(swapped, a, b)) * scale[:, HALF:]
 
 
-def assemble_kernel(place, mine, other, out):
+def assemble_kernel(mine, other, out):
+    core = place_of()[1]
+
     def write(source, block):
         for c in range(4):
             out[c, :, block * HALF : (block + 1) * HALF] = source[:, 4 * c : 4 * c + 4, :].reshape(SIZE, HALF)
 
-    @pl.when(place[1] == 0)
+    @pl.when(core == 0)
     def _():
         write(mine, 0)
         write(other, 1)
 
-    @pl.when(place[1] == 1)
+    @pl.when(core == 1)
     def _():
         write(mine, 1)
         write(other, 0)
@@ -441,6 +477,9 @@
 
 def whole(*shape):
     return pl.BlockSpec(shape, lambda *_: (0,) * len(shape))
+
+
+ANY = pl.BlockSpec(memory_space=pl.ANY)
 
 
 def stepped(*shape):
@@ -478,9 +517,21 @@
     return call(*scalars, *arrays)
 
 
-def pack(starts, place, own):
+def pack(starts, own):
     rows, columns = (2, HALF + 8, SIZE), (2, SIZE + 8, HALF)
-    return simple(pack_kernel, [starts, place], [own], [rows, rows, columns, columns], [], 1 << 10, 2 << 20)
+    return pl.pallas_call(
+        pack_kernel,
+        out_shape=shaped([rows, rows, columns, columns]),
+        grid_spec=pltpu.PrefetchScalarGridSpec(
+            num_scalar_prefetch=1,
+            grid=(),
+            in_specs=[ANY],
+            out_specs=[ANY] * 4,
+            scratch_shapes=[pltpu.VMEM((2, 8, SIZE), F32), pltpu.SemaphoreType.DMA((8,))],
+        ),
+        compiler_params=params(),
+        cost_estimate=cost(1 << 10, 2 << 20),
+    )(starts, own)
 
 
 def prepare(measured):
@@ -489,22 +540,26 @@
     return simple(prepare_kernel, [], arrays, measured.shape, [], 1 << 30, 3 << 20)
 
 
-def transforms(starts, place, own, halo, probe, measured):
-    mats = [jnp.asarray(x) for x in constants()]
-    arrays = [own, *halo, probe]
+def transforms(starts, own, halo, probe, measured):
+    mats = jnp.asarray(constants())
+    arrays = [own, *halo, probe, mats]
     count = measured.shape[0]
     halves = (64, 24, HALF)
     fields = (2, 2, SIZE, HALF)
     return pl.pallas_call(
         transform_kernel,
-        out_shape=shaped([halves, halves, (count, *fields), (count, *fields)]),
+        out_shape=shaped([halves, halves, (count, *fields), (count, *fields)])
+        + [jax.ShapeDtypeStruct((8, HALF), jnp.int32)],
         grid_spec=pltpu.PrefetchScalarGridSpec(
-            num_scalar_prefetch=2,
+            num_scalar_prefetch=1,
             grid=(count,),
-            in_specs=[whole(*x.shape) for x in arrays] + [stepped(SIZE, SIZE)] + [whole(*x.shape) for x in mats],
-            out_specs=[whole(*halves), whole(*halves), stepped(*fields), stepped(*fields)],
+            in_specs=[ANY] * len(arrays) + [stepped(SIZE, SIZE)],
+            out_specs=[whole(*halves), whole(*halves), stepped(*fields), stepped(*fields), whole(8, HALF)],
             scratch_shapes=[
                 pltpu.VMEM((2, 5, 2 * SIZE, HALF), F32),
+                pltpu.VMEM(probe.shape, F32),
+                pltpu.VMEM(mats.shape, BF),
+                pltpu.VMEM((8, 8, HALF), F32),
                 pltpu.VMEM((2, 5, SIZE, HALF), F32),
                 pltpu.VMEM((2, 2 * SIZE, 3 * SIZE), BF),
                 pltpu.VMEM((2, 2, 3 * SIZE, SIZE), BF),
@@ -512,14 +567,15 @@
                 pltpu.VMEM((2, 2 * SIZE, SIZE), F32),
                 pltpu.VMEM((2, 2 * SIZE, SIZE), F32),
                 pltpu.VMEM((2, 8, HALF), F32),
+                pltpu.SemaphoreType.DMA((24,)),
             ],
         ),
         compiler_params=params(),
         cost_estimate=cost(13 << 30, 12 << 20),
-    )(starts, place, *arrays, measured, *mats)
-
-
-def place_parts(starts, place, object_part, patch, probe):
+    )(starts, *arrays, measured)
+
+
+def place_parts(starts, object_part, patch, probe):
     count = patch.shape[0]
     fields = (2, 2, SIZE, HALF)
     rows, columns, corners = (2, HALF, SIZE), (2, SIZE, HALF), (2, 2, HALF, HALF)
@@ -528,7 +584,7 @@
         place_kernel,
         out_shape=shaped(shapes),
         grid_spec=pltpu.PrefetchScalarGridSpec(
-            num_scalar_prefetch=2,
+            num_scalar_prefetch=1,
             grid=(count,),
             in_specs=[stepped(*fields), stepped(*fields), whole(*probe.shape)],
             out_specs=[whole(*s) for s in shapes],
@@ -540,21 +596,21 @@
         ),
         compiler_params=params(),
         cost_estimate=cost(5 << 30, 8 << 20),
-    )(starts, place, object_part, patch, probe)
-
-
-def illuminate(starts, around, place, probe):
+    )(starts, object_part, patch, probe)
+
+
+def illuminate(starts, around, probe):
     scratch = [(2, SIZE, HALF), (7, 3 * SIZE, HALF)]
-    return simple(light_kernel, [starts, around, place], [probe], (SIZE, SIZE), scratch, 2 << 30, 4 << 20)
-
-
-def update(place, arrays):
+    return simple(light_kernel, [starts, around], [probe], (SIZE, SIZE), scratch, 2 << 30, 4 << 20)
+
+
+def update(arrays):
     shape = arrays[0].shape
-    return simple(update_kernel, [place], arrays, shape, [shape], 1 << 20, 3 << 20)
-
-
-def assemble(place, mine, other):
-    return simple(assemble_kernel, [place], [mine, other], (4, SIZE, SIZE), [], 1 << 20, 2 << 20)
+    return simple(update_kernel, [], arrays, shape, [shape], 1 << 20, 3 << 20)
+
+
+def assemble(mine, other):
+    return simple(assemble_kernel, [], [mine, other], (4, SIZE, SIZE), [], 1 << 20, 2 << 20)
 
 
 def pairs_from(first, count):
@@ -577,17 +633,16 @@
 
 
 def local(object_tile, probe, amplitudes, offsets):
-    starts = offsets[0, 0]
+    starts = offsets[0, 0].T
     measured = amplitudes[0, 0]
     core = lax.rem(lax.axis_index("col"), 2)
-    place = jnp.stack([lax.rem(lax.axis_index("row"), 2), core])
     devices = lax.axis_size("row") * lax.axis_size("col")
     groups = [[i for i in range(devices) if i % 2 == k] for k in range(2)]
 
     with jax.named_scope("object_halo"):
-        even, odd, cross, same = pack(starts, place, object_tile)
+        even, odd, cross, same = pack(starts, object_tile)
+        odd = swap_rows(odd, 1)
         even = swap_rows(even, 0)
-        odd = swap_rows(odd, 1)
         cross = swap_columns(cross, 1)
         same = swap_columns(same, 0)
     permuted = prepare(measured)
@@ -597,24 +652,24 @@
         same_corner = swap_columns(half_lanes(rows, core == 1), 0)
 
     halo = [even, odd, cross, same, cross_corner, same_corner]
-    keep, send, object_part, patch = transforms(starts, place, object_tile, halo, probe, permuted)
+    keep, send, object_part, patch, around = transforms(starts, object_tile, halo, probe, permuted)
 
     with jax.named_scope("probe_reduce"):
         chunk = keep + swap_columns(send, 0)
-        around = [x[0, -8:-7, :8] for x in halo[:4]]
-        around += [x[n, 0, -8:-7, :8] for x in halo[4:] for n in range(2)]
-        around = jnp.concatenate(around, 0).astype(jnp.int32)
         chunk, object_part, around = lax.optimization_barrier((chunk, object_part, around))
         chunk = lax.all_to_all(chunk, AXES, 0, 0, axis_index_groups=groups, tiled=True)
 
-    parts = place_parts(starts, place, object_part, patch, probe)
-    light = illuminate(starts, around, place, probe)
-    chunk, parts, light = lax.optimization_barrier((chunk, parts, light))
+    parts = place_parts(starts, object_part, patch, probe)
     center, even, odd, cross, same, cross_corner, same_corner, steps = parts
 
     with jax.named_scope("gradient_corners"):
         cross_corner = swap_columns(cross_corner, 1)
         same_corner = swap_columns(same_corner, 0)
+        cross = swap_columns(cross, 1)
+        same = swap_columns(same, 0)
+    around, steps = lax.optimization_barrier((around, steps))
+    light = illuminate(starts, around, probe)
+    chunk, light, center = lax.optimization_barrier((chunk, light, center))
 
     with jax.named_scope("probe_sum"):
         total = jnp.sum(chunk, axis=0)
@@ -625,17 +680,16 @@
         first = jnp.where(core == 0, cross_corner, same_corner)
         second = jnp.where(core == 0, same_corner, cross_corner)
         added = jnp.concatenate([first, second], -1)
+        odd = swap_rows(odd + added[1], 1)
         even = swap_rows(even + added[0], 0)
-        odd = swap_rows(odd + added[1], 1)
-        cross = swap_columns(cross, 1)
-        same = swap_columns(same, 0)
 
     with jax.named_scope("probe_gather"):
         spread_out = jnp.broadcast_to(quotient.reshape(1, 16, HALF), (devices // 2, 16, HALF))
         gathered = lax.all_to_all(spread_out, AXES, 0, 0, axis_index_groups=groups, tiled=True)
-        probe_update = assemble(place, gathered, swap_columns(gathered, 0)).reshape(probe.shape)
-
-    object_update = update(place, [center, even, odd, cross, same, light])
+        probe_update = assemble(gathered, swap_columns(gathered, 0)).reshape(probe.shape)
+
+    probe_update, even, odd = lax.optimization_barrier((probe_update, even, odd))
+    object_update = update([center, even, odd, cross, same, light])
     position_step = steps[:, 0].reshape(1, 1, -1, 2)
     return (object_update, probe_update, position_step, relative_error)
 

time: 129 us -> 125 us (0.969)
  the two profiles are of different devices: /device:TPU:25 before, /device:TPU:1 now
where the time goes in v3:
time: 125 us
  starting transfers between devices  47.7 us (38%)
  waiting for transfers between devices  32.4 us (26%)
  Pallas kernels  24.1 us (19%)
  local copies, waits for them, and re-layouts  13 us (10%)
  other arithmetic  4.16 us (3%)
  between operations  3.4 us (3%)
    ppermute x10, waiting for transfers between devices, swap_columns(): return lax.ppermute(value, 'col', pairs_from(first, lax.axis_size('col')))  20.8 us
    ppermute x10, starting transfers between devices, swap_columns(): return lax.ppermute(value, 'col', pairs_from(first, lax.axis_size('col')))  19.5 us
    all_to_all x1, starting transfers between devices, local(): lax.all_to_all(chunk, AXES, 0, 0, axis_index_groups=groups, tiled=True)  15.6 us
    pallas_call x1, Pallas kernels, transforms(): pl.pallas_call(transform_kernel, out_shape=shaped([halves, halves, (count...  14.5 us
    unnamed x29, local copies, waits for them, and re-layouts  11.4 us
    all_to_all x1, waiting for transfers between devices, local(): lax.all_to_all(spread_out, AXES, 0, 0, axis_index_groups=groups, tiled=True)  7.01 us
    all_to_all x1, starting transfers between devices, local(): lax.all_to_all(spread_out, AXES, 0, 0, axis_index_groups=groups, tiled=True)  6.75 us
    ppermute x4, starting transfers between devices, swap_rows(): return lax.ppermute(value, 'row', pairs_from(first, lax.axis_size('row')))  5.83 us
  transfers between devices with their start and end apart: 16, of which 6 were waited for; matrix products, arithmetic and copies ran while one was open for 3% of the time, Pallas kernels for 6%

profile of v3, /device:TPU:1, one launch (start us, length us, event | category | flops | bytes accessed | tf_op | source)
XLA Modules:
  0.0 124.7 jit_solution(8900515741206062481)
XLA Ops:
  0.6 0.0 copy-start
  0.6 1.0 copy-done
  1.7 0.7 copy-done.2
  2.4 0.8 object_halo.1
  3.1 2.2 %collective-permute-start = (f32[2,136,256]{2,1,0:T(8,128)S(1)}, f32[2,136,256]{2,1,0:T(8,128)S(1)}, u32[]{:S(2)}, u32[]{:S(2)}) collective-permute-start(f32[2,136,256]{2,1,0:T(8,128)S(1)} %get-tuple-element.34), channel_id=1, source_target_pairs={{0,16},{16,0},{32,48},{48,32},{64,80},{80,64},{96,112},{112,96},{1... | collective-permute-start | bytes 835592 | tf_op jit(solution)/shard_map/object_halo/ppermute | solution.py:624
  5.3 0.7 collective-permute-start.1
  6.0 0.0 copy-start.4
  6.0 1.2 copy-done.4
  7.2 1.0 copy-done.8
  8.2 1.0 copy-done.9
  9.2 1.3 %shard_map.102.measured = f32[4,256,256]{2,1,0:T(8,128)S(1)} custom-call(f32[4,256,256]{2,1,0:T(8,128)S(1)} %bitcast.23, bf16[768,256]{1,0:T(8,128)(2,1)S(1)} %copy-done.9, bf16[256,768]{1,0:T(8,128)(2,1)S(1)} %copy-done.8), custom_call_target="tpu_custom_call" | custom-call | flops 1073741824 | bytes 3145728 | tf_op jit(solution)/shard_map/pallas_call | solution.py:517
  10.5 0.0 copy-start.1
  10.5 0.0 copy-start.3
  10.5 0.0 copy-start.5
  10.6 0.7 collective-permute-done.even_strip
  11.3 0.0 collective-permute-done.1.odd_strip
  11.4 1.7 %collective-permute-start.5 = (f32[2,2,136,128]{3,2,1,0:T(8,128)S(1)}, f32[2,2,136,128]{3,2,1,0:T(8,128)S(1)}, u32[]{:S(2)}, u32[]{:S(2)}) collective-permute-start(f32[2,2,136,128]{3,2,1,0:T(8,128)S(1)} %get-tuple-element.72), channel_id=1, source_target_pairs={{0,1},{1,0},{2,3},{3,2},{4,5},{5,4},{6,7},{7,6},{8,9},{9,8},{10,11... | collective-permute-start | bytes 835592 | tf_op jit(solution)/shard_map/object_corners/ppermute | solution.py:628
  13.1 3.6 %collective-permute-start.4 = (f32[2,2,136,128]{3,2,1,0:T(8,128)S(1)}, f32[2,2,136,128]{3,2,1,0:T(8,128)S(1)}, u32[]{:S(2)}, u32[]{:S(2)}) collective-permute-start(f32[2,2,136,128]{3,2,1,0:T(8,128)S(1)} %get-tuple-element.73), channel_id=1, source_target_pairs={{1,2},{2,1},{3,4},{4,3},{5,6},{6,5},{7,8},{8,7},{9,10},{10,9},{11,... | collective-permute-start | bytes 835592 | tf_op jit(solution)/shard_map/object_corners/ppermute | solution.py:628
  16.7 1.9 %collective-permute-start.2 = (f32[2,264,128]{2,1,0:T(8,128)S(1)}, f32[2,264,128]{2,1,0:T(8,128)S(1)}, u32[]{:S(2)}, u32[]{:S(2)}) collective-permute-start(f32[2,264,128]{2,1,0:T(8,128)S(1)} %get-tuple-element.36), channel_id=1, source_target_pairs={{1,2},{2,1},{3,4},{4,3},{5,6},{6,5},{7,8},{8,7},{9,10},{10,9},{11,... | collective-permute-start | bytes 811016 | tf_op jit(solution)/shard_map/object_halo/ppermute | solution.py:628
  18.7 0.1 collective-permute-start.3
  18.8 12.4 %collective-permute-done.2.cross = f32[2,264,128]{2,1,0:T(8,128)S(1)} collective-permute-done((f32[2,264,128]{2,1,0:T(8,128)S(1)}, f32[2,264,128]{2,1,0:T(8,128)S(1)}, u32[]{:S(2)}, u32[]{:S(2)}) %collective-permute-start.2) | collective-permute-done | bytes 270368 | tf_op jit(solution)/shard_map/object_halo/ppermute | solution.py:628
  31.2 0.0 collective-permute-done.3.same
  31.2 0.0 collective-permute-done.5.same_corner
  31.2 0.0 collective-permute-done.4.cross_corner
  31.2 0.0 copy-done.7
  31.2 14.5 %shard_map.103 = (f32[64,24,128]{2,1,0:T(8,128)S(1)}, f32[64,24,128]{2,1,0:T(8,128)S(1)}, f32[4,2,2,256,128]{4,3,2,1,0:T(8,128)S(1)}, f32[4,2,2,256,128]{4,3,2,1,0:T(8,128)S(1)}, s32[8,128]{1,0:T(8,128)S(1)}) custom-call(s32[2,4]{1,0:T(2,128)S(1)} %bitcast.20, f32[2,256,256]{2,1,0:T(8,128)S(1)} %copy-done.1, ...), custom_call_target="tpu_custom_call" | custom-call | flops 13958643712 | bytes 12582912 | tf_op jit(solution)/shard_map/pallas_call | solution.py:549
  45.7 1.3 %copy-done.12 = f32[4,2,2,256,128]{4,3,2,1,0:T(8,128)} copy-done((f32[4,2,2,256,128]{4,3,2,1,0:T(8,128)}, f32[4,2,2,256,128]{4,3,2,1,0:T(8,128)S(1)}, u32[]{:S(2)}) %copy-start.12) | copy-done | bytes 2097176
  47.1 0.0 collective-permute-start.6
  47.1 2.3 %collective-permute-done.6 = f32[64,24,128]{2,1,0:T(8,128)S(1)} collective-permute-done((f32[64,24,128]{2,1,0:T(8,128)S(1)}, f32[64,24,128]{2,1,0:T(8,128)S(1)}, u32[]{:S(2)}, u32[]{:S(2)}) %collective-permute-start.6) | collective-permute-done | bytes 786464 | tf_op jit(solution)/shard_map/probe_reduce/ppermute | solution.py:628
  49.4 1.0 add.9
  50.3 15.6 %all-to-all-start = ((f32[64,24,128]{2,1,0:T(8,128)}), f32[64,24,128]{2,1,0:T(8,128)}, u32[]{:S(2)}, u32[]{:S(2)}) async-start(f32[64,24,128]{2,1,0:T(8,128)} %add.9), calls=%async_computation | async-start | bytes 1572864 | tf_op jit(solution)/shard_map/probe_reduce/all_to_all | solution.py:660
  65.9 0.0 copy-start.6
  65.9 1.2 copy-done.6
  67.2 1.6 %copy-done.11 = f32[4,2,2,256,128]{4,3,2,1,0:T(8,128)S(1)} copy-done((f32[4,2,2,256,128]{4,3,2,1,0:T(8,128)S(1)}, f32[4,2,2,256,128]{4,3,2,1,0:T(8,128)}, u32[]{:S(2)}) %copy-start.11) | copy-done | bytes 2097176
  68.7 1.6 %copy-done.13 = f32[4,2,2,256,128]{4,3,2,1,0:T(8,128)S(1)} copy-done((f32[4,2,2,256,128]{4,3,2,1,0:T(8,128)S(1)}, f32[4,2,2,256,128]{4,3,2,1,0:T(8,128)}, u32[]{:S(2)}) %copy-start.13) | copy-done | bytes 2097176
  70.3 3.4 %shard_map.104 = (f32[2,256,256]{2,1,0:T(8,128)S(1)}, f32[2,128,256]{2,1,0:T(8,128)S(1)}, f32[2,128,256]{2,1,0:T(8,128)S(1)}, f32[2,256,128]{2,1,0:T(8,128)S(1)}...) custom-call(s32[2,4]{1,0:T(2,128)S(1)} %bitcast.21, ...), custom_call_target="tpu_custom_call" | custom-call | flops 5368709120 | bytes 8388608 | tf_op jit(solution)/shard_map/pallas_call | solution.py:583
  73.8 2.1 %shard_map.105.light = f32[256,256]{1,0:T(8,128)S(1)} custom-call(s32[2,4]{1,0:T(2,128)S(1)} %bitcast.22, s32[8,128]{1,0:T(8,128)S(1)} %get-tuple-element.49.around, f32[2,2,256,256]{3,2,1,0:T(8,128)S(1)} %copy-done.6), custom_call_target="tpu_custom_call" | custom-call | flops 2147483648 | bytes 4194304 | tf_op jit(solution)/shard_map/pallas_call | solution.py:517
  75.9 3.9 %all-to-all-done = f32[64,24,128]{2,1,0:T(8,128)} async-done(((f32[64,24,128]{2,1,0:T(8,128)}), f32[64,24,128]{2,1,0:T(8,128)}, u32[]{:S(2)}, u32[]{:S(2)}) %all-to-all-start) | async-done | bytes 786464 | tf_op jit(solution)/shard_map/probe_reduce/all_to_all | solution.py:660
  79.8 1.2 reduce_sum.9
  81.1 0.8 broadcast_in_dim.2
  81.9 6.7 %all-to-all-start.1 = ((f32[64,16,128]{2,1,0:T(8,128)}), f32[64,16,128]{2,1,0:T(8,128)S(1)}, u32[]{:S(2)}, u32[]{:S(2)}) async-start(f32[64,16,128]{2,1,0:T(8,128)} %broadcast_in_dim.2), calls=%async_computation.1 | async-start | bytes 1048576 | tf_op jit(solution)/shard_map/probe_gather/all_to_all | solution.py:688
  88.6 4.4 %collective-permute-start.8 = (f32[2,2,128,128]{3,2,1,0:T(8,128)S(1)}, f32[2,2,128,128]{3,2,1,0:T(8,128)}, u32[]{:S(2)}, u32[]{:S(2)}) collective-permute-start(f32[2,2,128,128]{3,2,1,0:T(8,128)S(1)} %get-tuple-element.54), channel_id=1, source_target_pairs={{1,2},{2,1},{3,4},{4,3},{5,6},{6,5},{7,8},{8,7},{9,10},{10,9},{11,... | collective-permute-start | bytes 786440 | tf_op jit(solution)/shard_map/gradient_corners/ppermute | solution.py:628
  93.0 0.1 collective-permute-start.9
  93.1 7.0 %all-to-all-done.1.mine = f32[64,16,128]{2,1,0:T(8,128)S(1)} async-done(((f32[64,16,128]{2,1,0:T(8,128)}), f32[64,16,128]{2,1,0:T(8,128)S(1)}, u32[]{:S(2)}, u32[]{:S(2)}) %all-to-all-start.1) | async-done | bytes 524320 | tf_op jit(solution)/shard_map/probe_gather/all_to_all | solution.py:688
  100.2 3.2 %collective-permute-start.7 = (f32[64,16,128]{2,1,0:T(8,128)S(1)}, f32[64,16,128]{2,1,0:T(8,128)S(1)}, u32[]{:S(2)}, u32[]{:S(2)}) collective-permute-start(f32[64,16,128]{2,1,0:T(8,128)S(1)} %all-to-all-done.1.mine), channel_id=1, source_target_pairs={{0,1},{1,0},{2,3},{3,2},{4,5},{5,4},{6,7},{7,6},{8,9},{9,8},{10,11... | collective-permute-start | bytes 1572872 | tf_op jit(solution)/shard_map/probe_gather/ppermute | solution.py:628
  103.3 0.0 collective-permute-done.8
  103.3 0.0 collective-permute-done.9
  103.3 1.1 broadcast_select_fusion
  104.4 0.8 fusion.4
  105.2 0.7 collective-permute-start.11
  105.9 2.3 %collective-permute-start.10 = (f32[2,128,256]{2,1,0:T(8,128)}, f32[2,128,256]{2,1,0:T(8,128)S(1)}, u32[]{:S(2)}, u32[]{:S(2)}) collective-permute-start(f32[2,128,256]{2,1,0:T(8,128)} %get-tuple-element.75), channel_id=1, source_target_pairs={{0,16},{16,0},{32,48},{48,32},{64,80},{80,64},{96,112},{112,96},{1... | collective-permute-start | bytes 786440 | tf_op jit(solution)/shard_map/gradient_rows/ppermute | solution.py:624
  108.2 4.4 %collective-permute-start.12 = (f32[2,256,128]{2,1,0:T(8,128)S(1)}, f32[2,256,128]{2,1,0:T(8,128)S(1)}, u32[]{:S(2)}, u32[]{:S(2)}) collective-permute-start(f32[2,256,128]{2,1,0:T(8,128)S(1)} %get-tuple-element.59), channel_id=1, source_target_pairs={{1,2},{2,1},{3,4},{4,3},{5,6},{6,5},{7,8},{8,7},{9,10},{10,9},{11,... | collective-permute-start | bytes 786440 | tf_op jit(solution)/shard_map/gradient_corners/ppermute | solution.py:628
  112.6 0.1 collective-permute-start.13
  112.7 0.1 slice_reduce_fusion
  112.8 0.1 reshape_squeeze.3
  112.9 0.7 copy.12
  113.6 0.6 fusion.5
  115.5 0.0 collective-permute-done.7.other
  115.5 1.1 probe_gather.1
  116.5 0.0 collective-permute-done.11.odd
  116.5 0.0 collective-permute-done.10.even
  116.6 6.1 %collective-permute-done.12.cross = f32[2,256,128]{2,1,0:T(8,128)S(1)} collective-permute-done((f32[2,256,128]{2,1,0:T(8,128)S(1)}, f32[2,256,128]{2,1,0:T(8,128)S(1)}, u32[]{:S(2)}, u32[]{:S(2)}) %collective-permute-start.12) | collective-permute-done | bytes 262176 | tf_op jit(solution)/shard_map/gradient_corners/ppermute | solution.py:628
  122.6 0.0 collective-permute-done.13.same
  122.7 1.0 shard_map.106
  (17 shorter events, 0.1 us)
Async XLA Ops:
  0.6 1.0 copy-start
  1.7 0.7 copy-start.2
  3.1 8.2 %collective-permute-start = (f32[2,136,256]{2,1,0:T(8,128)S(1)}, f32[2,136,256]{2,1,0:T(8,128)S(1)}, u32[]{:S(2)}, u32[]{:S(2)}) collective-permute-start(f32[2,136,256]{2,1,0:T(8,128)S(1)} %get-tuple-element.34), channel_id=1, source_target_pairs={{0,16},{16,0},{32,48},{48,32},{64,80},{80,64},{96,112},{112,96},{1... | collective-permute-start | bytes 835592 | tf_op jit(solution)/shard_map/object_halo/ppermute | solution.py:624
  5.3 6.0 %collective-permute-start.1 = (f32[2,136,256]{2,1,0:T(8,128)S(1)}, f32[2,136,256]{2,1,0:T(8,128)S(1)}, u32[]{:S(2)}, u32[]{:S(2)}) collective-permute-start(f32[2,136,256]{2,1,0:T(8,128)S(1)} %get-tuple-element.35), channel_id=1, source_target_pairs={{16,32},{32,16},{48,64},{64,48},{80,96},{96,80},{17,33},{33,17},{4... | collective-permute-start | bytes 835592 | tf_op jit(solution)/shard_map/object_halo/ppermute | solution.py:624
  6.0 1.2 copy-start.4
  7.2 1.0 copy-start.8
  8.2 1.0 copy-start.9
  9.2 21.9 %copy-start.7 = (bf16[2,2,2,256,256]{4,3,2,1,0:T(8,128)(2,1)S(1)}, bf16[2,2,2,256,256]{4,3,2,1,0:T(8,128)(2,1)}, u32[]{:S(2)}) copy-start(bf16[2,2,2,256,256]{4,3,2,1,0:T(8,128)(2,1)} %constant.21.clone.matrices) | copy-start | bytes 3145732
  10.5 20.7 %copy-start.1 = (f32[2,256,256]{2,1,0:T(8,128)S(1)}, f32[2,256,256]{2,1,0:T(8,128)}, u32[]{:S(2)}) copy-start(f32[2,256,256]{2,1,0:T(8,128)} %own.3) | copy-start | bytes 1572868
  10.5 20.7 %copy-start.3 = (s32[1,1,4,2]{2,3,1,0:T(2,128)S(1)}, s32[1,1,4,2]{2,3,1,0:T(2,128)}, u32[]{:S(2)}) copy-start(s32[1,1,4,2]{2,3,1,0:T(2,128)} %param.10) | copy-start | bytes 100
  10.5 20.7 %copy-start.5 = (f32[2,2,256,256]{3,2,1,0:T(8,128)S(1)}, f32[2,2,256,256]{3,2,1,0:T(8,128)}, u32[]{:S(2)}) copy-start(f32[2,2,256,256]{3,2,1,0:T(8,128)} %probe.3) | copy-start | bytes 3145732
  11.4 19.8 %collective-permute-start.5 = (f32[2,2,136,128]{3,2,1,0:T(8,128)S(1)}, f32[2,2,136,128]{3,2,1,0:T(8,128)S(1)}, u32[]{:S(2)}, u32[]{:S(2)}) collective-permute-start(f32[2,2,136,128]{3,2,1,0:T(8,128)S(1)} %get-tuple-element.72), channel_id=1, source_target_pairs={{0,1},{1,0},{2,3},{3,2},{4,5},{5,4},{6,7},{7,6},{8,9},{9,8},{10,11... | collective-permute-start | bytes 835592 | tf_op jit(solution)/shard_map/object_corners/ppermute | solution.py:628
  13.1 18.0 %collective-permute-start.4 = (f32[2,2,136,128]{3,2,1,0:T(8,128)S(1)}, f32[2,2,136,128]{3,2,1,0:T(8,128)S(1)}, u32[]{:S(2)}, u32[]{:S(2)}) collective-permute-start(f32[2,2,136,128]{3,2,1,0:T(8,128)S(1)} %get-tuple-element.73), channel_id=1, source_target_pairs={{1,2},{2,1},{3,4},{4,3},{5,6},{6,5},{7,8},{8,7},{9,10},{10,9},{11,... | collective-permute-start | bytes 835592 | tf_op jit(solution)/shard_map/object_corners/ppermute | solution.py:628
  16.7 14.4 %collective-permute-start.2 = (f32[2,264,128]{2,1,0:T(8,128)S(1)}, f32[2,264,128]{2,1,0:T(8,128)S(1)}, u32[]{:S(2)}, u32[]{:S(2)}) collective-permute-start(f32[2,264,128]{2,1,0:T(8,128)S(1)} %get-tuple-element.36), channel_id=1, source_target_pairs={{1,2},{2,1},{3,4},{4,3},{5,6},{6,5},{7,8},{8,7},{9,10},{10,9},{11,... | collective-permute-start | bytes 811016 | tf_op jit(solution)/shard_map/object_halo/ppermute | solution.py:628
  18.7 12.5 %collective-permute-start.3 = (f32[2,264,128]{2,1,0:T(8,128)S(1)}, f32[2,264,128]{2,1,0:T(8,128)S(1)}, u32[]{:S(2)}, u32[]{:S(2)}) collective-permute-start(f32[2,264,128]{2,1,0:T(8,128)S(1)} %get-tuple-element.37), channel_id=1, source_target_pairs={{0,1},{1,0},{2,3},{3,2},{4,5},{5,4},{6,7},{7,6},{8,9},{9,8},{10,11... | collective-permute-start | bytes 811016 | tf_op jit(solution)/shard_map/object_halo/ppermute | solution.py:628
  45.7 1.4 %copy-start.12 = (f32[4,2,2,256,128]{4,3,2,1,0:T(8,128)}, f32[4,2,2,256,128]{4,3,2,1,0:T(8,128)S(1)}, u32[]{:S(2)}) copy-start(f32[4,2,2,256,128]{4,3,2,1,0:T(8,128)S(1)} %get-tuple-element.47.patch) | copy-start | bytes 6291460
  47.1 3.3 %copy-start.10 = (f32[4,2,2,256,128]{4,3,2,1,0:T(8,128)}, f32[4,2,2,256,128]{4,3,2,1,0:T(8,128)S(1)}, u32[]{:S(2)}) copy-start(f32[4,2,2,256,128]{4,3,2,1,0:T(8,128)S(1)} %get-tuple-element.46.object_part) | copy-start | bytes 6291460
  47.1 2.3 %collective-permute-start.6 = (f32[64,24,128]{2,1,0:T(8,128)S(1)}, f32[64,24,128]{2,1,0:T(8,128)S(1)}, u32[]{:S(2)}, u32[]{:S(2)}) collective-permute-start(f32[64,24,128]{2,1,0:T(8,128)S(1)} %get-tuple-element.41), channel_id=1, source_target_pairs={{0,1},{1,0},{2,3},{3,2},{4,5},{5,4},{6,7},{7,6},{8,9},{9,8},{10,11... | collective-permute-start | bytes 2359304 | tf_op jit(solution)/shard_map/probe_reduce/ppermute | solution.py:628
  50.3 29.5 %all-to-all-start = ((f32[64,24,128]{2,1,0:T(8,128)}), f32[64,24,128]{2,1,0:T(8,128)}, u32[]{:S(2)}, u32[]{:S(2)}) async-start(f32[64,24,128]{2,1,0:T(8,128)} %add.9), calls=%async_computation | async-start | bytes 1572864 | tf_op jit(solution)/shard_map/probe_reduce/all_to_all | solution.py:660
  65.9 1.2 copy-start.6
  67.1 1.6 %copy-start.11 = (f32[4,2,2,256,128]{4,3,2,1,0:T(8,128)S(1)}, f32[4,2,2,256,128]{4,3,2,1,0:T(8,128)}, u32[]{:S(2)}) copy-start(f32[4,2,2,256,128]{4,3,2,1,0:T(8,128)} %copy-done.10) | copy-start | bytes 6291460
  68.7 1.6 %copy-start.13 = (f32[4,2,2,256,128]{4,3,2,1,0:T(8,128)S(1)}, f32[4,2,2,256,128]{4,3,2,1,0:T(8,128)}, u32[]{:S(2)}) copy-start(f32[4,2,2,256,128]{4,3,2,1,0:T(8,128)} %copy-done.12) | copy-start | bytes 6291460
  81.9 18.3 %all-to-all-start.1 = ((f32[64,16,128]{2,1,0:T(8,128)}), f32[64,16,128]{2,1,0:T(8,128)S(1)}, u32[]{:S(2)}, u32[]{:S(2)}) async-start(f32[64,16,128]{2,1,0:T(8,128)} %broadcast_in_dim.2), calls=%async_computation.1 | async-start | bytes 1048576 | tf_op jit(solution)/shard_map/probe_gather/all_to_all | solution.py:688
  88.6 14.7 %collective-permute-start.8 = (f32[2,2,128,128]{3,2,1,0:T(8,128)S(1)}, f32[2,2,128,128]{3,2,1,0:T(8,128)}, u32[]{:S(2)}, u32[]{:S(2)}) collective-permute-start(f32[2,2,128,128]{3,2,1,0:T(8,128)S(1)} %get-tuple-element.54), channel_id=1, source_target_pairs={{1,2},{2,1},{3,4},{4,3},{5,6},{6,5},{7,8},{8,7},{9,10},{10,9},{11,... | collective-permute-start | bytes 786440 | tf_op jit(solution)/shard_map/gradient_corners/ppermute | solution.py:628
  93.0 10.3 %collective-permute-start.9 = (f32[2,2,128,128]{3,2,1,0:T(8,128)S(1)}, f32[2,2,128,128]{3,2,1,0:T(8,128)}, u32[]{:S(2)}, u32[]{:S(2)}) collective-permute-start(f32[2,2,128,128]{3,2,1,0:T(8,128)S(1)} %get-tuple-element.55), channel_id=1, source_target_pairs={{0,1},{1,0},{2,3},{3,2},{4,5},{5,4},{6,7},{7,6},{8,9},{9,8},{10,11... | collective-permute-start | bytes 786440 | tf_op jit(solution)/shard_map/gradient_corners/ppermute | solution.py:628
  100.2 15.3 %collective-permute-start.7 = (f32[64,16,128]{2,1,0:T(8,128)S(1)}, f32[64,16,128]{2,1,0:T(8,128)S(1)}, u32[]{:S(2)}, u32[]{:S(2)}) collective-permute-start(f32[64,16,128]{2,1,0:T(8,128)S(1)} %all-to-all-done.1.mine), channel_id=1, source_target_pairs={{0,1},{1,0},{2,3},{3,2},{4,5},{5,4},{6,7},{7,6},{8,9},{9,8},{10,11... | collective-permute-start | bytes 1572872 | tf_op jit(solution)/shard_map/probe_gather/ppermute | solution.py:628
  105.2 11.3 %collective-permute-start.11 = (f32[2,128,256]{2,1,0:T(8,128)}, f32[2,128,256]{2,1,0:T(8,128)S(1)}, u32[]{:S(2)}, u32[]{:S(2)}) collective-permute-start(f32[2,128,256]{2,1,0:T(8,128)} %get-tuple-element.74), channel_id=1, source_target_pairs={{16,32},{32,16},{48,64},{64,48},{80,96},{96,80},{17,33},{33,17},{4... | collective-permute-start | bytes 786440 | tf_op jit(solution)/shard_map/gradient_rows/ppermute | solution.py:624
  105.9 10.7 %collective-permute-start.10 = (f32[2,128,256]{2,1,0:T(8,128)}, f32[2,128,256]{2,1,0:T(8,128)S(1)}, u32[]{:S(2)}, u32[]{:S(2)}) collective-permute-start(f32[2,128,256]{2,1,0:T(8,128)} %get-tuple-element.75), channel_id=1, source_target_pairs={{0,16},{16,0},{32,48},{48,32},{64,80},{80,64},{96,112},{112,96},{1... | collective-permute-start | bytes 786440 | tf_op jit(solution)/shard_map/gradient_rows/ppermute | solution.py:624
  108.2 14.5 %collective-permute-start.12 = (f32[2,256,128]{2,1,0:T(8,128)S(1)}, f32[2,256,128]{2,1,0:T(8,128)S(1)}, u32[]{:S(2)}, u32[]{:S(2)}) collective-permute-start(f32[2,256,128]{2,1,0:T(8,128)S(1)} %get-tuple-element.59), channel_id=1, source_target_pairs={{1,2},{2,1},{3,4},{4,3},{5,6},{6,5},{7,8},{8,7},{9,10},{10,9},{11,... | collective-permute-start | bytes 786440 | tf_op jit(solution)/shard_map/gradient_corners/ppermute | solution.py:628
  112.6 10.0 %collective-permute-start.13 = (f32[2,256,128]{2,1,0:T(8,128)S(1)}, f32[2,256,128]{2,1,0:T(8,128)S(1)}, u32[]{:S(2)}, u32[]{:S(2)}) collective-permute-start(f32[2,256,128]{2,1,0:T(8,128)S(1)} %get-tuple-element.60), channel_id=1, source_target_pairs={{0,1},{1,0},{2,3},{3,2},{4,5},{5,4},{6,7},{7,6},{8,9},{9,8},{10,11... | collective-permute-start | bytes 786440 | tf_op jit(solution)/shard_map/gradient_corners/ppermute | solution.py:628

commit v4 on v3

--- a/solution.py
+++ b/solution.py
@@ -525,7 +525,7 @@
         grid_spec=pltpu.PrefetchScalarGridSpec(
             num_scalar_prefetch=1,
             grid=(),
-            in_specs=[ANY],
+            in_specs=[pl.BlockSpec(memory_space=pltpu.HBM)],
             out_specs=[ANY] * 4,
             scratch_shapes=[pltpu.VMEM((2, 8, SIZE), F32), pltpu.SemaphoreType.DMA((8,))],
         ),
@@ -647,19 +647,18 @@
         same = swap_columns(same, 0)
     permuted = prepare(measured)
     with jax.named_scope("object_corners"):
-        rows, permuted = lax.optimization_barrier((jnp.stack([even, odd]), permuted))
+        even, odd, cross, same, permuted = lax.optimization_barrier((even, odd, cross, same, permuted))
+        rows = jnp.stack([even, odd])
         cross_corner = swap_columns(half_lanes(rows, core == 0), 1)
         same_corner = swap_columns(half_lanes(rows, core == 1), 0)
 
     halo = [even, odd, cross, same, cross_corner, same_corner]
     keep, send, object_part, patch, around = transforms(starts, object_tile, halo, probe, permuted)
 
+    parts = place_parts(starts, object_part, patch, probe)
     with jax.named_scope("probe_reduce"):
-        chunk = keep + swap_columns(send, 0)
-        chunk, object_part, around = lax.optimization_barrier((chunk, object_part, around))
+        chunk, parts, around = lax.optimization_barrier((keep + swap_columns(send, 0), parts, around))
         chunk = lax.all_to_all(chunk, AXES, 0, 0, axis_index_groups=groups, tiled=True)
-
-    parts = place_parts(starts, object_part, patch, probe)
     center, even, odd, cross, same, cross_corner, same_corner, steps = parts
 
     with jax.named_scope("gradient_corners"):
@@ -667,9 +666,10 @@
         same_corner = swap_columns(same_corner, 0)
         cross = swap_columns(cross, 1)
         same = swap_columns(same, 0)
-    around, steps = lax.optimization_barrier((around, steps))
     light = illuminate(starts, around, probe)
-    chunk, light, center = lax.optimization_barrier((chunk, light, center))
+    chunk, light, cross_corner, same_corner, cross, same = lax.optimization_barrier(
+        (chunk, light, cross_corner, same_corner, cross, same)
+    )
 
     with jax.named_scope("probe_sum"):
         total = jnp.sum(chunk, axis=0)
@@ -686,9 +686,9 @@
     with jax.named_scope("probe_gather"):
         spread_out = jnp.broadcast_to(quotient.reshape(1, 16, HALF), (devices // 2, 16, HALF))
         gathered = lax.all_to_all(spread_out, AXES, 0, 0, axis_index_groups=groups, tiled=True)
+        gathered, odd, even = lax.optimization_barrier((gathered, odd, even))
         probe_update = assemble(gathered, swap_columns(gathered, 0)).reshape(probe.shape)
 
-    probe_update, even, odd = lax.optimization_barrier((probe_update, even, odd))
     object_update = update([center, even, odd, cross, same, light])
     position_step = steps[:, 0].reshape(1, 1, -1, 2)
     return (object_update, probe_update, position_step, relative_error)

time: 125 us -> 119 us (0.952)
  the two profiles are of different devices: /device:TPU:1 before, /device:TPU:25 now
where the time goes in v4:
time: 119 us
  starting transfers between devices  52.3 us (44%)
  waiting for transfers between devices  27.6 us (23%)
  Pallas kernels  24.6 us (21%)
  local copies, waits for them, and re-layouts  8.44 us (7%)
  between operations  3.37 us (3%)
  other arithmetic  2.39 us (2%)
    ppermute x10, waiting for transfers between devices, swap_columns(): return lax.ppermute(value, 'col', pairs_from(first, lax.axis_size('col')))  17.2 us
    ppermute x10, starting transfers between devices, swap_columns(): return lax.ppermute(value, 'col', pairs_from(first, lax.axis_size('col')))  16.9 us
    pallas_call x1, Pallas kernels, transforms(): pl.pallas_call(transform_kernel, out_shape=shaped([halves, halves, (count...  14.5 us
    ppermute x4, starting transfers between devices, swap_rows(): return lax.ppermute(value, 'row', pairs_from(first, lax.axis_size('row')))  12.5 us
    all_to_all x1, starting transfers between devices, local(): lax.all_to_all(chunk, AXES, 0, 0, axis_index_groups=groups, tiled=True)  12.2 us
    all_to_all x1, starting transfers between devices, local(): lax.all_to_all(spread_out, AXES, 0, 0, axis_index_groups=groups, tiled=True)  10.8 us
    ppermute x4, waiting for transfers between devices, swap_rows(): return lax.ppermute(value, 'row', pairs_from(first, lax.axis_size('row')))  10.4 us
    unnamed x25, local copies, waits for them, and re-layouts  6.82 us
  transfers between devices with their start and end apart: 16, of which 6 were waited for; matrix products, arithmetic and copies ran while one was open for 1% of the time, Pallas kernels for 7%

profile of v4, /device:TPU:25, one launch (start us, length us, event | category | flops | bytes accessed | tf_op | source)
XLA Modules:
  0.0 118.7 jit_solution(4932218525077916611)
XLA Ops:
  0.6 0.0 copy-start
  0.6 1.0 copy-done
  1.7 0.0 copy-start.2
  1.7 0.7 copy-done.2
  2.4 0.8 object_halo.1
  3.1 0.5 collective-permute-start
  3.7 6.0 %collective-permute-start.1 = (f32[2,136,256]{2,1,0:T(8,128)S(1)}, f32[2,136,256]{2,1,0:T(8,128)S(1)}, u32[]{:S(2)}, u32[]{:S(2)}) collective-permute-start(f32[2,136,256]{2,1,0:T(8,128)S(1)} %get-tuple-element.46), channel_id=1, source_target_pairs={{16,32},{32,16},{48,64},{64,48},{80,96},{96,80},{17,33},{33,17},{4... | collective-permute-start | bytes 835592 | tf_op jit(solution)/shard_map/object_halo/ppermute | solution.py:624
  9.7 3.8 %collective-permute-start.2 = (f32[2,264,128]{2,1,0:T(8,128)S(1)}, f32[2,264,128]{2,1,0:T(8,128)S(1)}, u32[]{:S(2)}, u32[]{:S(2)}) collective-permute-start(f32[2,264,128]{2,1,0:T(8,128)S(1)} %get-tuple-element.47), channel_id=1, source_target_pairs={{1,2},{2,1},{3,4},{4,3},{5,6},{6,5},{7,8},{8,7},{9,10},{10,9},{11,... | collective-permute-start | bytes 811016 | tf_op jit(solution)/shard_map/object_halo/ppermute | solution.py:628
  13.4 0.1 collective-permute-start.3
  13.5 0.0 copy-start.4
  13.5 1.2 %copy-done.4 = f32[1,1,4,256,256]{4,3,2,1,0:T(8,128)S(1)} copy-done((f32[1,1,4,256,256]{4,3,2,1,0:T(8,128)S(1)}, f32[1,1,4,256,256]{4,3,2,1,0:T(8,128)}, u32[]{:S(2)}) %copy-start.4) | copy-done | bytes 1048600
  14.8 0.0 copy-start.8
  14.8 1.0 copy-done.8
  15.8 1.0 copy-done.9
  16.8 1.3 %shard_map.102.measured = f32[4,256,256]{2,1,0:T(8,128)S(1)} custom-call(f32[4,256,256]{2,1,0:T(8,128)S(1)} %bitcast.23, bf16[768,256]{1,0:T(8,128)(2,1)S(1)} %copy-done.9, bf16[256,768]{1,0:T(8,128)(2,1)S(1)} %copy-done.8), custom_call_target="tpu_custom_call" | custom-call | flops 1073741824 | bytes 3145728 | tf_op jit(solution)/shard_map/pallas_call | solution.py:517
  18.1 1.7 %collective-permute-done.2.cross = f32[2,264,128]{2,1,0:T(8,128)S(1)} collective-permute-done((f32[2,264,128]{2,1,0:T(8,128)S(1)}, f32[2,264,128]{2,1,0:T(8,128)S(1)}, u32[]{:S(2)}, u32[]{:S(2)}) %collective-permute-start.2) | collective-permute-done | bytes 270368 | tf_op jit(solution)/shard_map/object_halo/ppermute | solution.py:628
  19.7 0.0 collective-permute-done.3.same
  19.7 0.0 collective-permute-done.even_strip
  19.7 0.0 collective-permute-done.1.odd_strip
  19.8 1.5 %collective-permute-start.5 = (f32[2,2,136,128]{3,2,1,0:T(8,128)S(1)}, f32[2,2,136,128]{3,2,1,0:T(8,128)S(1)}, u32[]{:S(2)}, u32[]{:S(2)}) collective-permute-start(f32[2,2,136,128]{3,2,1,0:T(8,128)S(1)} %get-tuple-element.94), channel_id=1, source_target_pairs={{0,1},{1,0},{2,3},{3,2},{4,5},{5,4},{6,7},{7,6},{8,9},{9,8},{10,11... | collective-permute-start | bytes 835592 | tf_op jit(solution)/shard_map/object_corners/ppermute | solution.py:628
  21.3 3.0 %collective-permute-start.4 = (f32[2,2,136,128]{3,2,1,0:T(8,128)S(1)}, f32[2,2,136,128]{3,2,1,0:T(8,128)S(1)}, u32[]{:S(2)}, u32[]{:S(2)}) collective-permute-start(f32[2,2,136,128]{3,2,1,0:T(8,128)S(1)} %get-tuple-element.95), channel_id=1, source_target_pairs={{1,2},{2,1},{3,4},{4,3},{5,6},{6,5},{7,8},{8,7},{9,10},{10,9},{11,... | collective-permute-start | bytes 835592 | tf_op jit(solution)/shard_map/object_corners/ppermute | solution.py:628
  24.3 0.0 collective-permute-done.5.same_corner
  24.3 6.4 %collective-permute-done.4.cross_corner = f32[2,2,136,128]{3,2,1,0:T(8,128)S(1)} collective-permute-done((f32[2,2,136,128]{3,2,1,0:T(8,128)S(1)}, f32[2,2,136,128]{3,2,1,0:T(8,128)S(1)}, u32[]{:S(2)}, u32[]{:S(2)}) %collective-permute-start.4) | collective-permute-done | bytes 278560 | tf_op jit(solution)/shard_map/object_corners/ppermute | solution.py:628
  30.7 0.0 copy-done.1
  30.7 0.0 copy-done.3
  30.7 0.0 copy-done.5
  30.7 0.0 copy-done.7
  30.7 14.5 %shard_map.103 = (f32[64,24,128]{2,1,0:T(8,128)S(1)}, f32[64,24,128]{2,1,0:T(8,128)S(1)}, f32[4,2,2,256,128]{4,3,2,1,0:T(8,128)S(1)}, f32[4,2,2,256,128]{4,3,2,1,0:T(8,128)S(1)}, s32[8,128]{1,0:T(8,128)S(1)}) custom-call(s32[2,4]{1,0:T(2,128)S(1)} %bitcast.20, f32[2,256,256]{2,1,0:T(8,128)S(1)} %copy-done.1, ...), custom_call_target="tpu_custom_call" | custom-call | flops 13958643712 | bytes 12582912 | tf_op jit(solution)/shard_map/pallas_call | solution.py:549
  45.3 0.1 collective-permute-start.6
  45.4 3.7 %shard_map.104 = (f32[2,256,256]{2,1,0:T(8,128)S(1)}, f32[2,128,256]{2,1,0:T(8,128)S(1)}, f32[2,128,256]{2,1,0:T(8,128)S(1)}, f32[2,256,128]{2,1,0:T(8,128)S(1)}...) custom-call(s32[2,4]{1,0:T(2,128)S(1)} %bitcast.21, ...), custom_call_target="tpu_custom_call" | custom-call | flops 5368709120 | bytes 8388608 | tf_op jit(solution)/shard_map/pallas_call | solution.py:583
  49.1 0.0 collective-permute-done.6
  49.1 1.0 add.9
  50.0 12.2 %all-to-all-start = ((f32[64,24,128]{2,1,0:T(8,128)}), f32[64,24,128]{2,1,0:T(8,128)}, u32[]{:S(2)}, u32[]{:S(2)}) async-start(f32[64,24,128]{2,1,0:T(8,128)} %add.9), calls=%async_computation | async-start | bytes 1572864 | tf_op jit(solution)/shard_map/probe_reduce/all_to_all | solution.py:661
  62.2 4.1 %collective-permute-start.7 = (f32[2,2,128,128]{3,2,1,0:T(8,128)S(1)}, f32[2,2,128,128]{3,2,1,0:T(8,128)S(1)}, u32[]{:S(2)}, u32[]{:S(2)}) collective-permute-start(f32[2,2,128,128]{3,2,1,0:T(8,128)S(1)} %get-tuple-element.70), channel_id=1, source_target_pairs={{1,2},{2,1},{3,4},{4,3},{5,6},{6,5},{7,8},{8,7},{9,10},{10,9},{11,... | collective-permute-start | bytes 786440 | tf_op jit(solution)/shard_map/gradient_corners/ppermute | solution.py:628
  66.3 0.1 collective-permute-start.8
  66.4 3.5 %collective-permute-start.9 = (f32[2,256,128]{2,1,0:T(8,128)S(1)}, f32[2,256,128]{2,1,0:T(8,128)S(1)}, u32[]{:S(2)}, u32[]{:S(2)}) collective-permute-start(f32[2,256,128]{2,1,0:T(8,128)S(1)} %get-tuple-element.72), channel_id=1, source_target_pairs={{1,2},{2,1},{3,4},{4,3},{5,6},{6,5},{7,8},{8,7},{9,10},{10,9},{11,... | collective-permute-start | bytes 786440 | tf_op jit(solution)/shard_map/gradient_corners/ppermute | solution.py:628
  69.9 0.1 collective-permute-start.10
  69.9 0.0 copy-start.6
  70.0 1.2 %copy-done.6 = f32[2,2,256,256]{3,2,1,0:T(8,128)S(1)} copy-done((f32[2,2,256,256]{3,2,1,0:T(8,128)S(1)}, f32[2,2,256,256]{3,2,1,0:T(8,128)}, u32[]{:S(2)}) %copy-start.6) | copy-done | bytes 1048600
  71.2 2.3 %shard_map.105.light = f32[256,256]{1,0:T(8,128)S(1)} custom-call(s32[2,4]{1,0:T(2,128)S(1)} %bitcast.22, s32[8,128]{1,0:T(8,128)S(1)} %get-tuple-element.69.around, f32[2,2,256,256]{3,2,1,0:T(8,128)S(1)} %copy-done.6), custom_call_target="tpu_custom_call" | custom-call | flops 2147483648 | bytes 4194304 | tf_op jit(solution)/shard_map/pallas_call | solution.py:517
  73.5 6.3 %collective-permute-done.7 = f32[2,2,128,128]{3,2,1,0:T(8,128)S(1)} collective-permute-done((f32[2,2,128,128]{3,2,1,0:T(8,128)S(1)}, f32[2,2,128,128]{3,2,1,0:T(8,128)S(1)}, u32[]{:S(2)}, u32[]{:S(2)}) %collective-permute-start.7) | collective-permute-done | bytes 262176 | tf_op jit(solution)/shard_map/gradient_corners/ppermute | solution.py:628
  79.8 0.0 collective-permute-done.8
  79.8 2.8 %collective-permute-done.9.cross = f32[2,256,128]{2,1,0:T(8,128)S(1)} collective-permute-done((f32[2,256,128]{2,1,0:T(8,128)S(1)}, f32[2,256,128]{2,1,0:T(8,128)S(1)}, u32[]{:S(2)}, u32[]{:S(2)}) %collective-permute-start.9) | collective-permute-done | bytes 262176 | tf_op jit(solution)/shard_map/gradient_corners/ppermute | solution.py:628
  82.6 0.0 copy-done.10
  82.6 0.0 collective-permute-done.10.same
  82.6 0.0 all-to-all-done
  82.6 1.3 %reduce_sum.9 = f32[24,128]{1,0:T(8,128)S(1)} reduce(f32[64,24,128]{2,1,0:T(8,128)} %all-to-all-done, f32[]{:T(128)} %constant.18.clone.1), dimensions={0}, to_apply=%region_0.1 | reduce | flops 193536 | bytes 798724 | tf_op jit(solution)/shard_map/probe_sum/reduce_sum | solution.py:675
  83.9 0.8 broadcast_in_dim.2
  84.8 10.8 %all-to-all-start.1 = ((f32[64,16,128]{2,1,0:T(8,128)}), f32[64,16,128]{2,1,0:T(8,128)S(1)}, u32[]{:S(2)}, u32[]{:S(2)}) async-start(f32[64,16,128]{2,1,0:T(8,128)} %broadcast_in_dim.2), calls=%async_computation.1 | async-start | bytes 1048576 | tf_op jit(solution)/shard_map/probe_gather/all_to_all | solution.py:688
  95.5 0.0 copy-done.11
  95.6 0.1 fusion.5
  95.7 0.6 collective-permute-start.12
  96.3 5.3 %collective-permute-start.11 = (f32[2,128,256]{2,1,0:T(8,128)S(1)}, f32[2,128,256]{2,1,0:T(8,128)S(1)}, u32[]{:S(2)}, u32[]{:S(2)}) collective-permute-start(f32[2,128,256]{2,1,0:T(8,128)S(1)} %get-tuple-element.97), channel_id=1, source_target_pairs={{16,32},{32,16},{48,64},{64,48},{80,96},{96,80},{17,33},{33,17},{4... | collective-permute-start | bytes 786440 | tf_op jit(solution)/shard_map/gradient_rows/ppermute | solution.py:624
  101.6 6.5 %collective-permute-done.12.even = f32[2,128,256]{2,1,0:T(8,128)S(1)} collective-permute-done((f32[2,128,256]{2,1,0:T(8,128)S(1)}, f32[2,128,256]{2,1,0:T(8,128)S(1)}, u32[]{:S(2)}, u32[]{:S(2)}) %collective-permute-start.12) | collective-permute-done | bytes 262176 | tf_op jit(solution)/shard_map/gradient_rows/ppermute | solution.py:624
  108.1 3.9 %collective-permute-done.11.odd = f32[2,128,256]{2,1,0:T(8,128)S(1)} collective-permute-done((f32[2,128,256]{2,1,0:T(8,128)S(1)}, f32[2,128,256]{2,1,0:T(8,128)S(1)}, u32[]{:S(2)}, u32[]{:S(2)}) %collective-permute-start.11) | collective-permute-done | bytes 262176 | tf_op jit(solution)/shard_map/gradient_rows/ppermute | solution.py:624
  112.0 0.0 all-to-all-done.1.mine
  112.0 0.8 collective-permute-start.13
  112.8 0.1 slice_reduce_fusion
  112.9 0.1 reshape_squeeze.3
  113.0 0.7 copy.12
  113.6 0.6 fusion.6
  115.5 1.0 shard_map.106
  116.5 0.0 collective-permute-done.13.other
  116.5 1.0 probe_gather.1
  (12 shorter events, 0.1 us)
Async XLA Ops:
  0.6 1.0 copy-start
  1.7 0.7 copy-start.2
  3.1 16.6 %collective-permute-start = (f32[2,136,256]{2,1,0:T(8,128)S(1)}, f32[2,136,256]{2,1,0:T(8,128)S(1)}, u32[]{:S(2)}, u32[]{:S(2)}) collective-permute-start(f32[2,136,256]{2,1,0:T(8,128)S(1)} %get-tuple-element.45), channel_id=1, source_target_pairs={{0,16},{16,0},{32,48},{48,32},{64,80},{80,64},{96,112},{112,96},{1... | collective-permute-start | bytes 835592 | tf_op jit(solution)/shard_map/object_halo/ppermute | solution.py:624
  3.7 16.1 %collective-permute-start.1 = (f32[2,136,256]{2,1,0:T(8,128)S(1)}, f32[2,136,256]{2,1,0:T(8,128)S(1)}, u32[]{:S(2)}, u32[]{:S(2)}) collective-permute-start(f32[2,136,256]{2,1,0:T(8,128)S(1)} %get-tuple-element.46), channel_id=1, source_target_pairs={{16,32},{32,16},{48,64},{64,48},{80,96},{96,80},{17,33},{33,17},{4... | collective-permute-start | bytes 835592 | tf_op jit(solution)/shard_map/object_halo/ppermute | solution.py:624
  9.7 10.1 %collective-permute-start.2 = (f32[2,264,128]{2,1,0:T(8,128)S(1)}, f32[2,264,128]{2,1,0:T(8,128)S(1)}, u32[]{:S(2)}, u32[]{:S(2)}) collective-permute-start(f32[2,264,128]{2,1,0:T(8,128)S(1)} %get-tuple-element.47), channel_id=1, source_target_pairs={{1,2},{2,1},{3,4},{4,3},{5,6},{6,5},{7,8},{8,7},{9,10},{10,9},{11,... | collective-permute-start | bytes 811016 | tf_op jit(solution)/shard_map/object_halo/ppermute | solution.py:628
  13.4 6.3 %collective-permute-start.3 = (f32[2,264,128]{2,1,0:T(8,128)S(1)}, f32[2,264,128]{2,1,0:T(8,128)S(1)}, u32[]{:S(2)}, u32[]{:S(2)}) collective-permute-start(f32[2,264,128]{2,1,0:T(8,128)S(1)} %get-tuple-element.48), channel_id=1, source_target_pairs={{0,1},{1,0},{2,3},{3,2},{4,5},{5,4},{6,7},{7,6},{8,9},{9,8},{10,11... | collective-permute-start | bytes 811016 | tf_op jit(solution)/shard_map/object_halo/ppermute | solution.py:628
  13.5 1.2 %copy-start.4 = (f32[1,1,4,256,256]{4,3,2,1,0:T(8,128)S(1)}, f32[1,1,4,256,256]{4,3,2,1,0:T(8,128)}, u32[]{:S(2)}) copy-start(f32[1,1,4,256,256]{4,3,2,1,0:T(8,128)} %param.9) | copy-start | bytes 3145732
  14.8 1.0 copy-start.8
  15.8 1.0 copy-start.9
  16.8 14.0 %copy-start.1 = (f32[2,256,256]{2,1,0:T(8,128)S(1)}, f32[2,256,256]{2,1,0:T(8,128)}, u32[]{:S(2)}) copy-start(f32[2,256,256]{2,1,0:T(8,128)} %own.3) | copy-start | bytes 1572868
  16.8 14.0 %copy-start.3 = (s32[1,1,4,2]{2,3,1,0:T(2,128)S(1)}, s32[1,1,4,2]{2,3,1,0:T(2,128)}, u32[]{:S(2)}) copy-start(s32[1,1,4,2]{2,3,1,0:T(2,128)} %param.10) | copy-start | bytes 100
  16.8 14.0 %copy-start.5 = (f32[2,2,256,256]{3,2,1,0:T(8,128)S(1)}, f32[2,2,256,256]{3,2,1,0:T(8,128)}, u32[]{:S(2)}) copy-start(f32[2,2,256,256]{3,2,1,0:T(8,128)} %probe.3) | copy-start | bytes 3145732
  16.8 14.0 %copy-start.7 = (bf16[2,2,2,256,256]{4,3,2,1,0:T(8,128)(2,1)S(1)}, bf16[2,2,2,256,256]{4,3,2,1,0:T(8,128)(2,1)}, u32[]{:S(2)}) copy-start(bf16[2,2,2,256,256]{4,3,2,1,0:T(8,128)(2,1)} %constant.21.clone.matrices) | copy-start | bytes 3145732
  19.8 4.5 %collective-permute-start.5 = (f32[2,2,136,128]{3,2,1,0:T(8,128)S(1)}, f32[2,2,136,128]{3,2,1,0:T(8,128)S(1)}, u32[]{:S(2)}, u32[]{:S(2)}) collective-permute-start(f32[2,2,136,128]{3,2,1,0:T(8,128)S(1)} %get-tuple-element.94), channel_id=1, source_target_pairs={{0,1},{1,0},{2,3},{3,2},{4,5},{5,4},{6,7},{7,6},{8,9},{9,8},{10,11... | collective-permute-start | bytes 835592 | tf_op jit(solution)/shard_map/object_corners/ppermute | solution.py:628
  21.3 9.5 %collective-permute-start.4 = (f32[2,2,136,128]{3,2,1,0:T(8,128)S(1)}, f32[2,2,136,128]{3,2,1,0:T(8,128)S(1)}, u32[]{:S(2)}, u32[]{:S(2)}) collective-permute-start(f32[2,2,136,128]{3,2,1,0:T(8,128)S(1)} %get-tuple-element.95), channel_id=1, source_target_pairs={{1,2},{2,1},{3,4},{4,3},{5,6},{6,5},{7,8},{8,7},{9,10},{10,9},{11,... | collective-permute-start | bytes 835592 | tf_op jit(solution)/shard_map/object_corners/ppermute | solution.py:628
  45.3 3.8 %collective-permute-start.6 = (f32[64,24,128]{2,1,0:T(8,128)S(1)}, f32[64,24,128]{2,1,0:T(8,128)S(1)}, u32[]{:S(2)}, u32[]{:S(2)}) collective-permute-start(f32[64,24,128]{2,1,0:T(8,128)S(1)} %get-tuple-element.55), channel_id=1, source_target_pairs={{0,1},{1,0},{2,3},{3,2},{4,5},{5,4},{6,7},{7,6},{8,9},{9,8},{10,11... | collective-permute-start | bytes 2359304 | tf_op jit(solution)/shard_map/probe_reduce/ppermute | solution.py:628
  50.0 32.6 %all-to-all-start = ((f32[64,24,128]{2,1,0:T(8,128)}), f32[64,24,128]{2,1,0:T(8,128)}, u32[]{:S(2)}, u32[]{:S(2)}) async-start(f32[64,24,128]{2,1,0:T(8,128)} %add.9), calls=%async_computation | async-start | bytes 1572864 | tf_op jit(solution)/shard_map/probe_reduce/all_to_all | solution.py:661
  62.2 17.6 %collective-permute-start.7 = (f32[2,2,128,128]{3,2,1,0:T(8,128)S(1)}, f32[2,2,128,128]{3,2,1,0:T(8,128)S(1)}, u32[]{:S(2)}, u32[]{:S(2)}) collective-permute-start(f32[2,2,128,128]{3,2,1,0:T(8,128)S(1)} %get-tuple-element.70), channel_id=1, source_target_pairs={{1,2},{2,1},{3,4},{4,3},{5,6},{6,5},{7,8},{8,7},{9,10},{10,9},{11,... | collective-permute-start | bytes 786440 | tf_op jit(solution)/shard_map/gradient_corners/ppermute | solution.py:628
  66.3 13.5 %collective-permute-start.8 = (f32[2,2,128,128]{3,2,1,0:T(8,128)S(1)}, f32[2,2,128,128]{3,2,1,0:T(8,128)S(1)}, u32[]{:S(2)}, u32[]{:S(2)}) collective-permute-start(f32[2,2,128,128]{3,2,1,0:T(8,128)S(1)} %get-tuple-element.71), channel_id=1, source_target_pairs={{0,1},{1,0},{2,3},{3,2},{4,5},{5,4},{6,7},{7,6},{8,9},{9,8},{10,11... | collective-permute-start | bytes 786440 | tf_op jit(solution)/shard_map/gradient_corners/ppermute | solution.py:628
  66.4 16.2 %collective-permute-start.9 = (f32[2,256,128]{2,1,0:T(8,128)S(1)}, f32[2,256,128]{2,1,0:T(8,128)S(1)}, u32[]{:S(2)}, u32[]{:S(2)}) collective-permute-start(f32[2,256,128]{2,1,0:T(8,128)S(1)} %get-tuple-element.72), channel_id=1, source_target_pairs={{1,2},{2,1},{3,4},{4,3},{5,6},{6,5},{7,8},{8,7},{9,10},{10,9},{11,... | collective-permute-start | bytes 786440 | tf_op jit(solution)/shard_map/gradient_corners/ppermute | solution.py:628
  69.9 12.8 %collective-permute-start.10 = (f32[2,256,128]{2,1,0:T(8,128)S(1)}, f32[2,256,128]{2,1,0:T(8,128)S(1)}, u32[]{:S(2)}, u32[]{:S(2)}) collective-permute-start(f32[2,256,128]{2,1,0:T(8,128)S(1)} %get-tuple-element.73), channel_id=1, source_target_pairs={{0,1},{1,0},{2,3},{3,2},{4,5},{5,4},{6,7},{7,6},{8,9},{9,8},{10,11... | collective-permute-start | bytes 786440 | tf_op jit(solution)/shard_map/gradient_corners/ppermute | solution.py:628
  69.9 1.2 %copy-start.6 = (f32[2,2,256,256]{3,2,1,0:T(8,128)S(1)}, f32[2,2,256,256]{3,2,1,0:T(8,128)}, u32[]{:S(2)}) copy-start(f32[2,2,256,256]{3,2,1,0:T(8,128)} %probe.3) | copy-start | bytes 3145732
  79.8 2.8 %copy-start.10 = (f32[2,2,128,128]{3,2,1,0:T(8,128)}, f32[2,2,128,128]{3,2,1,0:T(8,128)S(1)}, u32[]{:S(2)}) copy-start(f32[2,2,128,128]{3,2,1,0:T(8,128)S(1)} %collective-permute-done.8) | copy-start | bytes 786436
  82.6 12.9 %copy-start.11 = (f32[2,2,128,128]{3,2,1,0:T(8,128)S(1)}, f32[2,2,128,128]{3,2,1,0:T(8,128)}, u32[]{:S(2)}) copy-start(f32[2,2,128,128]{3,2,1,0:T(8,128)} %copy-done.10) | copy-start | bytes 786436
  84.8 27.2 %all-to-all-start.1 = ((f32[64,16,128]{2,1,0:T(8,128)}), f32[64,16,128]{2,1,0:T(8,128)S(1)}, u32[]{:S(2)}, u32[]{:S(2)}) async-start(f32[64,16,128]{2,1,0:T(8,128)} %broadcast_in_dim.2), calls=%async_computation.1 | async-start | bytes 1048576 | tf_op jit(solution)/shard_map/probe_gather/all_to_all | solution.py:688
  95.7 12.4 %collective-permute-start.12 = (f32[2,128,256]{2,1,0:T(8,128)S(1)}, f32[2,128,256]{2,1,0:T(8,128)S(1)}, u32[]{:S(2)}, u32[]{:S(2)}) collective-permute-start(f32[2,128,256]{2,1,0:T(8,128)S(1)} %get-tuple-element.96), channel_id=1, source_target_pairs={{0,16},{16,0},{32,48},{48,32},{64,80},{80,64},{96,112},{112,96},{1... | collective-permute-start | bytes 786440 | tf_op jit(solution)/shard_map/gradient_rows/ppermute | solution.py:624
  96.3 15.7 %collective-permute-start.11 = (f32[2,128,256]{2,1,0:T(8,128)S(1)}, f32[2,128,256]{2,1,0:T(8,128)S(1)}, u32[]{:S(2)}, u32[]{:S(2)}) collective-permute-start(f32[2,128,256]{2,1,0:T(8,128)S(1)} %get-tuple-element.97), channel_id=1, source_target_pairs={{16,32},{32,16},{48,64},{64,48},{80,96},{96,80},{17,33},{33,17},{4... | collective-permute-start | bytes 786440 | tf_op jit(solution)/shard_map/gradient_rows/ppermute | solution.py:624
  112.0 4.5 %collective-permute-start.13 = (f32[64,16,128]{2,1,0:T(8,128)S(1)}, f32[64,16,128]{2,1,0:T(8,128)S(1)}, u32[]{:S(2)}, u32[]{:S(2)}) collective-permute-start(f32[64,16,128]{2,1,0:T(8,128)S(1)} %all-to-all-done.1.mine), channel_id=1, source_target_pairs={{0,1},{1,0},{2,3},{3,2},{4,5},{5,4},{6,7},{7,6},{8,9},{9,8},{10,11... | collective-permute-start | bytes 1572872 | tf_op jit(solution)/shard_map/probe_gather/ppermute | solution.py:628

commit v5 on v4

--- a/solution.py
+++ b/solution.py
@@ -666,30 +666,28 @@
         same_corner = swap_columns(same_corner, 0)
         cross = swap_columns(cross, 1)
         same = swap_columns(same, 0)
-    light = illuminate(starts, around, probe)
-    chunk, light, cross_corner, same_corner, cross, same = lax.optimization_barrier(
-        (chunk, light, cross_corner, same_corner, cross, same)
-    )
+    with jax.named_scope("gradient_rows"):
+        first = jnp.where(core == 0, cross_corner, same_corner)
+        second = jnp.where(core == 0, same_corner, cross_corner)
+        added = jnp.concatenate([first, second], -1)
+        odd, even = odd + added[1], even + added[0]
+        light = illuminate(starts, around, probe)
+        chunk, light, odd, even = lax.optimization_barrier((chunk, light, odd, even))
+        odd = swap_rows(odd, 1)
+        even = swap_rows(even, 0)
+        object_update = update([center, even, odd, cross, same, light])
 
     with jax.named_scope("probe_sum"):
         total = jnp.sum(chunk, axis=0)
         quotient = total[:16].reshape(4, 4, HALF) / total[16:20]
         relative_error = (total[20, 0] / total[20, 1]).reshape(1)
 
-    with jax.named_scope("gradient_rows"):
-        first = jnp.where(core == 0, cross_corner, same_corner)
-        second = jnp.where(core == 0, same_corner, cross_corner)
-        added = jnp.concatenate([first, second], -1)
-        odd = swap_rows(odd + added[1], 1)
-        even = swap_rows(even + added[0], 0)
-
     with jax.named_scope("probe_gather"):
         spread_out = jnp.broadcast_to(quotient.reshape(1, 16, HALF), (devices // 2, 16, HALF))
         gathered = lax.all_to_all(spread_out, AXES, 0, 0, axis_index_groups=groups, tiled=True)
-        gathered, odd, even = lax.optimization_barrier((gathered, odd, even))
+        gathered, object_update = lax.optimization_barrier((gathered, object_update))
         probe_update = assemble(gathered, swap_columns(gathered, 0)).reshape(probe.shape)
 
-    object_update = update([center, even, odd, cross, same, light])
     position_step = steps[:, 0].reshape(1, 1, -1, 2)
     return (object_update, probe_update, position_step, relative_error)
 

time: 119 us -> 117 us (0.983)
  waiting for transfers between devices: 27.6 us -> 25.1 us
  local copies, waits for them, and re-layouts: 8.44 us -> 7.21 us
    ppermute x4, waiting for transfers between devices: 10.4 us -> 5.97 us  [swap_rows(): return lax.ppermute(value, 'row', pairs_from(first, lax.axis_size('row')))]
    ppermute x10, waiting for transfers between devices: 17.2 us -> 19.1 us  [swap_columns(): return lax.ppermute(value, 'col', pairs_from(first, lax.axis_size('col')))]
    unnamed x25 -> x19, local copies, waits for them, and re-layouts: 6.82 us -> 5.59 us
where the time goes in v5:
time: 117 us; the launch traced here: 116 us
  starting transfers between devices  53.1 us (45%)
  waiting for transfers between devices  25.1 us (21%)
  Pallas kernels  24.6 us (21%)
  local copies, waits for them, and re-layouts  7.21 us (6%)
  between operations  3.36 us (3%)
  other arithmetic  2.34 us (2%)
    ppermute x10, waiting for transfers between devices, swap_columns(): return lax.ppermute(value, 'col', pairs_from(first, lax.axis_size('col')))  19.1 us
    ppermute x10, starting transfers between devices, swap_columns(): return lax.ppermute(value, 'col', pairs_from(first, lax.axis_size('col')))  17.9 us
    pallas_call x1, Pallas kernels, transforms(): pl.pallas_call(transform_kernel, out_shape=shaped([halves, halves, (count...  14.4 us
    all_to_all x1, starting transfers between devices, local(): lax.all_to_all(chunk, AXES, 0, 0, axis_index_groups=groups, tiled=True)  12.2 us
    ppermute x4, starting transfers between devices, swap_rows(): return lax.ppermute(value, 'row', pairs_from(first, lax.axis_size('row')))  12.2 us
    all_to_all x1, starting transfers between devices, local(): lax.all_to_all(spread_out, AXES, 0, 0, axis_index_groups=groups, tiled=True)  10.8 us
    pallas_call x4, Pallas kernels, simple(): return call(*scalars, *arrays)  6.07 us
    ppermute x4, waiting for transfers between devices, swap_rows(): return lax.ppermute(value, 'row', pairs_from(first, lax.axis_size('row')))  5.97 us
  transfers between devices with their start and end apart: 16, of which 6 were waited for; matrix products, arithmetic and copies ran while one was open for 1% of the time, Pallas kernels for 7%

profile of v5, /device:TPU:25, one launch (start us, length us, event | category | flops | bytes accessed | tf_op | source)
XLA Modules:
  0.0 115.7 jit_solution(17706806524945330420)
XLA Ops:
  0.6 0.0 copy-start
  0.6 1.0 copy-done
  1.7 0.0 copy-start.2
  1.7 0.7 copy-done.2
  2.4 0.8 object_halo.1
  3.1 0.5 collective-permute-start
  3.7 6.0 %collective-permute-start.1 = (f32[2,136,256]{2,1,0:T(8,128)S(1)}, f32[2,136,256]{2,1,0:T(8,128)S(1)}, u32[]{:S(2)}, u32[]{:S(2)}) collective-permute-start(f32[2,136,256]{2,1,0:T(8,128)S(1)} %get-tuple-element.43), channel_id=1, source_target_pairs={{16,32},{32,16},{48,64},{64,48},{80,96},{96,80},{17,33},{33,17},{4... | collective-permute-start | bytes 835592 | tf_op jit(solution)/shard_map/object_halo/ppermute | solution.py:624
  9.7 3.8 %collective-permute-start.2 = (f32[2,264,128]{2,1,0:T(8,128)S(1)}, f32[2,264,128]{2,1,0:T(8,128)S(1)}, u32[]{:S(2)}, u32[]{:S(2)}) collective-permute-start(f32[2,264,128]{2,1,0:T(8,128)S(1)} %get-tuple-element.44), channel_id=1, source_target_pairs={{1,2},{2,1},{3,4},{4,3},{5,6},{6,5},{7,8},{8,7},{9,10},{10,9},{11,... | collective-permute-start | bytes 811016 | tf_op jit(solution)/shard_map/object_halo/ppermute | solution.py:628
  13.4 0.1 collective-permute-start.3
  13.5 0.0 copy-start.4
  13.5 1.2 %copy-done.4 = f32[1,1,4,256,256]{4,3,2,1,0:T(8,128)S(1)} copy-done((f32[1,1,4,256,256]{4,3,2,1,0:T(8,128)S(1)}, f32[1,1,4,256,256]{4,3,2,1,0:T(8,128)}, u32[]{:S(2)}) %copy-start.4) | copy-done | bytes 1048600
  14.8 0.0 copy-start.7
  14.8 1.0 copy-done.7
  15.8 0.0 copy-start.8
  15.8 1.0 copy-done.8
  16.8 0.0 copy-start.1
  16.8 0.0 copy-start.3
  16.8 0.0 copy-start.5
  16.8 1.3 %shard_map.102.measured = f32[4,256,256]{2,1,0:T(8,128)S(1)} custom-call(f32[4,256,256]{2,1,0:T(8,128)S(1)} %bitcast.23, bf16[768,256]{1,0:T(8,128)(2,1)S(1)} %copy-done.8, bf16[256,768]{1,0:T(8,128)(2,1)S(1)} %copy-done.7), custom_call_target="tpu_custom_call" | custom-call | flops 1073741824 | bytes 3145728 | tf_op jit(solution)/shard_map/pallas_call | solution.py:517
  18.1 1.7 %collective-permute-done.2.cross = f32[2,264,128]{2,1,0:T(8,128)S(1)} collective-permute-done((f32[2,264,128]{2,1,0:T(8,128)S(1)}, f32[2,264,128]{2,1,0:T(8,128)S(1)}, u32[]{:S(2)}, u32[]{:S(2)}) %collective-permute-start.2) | collective-permute-done | bytes 270368 | tf_op jit(solution)/shard_map/object_halo/ppermute | solution.py:628
  19.7 0.0 collective-permute-done.3.same
  19.7 0.0 collective-permute-done.even_strip
  19.7 0.0 collective-permute-done.1.odd_strip
  19.8 1.5 %collective-permute-start.5 = (f32[2,2,136,128]{3,2,1,0:T(8,128)S(1)}, f32[2,2,136,128]{3,2,1,0:T(8,128)S(1)}, u32[]{:S(2)}, u32[]{:S(2)}) collective-permute-start(f32[2,2,136,128]{3,2,1,0:T(8,128)S(1)} %get-tuple-element.88), channel_id=1, source_target_pairs={{0,1},{1,0},{2,3},{3,2},{4,5},{5,4},{6,7},{7,6},{8,9},{9,8},{10,11... | collective-permute-start | bytes 835592 | tf_op jit(solution)/shard_map/object_corners/ppermute | solution.py:628
  21.3 3.0 %collective-permute-start.4 = (f32[2,2,136,128]{3,2,1,0:T(8,128)S(1)}, f32[2,2,136,128]{3,2,1,0:T(8,128)S(1)}, u32[]{:S(2)}, u32[]{:S(2)}) collective-permute-start(f32[2,2,136,128]{3,2,1,0:T(8,128)S(1)} %get-tuple-element.89), channel_id=1, source_target_pairs={{1,2},{2,1},{3,4},{4,3},{5,6},{6,5},{7,8},{8,7},{9,10},{10,9},{11,... | collective-permute-start | bytes 835592 | tf_op jit(solution)/shard_map/object_corners/ppermute | solution.py:628
  24.3 0.0 collective-permute-done.5.same_corner
  24.3 6.4 %collective-permute-done.4.cross_corner = f32[2,2,136,128]{3,2,1,0:T(8,128)S(1)} collective-permute-done((f32[2,2,136,128]{3,2,1,0:T(8,128)S(1)}, f32[2,2,136,128]{3,2,1,0:T(8,128)S(1)}, u32[]{:S(2)}, u32[]{:S(2)}) %collective-permute-start.4) | collective-permute-done | bytes 278560 | tf_op jit(solution)/shard_map/object_corners/ppermute | solution.py:628
  30.7 0.0 copy-done.1
  30.7 0.0 copy-done.3
  30.7 0.0 copy-done.5
  30.7 0.0 copy-done.6
  30.7 14.4 %shard_map.103 = (f32[64,24,128]{2,1,0:T(8,128)S(1)}, f32[64,24,128]{2,1,0:T(8,128)S(1)}, f32[4,2,2,256,128]{4,3,2,1,0:T(8,128)S(1)}, f32[4,2,2,256,128]{4,3,2,1,0:T(8,128)S(1)}, s32[8,128]{1,0:T(8,128)S(1)}) custom-call(s32[2,4]{1,0:T(2,128)S(1)} %bitcast.20, f32[2,256,256]{2,1,0:T(8,128)S(1)} %copy-done.1, ...), custom_call_target="tpu_custom_call" | custom-call | flops 13958643712 | bytes 12582912 | tf_op jit(solution)/shard_map/pallas_call | solution.py:549
  45.1 0.1 collective-permute-start.6
  45.2 3.4 %shard_map.104 = (f32[2,256,256]{2,1,0:T(8,128)S(1)}, f32[2,128,256]{2,1,0:T(8,128)S(1)}, f32[2,128,256]{2,1,0:T(8,128)S(1)}, f32[2,256,128]{2,1,0:T(8,128)S(1)}...) custom-call(s32[2,4]{1,0:T(2,128)S(1)} %bitcast.21, ...), custom_call_target="tpu_custom_call" | custom-call | flops 5368709120 | bytes 8388608 | tf_op jit(solution)/shard_map/pallas_call | solution.py:583
  48.6 0.0 collective-permute-done.6
  48.7 1.0 add.9
  49.6 12.2 %all-to-all-start = ((f32[64,24,128]{2,1,0:T(8,128)}), f32[64,24,128]{2,1,0:T(8,128)}, u32[]{:S(2)}, u32[]{:S(2)}) async-start(f32[64,24,128]{2,1,0:T(8,128)} %add.9), calls=%async_computation | async-start | bytes 1572864 | tf_op jit(solution)/shard_map/probe_reduce/all_to_all | solution.py:661
  61.8 4.1 %collective-permute-start.7 = (f32[2,2,128,128]{3,2,1,0:T(8,128)S(1)}, f32[2,2,128,128]{3,2,1,0:T(8,128)S(1)}, u32[]{:S(2)}, u32[]{:S(2)}) collective-permute-start(f32[2,2,128,128]{3,2,1,0:T(8,128)S(1)} %get-tuple-element.67), channel_id=1, source_target_pairs={{1,2},{2,1},{3,4},{4,3},{5,6},{6,5},{7,8},{8,7},{9,10},{10,9},{11,... | collective-permute-start | bytes 786440 | tf_op jit(solution)/shard_map/gradient_corners/ppermute | solution.py:628
  65.9 0.1 collective-permute-start.8
  66.0 2.8 %gradient_rows.2.light = f32[256,256]{1,0:T(8,128)S(1)} custom-call(s32[2,4]{1,0:T(2,128)S(1)} %bitcast.22, s32[8,128]{1,0:T(8,128)S(1)} %get-tuple-element.65.around, f32[2,2,256,256]{3,2,1,0:T(8,128)S(1)} %copy-done.5), custom_call_target="tpu_custom_call" | custom-call | flops 2147483648 | bytes 4194304 | tf_op jit(solution)/shard_map/gradient_rows/pallas_call | solution.py:517
  68.8 7.9 %collective-permute-done.7 = f32[2,2,128,128]{3,2,1,0:T(8,128)S(1)} collective-permute-done((f32[2,2,128,128]{3,2,1,0:T(8,128)S(1)}, f32[2,2,128,128]{3,2,1,0:T(8,128)S(1)}, u32[]{:S(2)}, u32[]{:S(2)}) %collective-permute-start.7) | collective-permute-done | bytes 262176 | tf_op jit(solution)/shard_map/gradient_corners/ppermute | solution.py:628
  76.6 0.0 collective-permute-done.8
  76.7 0.1 fusion.5
  76.7 0.0 all-to-all-done
  76.8 1.2 %reduce_sum.9 = f32[24,128]{1,0:T(8,128)S(1)} reduce(f32[64,24,128]{2,1,0:T(8,128)} %all-to-all-done, f32[]{:T(128)} %constant.18.clone.1), dimensions={0}, to_apply=%region_0.1 | reduce | flops 193536 | bytes 798724 | tf_op jit(solution)/shard_map/probe_sum/reduce_sum | solution.py:681
  78.0 0.8 broadcast_in_dim.2
  78.8 10.8 %all-to-all-start.1 = ((f32[64,16,128]{2,1,0:T(8,128)}), f32[64,16,128]{2,1,0:T(8,128)S(1)}, u32[]{:S(2)}, u32[]{:S(2)}) async-start(f32[64,16,128]{2,1,0:T(8,128)} %broadcast_in_dim.2), calls=%async_computation.1 | async-start | bytes 1048576 | tf_op jit(solution)/shard_map/probe_gather/all_to_all | solution.py:687
  89.6 3.7 %collective-permute-start.11 = (f32[2,256,128]{2,1,0:T(8,128)S(1)}, f32[2,256,128]{2,1,0:T(8,128)S(1)}, u32[]{:S(2)}, u32[]{:S(2)}) collective-permute-start(f32[2,256,128]{2,1,0:T(8,128)S(1)} %get-tuple-element.74), channel_id=1, source_target_pairs={{1,2},{2,1},{3,4},{4,3},{5,6},{6,5},{7,8},{8,7},{9,10},{10,9},{11,... | collective-permute-start | bytes 786440 | tf_op jit(solution)/shard_map/gradient_corners/ppermute | solution.py:628
  93.3 0.1 collective-permute-start.12
  93.4 0.6 collective-permute-start.9
  94.0 5.0 %collective-permute-start.10 = (f32[2,128,256]{2,1,0:T(8,128)S(1)}, f32[2,128,256]{2,1,0:T(8,128)S(1)}, u32[]{:S(2)}, u32[]{:S(2)}) collective-permute-start(f32[2,128,256]{2,1,0:T(8,128)S(1)} %get-tuple-element.73), channel_id=1, source_target_pairs={{16,32},{32,16},{48,64},{64,48},{80,96},{96,80},{17,33},{33,17},{4... | collective-permute-start | bytes 786440 | tf_op jit(solution)/shard_map/gradient_rows/ppermute | solution.py:624
  99.1 3.2 %collective-permute-done.11.cross = f32[2,256,128]{2,1,0:T(8,128)S(1)} collective-permute-done((f32[2,256,128]{2,1,0:T(8,128)S(1)}, f32[2,256,128]{2,1,0:T(8,128)S(1)}, u32[]{:S(2)}, u32[]{:S(2)}) %collective-permute-start.11) | collective-permute-done | bytes 262176 | tf_op jit(solution)/shard_map/gradient_corners/ppermute | solution.py:628
  102.3 0.0 collective-permute-done.12.same
  102.3 1.2 %collective-permute-done.9.even = f32[2,128,256]{2,1,0:T(8,128)S(1)} collective-permute-done((f32[2,128,256]{2,1,0:T(8,128)S(1)}, f32[2,128,256]{2,1,0:T(8,128)S(1)}, u32[]{:S(2)}, u32[]{:S(2)}) %collective-permute-start.9) | collective-permute-done | bytes 262176 | tf_op jit(solution)/shard_map/gradient_rows/ppermute | solution.py:624
  103.4 4.8 %collective-permute-done.10.odd = f32[2,128,256]{2,1,0:T(8,128)S(1)} collective-permute-done((f32[2,128,256]{2,1,0:T(8,128)S(1)}, f32[2,128,256]{2,1,0:T(8,128)S(1)}, u32[]{:S(2)}, u32[]{:S(2)}) %collective-permute-start.10) | collective-permute-done | bytes 262176 | tf_op jit(solution)/shard_map/gradient_rows/ppermute | solution.py:624
  108.2 1.0 gradient_rows.3
  109.2 0.0 all-to-all-done.1.mine
  109.2 1.6 %collective-permute-start.13 = (f32[64,16,128]{2,1,0:T(8,128)S(1)}, f32[64,16,128]{2,1,0:T(8,128)S(1)}, u32[]{:S(2)}, u32[]{:S(2)}) collective-permute-start(f32[64,16,128]{2,1,0:T(8,128)S(1)} %all-to-all-done.1.mine), channel_id=1, source_target_pairs={{0,1},{1,0},{2,3},{3,2},{4,5},{5,4},{6,7},{7,6},{8,9},{9,8},{10,11... | collective-permute-start | bytes 1572872 | tf_op jit(solution)/shard_map/probe_gather/ppermute | solution.py:628
  110.7 0.1 slice_reduce_fusion
  110.9 0.1 reshape_squeeze.3
  110.9 0.7 copy.12
  111.6 0.6 fusion.6
  113.5 0.0 collective-permute-done.13.other
  113.5 1.1 probe_gather.1
  (6 shorter events, 0.1 us)
Async XLA Ops:
  0.6 1.0 copy-start
  1.7 0.7 copy-start.2
  3.1 16.6 %collective-permute-start = (f32[2,136,256]{2,1,0:T(8,128)S(1)}, f32[2,136,256]{2,1,0:T(8,128)S(1)}, u32[]{:S(2)}, u32[]{:S(2)}) collective-permute-start(f32[2,136,256]{2,1,0:T(8,128)S(1)} %get-tuple-element.42), channel_id=1, source_target_pairs={{0,16},{16,0},{32,48},{48,32},{64,80},{80,64},{96,112},{112,96},{1... | collective-permute-start | bytes 835592 | tf_op jit(solution)/shard_map/object_halo/ppermute | solution.py:624
  3.7 16.1 %collective-permute-start.1 = (f32[2,136,256]{2,1,0:T(8,128)S(1)}, f32[2,136,256]{2,1,0:T(8,128)S(1)}, u32[]{:S(2)}, u32[]{:S(2)}) collective-permute-start(f32[2,136,256]{2,1,0:T(8,128)S(1)} %get-tuple-element.43), channel_id=1, source_target_pairs={{16,32},{32,16},{48,64},{64,48},{80,96},{96,80},{17,33},{33,17},{4... | collective-permute-start | bytes 835592 | tf_op jit(solution)/shard_map/object_halo/ppermute | solution.py:624
  9.7 10.1 %collective-permute-start.2 = (f32[2,264,128]{2,1,0:T(8,128)S(1)}, f32[2,264,128]{2,1,0:T(8,128)S(1)}, u32[]{:S(2)}, u32[]{:S(2)}) collective-permute-start(f32[2,264,128]{2,1,0:T(8,128)S(1)} %get-tuple-element.44), channel_id=1, source_target_pairs={{1,2},{2,1},{3,4},{4,3},{5,6},{6,5},{7,8},{8,7},{9,10},{10,9},{11,... | collective-permute-start | bytes 811016 | tf_op jit(solution)/shard_map/object_halo/ppermute | solution.py:628
  13.4 6.3 %collective-permute-start.3 = (f32[2,264,128]{2,1,0:T(8,128)S(1)}, f32[2,264,128]{2,1,0:T(8,128)S(1)}, u32[]{:S(2)}, u32[]{:S(2)}) collective-permute-start(f32[2,264,128]{2,1,0:T(8,128)S(1)} %get-tuple-element.45), channel_id=1, source_target_pairs={{0,1},{1,0},{2,3},{3,2},{4,5},{5,4},{6,7},{7,6},{8,9},{9,8},{10,11... | collective-permute-start | bytes 811016 | tf_op jit(solution)/shard_map/object_halo/ppermute | solution.py:628
  13.5 1.2 %copy-start.4 = (f32[1,1,4,256,256]{4,3,2,1,0:T(8,128)S(1)}, f32[1,1,4,256,256]{4,3,2,1,0:T(8,128)}, u32[]{:S(2)}) copy-start(f32[1,1,4,256,256]{4,3,2,1,0:T(8,128)} %param.9) | copy-start | bytes 3145732
  14.8 1.0 copy-start.7
  15.8 1.0 copy-start.8
  16.8 14.0 %copy-start.1 = (f32[2,256,256]{2,1,0:T(8,128)S(1)}, f32[2,256,256]{2,1,0:T(8,128)}, u32[]{:S(2)}) copy-start(f32[2,256,256]{2,1,0:T(8,128)} %own.3) | copy-start | bytes 1572868
  16.8 14.0 %copy-start.3 = (s32[1,1,4,2]{2,3,1,0:T(2,128)S(1)}, s32[1,1,4,2]{2,3,1,0:T(2,128)}, u32[]{:S(2)}) copy-start(s32[1,1,4,2]{2,3,1,0:T(2,128)} %param.10) | copy-start | bytes 100
  16.8 14.0 %copy-start.5 = (f32[2,2,256,256]{3,2,1,0:T(8,128)S(1)}, f32[2,2,256,256]{3,2,1,0:T(8,128)}, u32[]{:S(2)}) copy-start(f32[2,2,256,256]{3,2,1,0:T(8,128)} %probe.3) | copy-start | bytes 3145732
  16.8 14.0 %copy-start.6 = (bf16[2,2,2,256,256]{4,3,2,1,0:T(8,128)(2,1)S(1)}, bf16[2,2,2,256,256]{4,3,2,1,0:T(8,128)(2,1)}, u32[]{:S(2)}) copy-start(bf16[2,2,2,256,256]{4,3,2,1,0:T(8,128)(2,1)} %constant.21.clone.matrices) | copy-start | bytes 3145732
  19.8 4.5 %collective-permute-start.5 = (f32[2,2,136,128]{3,2,1,0:T(8,128)S(1)}, f32[2,2,136,128]{3,2,1,0:T(8,128)S(1)}, u32[]{:S(2)}, u32[]{:S(2)}) collective-permute-start(f32[2,2,136,128]{3,2,1,0:T(8,128)S(1)} %get-tuple-element.88), channel_id=1, source_target_pairs={{0,1},{1,0},{2,3},{3,2},{4,5},{5,4},{6,7},{7,6},{8,9},{9,8},{10,11... | collective-permute-start | bytes 835592 | tf_op jit(solution)/shard_map/object_corners/ppermute | solution.py:628
  21.3 9.5 %collective-permute-start.4 = (f32[2,2,136,128]{3,2,1,0:T(8,128)S(1)}, f32[2,2,136,128]{3,2,1,0:T(8,128)S(1)}, u32[]{:S(2)}, u32[]{:S(2)}) collective-permute-start(f32[2,2,136,128]{3,2,1,0:T(8,128)S(1)} %get-tuple-element.89), channel_id=1, source_target_pairs={{1,2},{2,1},{3,4},{4,3},{5,6},{6,5},{7,8},{8,7},{9,10},{10,9},{11,... | collective-permute-start | bytes 835592 | tf_op jit(solution)/shard_map/object_corners/ppermute | solution.py:628
  45.1 3.5 %collective-permute-start.6 = (f32[64,24,128]{2,1,0:T(8,128)S(1)}, f32[64,24,128]{2,1,0:T(8,128)S(1)}, u32[]{:S(2)}, u32[]{:S(2)}) collective-permute-start(f32[64,24,128]{2,1,0:T(8,128)S(1)} %get-tuple-element.52), channel_id=1, source_target_pairs={{0,1},{1,0},{2,3},{3,2},{4,5},{5,4},{6,7},{7,6},{8,9},{9,8},{10,11... | collective-permute-start | bytes 2359304 | tf_op jit(solution)/shard_map/probe_reduce/ppermute | solution.py:628
  49.6 27.1 %all-to-all-start = ((f32[64,24,128]{2,1,0:T(8,128)}), f32[64,24,128]{2,1,0:T(8,128)}, u32[]{:S(2)}, u32[]{:S(2)}) async-start(f32[64,24,128]{2,1,0:T(8,128)} %add.9), calls=%async_computation | async-start | bytes 1572864 | tf_op jit(solution)/shard_map/probe_reduce/all_to_all | solution.py:661
  61.8 14.8 %collective-permute-start.7 = (f32[2,2,128,128]{3,2,1,0:T(8,128)S(1)}, f32[2,2,128,128]{3,2,1,0:T(8,128)S(1)}, u32[]{:S(2)}, u32[]{:S(2)}) collective-permute-start(f32[2,2,128,128]{3,2,1,0:T(8,128)S(1)} %get-tuple-element.67), channel_id=1, source_target_pairs={{1,2},{2,1},{3,4},{4,3},{5,6},{6,5},{7,8},{8,7},{9,10},{10,9},{11,... | collective-permute-start | bytes 786440 | tf_op jit(solution)/shard_map/gradient_corners/ppermute | solution.py:628
  65.9 10.7 %collective-permute-start.8 = (f32[2,2,128,128]{3,2,1,0:T(8,128)S(1)}, f32[2,2,128,128]{3,2,1,0:T(8,128)S(1)}, u32[]{:S(2)}, u32[]{:S(2)}) collective-permute-start(f32[2,2,128,128]{3,2,1,0:T(8,128)S(1)} %get-tuple-element.68), channel_id=1, source_target_pairs={{0,1},{1,0},{2,3},{3,2},{4,5},{5,4},{6,7},{7,6},{8,9},{9,8},{10,11... | collective-permute-start | bytes 786440 | tf_op jit(solution)/shard_map/gradient_corners/ppermute | solution.py:628
  78.8 30.4 %all-to-all-start.1 = ((f32[64,16,128]{2,1,0:T(8,128)}), f32[64,16,128]{2,1,0:T(8,128)S(1)}, u32[]{:S(2)}, u32[]{:S(2)}) async-start(f32[64,16,128]{2,1,0:T(8,128)} %broadcast_in_dim.2), calls=%async_computation.1 | async-start | bytes 1048576 | tf_op jit(solution)/shard_map/probe_gather/all_to_all | solution.py:687
  89.6 12.6 %collective-permute-start.11 = (f32[2,256,128]{2,1,0:T(8,128)S(1)}, f32[2,256,128]{2,1,0:T(8,128)S(1)}, u32[]{:S(2)}, u32[]{:S(2)}) collective-permute-start(f32[2,256,128]{2,1,0:T(8,128)S(1)} %get-tuple-element.74), channel_id=1, source_target_pairs={{1,2},{2,1},{3,4},{4,3},{5,6},{6,5},{7,8},{8,7},{9,10},{10,9},{11,... | collective-permute-start | bytes 786440 | tf_op jit(solution)/shard_map/gradient_corners/ppermute | solution.py:628
  93.3 8.9 %collective-permute-start.12 = (f32[2,256,128]{2,1,0:T(8,128)S(1)}, f32[2,256,128]{2,1,0:T(8,128)S(1)}, u32[]{:S(2)}, u32[]{:S(2)}) collective-permute-start(f32[2,256,128]{2,1,0:T(8,128)S(1)} %get-tuple-element.75), channel_id=1, source_target_pairs={{0,1},{1,0},{2,3},{3,2},{4,5},{5,4},{6,7},{7,6},{8,9},{9,8},{10,11... | collective-permute-start | bytes 786440 | tf_op jit(solution)/shard_map/gradient_corners/ppermute | solution.py:628
  93.4 10.0 %collective-permute-start.9 = (f32[2,128,256]{2,1,0:T(8,128)S(1)}, f32[2,128,256]{2,1,0:T(8,128)S(1)}, u32[]{:S(2)}, u32[]{:S(2)}) collective-permute-start(f32[2,128,256]{2,1,0:T(8,128)S(1)} %get-tuple-element.72), channel_id=1, source_target_pairs={{0,16},{16,0},{32,48},{48,32},{64,80},{80,64},{96,112},{112,96},{1... | collective-permute-start | bytes 786440 | tf_op jit(solution)/shard_map/gradient_rows/ppermute | solution.py:624
  94.0 14.2 %collective-permute-start.10 = (f32[2,128,256]{2,1,0:T(8,128)S(1)}, f32[2,128,256]{2,1,0:T(8,128)S(1)}, u32[]{:S(2)}, u32[]{:S(2)}) collective-permute-start(f32[2,128,256]{2,1,0:T(8,128)S(1)} %get-tuple-element.73), channel_id=1, source_target_pairs={{16,32},{32,16},{48,64},{64,48},{80,96},{96,80},{17,33},{33,17},{4... | collective-permute-start | bytes 786440 | tf_op jit(solution)/shard_map/gradient_rows/ppermute | solution.py:624
  109.2 4.3 %collective-permute-start.13 = (f32[64,16,128]{2,1,0:T(8,128)S(1)}, f32[64,16,128]{2,1,0:T(8,128)S(1)}, u32[]{:S(2)}, u32[]{:S(2)}) collective-permute-start(f32[64,16,128]{2,1,0:T(8,128)S(1)} %all-to-all-done.1.mine), channel_id=1, source_target_pairs={{0,1},{1,0},{2,3},{3,2},{4,5},{5,4},{6,7},{7,6},{8,9},{9,8},{10,11... | collective-permute-start | bytes 1572872 | tf_op jit(solution)/shard_map/probe_gather/ppermute | solution.py:628

commit v6 on v5

--- a/solution.py
+++ b/solution.py
@@ -140,7 +140,7 @@
 
 
 def transform_kernel(
-    starts, own, even_strip, odd_strip, cross, same, cross_corner, same_corner, probe_in, matrices, measured,
+    starts, own, odd_strip, even_strip, cross, same, cross_corner, same_corner, probe_in, matrices, measured,
     keep, send, object_part, patch, around,
     tile, probe, mats, offsets, totals, xs, zs, gs, ys, back, sums, sems,
 ):
@@ -157,14 +157,14 @@
         moves = [(probe_in, probe)]
         for block, strip, corner in ((cross_block, cross, cross_corner), (same_block, same, same_corner)):
             moves.append((strip.at[:, :SIZE, :], tile.at[:, block, center, :]))
-            moves.append((corner.at[0, :, :HALF, :], tile.at[:, block, even_rows, :]))
-            moves.append((corner.at[1, :, :HALF, :], tile.at[:, block, odd_rows, :]))
+            moves.append((corner.at[1, :, :HALF, :], tile.at[:, block, even_rows, :]))
+            moves.append((corner.at[0, :, :HALF, :], tile.at[:, block, odd_rows, :]))
         for b in range(2):
             span = pl.ds(b * HALF, HALF)
             moves.append((own.at[:, :, span], tile.at[:, 1 + b, center, :]))
             moves.append((even_strip.at[:, :HALF, span], tile.at[:, 1 + b, even_rows, :]))
             moves.append((odd_strip.at[:, :HALF, span], tile.at[:, 1 + b, odd_rows, :]))
-        strips = [x.at[0] for x in (even_strip, odd_strip, cross, same)]
+        strips = [x.at[0] for x in (odd_strip, even_strip, cross, same)]
         strips += [x.at[n, 0] for x in (cross_corner, same_corner) for n in range(2)]
         for n, strip in enumerate(strips):
             moves.append((strip.at[pl.ds(strip.shape[0] - 8, 8), pl.ds(0, HALF)], offsets.at[n]))
@@ -394,8 +394,8 @@
     lanes = lane_index(CHUNK)
     row_odd, core = place_of()
     even, cross = 1 - 2 * row_odd, 2 * core - 1
-    neighbours = [(even, None), (-even, None), (None, cross), (None, -cross)]
-    neighbours += [(even, cross), (-even, cross), (even, -cross), (-even, -cross)]
+    neighbours = [(-even, None), (even, None), (None, cross), (None, -cross)]
+    neighbours += [(-even, cross), (even, cross), (-even, -cross), (even, -cross)]
 
     def add(row, col, down, right):
         rows, source_row, row = (SIZE, 0, row + HALF) if down is None else (
@@ -436,6 +436,15 @@
 
     light[:, :HALF] = accum[2, 256:512]
     light[:, HALF:] = accum[3, 256:512]
+
+
+def quotient_kernel(chunk, spread_out, ratio):
+    total = jnp.sum(chunk[...], axis=0)
+    power = total[16:20]
+    for c in range(4):
+        quotient = total[4 * c : 4 * c + 4] / power
+        spread_out[:, 4 * c : 4 * c + 4, :] = jnp.broadcast_to(quotient[None], (64, 4, HALF))
+    ratio[...] = jnp.broadcast_to(total[20:21, 0:1] / total[20:21, 1:2], (8, HALF))
 
 
 def update_kernel(center, even, odd, cross, same, light, out, total):
@@ -647,12 +656,12 @@
         same = swap_columns(same, 0)
     permuted = prepare(measured)
     with jax.named_scope("object_corners"):
-        even, odd, cross, same, permuted = lax.optimization_barrier((even, odd, cross, same, permuted))
-        rows = jnp.stack([even, odd])
+        odd, even, cross, same, permuted = lax.optimization_barrier((odd, even, cross, same, permuted))
+        rows = jnp.stack([odd, even])
         cross_corner = swap_columns(half_lanes(rows, core == 0), 1)
         same_corner = swap_columns(half_lanes(rows, core == 1), 0)
 
-    halo = [even, odd, cross, same, cross_corner, same_corner]
+    halo = [odd, even, cross, same, cross_corner, same_corner]
     keep, send, object_part, patch, around = transforms(starts, object_tile, halo, probe, permuted)
 
     parts = place_parts(starts, object_part, patch, probe)
@@ -677,17 +686,12 @@
         even = swap_rows(even, 0)
         object_update = update([center, even, odd, cross, same, light])
 
-    with jax.named_scope("probe_sum"):
-        total = jnp.sum(chunk, axis=0)
-        quotient = total[:16].reshape(4, 4, HALF) / total[16:20]
-        relative_error = (total[20, 0] / total[20, 1]).reshape(1)
-
     with jax.named_scope("probe_gather"):
-        spread_out = jnp.broadcast_to(quotient.reshape(1, 16, HALF), (devices // 2, 16, HALF))
+        spread_out, ratio = simple(quotient_kernel, [], [chunk], [(64, 16, HALF), (8, HALF)], [], 1 << 20, 2 << 20)
         gathered = lax.all_to_all(spread_out, AXES, 0, 0, axis_index_groups=groups, tiled=True)
-        gathered, object_update = lax.optimization_barrier((gathered, object_update))
         probe_update = assemble(gathered, swap_columns(gathered, 0)).reshape(probe.shape)
 
+    relative_error = ratio[0, :1]
     position_step = steps[:, 0].reshape(1, 1, -1, 2)
     return (object_update, probe_update, position_step, relative_error)
 

time: 117 us -> 120 us (1.026)
  blocking collectives: 0 us -> 22.1 us
  starting transfers between devices: 53.1 us -> 39.6 us
  waiting for transfers between devices: 25.1 us -> 21.7 us
  between operations: 3.36 us -> 0.86 us
    all_to_all x0 -> x1, blocking collectives: none -> 22.1 us  [local(): lax.all_to_all(spread_out, AXES, 0, 0, axis_index_groups=groups, tiled=True)]
    all_to_all x1 -> x0, starting transfers between devices: 10.8 us -> none  [local(): lax.all_to_all(spread_out, AXES, 0, 0, axis_index_groups=groups, tiled=True)]
    ppermute x10, waiting for transfers between devices: 19.1 us -> 14.9 us  [swap_columns(): return lax.ppermute(value, 'col', pairs_from(first, lax.axis_size('col')))]
    ppermute x4, starting transfers between devices: 12.2 us -> 10 us  [swap_rows(): return lax.ppermute(value, 'row', pairs_from(first, lax.axis_size('row')))]
    ppermute x10, starting transfers between devices: 17.9 us -> 16 us  [swap_columns(): return lax.ppermute(value, 'col', pairs_from(first, lax.axis_size('col')))]
    all_to_all x1, starting transfers between devices: 12.2 us -> 13.6 us  [local(): lax.all_to_all(chunk, AXES, 0, 0, axis_index_groups=groups, tiled=True)]
    unnamed x19 -> x21, local copies, waits for them, and re-layouts: 5.59 us -> 6.82 us
    reduce_sum x1 -> x0, other arithmetic: 1.22 us -> none  [local(): total = jnp.sum(chunk, axis=0)]
  transfers between devices with their start and end apart: 16 -> 15, of which waited for: 6 -> 5; matrix products, arithmetic and copies ran while one was open for 1% -> 2% of each run, Pallas kernels for 7% -> 7%
where the time goes in v6:
time: 120 us; the launch traced here: 119 us
  starting transfers between devices  39.6 us (33%)
  Pallas kernels  24.8 us (21%)
  blocking collectives  22.1 us (18%)
  waiting for transfers between devices  21.7 us (18%)
  local copies, waits for them, and re-layouts  7.53 us (6%)
  other arithmetic  1.9 us (2%)
    all_to_all x1, blocking collectives, local(): lax.all_to_all(spread_out, AXES, 0, 0, axis_index_groups=groups, tiled=True)  22.1 us
    ppermute x10, starting transfers between devices, swap_columns(): return lax.ppermute(value, 'col', pairs_from(first, lax.axis_size('col')))  16 us
    ppermute x10, waiting for transfers between devices, swap_columns(): return lax.ppermute(value, 'col', pairs_from(first, lax.axis_size('col')))  14.9 us
    pallas_call x1, Pallas kernels, transforms(): pl.pallas_call(transform_kernel, out_shape=shaped([halves, halves, (count...  14.3 us
    all_to_all x1, starting transfers between devices, local(): lax.all_to_all(chunk, AXES, 0, 0, axis_index_groups=groups, tiled=True)  13.6 us
    ppermute x4, starting transfers between devices, swap_rows(): return lax.ppermute(value, 'row', pairs_from(first, lax.axis_size('row')))  10 us
    ppermute x4, waiting for transfers between devices, swap_rows(): return lax.ppermute(value, 'row', pairs_from(first, lax.axis_size('row')))  6.82 us
    unnamed x21, local copies, waits for them, and re-layouts  6.82 us
  transfers between devices with their start and end apart: 15, of which 5 were waited for; matrix products, arithmetic and copies ran while one was open for 2% of the time, Pallas kernels for 7%

profile of v6, /device:TPU:25, one launch (start us, length us, event | category | flops | bytes accessed | tf_op | source)
XLA Modules:
  0.0 118.5 jit_solution(4800796397160571965)
XLA Ops:
  0.6 0.0 copy-start
  0.6 1.0 copy-done
  1.7 0.0 copy-start.2
  1.7 0.7 copy-done.2
  2.4 0.8 object_halo.1
  3.1 5.2 %collective-permute-start = (f32[2,136,256]{2,1,0:T(8,128)S(1)}, f32[2,136,256]{2,1,0:T(8,128)S(1)}, u32[]{:S(2)}, u32[]{:S(2)}) collective-permute-start(f32[2,136,256]{2,1,0:T(8,128)S(1)} %get-tuple-element.42), channel_id=1, source_target_pairs={{16,32},{32,16},{48,64},{64,48},{80,96},{96,80},{17,33},{33,17},{4... | collective-permute-start | bytes 835592 | tf_op jit(solution)/shard_map/object_halo/ppermute | solution.py:633
  8.3 0.1 collective-permute-start.1
  8.4 3.5 %collective-permute-start.2 = (f32[2,264,128]{2,1,0:T(8,128)S(1)}, f32[2,264,128]{2,1,0:T(8,128)S(1)}, u32[]{:S(2)}, u32[]{:S(2)}) collective-permute-start(f32[2,264,128]{2,1,0:T(8,128)S(1)} %get-tuple-element.44), channel_id=1, source_target_pairs={{1,2},{2,1},{3,4},{4,3},{5,6},{6,5},{7,8},{8,7},{9,10},{10,9},{11,... | collective-permute-start | bytes 811016 | tf_op jit(solution)/shard_map/object_halo/ppermute | solution.py:637
  11.9 0.1 collective-permute-start.3
  12.0 0.0 copy-start.4
  12.0 1.2 %copy-done.4 = f32[1,1,4,256,256]{4,3,2,1,0:T(8,128)S(1)} copy-done((f32[1,1,4,256,256]{4,3,2,1,0:T(8,128)S(1)}, f32[1,1,4,256,256]{4,3,2,1,0:T(8,128)}, u32[]{:S(2)}) %copy-start.4) | copy-done | bytes 1048600
  13.2 0.0 copy-start.8
  13.2 1.0 copy-done.8
  14.2 0.0 copy-start.9
  14.2 1.0 copy-done.9
  15.2 0.0 copy-start.1
  15.2 0.0 copy-start.3
  15.2 0.0 copy-start.5
  15.2 1.3 %shard_map.102.measured = f32[4,256,256]{2,1,0:T(8,128)S(1)} custom-call(f32[4,256,256]{2,1,0:T(8,128)S(1)} %bitcast.22, bf16[768,256]{1,0:T(8,128)(2,1)S(1)} %copy-done.9, bf16[256,768]{1,0:T(8,128)(2,1)S(1)} %copy-done.8), custom_call_target="tpu_custom_call" | custom-call | flops 1073741824 | bytes 3145728 | tf_op jit(solution)/shard_map/pallas_call | solution.py:526
  16.5 1.7 %collective-permute-done.2.cross = f32[2,264,128]{2,1,0:T(8,128)S(1)} collective-permute-done((f32[2,264,128]{2,1,0:T(8,128)S(1)}, f32[2,264,128]{2,1,0:T(8,128)S(1)}, u32[]{:S(2)}, u32[]{:S(2)}) %collective-permute-start.2) | collective-permute-done | bytes 270368 | tf_op jit(solution)/shard_map/object_halo/ppermute | solution.py:637
  18.2 0.0 collective-permute-done.3.same
  18.2 0.0 collective-permute-done.odd_strip
  18.2 0.0 collective-permute-done.1.even_strip
  18.2 1.2 collective-permute-start.5
  19.4 3.3 %collective-permute-start.4 = (f32[2,2,136,128]{3,2,1,0:T(8,128)S(1)}, f32[2,2,136,128]{3,2,1,0:T(8,128)S(1)}, u32[]{:S(2)}, u32[]{:S(2)}) collective-permute-start(f32[2,2,136,128]{3,2,1,0:T(8,128)S(1)} %get-tuple-element.89), channel_id=1, source_target_pairs={{1,2},{2,1},{3,4},{4,3},{5,6},{6,5},{7,8},{8,7},{9,10},{10,9},{11,... | collective-permute-start | bytes 835592 | tf_op jit(solution)/shard_map/object_corners/ppermute | solution.py:637
  22.7 0.0 collective-permute-done.5.same_corner
  22.7 6.4 %collective-permute-done.4.cross_corner = f32[2,2,136,128]{3,2,1,0:T(8,128)S(1)} collective-permute-done((f32[2,2,136,128]{3,2,1,0:T(8,128)S(1)}, f32[2,2,136,128]{3,2,1,0:T(8,128)S(1)}, u32[]{:S(2)}, u32[]{:S(2)}) %collective-permute-start.4) | collective-permute-done | bytes 278560 | tf_op jit(solution)/shard_map/object_corners/ppermute | solution.py:637
  29.2 0.0 copy-done.1
  29.2 0.0 copy-done.3
  29.2 0.0 copy-done.5
  29.2 0.0 copy-done.7
  29.2 14.3 %shard_map.103 = (f32[64,24,128]{2,1,0:T(8,128)S(1)}, f32[64,24,128]{2,1,0:T(8,128)S(1)}, f32[4,2,2,256,128]{4,3,2,1,0:T(8,128)S(1)}, f32[4,2,2,256,128]{4,3,2,1,0:T(8,128)S(1)}, s32[8,128]{1,0:T(8,128)S(1)}) custom-call(s32[2,4]{1,0:T(2,128)S(1)} %bitcast.19, f32[2,256,256]{2,1,0:T(8,128)S(1)} %copy-done.1, ...), custom_call_target="tpu_custom_call" | custom-call | flops 13958643712 | bytes 12582912 | tf_op jit(solution)/shard_map/pallas_call | solution.py:558
  43.5 0.1 collective-permute-start.6
  43.6 3.5 %shard_map.104 = (f32[2,256,256]{2,1,0:T(8,128)S(1)}, f32[2,128,256]{2,1,0:T(8,128)S(1)}, f32[2,128,256]{2,1,0:T(8,128)S(1)}, f32[2,256,128]{2,1,0:T(8,128)S(1)}...) custom-call(s32[2,4]{1,0:T(2,128)S(1)} %bitcast.20, ...), custom_call_target="tpu_custom_call" | custom-call | flops 5368709120 | bytes 8388608 | tf_op jit(solution)/shard_map/pallas_call | solution.py:592
  47.1 0.0 collective-permute-done.6
  47.1 1.0 add.9
  48.1 13.6 %all-to-all-start = ((f32[64,24,128]{2,1,0:T(8,128)}), f32[64,24,128]{2,1,0:T(8,128)S(1)}, u32[]{:S(2)}, u32[]{:S(2)}) async-start(f32[64,24,128]{2,1,0:T(8,128)} %add.9), calls=%async_computation | async-start | bytes 1572864 | tf_op jit(solution)/shard_map/probe_reduce/all_to_all | solution.py:670
  61.7 4.0 %collective-permute-start.7 = (f32[2,2,128,128]{3,2,1,0:T(8,128)S(1)}, f32[2,2,128,128]{3,2,1,0:T(8,128)S(1)}, u32[]{:S(2)}, u32[]{:S(2)}) collective-permute-start(f32[2,2,128,128]{3,2,1,0:T(8,128)S(1)} %get-tuple-element.68), channel_id=1, source_target_pairs={{1,2},{2,1},{3,4},{4,3},{5,6},{6,5},{7,8},{8,7},{9,10},{10,9},{11,... | collective-permute-start | bytes 786440 | tf_op jit(solution)/shard_map/gradient_corners/ppermute | solution.py:637
  65.8 0.1 collective-permute-start.8
  65.9 0.0 copy-start.6
  65.9 1.2 %copy-done.6 = f32[2,2,256,256]{3,2,1,0:T(8,128)S(1)} copy-done((f32[2,2,256,256]{3,2,1,0:T(8,128)S(1)}, f32[2,2,256,256]{3,2,1,0:T(8,128)}, u32[]{:S(2)}) %copy-start.6) | copy-done | bytes 1048600
  67.1 2.8 %gradient_rows.2.light = f32[256,256]{1,0:T(8,128)S(1)} custom-call(s32[2,4]{1,0:T(2,128)S(1)} %bitcast.21, s32[8,128]{1,0:T(8,128)S(1)} %get-tuple-element.66.around, f32[2,2,256,256]{3,2,1,0:T(8,128)S(1)} %copy-done.6), custom_call_target="tpu_custom_call" | custom-call | flops 2147483648 | bytes 4194304 | tf_op jit(solution)/shard_map/gradient_rows/pallas_call | solution.py:526
  69.9 6.8 %collective-permute-done.7 = f32[2,2,128,128]{3,2,1,0:T(8,128)S(1)} collective-permute-done((f32[2,2,128,128]{3,2,1,0:T(8,128)S(1)}, f32[2,2,128,128]{3,2,1,0:T(8,128)S(1)}, u32[]{:S(2)}, u32[]{:S(2)}) %collective-permute-start.7) | collective-permute-done | bytes 262176 | tf_op jit(solution)/shard_map/gradient_corners/ppermute | solution.py:637
  76.7 0.0 collective-permute-done.8
  76.7 0.9 fusion.5
  77.6 0.0 all-to-all-done.chunk
  77.6 0.2 probe_gather.2
  77.8 22.1 %all_to_all.10.mine = f32[64,16,128]{2,1,0:T(8,128)S(1)} all-to-all(f32[64,16,128]{2,1,0:T(8,128)S(1)} %get-tuple-element.77), channel_id=1, replica_groups={{0,2,4,6,8,10,12,14,16,18,20,22,24,26,28,30,32,34,36,38,40,42,44,46,48,..., dimensions={0} | all-to-all | bytes 1048576 | tf_op jit(solution)/shard_map/probe_gather/all_to_all | solution.py:691
  99.8 1.7 %collective-permute-start.13 = (f32[64,16,128]{2,1,0:T(8,128)S(1)}, f32[64,16,128]{2,1,0:T(8,128)S(1)}, u32[]{:S(2)}, u32[]{:S(2)}) collective-permute-start(f32[64,16,128]{2,1,0:T(8,128)S(1)} %all_to_all.10.mine), channel_id=1, source_target_pairs={{0,1},{1,0},{2,3},{3,2},{4,5},{5,4},{6,7},{7,6},{8,9},{9,8},{10,11... | collective-permute-start | bytes 1572872 | tf_op jit(solution)/shard_map/probe_gather/ppermute | solution.py:637
  101.5 2.0 %collective-permute-start.11 = (f32[2,256,128]{2,1,0:T(8,128)S(1)}, f32[2,256,128]{2,1,0:T(8,128)S(1)}, u32[]{:S(2)}, u32[]{:S(2)}) collective-permute-start(f32[2,256,128]{2,1,0:T(8,128)S(1)} %get-tuple-element.73), channel_id=1, source_target_pairs={{1,2},{2,1},{3,4},{4,3},{5,6},{6,5},{7,8},{8,7},{9,10},{10,9},{11,... | collective-permute-start | bytes 786440 | tf_op jit(solution)/shard_map/gradient_corners/ppermute | solution.py:637
  103.5 0.1 collective-permute-start.12
  103.5 0.1 collective-permute-start.9
  103.7 4.7 %collective-permute-start.10 = (f32[2,128,256]{2,1,0:T(8,128)}, f32[2,128,256]{2,1,0:T(8,128)S(1)}, u32[]{:S(2)}, u32[]{:S(2)}) collective-permute-start(f32[2,128,256]{2,1,0:T(8,128)} %get-tuple-element.72), channel_id=1, source_target_pairs={{16,32},{32,16},{48,64},{64,48},{80,96},{96,80},{17,33},{33,17},{4... | collective-permute-start | bytes 786440 | tf_op jit(solution)/shard_map/gradient_rows/ppermute | solution.py:633
  108.3 0.1 slice_reduce_fusion
  108.4 0.1 reshape_squeeze.3
  108.5 0.7 copy.12
  109.2 0.5 slice.25
  109.7 0.0 collective-permute-done.11.cross
  109.7 0.0 collective-permute-done.12.same
  109.7 1.6 %collective-permute-done.9.even = f32[2,128,256]{2,1,0:T(8,128)S(1)} collective-permute-done((f32[2,128,256]{2,1,0:T(8,128)}, f32[2,128,256]{2,1,0:T(8,128)S(1)}, u32[]{:S(2)}, u32[]{:S(2)}) %collective-permute-start.9) | collective-permute-done | bytes 262176 | tf_op jit(solution)/shard_map/gradient_rows/ppermute | solution.py:633
  111.3 5.2 %collective-permute-done.10.odd = f32[2,128,256]{2,1,0:T(8,128)S(1)} collective-permute-done((f32[2,128,256]{2,1,0:T(8,128)}, f32[2,128,256]{2,1,0:T(8,128)S(1)}, u32[]{:S(2)}, u32[]{:S(2)}) %collective-permute-start.10) | collective-permute-done | bytes 262176 | tf_op jit(solution)/shard_map/gradient_rows/ppermute | solution.py:633
  116.5 1.0 gradient_rows.3
  117.5 0.0 collective-permute-done.13.other
  117.5 1.0 probe_gather.3
  (3 shorter events, 0.1 us)
Async XLA Ops:
  0.6 1.0 copy-start
  1.7 0.7 copy-start.2
  3.1 15.0 %collective-permute-start = (f32[2,136,256]{2,1,0:T(8,128)S(1)}, f32[2,136,256]{2,1,0:T(8,128)S(1)}, u32[]{:S(2)}, u32[]{:S(2)}) collective-permute-start(f32[2,136,256]{2,1,0:T(8,128)S(1)} %get-tuple-element.42), channel_id=1, source_target_pairs={{16,32},{32,16},{48,64},{64,48},{80,96},{96,80},{17,33},{33,17},{4... | collective-permute-start | bytes 835592 | tf_op jit(solution)/shard_map/object_halo/ppermute | solution.py:633
  8.3 9.9 %collective-permute-start.1 = (f32[2,136,256]{2,1,0:T(8,128)S(1)}, f32[2,136,256]{2,1,0:T(8,128)S(1)}, u32[]{:S(2)}, u32[]{:S(2)}) collective-permute-start(f32[2,136,256]{2,1,0:T(8,128)S(1)} %get-tuple-element.43), channel_id=1, source_target_pairs={{0,16},{16,0},{32,48},{48,32},{64,80},{80,64},{96,112},{112,96},{1... | collective-permute-start | bytes 835592 | tf_op jit(solution)/shard_map/object_halo/ppermute | solution.py:633
  8.4 9.8 %collective-permute-start.2 = (f32[2,264,128]{2,1,0:T(8,128)S(1)}, f32[2,264,128]{2,1,0:T(8,128)S(1)}, u32[]{:S(2)}, u32[]{:S(2)}) collective-permute-start(f32[2,264,128]{2,1,0:T(8,128)S(1)} %get-tuple-element.44), channel_id=1, source_target_pairs={{1,2},{2,1},{3,4},{4,3},{5,6},{6,5},{7,8},{8,7},{9,10},{10,9},{11,... | collective-permute-start | bytes 811016 | tf_op jit(solution)/shard_map/object_halo/ppermute | solution.py:637
  11.9 6.3 %collective-permute-start.3 = (f32[2,264,128]{2,1,0:T(8,128)S(1)}, f32[2,264,128]{2,1,0:T(8,128)S(1)}, u32[]{:S(2)}, u32[]{:S(2)}) collective-permute-start(f32[2,264,128]{2,1,0:T(8,128)S(1)} %get-tuple-element.45), channel_id=1, source_target_pairs={{0,1},{1,0},{2,3},{3,2},{4,5},{5,4},{6,7},{7,6},{8,9},{9,8},{10,11... | collective-permute-start | bytes 811016 | tf_op jit(solution)/shard_map/object_halo/ppermute | solution.py:637
  12.0 1.2 %copy-start.4 = (f32[1,1,4,256,256]{4,3,2,1,0:T(8,128)S(1)}, f32[1,1,4,256,256]{4,3,2,1,0:T(8,128)}, u32[]{:S(2)}) copy-start(f32[1,1,4,256,256]{4,3,2,1,0:T(8,128)} %param.9) | copy-start | bytes 3145732
  13.2 1.0 copy-start.8
  14.2 1.0 copy-start.9
  15.2 14.0 %copy-start.1 = (f32[2,256,256]{2,1,0:T(8,128)S(1)}, f32[2,256,256]{2,1,0:T(8,128)}, u32[]{:S(2)}) copy-start(f32[2,256,256]{2,1,0:T(8,128)} %own.3) | copy-start | bytes 1572868
  15.2 14.0 %copy-start.3 = (s32[1,1,4,2]{2,3,1,0:T(2,128)S(1)}, s32[1,1,4,2]{2,3,1,0:T(2,128)}, u32[]{:S(2)}) copy-start(s32[1,1,4,2]{2,3,1,0:T(2,128)} %param.10) | copy-start | bytes 100
  15.2 14.0 %copy-start.5 = (f32[2,2,256,256]{3,2,1,0:T(8,128)S(1)}, f32[2,2,256,256]{3,2,1,0:T(8,128)}, u32[]{:S(2)}) copy-start(f32[2,2,256,256]{3,2,1,0:T(8,128)} %probe.3) | copy-start | bytes 3145732
  15.2 14.0 %copy-start.7 = (bf16[2,2,2,256,256]{4,3,2,1,0:T(8,128)(2,1)S(1)}, bf16[2,2,2,256,256]{4,3,2,1,0:T(8,128)(2,1)}, u32[]{:S(2)}) copy-start(bf16[2,2,2,256,256]{4,3,2,1,0:T(8,128)(2,1)} %constant.19.clone.matrices) | copy-start | bytes 3145732
  18.2 4.5 %collective-permute-start.5 = (f32[2,2,136,128]{3,2,1,0:T(8,128)S(1)}, f32[2,2,136,128]{3,2,1,0:T(8,128)S(1)}, u32[]{:S(2)}, u32[]{:S(2)}) collective-permute-start(f32[2,2,136,128]{3,2,1,0:T(8,128)S(1)} %get-tuple-element.88), channel_id=1, source_target_pairs={{0,1},{1,0},{2,3},{3,2},{4,5},{5,4},{6,7},{7,6},{8,9},{9,8},{10,11... | collective-permute-start | bytes 835592 | tf_op jit(solution)/shard_map/object_corners/ppermute | solution.py:637
  19.4 9.8 %collective-permute-start.4 = (f32[2,2,136,128]{3,2,1,0:T(8,128)S(1)}, f32[2,2,136,128]{3,2,1,0:T(8,128)S(1)}, u32[]{:S(2)}, u32[]{:S(2)}) collective-permute-start(f32[2,2,136,128]{3,2,1,0:T(8,128)S(1)} %get-tuple-element.89), channel_id=1, source_target_pairs={{1,2},{2,1},{3,4},{4,3},{5,6},{6,5},{7,8},{8,7},{9,10},{10,9},{11,... | collective-permute-start | bytes 835592 | tf_op jit(solution)/shard_map/object_corners/ppermute | solution.py:637
  43.5 3.6 %collective-permute-start.6 = (f32[64,24,128]{2,1,0:T(8,128)S(1)}, f32[64,24,128]{2,1,0:T(8,128)S(1)}, u32[]{:S(2)}, u32[]{:S(2)}) collective-permute-start(f32[64,24,128]{2,1,0:T(8,128)S(1)} %get-tuple-element.52), channel_id=1, source_target_pairs={{0,1},{1,0},{2,3},{3,2},{4,5},{5,4},{6,7},{7,6},{8,9},{9,8},{10,11... | collective-permute-start | bytes 2359304 | tf_op jit(solution)/shard_map/probe_reduce/ppermute | solution.py:637
  48.1 29.5 %all-to-all-start = ((f32[64,24,128]{2,1,0:T(8,128)}), f32[64,24,128]{2,1,0:T(8,128)S(1)}, u32[]{:S(2)}, u32[]{:S(2)}) async-start(f32[64,24,128]{2,1,0:T(8,128)} %add.9), calls=%async_computation | async-start | bytes 1572864 | tf_op jit(solution)/shard_map/probe_reduce/all_to_all | solution.py:670
  61.7 14.9 %collective-permute-start.7 = (f32[2,2,128,128]{3,2,1,0:T(8,128)S(1)}, f32[2,2,128,128]{3,2,1,0:T(8,128)S(1)}, u32[]{:S(2)}, u32[]{:S(2)}) collective-permute-start(f32[2,2,128,128]{3,2,1,0:T(8,128)S(1)} %get-tuple-element.68), channel_id=1, source_target_pairs={{1,2},{2,1},{3,4},{4,3},{5,6},{6,5},{7,8},{8,7},{9,10},{10,9},{11,... | collective-permute-start | bytes 786440 | tf_op jit(solution)/shard_map/gradient_corners/ppermute | solution.py:637
  65.8 10.9 %collective-permute-start.8 = (f32[2,2,128,128]{3,2,1,0:T(8,128)S(1)}, f32[2,2,128,128]{3,2,1,0:T(8,128)S(1)}, u32[]{:S(2)}, u32[]{:S(2)}) collective-permute-start(f32[2,2,128,128]{3,2,1,0:T(8,128)S(1)} %get-tuple-element.69), channel_id=1, source_target_pairs={{0,1},{1,0},{2,3},{3,2},{4,5},{5,4},{6,7},{7,6},{8,9},{9,8},{10,11... | collective-permute-start | bytes 786440 | tf_op jit(solution)/shard_map/gradient_corners/ppermute | solution.py:637
  65.9 1.2 %copy-start.6 = (f32[2,2,256,256]{3,2,1,0:T(8,128)S(1)}, f32[2,2,256,256]{3,2,1,0:T(8,128)}, u32[]{:S(2)}) copy-start(f32[2,2,256,256]{3,2,1,0:T(8,128)} %probe.3) | copy-start | bytes 3145732
  99.8 17.7 %collective-permute-start.13 = (f32[64,16,128]{2,1,0:T(8,128)S(1)}, f32[64,16,128]{2,1,0:T(8,128)S(1)}, u32[]{:S(2)}, u32[]{:S(2)}) collective-permute-start(f32[64,16,128]{2,1,0:T(8,128)S(1)} %all_to_all.10.mine), channel_id=1, source_target_pairs={{0,1},{1,0},{2,3},{3,2},{4,5},{5,4},{6,7},{7,6},{8,9},{9,8},{10,11... | collective-permute-start | bytes 1572872 | tf_op jit(solution)/shard_map/probe_gather/ppermute | solution.py:637
  101.5 8.2 %collective-permute-start.11 = (f32[2,256,128]{2,1,0:T(8,128)S(1)}, f32[2,256,128]{2,1,0:T(8,128)S(1)}, u32[]{:S(2)}, u32[]{:S(2)}) collective-permute-start(f32[2,256,128]{2,1,0:T(8,128)S(1)} %get-tuple-element.73), channel_id=1, source_target_pairs={{1,2},{2,1},{3,4},{4,3},{5,6},{6,5},{7,8},{8,7},{9,10},{10,9},{11,... | collective-permute-start | bytes 786440 | tf_op jit(solution)/shard_map/gradient_corners/ppermute | solution.py:637
  103.5 6.2 %collective-permute-start.12 = (f32[2,256,128]{2,1,0:T(8,128)S(1)}, f32[2,256,128]{2,1,0:T(8,128)S(1)}, u32[]{:S(2)}, u32[]{:S(2)}) collective-permute-start(f32[2,256,128]{2,1,0:T(8,128)S(1)} %get-tuple-element.74), channel_id=1, source_target_pairs={{0,1},{1,0},{2,3},{3,2},{4,5},{5,4},{6,7},{7,6},{8,9},{9,8},{10,11... | collective-permute-start | bytes 786440 | tf_op jit(solution)/shard_map/gradient_corners/ppermute | solution.py:637
  103.5 7.8 %collective-permute-start.9 = (f32[2,128,256]{2,1,0:T(8,128)}, f32[2,128,256]{2,1,0:T(8,128)S(1)}, u32[]{:S(2)}, u32[]{:S(2)}) collective-permute-start(f32[2,128,256]{2,1,0:T(8,128)} %get-tuple-element.71), channel_id=1, source_target_pairs={{0,16},{16,0},{32,48},{48,32},{64,80},{80,64},{96,112},{112,96},{1... | collective-permute-start | bytes 786440 | tf_op jit(solution)/shard_map/gradient_rows/ppermute | solution.py:633
  103.7 12.9 %collective-permute-start.10 = (f32[2,128,256]{2,1,0:T(8,128)}, f32[2,128,256]{2,1,0:T(8,128)S(1)}, u32[]{:S(2)}, u32[]{:S(2)}) collective-permute-start(f32[2,128,256]{2,1,0:T(8,128)} %get-tuple-element.72), channel_id=1, source_target_pairs={{16,32},{32,16},{48,64},{64,48},{80,96},{96,80},{17,33},{33,17},{4... | collective-permute-start | bytes 786440 | tf_op jit(solution)/shard_map/gradient_rows/ppermute | solution.py:633

commit v7 on v6

--- a/solution.py
+++ b/solution.py
@@ -302,11 +302,11 @@
     @pl.when(step == pl.num_programs(0) - 1)
     def _():
         core = place_of()[1]
-        scalar = jnp.where(lax.broadcasted_iota(jnp.int32, (1, 4, HALF), 2) == 0, jnp.sum(sums[0]), jnp.sum(sums[1]))
+        scalar = jnp.where(lax.broadcasted_iota(jnp.int32, (1, 8, HALF), 2) == 0, jnp.sum(sums[0]), jnp.sum(sums[1]))
         for out, block in ((keep, core), (send, 1 - core)):
             for c in range(5):
-                out[:, 4 * c : 4 * c + 4, :] = totals[block, c].reshape(64, 4, HALF)
-            out[:, 20:24, :] = jnp.broadcast_to(scalar, (64, 4, HALF))
+                out[:, 16 * c : 16 * c + 16, :] = totals[block, c].reshape(16, 16, HALF)
+            out[:, 80:88, :] = jnp.broadcast_to(scalar, (16, 8, HALF))
 
 
 def place_kernel(
@@ -438,13 +438,19 @@
     light[:, HALF:] = accum[3, 256:512]
 
 
-def quotient_kernel(chunk, spread_out, ratio):
-    total = jnp.sum(chunk[...], axis=0)
-    power = total[16:20]
+def sum_kernel(chunk, total):
+    total[...] = jnp.sum(chunk[...], axis=0)
+
+
+def quotient_kernel(own, first, second, third, spread_out, ratio, held):
+    z = 2 * lax.div(lax.axis_index("row"), 4) + lax.rem(lax.div(lax.axis_index("col"), 2), 2)
+    for distance, part in enumerate((own, first, second, third)):
+        held[lax.rem(z + 4 - distance, 4)] = part[...]
+    total = (held[0] + held[1]) + (held[2] + held[3])
     for c in range(4):
-        quotient = total[4 * c : 4 * c + 4] / power
-        spread_out[:, 4 * c : 4 * c + 4, :] = jnp.broadcast_to(quotient[None], (64, 4, HALF))
-    ratio[...] = jnp.broadcast_to(total[20:21, 0:1] / total[20:21, 1:2], (8, HALF))
+        quotient = total[16 * c : 16 * c + 16] / total[64:80]
+        spread_out[:, 16 * c : 16 * c + 16, :] = jnp.broadcast_to(quotient[None], (16, 16, HALF))
+    ratio[...] = jnp.broadcast_to(total[80:81, 0:1] / total[80:81, 1:2], (8, HALF))
 
 
 def update_kernel(center, even, odd, cross, same, light, out, total):
@@ -471,7 +477,7 @@
 
     def write(source, block):
         for c in range(4):
-            out[c, :, block * HALF : (block + 1) * HALF] = source[:, 4 * c : 4 * c + 4, :].reshape(SIZE, HALF)
+            out[c, :, block * HALF : (block + 1) * HALF] = source[:, 16 * c : 16 * c + 16, :].reshape(SIZE, HALF)
 
     @pl.when(core == 0)
     def _():
@@ -553,7 +559,7 @@
     mats = jnp.asarray(constants())
     arrays = [own, *halo, probe, mats]
     count = measured.shape[0]
-    halves = (64, 24, HALF)
+    halves = (16, 88, HALF)
     fields = (2, 2, SIZE, HALF)
     return pl.pallas_call(
         transform_kernel,
@@ -637,6 +643,24 @@
     return lax.ppermute(value, "col", pairs_from(first, lax.axis_size("col")))
 
 
+def along_z(value, distance):
+    pairs = []
+    for row in range(lax.axis_size("row")):
+        for col in range(lax.axis_size("col")):
+            z = (2 * (row // 4) + col // 2 % 2 + distance) % 4
+            target = (4 * (z // 2) + row % 4) * 16 + col // 4 * 4 + 2 * (z % 2) + col % 2
+            pairs.append((row * 16 + col, target))
+    return lax.ppermute(value, AXES, pairs)
+
+
+def planes():
+    groups = {}
+    for row in range(lax.axis_size("row")):
+        for col in range(lax.axis_size("col")):
+            groups.setdefault((row // 4, col % 4), []).append(row * 16 + col)
+    return list(groups.values())
+
+
 def half_lanes(value, first):
     return jnp.where(first, value[..., :HALF], value[..., HALF:])
 
@@ -645,8 +669,7 @@
     starts = offsets[0, 0].T
     measured = amplitudes[0, 0]
     core = lax.rem(lax.axis_index("col"), 2)
-    devices = lax.axis_size("row") * lax.axis_size("col")
-    groups = [[i for i in range(devices) if i % 2 == k] for k in range(2)]
+    groups = planes()
 
     with jax.named_scope("object_halo"):
         even, odd, cross, same = pack(starts, object_tile)
@@ -684,13 +707,19 @@
         chunk, light, odd, even = lax.optimization_barrier((chunk, light, odd, even))
         odd = swap_rows(odd, 1)
         even = swap_rows(even, 0)
-        object_update = update([center, even, odd, cross, same, light])
+
+    with jax.named_scope("probe_sum"):
+        total = simple(sum_kernel, [], [chunk], (88, HALF), [], 1 << 20, 1 << 20)
+        parts = [total] + [along_z(total, d) for d in (1, 2, 3)]
+        shapes = [(16, 64, HALF), (8, HALF)]
+        spread_out, ratio = simple(quotient_kernel, [], parts, shapes, [(4, 88, HALF)], 1 << 20, 2 << 20)
 
     with jax.named_scope("probe_gather"):
-        spread_out, ratio = simple(quotient_kernel, [], [chunk], [(64, 16, HALF), (8, HALF)], [], 1 << 20, 2 << 20)
         gathered = lax.all_to_all(spread_out, AXES, 0, 0, axis_index_groups=groups, tiled=True)
+        gathered, odd, even, cross, same = lax.optimization_barrier((gathered, odd, even, cross, same))
         probe_update = assemble(gathered, swap_columns(gathered, 0)).reshape(probe.shape)
 
+    object_update = update([center, even, odd, cross, same, light])
     relative_error = ratio[0, :1]
     position_step = steps[:, 0].reshape(1, 1, -1, 2)
     return (object_update, probe_update, position_step, relative_error)

time: 120 us -> 112 us (0.933)
  blocking collectives: 22.1 us -> 0 us
  waiting for transfers between devices: 21.7 us -> 28.3 us
  starting transfers between devices: 39.6 us -> 46.1 us
  Pallas kernels: 24.8 us -> 26.2 us
    all_to_all x1 -> x0, blocking collectives: 22.1 us -> none  [local(): lax.all_to_all(spread_out, AXES, 0, 0, axis_index_groups=groups, tiled=True)]
    all_to_all x1, waiting for transfers between devices: 0.01 us -> 7.03 us  [local(): lax.all_to_all(chunk, AXES, 0, 0, axis_index_groups=groups, tiled=True)]
    ppermute x10, waiting for transfers between devices: 14.9 us -> 8.4 us  [swap_columns(): return lax.ppermute(value, 'col', pairs_from(first, lax.axis_size('col')))]
    all_to_all x0 -> x1, starting transfers between devices: none -> 5.62 us  [local(): lax.all_to_all(spread_out, AXES, 0, 0, axis_index_groups=groups, tiled=True)]
    all_to_all x1, starting transfers between devices: 13.6 us -> 9.26 us  [local(): lax.all_to_all(chunk, AXES, 0, 0, axis_index_groups=groups, tiled=True)]
    ppermute x0 -> x3, waiting for transfers between devices: none -> 3.92 us  [along_z(): return lax.ppermute(value, AXES, pairs)]
    ppermute x0 -> x3, starting transfers between devices: none -> 3.13 us  [along_z(): return lax.ppermute(value, AXES, pairs)]
    ppermute x10, starting transfers between devices: 16 us -> 18.6 us  [swap_columns(): return lax.ppermute(value, 'col', pairs_from(first, lax.axis_size('col')))]
  transfers between devices with their start and end apart: 15 -> 19, of which waited for: 5 -> 8; matrix products, arithmetic and copies ran while one was open for 2% -> 1% of each run, Pallas kernels for 7% -> 8%
where the time goes in v7:
time: 112 us; the launch traced here: 110 us
  starting transfers between devices  46.1 us (41%)
  waiting for transfers between devices  28.3 us (25%)
  Pallas kernels  26.2 us (23%)
  local copies, waits for them, and re-layouts  7.52 us (7%)
    ppermute x10, starting transfers between devices, swap_columns(): return lax.ppermute(value, 'col', pairs_from(first, lax.axis_size('col')))  18.6 us
    pallas_call x1, Pallas kernels, transforms(): pl.pallas_call(transform_kernel, out_shape=shaped([halves, halves, (count...  14.3 us
    ppermute x4, starting transfers between devices, swap_rows(): return lax.ppermute(value, 'row', pairs_from(first, lax.axis_size('row')))  9.41 us
    all_to_all x1, starting transfers between devices, local(): lax.all_to_all(chunk, AXES, 0, 0, axis_index_groups=groups, tiled=True)  9.26 us
    ppermute x4, waiting for transfers between devices, swap_rows(): return lax.ppermute(value, 'row', pairs_from(first, lax.axis_size('row')))  8.92 us
    ppermute x10, waiting for transfers between devices, swap_columns(): return lax.ppermute(value, 'col', pairs_from(first, lax.axis_size('col')))  8.4 us
    all_to_all x1, waiting for transfers between devices, local(): lax.all_to_all(chunk, AXES, 0, 0, axis_index_groups=groups, tiled=True)  7.03 us
    pallas_call x6, Pallas kernels, simple(): return call(*scalars, *arrays)  6.98 us
  transfers between devices with their start and end apart: 19, of which 8 were waited for; matrix products, arithmetic and copies ran while one was open for 1% of the time, Pallas kernels for 8%

profile of v7, /device:TPU:25, one launch (start us, length us, event | category | flops | bytes accessed | tf_op | source)
XLA Modules:
  0.0 110.0 jit_solution(14090994050871671503)
XLA Ops:
  0.6 0.0 copy-start
  0.6 1.0 copy-done
  1.7 0.7 copy-done.2
  2.4 0.8 object_halo.1
  3.1 5.2 %collective-permute-start = (f32[2,136,256]{2,1,0:T(8,128)S(1)}, f32[2,136,256]{2,1,0:T(8,128)S(1)}, u32[]{:S(2)}, u32[]{:S(2)}) collective-permute-start(f32[2,136,256]{2,1,0:T(8,128)S(1)} %get-tuple-element.47), channel_id=1, source_target_pairs={{16,32},{32,16},{48,64},{64,48},{80,96},{96,80},{17,33},{33,17},{4... | collective-permute-start | bytes 835592 | tf_op jit(solution)/shard_map/object_halo/ppermute | solution.py:639
  8.3 0.1 collective-permute-start.1
  8.4 3.5 %collective-permute-start.2 = (f32[2,264,128]{2,1,0:T(8,128)S(1)}, f32[2,264,128]{2,1,0:T(8,128)S(1)}, u32[]{:S(2)}, u32[]{:S(2)}) collective-permute-start(f32[2,264,128]{2,1,0:T(8,128)S(1)} %get-tuple-element.49), channel_id=1, source_target_pairs={{1,2},{2,1},{3,4},{4,3},{5,6},{6,5},{7,8},{8,7},{9,10},{10,9},{11,... | collective-permute-start | bytes 811016 | tf_op jit(solution)/shard_map/object_halo/ppermute | solution.py:643
  11.9 0.1 collective-permute-start.3
  12.0 0.0 copy-start.4
  12.0 1.2 %copy-done.4 = f32[1,1,4,256,256]{4,3,2,1,0:T(8,128)S(1)} copy-done((f32[1,1,4,256,256]{4,3,2,1,0:T(8,128)S(1)}, f32[1,1,4,256,256]{4,3,2,1,0:T(8,128)}, u32[]{:S(2)}) %copy-start.4) | copy-done | bytes 1048600
  13.2 1.0 copy-done.8
  14.2 1.0 copy-done.9
  15.2 1.3 %shard_map.102.measured = f32[4,256,256]{2,1,0:T(8,128)S(1)} custom-call(f32[4,256,256]{2,1,0:T(8,128)S(1)} %bitcast.22, bf16[768,256]{1,0:T(8,128)(2,1)S(1)} %copy-done.9, bf16[256,768]{1,0:T(8,128)(2,1)S(1)} %copy-done.8), custom_call_target="tpu_custom_call" | custom-call | flops 1073741824 | bytes 3145728 | tf_op jit(solution)/shard_map/pallas_call | solution.py:532
  16.5 1.7 %collective-permute-done.2.cross = f32[2,264,128]{2,1,0:T(8,128)S(1)} collective-permute-done((f32[2,264,128]{2,1,0:T(8,128)S(1)}, f32[2,264,128]{2,1,0:T(8,128)S(1)}, u32[]{:S(2)}, u32[]{:S(2)}) %collective-permute-start.2) | collective-permute-done | bytes 270368 | tf_op jit(solution)/shard_map/object_halo/ppermute | solution.py:643
  18.2 0.0 collective-permute-done.3.same
  18.2 0.0 collective-permute-done.odd_strip
  18.2 0.0 collective-permute-done.1.even_strip
  18.2 1.2 %collective-permute-start.5 = (f32[2,2,136,128]{3,2,1,0:T(8,128)S(1)}, f32[2,2,136,128]{3,2,1,0:T(8,128)S(1)}, u32[]{:S(2)}, u32[]{:S(2)}) collective-permute-start(f32[2,2,136,128]{3,2,1,0:T(8,128)S(1)} %get-tuple-element.98), channel_id=1, source_target_pairs={{0,1},{1,0},{2,3},{3,2},{4,5},{5,4},{6,7},{7,6},{8,9},{9,8},{10,11... | collective-permute-start | bytes 835592 | tf_op jit(solution)/shard_map/object_corners/ppermute | solution.py:643
  19.4 3.3 %collective-permute-start.4 = (f32[2,2,136,128]{3,2,1,0:T(8,128)S(1)}, f32[2,2,136,128]{3,2,1,0:T(8,128)S(1)}, u32[]{:S(2)}, u32[]{:S(2)}) collective-permute-start(f32[2,2,136,128]{3,2,1,0:T(8,128)S(1)} %get-tuple-element.99), channel_id=1, source_target_pairs={{1,2},{2,1},{3,4},{4,3},{5,6},{6,5},{7,8},{8,7},{9,10},{10,9},{11,... | collective-permute-start | bytes 835592 | tf_op jit(solution)/shard_map/object_corners/ppermute | solution.py:643
  22.7 0.0 collective-permute-done.5.same_corner
  22.7 6.4 %collective-permute-done.4.cross_corner = f32[2,2,136,128]{3,2,1,0:T(8,128)S(1)} collective-permute-done((f32[2,2,136,128]{3,2,1,0:T(8,128)S(1)}, f32[2,2,136,128]{3,2,1,0:T(8,128)S(1)}, u32[]{:S(2)}, u32[]{:S(2)}) %collective-permute-start.4) | collective-permute-done | bytes 278560 | tf_op jit(solution)/shard_map/object_corners/ppermute | solution.py:643
  29.2 0.0 copy-done.1
  29.2 0.0 copy-done.3
  29.2 0.0 copy-done.5
  29.2 0.0 copy-done.7
  29.2 14.3 %shard_map.103 = (f32[16,88,128]{2,1,0:T(8,128)S(1)}, f32[16,88,128]{2,1,0:T(8,128)S(1)}, f32[4,2,2,256,128]{4,3,2,1,0:T(8,128)S(1)}, f32[4,2,2,256,128]{4,3,2,1,0:T(8,128)S(1)}, s32[8,128]{1,0:T(8,128)S(1)}) custom-call(s32[2,4]{1,0:T(2,128)S(1)} %bitcast.19, f32[2,256,256]{2,1,0:T(8,128)S(1)} %copy-done.1, ...), custom_call_target="tpu_custom_call" | custom-call | flops 13958643712 | bytes 12582912 | tf_op jit(solution)/shard_map/pallas_call | solution.py:564
  43.4 0.1 collective-permute-start.6
  43.5 4.2 %shard_map.104 = (f32[2,256,256]{2,1,0:T(8,128)S(1)}, f32[2,128,256]{2,1,0:T(8,128)S(1)}, f32[2,128,256]{2,1,0:T(8,128)S(1)}, f32[2,256,128]{2,1,0:T(8,128)}, f3...) custom-call(s32[2,4]{1,0:T(2,128)S(1)} %bitcast.20, ...), custom_call_target="tpu_custom_call" | custom-call | flops 5368709120 | bytes 8388608 | tf_op jit(solution)/shard_map/pallas_call | solution.py:598
  47.8 0.0 collective-permute-done.6
  47.8 0.9 add.9
  48.7 4.4 %collective-permute-start.7 = (f32[2,2,128,128]{3,2,1,0:T(8,128)}, f32[2,2,128,128]{3,2,1,0:T(8,128)S(1)}, u32[]{:S(2)}, u32[]{:S(2)}) collective-permute-start(f32[2,2,128,128]{3,2,1,0:T(8,128)} %get-tuple-element.73), channel_id=1, source_target_pairs={{1,2},{2,1},{3,4},{4,3},{5,6},{6,5},{7,8},{8,7},{9,10},{10,9},{11,... | collective-permute-start | bytes 786440 | tf_op jit(solution)/shard_map/gradient_corners/ppermute | solution.py:643
  53.1 0.1 collective-permute-start.8
  53.2 9.3 %all-to-all-start = ((f32[16,88,128]{2,1,0:T(8,128)}), f32[16,88,128]{2,1,0:T(8,128)S(1)}, u32[]{:S(2)}, u32[]{:S(2)}) async-start(f32[16,88,128]{2,1,0:T(8,128)} %add.9), calls=%async_computation | async-start | bytes 1441792 | tf_op jit(solution)/shard_map/probe_reduce/all_to_all | solution.py:693
  62.5 1.2 %copy-done.6 = f32[2,2,256,256]{3,2,1,0:T(8,128)S(1)} copy-done((f32[2,2,256,256]{3,2,1,0:T(8,128)S(1)}, f32[2,2,256,256]{3,2,1,0:T(8,128)}, u32[]{:S(2)}) %copy-start.6) | copy-done | bytes 1048600
  63.7 2.8 %gradient_rows.1.light = f32[256,256]{1,0:T(8,128)S(1)} custom-call(s32[2,4]{1,0:T(2,128)S(1)} %bitcast.21, s32[8,128]{1,0:T(8,128)S(1)} %get-tuple-element.71.around, f32[2,2,256,256]{3,2,1,0:T(8,128)S(1)} %copy-done.6), custom_call_target="tpu_custom_call" | custom-call | flops 2147483648 | bytes 4194304 | tf_op jit(solution)/shard_map/gradient_rows/pallas_call | solution.py:532
  66.5 0.0 collective-permute-done.7
  66.5 0.0 collective-permute-done.8
  66.5 0.1 fusion.5
  66.6 7.0 %all-to-all-done.chunk = f32[16,88,128]{2,1,0:T(8,128)S(1)} async-done(((f32[16,88,128]{2,1,0:T(8,128)}), f32[16,88,128]{2,1,0:T(8,128)S(1)}, u32[]{:S(2)}, u32[]{:S(2)}) %all-to-all-start) | async-done | bytes 720928 | tf_op jit(solution)/shard_map/probe_reduce/all_to_all | solution.py:693
  73.7 2.5 %collective-permute-start.11 = (f32[88,128]{1,0:T(8,128)S(1)}, f32[88,128]{1,0:T(8,128)S(1)}, u32[]{:S(2)}, u32[]{:S(2)}) collective-permute-start(f32[88,128]{1,0:T(8,128)S(1)} %probe_sum.2.own), channel_id=1, source_target_pairs={{0,66},{1,67},{2,0},{3,1},{4,70},{5,71},{6,4},{7,5},{8,74},{9,75},... | collective-permute-start | bytes 135176 | tf_op jit(solution)/shard_map/probe_sum/ppermute | solution.py:653
  76.1 0.0 collective-permute-start.10
  76.1 0.7 collective-permute-start.9
  76.8 0.5 collective-permute-done.11.third
  77.3 3.4 %collective-permute-done.10.second = f32[88,128]{1,0:T(8,128)S(1)} collective-permute-done((f32[88,128]{1,0:T(8,128)S(1)}, f32[88,128]{1,0:T(8,128)S(1)}, u32[]{:S(2)}, u32[]{:S(2)}) %collective-permute-start.10) | collective-permute-done | bytes 45088 | tf_op jit(solution)/shard_map/probe_sum/ppermute | solution.py:653
  80.6 0.1 collective-permute-done.9.first
  80.7 0.9 probe_sum.3
  81.6 5.6 %all-to-all-start.1 = ((f32[16,64,128]{2,1,0:T(8,128)}), f32[16,64,128]{2,1,0:T(8,128)S(1)}, u32[]{:S(2)}, u32[]{:S(2)}) async-start(f32[16,64,128]{2,1,0:T(8,128)} %get-tuple-element.77), calls=%async_computation.1 | async-start | bytes 1048576 | tf_op jit(solution)/shard_map/probe_gather/all_to_all | solution.py:718
  87.2 4.5 %collective-permute-start.14 = (f32[2,256,128]{2,1,0:T(8,128)}, f32[2,256,128]{2,1,0:T(8,128)S(1)}, u32[]{:S(2)}, u32[]{:S(2)}) collective-permute-start(f32[2,256,128]{2,1,0:T(8,128)} %get-tuple-element.80), channel_id=1, source_target_pairs={{1,2},{2,1},{3,4},{4,3},{5,6},{6,5},{7,8},{8,7},{9,10},{10,9},{11,... | collective-permute-start | bytes 786440 | tf_op jit(solution)/shard_map/gradient_corners/ppermute | solution.py:643
  91.8 0.1 collective-permute-start.15
  91.8 4.1 %collective-permute-start.12 = (f32[2,128,256]{2,1,0:T(8,128)S(1)}, f32[2,128,256]{2,1,0:T(8,128)S(1)}, u32[]{:S(2)}, u32[]{:S(2)}) collective-permute-start(f32[2,128,256]{2,1,0:T(8,128)S(1)} %get-tuple-element.78), channel_id=1, source_target_pairs={{16,32},{32,16},{48,64},{64,48},{80,96},{96,80},{17,33},{33,17},{4... | collective-permute-start | bytes 786440 | tf_op jit(solution)/shard_map/gradient_rows/ppermute | solution.py:639
  95.9 0.1 collective-permute-start.13
  96.0 0.3 collective-permute-done.14.cross
  96.3 0.0 collective-permute-done.15.same
  96.3 8.9 %collective-permute-done.12.odd = f32[2,128,256]{2,1,0:T(8,128)S(1)} collective-permute-done((f32[2,128,256]{2,1,0:T(8,128)S(1)}, f32[2,128,256]{2,1,0:T(8,128)S(1)}, u32[]{:S(2)}, u32[]{:S(2)}) %collective-permute-start.12) | collective-permute-done | bytes 262176 | tf_op jit(solution)/shard_map/gradient_rows/ppermute | solution.py:639
  105.2 0.0 collective-permute-done.13.even
  105.2 0.0 all-to-all-done.1.mine
  105.2 1.4 %collective-permute-start.16 = (f32[16,64,128]{2,1,0:T(8,128)S(1)}, f32[16,64,128]{2,1,0:T(8,128)S(1)}, u32[]{:S(2)}, u32[]{:S(2)}) collective-permute-start(f32[16,64,128]{2,1,0:T(8,128)S(1)} %all-to-all-done.1.mine), channel_id=1, source_target_pairs={{0,1},{1,0},{2,3},{3,2},{4,5},{5,4},{6,7},{7,6},{8,9},{9,8},{10,11... | collective-permute-start | bytes 1572872 | tf_op jit(solution)/shard_map/probe_gather/ppermute | solution.py:643
  106.6 0.1 slice_reduce_fusion
  106.7 0.1 reshape_squeeze.3
  106.8 0.7 copy.12
  107.5 0.5 slice.25
  108.0 1.0 shard_map.105
  109.0 0.0 collective-permute-done.16.other
  109.0 1.1 probe_gather.1
  (11 shorter events, 0.1 us)
Async XLA Ops:
  0.6 1.0 copy-start
  1.7 0.7 copy-start.2
  3.1 15.0 %collective-permute-start = (f32[2,136,256]{2,1,0:T(8,128)S(1)}, f32[2,136,256]{2,1,0:T(8,128)S(1)}, u32[]{:S(2)}, u32[]{:S(2)}) collective-permute-start(f32[2,136,256]{2,1,0:T(8,128)S(1)} %get-tuple-element.47), channel_id=1, source_target_pairs={{16,32},{32,16},{48,64},{64,48},{80,96},{96,80},{17,33},{33,17},{4... | collective-permute-start | bytes 835592 | tf_op jit(solution)/shard_map/object_halo/ppermute | solution.py:639
  8.3 9.9 %collective-permute-start.1 = (f32[2,136,256]{2,1,0:T(8,128)S(1)}, f32[2,136,256]{2,1,0:T(8,128)S(1)}, u32[]{:S(2)}, u32[]{:S(2)}) collective-permute-start(f32[2,136,256]{2,1,0:T(8,128)S(1)} %get-tuple-element.48), channel_id=1, source_target_pairs={{0,16},{16,0},{32,48},{48,32},{64,80},{80,64},{96,112},{112,96},{1... | collective-permute-start | bytes 835592 | tf_op jit(solution)/shard_map/object_halo/ppermute | solution.py:639
  8.4 9.8 %collective-permute-start.2 = (f32[2,264,128]{2,1,0:T(8,128)S(1)}, f32[2,264,128]{2,1,0:T(8,128)S(1)}, u32[]{:S(2)}, u32[]{:S(2)}) collective-permute-start(f32[2,264,128]{2,1,0:T(8,128)S(1)} %get-tuple-element.49), channel_id=1, source_target_pairs={{1,2},{2,1},{3,4},{4,3},{5,6},{6,5},{7,8},{8,7},{9,10},{10,9},{11,... | collective-permute-start | bytes 811016 | tf_op jit(solution)/shard_map/object_halo/ppermute | solution.py:643
  11.9 6.3 %collective-permute-start.3 = (f32[2,264,128]{2,1,0:T(8,128)S(1)}, f32[2,264,128]{2,1,0:T(8,128)S(1)}, u32[]{:S(2)}, u32[]{:S(2)}) collective-permute-start(f32[2,264,128]{2,1,0:T(8,128)S(1)} %get-tuple-element.50), channel_id=1, source_target_pairs={{0,1},{1,0},{2,3},{3,2},{4,5},{5,4},{6,7},{7,6},{8,9},{9,8},{10,11... | collective-permute-start | bytes 811016 | tf_op jit(solution)/shard_map/object_halo/ppermute | solution.py:643
  12.0 1.2 %copy-start.4 = (f32[1,1,4,256,256]{4,3,2,1,0:T(8,128)S(1)}, f32[1,1,4,256,256]{4,3,2,1,0:T(8,128)}, u32[]{:S(2)}) copy-start(f32[1,1,4,256,256]{4,3,2,1,0:T(8,128)} %param.9) | copy-start | bytes 3145732
  13.2 1.0 copy-start.8
  14.2 1.0 copy-start.9
  15.2 14.0 %copy-start.1 = (f32[2,256,256]{2,1,0:T(8,128)S(1)}, f32[2,256,256]{2,1,0:T(8,128)}, u32[]{:S(2)}) copy-start(f32[2,256,256]{2,1,0:T(8,128)} %own.3) | copy-start | bytes 1572868
  15.2 14.0 %copy-start.3 = (s32[1,1,4,2]{2,3,1,0:T(2,128)S(1)}, s32[1,1,4,2]{2,3,1,0:T(2,128)}, u32[]{:S(2)}) copy-start(s32[1,1,4,2]{2,3,1,0:T(2,128)} %param.10) | copy-start | bytes 100
  15.2 14.0 %copy-start.5 = (f32[2,2,256,256]{3,2,1,0:T(8,128)S(1)}, f32[2,2,256,256]{3,2,1,0:T(8,128)}, u32[]{:S(2)}) copy-start(f32[2,2,256,256]{3,2,1,0:T(8,128)} %probe.3) | copy-start | bytes 3145732
  15.2 14.0 %copy-start.7 = (bf16[2,2,2,256,256]{4,3,2,1,0:T(8,128)(2,1)S(1)}, bf16[2,2,2,256,256]{4,3,2,1,0:T(8,128)(2,1)}, u32[]{:S(2)}) copy-start(bf16[2,2,2,256,256]{4,3,2,1,0:T(8,128)(2,1)} %constant.19.clone.matrices) | copy-start | bytes 3145732
  18.2 4.5 %collective-permute-start.5 = (f32[2,2,136,128]{3,2,1,0:T(8,128)S(1)}, f32[2,2,136,128]{3,2,1,0:T(8,128)S(1)}, u32[]{:S(2)}, u32[]{:S(2)}) collective-permute-start(f32[2,2,136,128]{3,2,1,0:T(8,128)S(1)} %get-tuple-element.98), channel_id=1, source_target_pairs={{0,1},{1,0},{2,3},{3,2},{4,5},{5,4},{6,7},{7,6},{8,9},{9,8},{10,11... | collective-permute-start | bytes 835592 | tf_op jit(solution)/shard_map/object_corners/ppermute | solution.py:643
  19.4 9.8 %collective-permute-start.4 = (f32[2,2,136,128]{3,2,1,0:T(8,128)S(1)}, f32[2,2,136,128]{3,2,1,0:T(8,128)S(1)}, u32[]{:S(2)}, u32[]{:S(2)}) collective-permute-start(f32[2,2,136,128]{3,2,1,0:T(8,128)S(1)} %get-tuple-element.99), channel_id=1, source_target_pairs={{1,2},{2,1},{3,4},{4,3},{5,6},{6,5},{7,8},{8,7},{9,10},{10,9},{11,... | collective-permute-start | bytes 835592 | tf_op jit(solution)/shard_map/object_corners/ppermute | solution.py:643
  43.4 4.3 %collective-permute-start.6 = (f32[16,88,128]{2,1,0:T(8,128)S(1)}, f32[16,88,128]{2,1,0:T(8,128)S(1)}, u32[]{:S(2)}, u32[]{:S(2)}) collective-permute-start(f32[16,88,128]{2,1,0:T(8,128)S(1)} %get-tuple-element.57), channel_id=1, source_target_pairs={{0,1},{1,0},{2,3},{3,2},{4,5},{5,4},{6,7},{7,6},{8,9},{9,8},{10,11... | collective-permute-start | bytes 2162696 | tf_op jit(solution)/shard_map/probe_reduce/ppermute | solution.py:643
  48.7 17.8 %collective-permute-start.7 = (f32[2,2,128,128]{3,2,1,0:T(8,128)}, f32[2,2,128,128]{3,2,1,0:T(8,128)S(1)}, u32[]{:S(2)}, u32[]{:S(2)}) collective-permute-start(f32[2,2,128,128]{3,2,1,0:T(8,128)} %get-tuple-element.73), channel_id=1, source_target_pairs={{1,2},{2,1},{3,4},{4,3},{5,6},{6,5},{7,8},{8,7},{9,10},{10,9},{11,... | collective-permute-start | bytes 786440 | tf_op jit(solution)/shard_map/gradient_corners/ppermute | solution.py:643
  53.1 13.3 %collective-permute-start.8 = (f32[2,2,128,128]{3,2,1,0:T(8,128)S(1)}, f32[2,2,128,128]{3,2,1,0:T(8,128)S(1)}, u32[]{:S(2)}, u32[]{:S(2)}) collective-permute-start(f32[2,2,128,128]{3,2,1,0:T(8,128)S(1)} %get-tuple-element.74), channel_id=1, source_target_pairs={{0,1},{1,0},{2,3},{3,2},{4,5},{5,4},{6,7},{7,6},{8,9},{9,8},{10,11... | collective-permute-start | bytes 786440 | tf_op jit(solution)/shard_map/gradient_corners/ppermute | solution.py:643
  53.2 20.4 %all-to-all-start = ((f32[16,88,128]{2,1,0:T(8,128)}), f32[16,88,128]{2,1,0:T(8,128)S(1)}, u32[]{:S(2)}, u32[]{:S(2)}) async-start(f32[16,88,128]{2,1,0:T(8,128)} %add.9), calls=%async_computation | async-start | bytes 1441792 | tf_op jit(solution)/shard_map/probe_reduce/all_to_all | solution.py:693
  62.5 1.2 %copy-start.6 = (f32[2,2,256,256]{3,2,1,0:T(8,128)S(1)}, f32[2,2,256,256]{3,2,1,0:T(8,128)}, u32[]{:S(2)}) copy-start(f32[2,2,256,256]{3,2,1,0:T(8,128)} %probe.3) | copy-start | bytes 3145732
  73.7 3.6 %collective-permute-start.11 = (f32[88,128]{1,0:T(8,128)S(1)}, f32[88,128]{1,0:T(8,128)S(1)}, u32[]{:S(2)}, u32[]{:S(2)}) collective-permute-start(f32[88,128]{1,0:T(8,128)S(1)} %probe_sum.2.own), channel_id=1, source_target_pairs={{0,66},{1,67},{2,0},{3,1},{4,70},{5,71},{6,4},{7,5},{8,74},{9,75},... | collective-permute-start | bytes 135176 | tf_op jit(solution)/shard_map/probe_sum/ppermute | solution.py:653
  76.1 4.5 %collective-permute-start.10 = (f32[88,128]{1,0:T(8,128)S(1)}, f32[88,128]{1,0:T(8,128)S(1)}, u32[]{:S(2)}, u32[]{:S(2)}) collective-permute-start(f32[88,128]{1,0:T(8,128)S(1)} %probe_sum.2.own), channel_id=1, source_target_pairs={{0,64},{1,65},{2,66},{3,67},{4,68},{5,69},{6,70},{7,71},{8,72},{9,... | collective-permute-start | bytes 135176 | tf_op jit(solution)/shard_map/probe_sum/ppermute | solution.py:653
  76.1 4.6 %collective-permute-start.9 = (f32[88,128]{1,0:T(8,128)S(1)}, f32[88,128]{1,0:T(8,128)S(1)}, u32[]{:S(2)}, u32[]{:S(2)}) collective-permute-start(f32[88,128]{1,0:T(8,128)S(1)} %probe_sum.2.own), channel_id=1, source_target_pairs={{0,2},{1,3},{2,64},{3,65},{4,6},{5,7},{6,68},{7,69},{8,10},{9,11},... | collective-permute-start | bytes 135176 | tf_op jit(solution)/shard_map/probe_sum/ppermute | solution.py:653
  81.6 23.6 %all-to-all-start.1 = ((f32[16,64,128]{2,1,0:T(8,128)}), f32[16,64,128]{2,1,0:T(8,128)S(1)}, u32[]{:S(2)}, u32[]{:S(2)}) async-start(f32[16,64,128]{2,1,0:T(8,128)} %get-tuple-element.77), calls=%async_computation.1 | async-start | bytes 1048576 | tf_op jit(solution)/shard_map/probe_gather/all_to_all | solution.py:718
  87.2 9.1 %collective-permute-start.14 = (f32[2,256,128]{2,1,0:T(8,128)}, f32[2,256,128]{2,1,0:T(8,128)S(1)}, u32[]{:S(2)}, u32[]{:S(2)}) collective-permute-start(f32[2,256,128]{2,1,0:T(8,128)} %get-tuple-element.80), channel_id=1, source_target_pairs={{1,2},{2,1},{3,4},{4,3},{5,6},{6,5},{7,8},{8,7},{9,10},{10,9},{11,... | collective-permute-start | bytes 786440 | tf_op jit(solution)/shard_map/gradient_corners/ppermute | solution.py:643
  91.8 4.5 %collective-permute-start.15 = (f32[2,256,128]{2,1,0:T(8,128)S(1)}, f32[2,256,128]{2,1,0:T(8,128)S(1)}, u32[]{:S(2)}, u32[]{:S(2)}) collective-permute-start(f32[2,256,128]{2,1,0:T(8,128)S(1)} %get-tuple-element.81), channel_id=1, source_target_pairs={{0,1},{1,0},{2,3},{3,2},{4,5},{5,4},{6,7},{7,6},{8,9},{9,8},{10,11... | collective-permute-start | bytes 786440 | tf_op jit(solution)/shard_map/gradient_corners/ppermute | solution.py:643
  91.8 13.4 %collective-permute-start.12 = (f32[2,128,256]{2,1,0:T(8,128)S(1)}, f32[2,128,256]{2,1,0:T(8,128)S(1)}, u32[]{:S(2)}, u32[]{:S(2)}) collective-permute-start(f32[2,128,256]{2,1,0:T(8,128)S(1)} %get-tuple-element.78), channel_id=1, source_target_pairs={{16,32},{32,16},{48,64},{64,48},{80,96},{96,80},{17,33},{33,17},{4... | collective-permute-start | bytes 786440 | tf_op jit(solution)/shard_map/gradient_rows/ppermute | solution.py:639
  95.9 9.3 %collective-permute-start.13 = (f32[2,128,256]{2,1,0:T(8,128)S(1)}, f32[2,128,256]{2,1,0:T(8,128)S(1)}, u32[]{:S(2)}, u32[]{:S(2)}) collective-permute-start(f32[2,128,256]{2,1,0:T(8,128)S(1)} %get-tuple-element.79), channel_id=1, source_target_pairs={{0,16},{16,0},{32,48},{48,32},{64,80},{80,64},{96,112},{112,96},{1... | collective-permute-start | bytes 786440 | tf_op jit(solution)/shard_map/gradient_rows/ppermute | solution.py:639
  105.2 3.7 %collective-permute-start.16 = (f32[16,64,128]{2,1,0:T(8,128)S(1)}, f32[16,64,128]{2,1,0:T(8,128)S(1)}, u32[]{:S(2)}, u32[]{:S(2)}) collective-permute-start(f32[16,64,128]{2,1,0:T(8,128)S(1)} %all-to-all-done.1.mine), channel_id=1, source_target_pairs={{0,1},{1,0},{2,3},{3,2},{4,5},{5,4},{6,7},{7,6},{8,9},{9,8},{10,11... | collective-permute-start | bytes 1572872 | tf_op jit(solution)/shard_map/probe_gather/ppermute | solution.py:643

commit v8 on v7

--- a/solution.py
+++ b/solution.py
@@ -704,22 +704,23 @@
         added = jnp.concatenate([first, second], -1)
         odd, even = odd + added[1], even + added[0]
         light = illuminate(starts, around, probe)
-        chunk, light, odd, even = lax.optimization_barrier((chunk, light, odd, even))
+        tied = (chunk, light, odd, even, cross, same)
+        chunk, light, odd, even, cross, same = lax.optimization_barrier(tied)
         odd = swap_rows(odd, 1)
         even = swap_rows(even, 0)
+        object_update = update([center, even, odd, cross, same, light])
 
     with jax.named_scope("probe_sum"):
         total = simple(sum_kernel, [], [chunk], (88, HALF), [], 1 << 20, 1 << 20)
         parts = [total] + [along_z(total, d) for d in (1, 2, 3)]
         shapes = [(16, 64, HALF), (8, HALF)]
         spread_out, ratio = simple(quotient_kernel, [], parts, shapes, [(4, 88, HALF)], 1 << 20, 2 << 20)
+        spread_out, object_update = lax.optimization_barrier((spread_out, object_update))
 
     with jax.named_scope("probe_gather"):
         gathered = lax.all_to_all(spread_out, AXES, 0, 0, axis_index_groups=groups, tiled=True)
-        gathered, odd, even, cross, same = lax.optimization_barrier((gathered, odd, even, cross, same))
         probe_update = assemble(gathered, swap_columns(gathered, 0)).reshape(probe.shape)
 
-    object_update = update([center, even, odd, cross, same, light])
     relative_error = ratio[0, :1]
     position_step = steps[:, 0].reshape(1, 1, -1, 2)
     return (object_update, probe_update, position_step, relative_error)

time: 112 us -> 113 us (level)
  the two profiles are of different devices: /device:TPU:25 before, /device:TPU:1 now
where the time goes in v8:
time: 113 us; the launch traced here: 112 us
  starting transfers between devices  38 us (34%)
  Pallas kernels  24.7 us (22%)
  waiting for transfers between devices  24 us (21%)
  blocking collectives  14.6 us (13%)
  local copies, waits for them, and re-layouts  7.52 us (7%)
  other arithmetic  2.82 us (2%)
    ppermute x10, starting transfers between devices, swap_columns(): return lax.ppermute(value, 'col', pairs_from(first, lax.axis_size('col')))  19.1 us
    all_to_all x1, blocking collectives, local(): lax.all_to_all(spread_out, AXES, 0, 0, axis_index_groups=groups, tiled=True)  14.6 us
    pallas_call x1, Pallas kernels, transforms(): pl.pallas_call(transform_kernel, out_shape=shaped([halves, halves, (count...  14.3 us
    ppermute x10, waiting for transfers between devices, swap_columns(): return lax.ppermute(value, 'col', pairs_from(first, lax.axis_size('col')))  12.6 us
    ppermute x3, starting transfers between devices, along_z(): return lax.ppermute(value, AXES, pairs)  8.18 us
    unnamed x21, local copies, waits for them, and re-layouts  6.81 us
    ppermute x3, waiting for transfers between devices, along_z(): return lax.ppermute(value, AXES, pairs)  6.66 us
    ppermute x4, starting transfers between devices, swap_rows(): return lax.ppermute(value, 'row', pairs_from(first, lax.axis_size('row')))  6.08 us
  transfers between devices with their start and end apart: 18, of which 5 were waited for; matrix products, arithmetic and copies ran while one was open for 3% of the time, Pallas kernels for 7%

profile of v8, /device:TPU:1, one launch (start us, length us, event | category | flops | bytes accessed | tf_op | source)
XLA Modules:
  0.0 112.4 jit_solution(11906947496500664115)
XLA Ops:
  0.6 0.0 copy-start
  0.6 1.0 copy-done
  1.7 0.7 copy-done.2
  2.4 0.8 object_halo.1
  3.1 0.7 collective-permute-start
  3.8 4.7 %collective-permute-start.1 = (f32[2,136,256]{2,1,0:T(8,128)S(1)}, f32[2,136,256]{2,1,0:T(8,128)S(1)}, u32[]{:S(2)}, u32[]{:S(2)}) collective-permute-start(f32[2,136,256]{2,1,0:T(8,128)S(1)} %get-tuple-element.47), channel_id=1, source_target_pairs={{0,16},{16,0},{32,48},{48,32},{64,80},{80,64},{96,112},{112,96},{1... | collective-permute-start | bytes 835592 | tf_op jit(solution)/shard_map/object_halo/ppermute | solution.py:639
  8.5 4.7 %collective-permute-start.2 = (f32[2,264,128]{2,1,0:T(8,128)S(1)}, f32[2,264,128]{2,1,0:T(8,128)S(1)}, u32[]{:S(2)}, u32[]{:S(2)}) collective-permute-start(f32[2,264,128]{2,1,0:T(8,128)S(1)} %get-tuple-element.48), channel_id=1, source_target_pairs={{1,2},{2,1},{3,4},{4,3},{5,6},{6,5},{7,8},{8,7},{9,10},{10,9},{11,... | collective-permute-start | bytes 811016 | tf_op jit(solution)/shard_map/object_halo/ppermute | solution.py:643
  13.2 0.1 collective-permute-start.3
  13.3 0.0 copy-start.4
  13.3 1.2 %copy-done.4 = f32[1,1,4,256,256]{4,3,2,1,0:T(8,128)S(1)} copy-done((f32[1,1,4,256,256]{4,3,2,1,0:T(8,128)S(1)}, f32[1,1,4,256,256]{4,3,2,1,0:T(8,128)}, u32[]{:S(2)}) %copy-start.4) | copy-done | bytes 1048600
  14.5 1.0 copy-done.8
  15.5 1.0 copy-done.9
  16.5 1.3 %shard_map.102.measured = f32[4,256,256]{2,1,0:T(8,128)S(1)} custom-call(f32[4,256,256]{2,1,0:T(8,128)S(1)} %bitcast.22, bf16[768,256]{1,0:T(8,128)(2,1)S(1)} %copy-done.9, bf16[256,768]{1,0:T(8,128)(2,1)S(1)} %copy-done.8), custom_call_target="tpu_custom_call" | custom-call | flops 1073741824 | bytes 3145728 | tf_op jit(solution)/shard_map/pallas_call | solution.py:532
  17.8 6.0 %collective-permute-done.2.cross = f32[2,264,128]{2,1,0:T(8,128)S(1)} collective-permute-done((f32[2,264,128]{2,1,0:T(8,128)S(1)}, f32[2,264,128]{2,1,0:T(8,128)S(1)}, u32[]{:S(2)}, u32[]{:S(2)}) %collective-permute-start.2) | collective-permute-done | bytes 270368 | tf_op jit(solution)/shard_map/object_halo/ppermute | solution.py:643
  23.8 0.0 collective-permute-done.3.same
  23.8 0.0 collective-permute-done.odd_strip
  23.8 0.0 collective-permute-done.1.even_strip
  23.9 0.1 collective-permute-start.5
  24.0 4.4 %collective-permute-start.4 = (f32[2,2,136,128]{3,2,1,0:T(8,128)S(1)}, f32[2,2,136,128]{3,2,1,0:T(8,128)S(1)}, u32[]{:S(2)}, u32[]{:S(2)}) collective-permute-start(f32[2,2,136,128]{3,2,1,0:T(8,128)S(1)} %get-tuple-element.97), channel_id=1, source_target_pairs={{1,2},{2,1},{3,4},{4,3},{5,6},{6,5},{7,8},{8,7},{9,10},{10,9},{11,... | collective-permute-start | bytes 835592 | tf_op jit(solution)/shard_map/object_corners/ppermute | solution.py:643
  28.4 0.0 collective-permute-done.5.same_corner
  28.4 6.4 %collective-permute-done.4.cross_corner = f32[2,2,136,128]{3,2,1,0:T(8,128)S(1)} collective-permute-done((f32[2,2,136,128]{3,2,1,0:T(8,128)S(1)}, f32[2,2,136,128]{3,2,1,0:T(8,128)S(1)}, u32[]{:S(2)}, u32[]{:S(2)}) %collective-permute-start.4) | collective-permute-done | bytes 278560 | tf_op jit(solution)/shard_map/object_corners/ppermute | solution.py:643
  34.8 0.0 copy-done.1
  34.8 0.0 copy-done.3
  34.8 0.0 copy-done.7
  34.8 14.3 %shard_map.103 = (f32[16,88,128]{2,1,0:T(8,128)S(1)}, f32[16,88,128]{2,1,0:T(8,128)S(1)}, f32[4,2,2,256,128]{4,3,2,1,0:T(8,128)S(1)}, f32[4,2,2,256,128]{4,3,2,1,0:T(8,128)S(1)}, s32[8,128]{1,0:T(8,128)S(1)}) custom-call(s32[2,4]{1,0:T(2,128)S(1)} %bitcast.19, f32[2,256,256]{2,1,0:T(8,128)S(1)} %copy-done.1, ...), custom_call_target="tpu_custom_call" | custom-call | flops 13958643712 | bytes 12582912 | tf_op jit(solution)/shard_map/pallas_call | solution.py:564
  49.1 0.1 collective-permute-start.6
  49.2 4.2 %shard_map.104 = (f32[2,256,256]{2,1,0:T(8,128)S(1)}, f32[2,128,256]{2,1,0:T(8,128)S(1)}, f32[2,128,256]{2,1,0:T(8,128)S(1)}, f32[2,256,128]{2,1,0:T(8,128)S(1)}...) custom-call(s32[2,4]{1,0:T(2,128)S(1)} %bitcast.20, ...), custom_call_target="tpu_custom_call" | custom-call | flops 5368709120 | bytes 8388608 | tf_op jit(solution)/shard_map/pallas_call | solution.py:598
  53.4 0.0 collective-permute-done.6
  53.4 0.9 add.9
  54.3 4.4 %collective-permute-start.7 = (f32[2,2,128,128]{3,2,1,0:T(8,128)}, f32[2,2,128,128]{3,2,1,0:T(8,128)}, u32[]{:S(2)}, u32[]{:S(2)}) collective-permute-start(f32[2,2,128,128]{3,2,1,0:T(8,128)} %get-tuple-element.71), channel_id=1, source_target_pairs={{1,2},{2,1},{3,4},{4,3},{5,6},{6,5},{7,8},{8,7},{9,10},{10,9},{11,... | collective-permute-start | bytes 786440 | tf_op jit(solution)/shard_map/gradient_corners/ppermute | solution.py:643
  58.7 0.1 collective-permute-start.8
  58.8 4.6 %all-to-all-start = ((f32[16,88,128]{2,1,0:T(8,128)}), f32[16,88,128]{2,1,0:T(8,128)S(1)}, u32[]{:S(2)}, u32[]{:S(2)}) async-start(f32[16,88,128]{2,1,0:T(8,128)} %add.9), calls=%async_computation | async-start | bytes 1441792 | tf_op jit(solution)/shard_map/probe_reduce/all_to_all | solution.py:693
  63.4 3.3 %collective-permute-start.9 = (f32[2,256,128]{2,1,0:T(8,128)S(1)}, f32[2,256,128]{2,1,0:T(8,128)S(1)}, u32[]{:S(2)}, u32[]{:S(2)}) collective-permute-start(f32[2,256,128]{2,1,0:T(8,128)S(1)} %get-tuple-element.74), channel_id=1, source_target_pairs={{1,2},{2,1},{3,4},{4,3},{5,6},{6,5},{7,8},{8,7},{9,10},{10,9},{11,... | collective-permute-start | bytes 786440 | tf_op jit(solution)/shard_map/gradient_corners/ppermute | solution.py:643
  66.7 0.1 collective-permute-start.10
  66.8 0.0 copy-start.6
  66.8 1.2 %copy-done.6 = f32[2,2,256,256]{3,2,1,0:T(8,128)S(1)} copy-done((f32[2,2,256,256]{3,2,1,0:T(8,128)S(1)}, f32[2,2,256,256]{3,2,1,0:T(8,128)}, u32[]{:S(2)}) %copy-start.6) | copy-done | bytes 1048600
  68.0 2.0 %gradient_rows.2.light = f32[256,256]{1,0:T(8,128)S(1)} custom-call(s32[2,4]{1,0:T(2,128)S(1)} %bitcast.21, s32[8,128]{1,0:T(8,128)S(1)} %get-tuple-element.69.around, f32[2,2,256,256]{3,2,1,0:T(8,128)S(1)} %copy-done.6), custom_call_target="tpu_custom_call" | custom-call | flops 2147483648 | bytes 4194304 | tf_op jit(solution)/shard_map/gradient_rows/pallas_call | solution.py:532
  70.0 0.0 collective-permute-done.7
  70.0 0.0 collective-permute-done.8
  70.0 1.1 broadcast_select_fusion.2
  71.1 0.8 fusion.5
  71.9 0.0 collective-permute-done.9.cross
  71.9 0.0 collective-permute-done.10.same
  71.9 4.7 %all-to-all-done.chunk = f32[16,88,128]{2,1,0:T(8,128)S(1)} async-done(((f32[16,88,128]{2,1,0:T(8,128)}), f32[16,88,128]{2,1,0:T(8,128)S(1)}, u32[]{:S(2)}, u32[]{:S(2)}) %all-to-all-start) | async-done | bytes 720928 | tf_op jit(solution)/shard_map/probe_reduce/all_to_all | solution.py:693
  76.6 0.0 collective-permute-start.14
  76.6 0.7 collective-permute-start.15
  77.3 7.5 %collective-permute-start.13 = (f32[88,128]{1,0:T(8,128)S(1)}, f32[88,128]{1,0:T(8,128)S(1)}, u32[]{:S(2)}, u32[]{:S(2)}) collective-permute-start(f32[88,128]{1,0:T(8,128)S(1)} %probe_sum.2.own), channel_id=1, source_target_pairs={{0,66},{1,67},{2,0},{3,1},{4,70},{5,71},{6,4},{7,5},{8,74},{9,75},... | collective-permute-start | bytes 135176 | tf_op jit(solution)/shard_map/probe_sum/ppermute | solution.py:653
  84.8 0.0 collective-permute-start.12
  84.8 0.7 collective-permute-start.11
  85.5 6.7 %collective-permute-done.13.third = f32[88,128]{1,0:T(8,128)S(1)} collective-permute-done((f32[88,128]{1,0:T(8,128)S(1)}, f32[88,128]{1,0:T(8,128)S(1)}, u32[]{:S(2)}, u32[]{:S(2)}) %collective-permute-start.13) | collective-permute-done | bytes 45088 | tf_op jit(solution)/shard_map/probe_sum/ppermute | solution.py:653
  92.1 0.0 collective-permute-done.12.second
  92.1 0.0 collective-permute-done.11.first
  92.1 0.1 probe_sum.3
  92.3 0.0 collective-permute-done.14.even
  92.3 0.0 collective-permute-done.15.odd
  92.3 1.0 gradient_rows.3
  93.3 14.6 %all_to_all.10.mine = f32[16,64,128]{2,1,0:T(8,128)S(1)} all-to-all(f32[16,64,128]{2,1,0:T(8,128)S(1)} %get-tuple-element.85), channel_id=1, replica_groups={{0,4,8,12,16,20,24,28,32,36,40,44,48,52,56,60},{1,5,9,13,17,21,25,29,33..., dimensions={0} | all-to-all | bytes 1048576 | tf_op jit(solution)/shard_map/probe_gather/all_to_all | solution.py:721
  107.9 2.0 %collective-permute-start.16 = (f32[16,64,128]{2,1,0:T(8,128)S(1)}, f32[16,64,128]{2,1,0:T(8,128)S(1)}, u32[]{:S(2)}, u32[]{:S(2)}) collective-permute-start(f32[16,64,128]{2,1,0:T(8,128)S(1)} %all_to_all.10.mine), channel_id=1, source_target_pairs={{0,1},{1,0},{2,3},{3,2},{4,5},{5,4},{6,7},{7,6},{8,9},{9,8},{10,11... | collective-permute-start | bytes 1572872 | tf_op jit(solution)/shard_map/probe_gather/ppermute | solution.py:643
  109.8 0.1 slice_reduce_fusion
  110.0 0.1 reshape_squeeze.3
  110.0 0.7 copy.12
  110.7 0.5 slice.25
  111.2 0.2 collective-permute-done.16.other
  111.4 1.1 probe_gather.1
  (10 shorter events, 0.1 us)
Async XLA Ops:
  0.6 1.0 copy-start
  1.7 0.7 copy-start.2
  3.1 20.7 %collective-permute-start = (f32[2,136,256]{2,1,0:T(8,128)S(1)}, f32[2,136,256]{2,1,0:T(8,128)S(1)}, u32[]{:S(2)}, u32[]{:S(2)}) collective-permute-start(f32[2,136,256]{2,1,0:T(8,128)S(1)} %get-tuple-element.46), channel_id=1, source_target_pairs={{16,32},{32,16},{48,64},{64,48},{80,96},{96,80},{17,33},{33,17},{4... | collective-permute-start | bytes 835592 | tf_op jit(solution)/shard_map/object_halo/ppermute | solution.py:639
  3.8 20.0 %collective-permute-start.1 = (f32[2,136,256]{2,1,0:T(8,128)S(1)}, f32[2,136,256]{2,1,0:T(8,128)S(1)}, u32[]{:S(2)}, u32[]{:S(2)}) collective-permute-start(f32[2,136,256]{2,1,0:T(8,128)S(1)} %get-tuple-element.47), channel_id=1, source_target_pairs={{0,16},{16,0},{32,48},{48,32},{64,80},{80,64},{96,112},{112,96},{1... | collective-permute-start | bytes 835592 | tf_op jit(solution)/shard_map/object_halo/ppermute | solution.py:639
  8.5 15.3 %collective-permute-start.2 = (f32[2,264,128]{2,1,0:T(8,128)S(1)}, f32[2,264,128]{2,1,0:T(8,128)S(1)}, u32[]{:S(2)}, u32[]{:S(2)}) collective-permute-start(f32[2,264,128]{2,1,0:T(8,128)S(1)} %get-tuple-element.48), channel_id=1, source_target_pairs={{1,2},{2,1},{3,4},{4,3},{5,6},{6,5},{7,8},{8,7},{9,10},{10,9},{11,... | collective-permute-start | bytes 811016 | tf_op jit(solution)/shard_map/object_halo/ppermute | solution.py:643
  13.2 10.6 %collective-permute-start.3 = (f32[2,264,128]{2,1,0:T(8,128)S(1)}, f32[2,264,128]{2,1,0:T(8,128)S(1)}, u32[]{:S(2)}, u32[]{:S(2)}) collective-permute-start(f32[2,264,128]{2,1,0:T(8,128)S(1)} %get-tuple-element.49), channel_id=1, source_target_pairs={{0,1},{1,0},{2,3},{3,2},{4,5},{5,4},{6,7},{7,6},{8,9},{9,8},{10,11... | collective-permute-start | bytes 811016 | tf_op jit(solution)/shard_map/object_halo/ppermute | solution.py:643
  13.3 1.2 %copy-start.4 = (f32[1,1,4,256,256]{4,3,2,1,0:T(8,128)S(1)}, f32[1,1,4,256,256]{4,3,2,1,0:T(8,128)}, u32[]{:S(2)}) copy-start(f32[1,1,4,256,256]{4,3,2,1,0:T(8,128)} %param.9) | copy-start | bytes 3145732
  14.5 1.0 copy-start.8
  15.5 1.0 copy-start.9
  16.5 18.3 %copy-start.1 = (f32[2,256,256]{2,1,0:T(8,128)S(1)}, f32[2,256,256]{2,1,0:T(8,128)}, u32[]{:S(2)}) copy-start(f32[2,256,256]{2,1,0:T(8,128)} %own.3) | copy-start | bytes 1572868
  16.5 18.3 %copy-start.3 = (s32[1,1,4,2]{2,3,1,0:T(2,128)S(1)}, s32[1,1,4,2]{2,3,1,0:T(2,128)}, u32[]{:S(2)}) copy-start(s32[1,1,4,2]{2,3,1,0:T(2,128)} %param.10) | copy-start | bytes 100
  16.5 18.3 %copy-start.5 = (f32[2,2,256,256]{3,2,1,0:T(8,128)S(1)}, f32[2,2,256,256]{3,2,1,0:T(8,128)}, u32[]{:S(2)}) copy-start(f32[2,2,256,256]{3,2,1,0:T(8,128)} %probe.3) | copy-start | bytes 3145732
  16.5 18.3 %copy-start.7 = (bf16[2,2,2,256,256]{4,3,2,1,0:T(8,128)(2,1)S(1)}, bf16[2,2,2,256,256]{4,3,2,1,0:T(8,128)(2,1)}, u32[]{:S(2)}) copy-start(bf16[2,2,2,256,256]{4,3,2,1,0:T(8,128)(2,1)} %constant.19.clone.matrices) | copy-start | bytes 3145732
  23.9 4.5 %collective-permute-start.5 = (f32[2,2,136,128]{3,2,1,0:T(8,128)S(1)}, f32[2,2,136,128]{3,2,1,0:T(8,128)S(1)}, u32[]{:S(2)}, u32[]{:S(2)}) collective-permute-start(f32[2,2,136,128]{3,2,1,0:T(8,128)S(1)} %get-tuple-element.96), channel_id=1, source_target_pairs={{0,1},{1,0},{2,3},{3,2},{4,5},{5,4},{6,7},{7,6},{8,9},{9,8},{10,11... | collective-permute-start | bytes 835592 | tf_op jit(solution)/shard_map/object_corners/ppermute | solution.py:643
  24.0 10.9 %collective-permute-start.4 = (f32[2,2,136,128]{3,2,1,0:T(8,128)S(1)}, f32[2,2,136,128]{3,2,1,0:T(8,128)S(1)}, u32[]{:S(2)}, u32[]{:S(2)}) collective-permute-start(f32[2,2,136,128]{3,2,1,0:T(8,128)S(1)} %get-tuple-element.97), channel_id=1, source_target_pairs={{1,2},{2,1},{3,4},{4,3},{5,6},{6,5},{7,8},{8,7},{9,10},{10,9},{11,... | collective-permute-start | bytes 835592 | tf_op jit(solution)/shard_map/object_corners/ppermute | solution.py:643
  49.1 4.3 %collective-permute-start.6 = (f32[16,88,128]{2,1,0:T(8,128)S(1)}, f32[16,88,128]{2,1,0:T(8,128)S(1)}, u32[]{:S(2)}, u32[]{:S(2)}) collective-permute-start(f32[16,88,128]{2,1,0:T(8,128)S(1)} %get-tuple-element.56), channel_id=1, source_target_pairs={{0,1},{1,0},{2,3},{3,2},{4,5},{5,4},{6,7},{7,6},{8,9},{9,8},{10,11... | collective-permute-start | bytes 2162696 | tf_op jit(solution)/shard_map/probe_reduce/ppermute | solution.py:643
  54.3 15.7 %collective-permute-start.7 = (f32[2,2,128,128]{3,2,1,0:T(8,128)}, f32[2,2,128,128]{3,2,1,0:T(8,128)}, u32[]{:S(2)}, u32[]{:S(2)}) collective-permute-start(f32[2,2,128,128]{3,2,1,0:T(8,128)} %get-tuple-element.71), channel_id=1, source_target_pairs={{1,2},{2,1},{3,4},{4,3},{5,6},{6,5},{7,8},{8,7},{9,10},{10,9},{11,... | collective-permute-start | bytes 786440 | tf_op jit(solution)/shard_map/gradient_corners/ppermute | solution.py:643
  58.7 11.3 %collective-permute-start.8 = (f32[2,2,128,128]{3,2,1,0:T(8,128)S(1)}, f32[2,2,128,128]{3,2,1,0:T(8,128)}, u32[]{:S(2)}, u32[]{:S(2)}) collective-permute-start(f32[2,2,128,128]{3,2,1,0:T(8,128)S(1)} %get-tuple-element.72), channel_id=1, source_target_pairs={{0,1},{1,0},{2,3},{3,2},{4,5},{5,4},{6,7},{7,6},{8,9},{9,8},{10,11... | collective-permute-start | bytes 786440 | tf_op jit(solution)/shard_map/gradient_corners/ppermute | solution.py:643
  58.8 17.8 %all-to-all-start = ((f32[16,88,128]{2,1,0:T(8,128)}), f32[16,88,128]{2,1,0:T(8,128)S(1)}, u32[]{:S(2)}, u32[]{:S(2)}) async-start(f32[16,88,128]{2,1,0:T(8,128)} %add.9), calls=%async_computation | async-start | bytes 1441792 | tf_op jit(solution)/shard_map/probe_reduce/all_to_all | solution.py:693
  63.4 8.5 %collective-permute-start.9 = (f32[2,256,128]{2,1,0:T(8,128)S(1)}, f32[2,256,128]{2,1,0:T(8,128)S(1)}, u32[]{:S(2)}, u32[]{:S(2)}) collective-permute-start(f32[2,256,128]{2,1,0:T(8,128)S(1)} %get-tuple-element.74), channel_id=1, source_target_pairs={{1,2},{2,1},{3,4},{4,3},{5,6},{6,5},{7,8},{8,7},{9,10},{10,9},{11,... | collective-permute-start | bytes 786440 | tf_op jit(solution)/shard_map/gradient_corners/ppermute | solution.py:643
  66.7 5.2 %collective-permute-start.10 = (f32[2,256,128]{2,1,0:T(8,128)S(1)}, f32[2,256,128]{2,1,0:T(8,128)S(1)}, u32[]{:S(2)}, u32[]{:S(2)}) collective-permute-start(f32[2,256,128]{2,1,0:T(8,128)S(1)} %get-tuple-element.75), channel_id=1, source_target_pairs={{0,1},{1,0},{2,3},{3,2},{4,5},{5,4},{6,7},{7,6},{8,9},{9,8},{10,11... | collective-permute-start | bytes 786440 | tf_op jit(solution)/shard_map/gradient_corners/ppermute | solution.py:643
  66.8 1.2 %copy-start.6 = (f32[2,2,256,256]{3,2,1,0:T(8,128)S(1)}, f32[2,2,256,256]{3,2,1,0:T(8,128)}, u32[]{:S(2)}) copy-start(f32[2,2,256,256]{3,2,1,0:T(8,128)} %probe.3) | copy-start | bytes 3145732
  76.6 15.7 %collective-permute-start.14 = (f32[2,128,256]{2,1,0:T(8,128)}, f32[2,128,256]{2,1,0:T(8,128)S(1)}, u32[]{:S(2)}, u32[]{:S(2)}) collective-permute-start(f32[2,128,256]{2,1,0:T(8,128)} %get-tuple-element.79), channel_id=1, source_target_pairs={{0,16},{16,0},{32,48},{48,32},{64,80},{80,64},{96,112},{112,96},{1... | collective-permute-start | bytes 786440 | tf_op jit(solution)/shard_map/gradient_rows/ppermute | solution.py:639
  76.6 15.7 %collective-permute-start.15 = (f32[2,128,256]{2,1,0:T(8,128)S(1)}, f32[2,128,256]{2,1,0:T(8,128)S(1)}, u32[]{:S(2)}, u32[]{:S(2)}) collective-permute-start(f32[2,128,256]{2,1,0:T(8,128)S(1)} %get-tuple-element.80), channel_id=1, source_target_pairs={{16,32},{32,16},{48,64},{64,48},{80,96},{96,80},{17,33},{33,17},{4... | collective-permute-start | bytes 786440 | tf_op jit(solution)/shard_map/gradient_rows/ppermute | solution.py:639
  77.3 14.8 %collective-permute-start.13 = (f32[88,128]{1,0:T(8,128)S(1)}, f32[88,128]{1,0:T(8,128)S(1)}, u32[]{:S(2)}, u32[]{:S(2)}) collective-permute-start(f32[88,128]{1,0:T(8,128)S(1)} %probe_sum.2.own), channel_id=1, source_target_pairs={{0,66},{1,67},{2,0},{3,1},{4,70},{5,71},{6,4},{7,5},{8,74},{9,75},... | collective-permute-start | bytes 135176 | tf_op jit(solution)/shard_map/probe_sum/ppermute | solution.py:653
  84.8 7.3 %collective-permute-start.12 = (f32[88,128]{1,0:T(8,128)S(1)}, f32[88,128]{1,0:T(8,128)S(1)}, u32[]{:S(2)}, u32[]{:S(2)}) collective-permute-start(f32[88,128]{1,0:T(8,128)S(1)} %probe_sum.2.own), channel_id=1, source_target_pairs={{0,64},{1,65},{2,66},{3,67},{4,68},{5,69},{6,70},{7,71},{8,72},{9,... | collective-permute-start | bytes 135176 | tf_op jit(solution)/shard_map/probe_sum/ppermute | solution.py:653
  84.8 7.3 %collective-permute-start.11 = (f32[88,128]{1,0:T(8,128)S(1)}, f32[88,128]{1,0:T(8,128)S(1)}, u32[]{:S(2)}, u32[]{:S(2)}) collective-permute-start(f32[88,128]{1,0:T(8,128)S(1)} %probe_sum.2.own), channel_id=1, source_target_pairs={{0,2},{1,3},{2,64},{3,65},{4,6},{5,7},{6,68},{7,69},{8,10},{9,11},... | collective-permute-start | bytes 135176 | tf_op jit(solution)/shard_map/probe_sum/ppermute | solution.py:653
  107.9 3.5 %collective-permute-start.16 = (f32[16,64,128]{2,1,0:T(8,128)S(1)}, f32[16,64,128]{2,1,0:T(8,128)S(1)}, u32[]{:S(2)}, u32[]{:S(2)}) collective-permute-start(f32[16,64,128]{2,1,0:T(8,128)S(1)} %all_to_all.10.mine), channel_id=1, source_target_pairs={{0,1},{1,0},{2,3},{3,2},{4,5},{5,4},{6,7},{7,6},{8,9},{9,8},{10,11... | collective-permute-start | bytes 1572872 | tf_op jit(solution)/shard_map/probe_gather/ppermute | solution.py:643

commit v9 on v7

--- a/solution.py
+++ b/solution.py
@@ -14,6 +14,7 @@
 SIZE = 256
 HALF = 128
 CHUNK = 32
+WIDTH = 2
 BF = jnp.bfloat16
 F32 = jnp.float32
 AXES = ("row", "col")
@@ -141,73 +142,51 @@
 
 def transform_kernel(
     starts, own, odd_strip, even_strip, cross, same, cross_corner, same_corner, probe_in, matrices, measured,
-    keep, send, object_part, patch, around,
-    tile, probe, mats, offsets, totals, xs, zs, gs, ys, back, sums, sems,
+    keep, send, around, center, even, odd, cross_out, same_out, steps,
+    tile, probe, mats, offsets, totals, sums, accum, power, sems, *slots,
 ):
     step = pl.program_id(0)
     modes = probe.shape[0]
     lanes = lane_index(CHUNK)
-    late = pltpu.make_async_copy(matrices, mats, sems.at[0])
+    width = measured.shape[0]
+    per_slot = len(slots) // width
+    slots = [slots[n * per_slot : (n + 1) * per_slot] for n in range(width)]
 
     @pl.when(step == 0)
     def _():
-        late.start()
         even_rows, odd_rows, cross_block, same_block = sides()
-        center = pl.ds(HALF, SIZE)
-        moves = [(probe_in, probe)]
+        middle = pl.ds(HALF, SIZE)
+        moves = [(probe_in, probe), (matrices, mats)]
         for block, strip, corner in ((cross_block, cross, cross_corner), (same_block, same, same_corner)):
-            moves.append((strip.at[:, :SIZE, :], tile.at[:, block, center, :]))
+            moves.append((strip.at[:, :SIZE, :], tile.at[:, block, middle, :]))
             moves.append((corner.at[1, :, :HALF, :], tile.at[:, block, even_rows, :]))
             moves.append((corner.at[0, :, :HALF, :], tile.at[:, block, odd_rows, :]))
         for b in range(2):
             span = pl.ds(b * HALF, HALF)
-            moves.append((own.at[:, :, span], tile.at[:, 1 + b, center, :]))
+            moves.append((own.at[:, :, span], tile.at[:, 1 + b, middle, :]))
             moves.append((even_strip.at[:, :HALF, span], tile.at[:, 1 + b, even_rows, :]))
             moves.append((odd_strip.at[:, :HALF, span], tile.at[:, 1 + b, odd_rows, :]))
         strips = [x.at[0] for x in (odd_strip, even_strip, cross, same)]
         strips += [x.at[n, 0] for x in (cross_corner, same_corner) for n in range(2)]
         for n, strip in enumerate(strips):
             moves.append((strip.at[pl.ds(strip.shape[0] - 8, 8), pl.ds(0, HALF)], offsets.at[n]))
-        copies = [pltpu.make_async_copy(x, y, sems.at[1 + n]) for n, (x, y) in enumerate(moves)]
+        copies = [pltpu.make_async_copy(x, y, sems.at[n]) for n, (x, y) in enumerate(moves)]
         for copy in copies:
             copy.start()
         tile[:, 4] = jnp.zeros((2, 2 * SIZE, HALF), F32)
         totals[...] = jnp.zeros_like(totals)
         sums[...] = jnp.zeros_like(sums)
+        accum[...] = jnp.zeros_like(accum)
+        for slot in slots:
+            slot[4][:, :, 0:8, :] = jnp.zeros((2, 2, 8, HALF), F32)
+            slot[4][:, :, 264:272, :] = jnp.zeros((2, 2, 8, HALF), F32)
         for copy in copies:
             copy.wait()
+        for i in range(0, SIZE, CHUNK):
+            part = pl.ds(i, CHUNK)
+            power[part] = probe_power(probe, part)
         for n in range(8):
             around[pl.ds(n, 1), :] = offsets[n, :1, :].astype(jnp.int32)
-
-    row, col = starts[0, step], starts[1, step]
-    base, shift = col // HALF, lax.rem(col, HALF)
-
-    for i in range(0, SIZE, CHUNK):
-        part = pl.ds(i, CHUNK)
-        where = pl.ds(row + i, CHUNK)
-        obj = []
-        for p in range(2):
-            blocks = [tile[p, base + b, where, :] for b in range(3)]
-            obj.append(gather_lanes(blocks, shift, lanes))
-            for b in range(2):
-                patch[0, p, b, part, :] = obj[p][b]
-        for m in range(modes):
-            wave = []
-            for b in range(2):
-                span = slice(b * HALF, (b + 1) * HALF)
-                pr, pi = probe[m, 0, part, span], probe[m, 1, part, span]
-                wave.append((pr * obj[0][b] - pi * obj[1][b], pr * obj[1][b] + pi * obj[0][b]))
-            for odd in range(2):
-                for p in range(2):
-                    high, low = split2(wave[0][p] - wave[1][p] if odd else wave[0][p] + wave[1][p])
-                    at = pl.ds(m * SIZE + i, CHUNK)
-                    xs[odd, at, p * HALF : (p + 1) * HALF] = high
-                    xs[odd, at, SIZE + p * HALF : SIZE + (p + 1) * HALF] = low
-                    xs[odd, at, 2 * SIZE + p * HALF : 2 * SIZE + (p + 1) * HALF] = high
-
-    @pl.when(step == 0)
-    def _():
-        late.wait()
 
     def right(odd, transposed):
         high, low = mats[odd, transposed, 0], mats[odd, transposed, 1]
@@ -217,87 +196,172 @@
         high, low = mats[odd, transposed, 0], mats[odd, transposed, 1]
         return jnp.concatenate([high, low, high], 1)
 
-    for odd in range(2):
-        ys[odd] = dot(xs[odd], right(odd, 0))
-
-    for m in range(modes):
+    def position(n):
+        col = starts[1, width * step + n]
+        return starts[0, width * step + n], col // HALF, lax.rem(col, HALF)
+
+    def enter(n):
+        xs, patch = slots[n][0], slots[n][4]
+        row, base, shift = position(n)
+        for i in range(0, SIZE, CHUNK):
+            part = pl.ds(i, CHUNK)
+            where = pl.ds(row + i, CHUNK)
+            obj = []
+            for p in range(2):
+                blocks = [tile[p, base + b, where, :] for b in range(3)]
+                obj.append(gather_lanes(blocks, shift, lanes))
+                for b in range(2):
+                    patch[p, b, pl.ds(8 + i, CHUNK), :] = obj[p][b]
+            for m in range(modes):
+                wave = []
+                for b in range(2):
+                    span = slice(b * HALF, (b + 1) * HALF)
+                    pr, pi = probe[m, 0, part, span], probe[m, 1, part, span]
+                    wave.append((pr * obj[0][b] - pi * obj[1][b], pr * obj[1][b] + pi * obj[0][b]))
+                for odd in range(2):
+                    for p in range(2):
+                        high, low = split2(wave[0][p] - wave[1][p] if odd else wave[0][p] + wave[1][p])
+                        at = pl.ds(m * SIZE + i, CHUNK)
+                        xs[odd, at, p * HALF : (p + 1) * HALF] = high
+                        xs[odd, at, SIZE + p * HALF : SIZE + (p + 1) * HALF] = low
+                        xs[odd, at, 2 * SIZE + p * HALF : 2 * SIZE + (p + 1) * HALF] = high
+
+    def lanes_forward(n):
+        xs, ys = slots[n][0], slots[n][2]
         for odd in range(2):
-            lane_span = slice(odd * HALF, (odd + 1) * HALF)
+            ys[odd] = dot(xs[odd], right(odd, 0))
+
+    def rows_split(n):
+        zs, ys = slots[n][1], slots[n][2]
+        for m in range(modes):
+            for odd in range(2):
+                lane_span = slice(odd * HALF, (odd + 1) * HALF)
+                for i in range(0, HALF, CHUNK):
+                    top = ys[odd, pl.ds(m * SIZE + i, CHUNK), :]
+                    bottom = ys[odd, pl.ds(m * SIZE + HALF + i, CHUNK), :]
+                    for odd_row in range(2):
+                        high, low = split2(top - bottom if odd_row else top + bottom)
+                        for p in range(2):
+                            span = slice(p * HALF, (p + 1) * HALF)
+                            at = p * HALF + i
+                            zs[m, odd_row, pl.ds(at, CHUNK), lane_span] = high[:, span]
+                            zs[m, odd_row, pl.ds(SIZE + at, CHUNK), lane_span] = high[:, span]
+                            zs[m, odd_row, pl.ds(2 * SIZE + at, CHUNK), lane_span] = low[:, span]
+
+    def rows_forward(n):
+        zs, fs = slots[n][1], slots[n][3]
+        for odd_row in range(2):
+            for m in range(modes):
+                fs[m, odd_row] = dot(left(odd_row, 1), zs[m, odd_row])
+
+    def scale(n):
+        zs, fs = slots[n][1], slots[n][3]
+        error = jnp.zeros((8, HALF), F32)
+        energy = jnp.zeros((8, HALF), F32)
+        for odd_row in range(2):
             for i in range(0, HALF, CHUNK):
-                top = ys[odd, pl.ds(m * SIZE + i, CHUNK), :]
-                bottom = ys[odd, pl.ds(m * SIZE + HALF + i, CHUNK), :]
-                for odd_row in range(2):
-                    high, low = split2(top - bottom if odd_row else top + bottom)
+                parts = [[fs[m, odd_row, pl.ds(p * HALF + i, CHUNK), :] for p in range(2)] for m in range(modes)]
+                intensity = parts[0][0] ** 2 + parts[0][1] ** 2 + (parts[1][0] ** 2 + parts[1][1] ** 2)
+                intensity = jnp.maximum(intensity, intensity_floor)
+                inverse = lax.rsqrt(intensity)
+                modulus = intensity * inverse
+                amplitude = measured[n, pl.ds(odd_row * HALF + i, CHUNK), :]
+                factor = 1.0 - amplitude * inverse
+                misfit = (modulus - amplitude) ** 2
+                strength = amplitude**2
+                error = error + fold8(misfit[:, :HALF]) + fold8(misfit[:, HALF:])
+                energy = energy + fold8(strength[:, :HALF]) + fold8(strength[:, HALF:])
+                for m in range(modes):
                     for p in range(2):
-                        span = slice(p * HALF, (p + 1) * HALF)
+                        high, low = split2(parts[m][p] * factor)
                         at = p * HALF + i
-                        zs[m, odd_row, pl.ds(at, CHUNK), lane_span] = high[:, span]
-                        zs[m, odd_row, pl.ds(SIZE + at, CHUNK), lane_span] = high[:, span]
-                        zs[m, odd_row, pl.ds(2 * SIZE + at, CHUNK), lane_span] = low[:, span]
-
-    error = jnp.zeros((8, HALF), F32)
-    energy = jnp.zeros((8, HALF), F32)
-    for odd_row in range(2):
-        far = [dot(left(odd_row, 1), zs[m, odd_row]) for m in range(modes)]
-        for i in range(0, HALF, CHUNK):
-            parts = [(f[i : i + CHUNK], f[HALF + i : HALF + i + CHUNK]) for f in far]
-            intensity = parts[0][0] ** 2 + parts[0][1] ** 2 + (parts[1][0] ** 2 + parts[1][1] ** 2)
-            intensity = jnp.maximum(intensity, intensity_floor)
-            inverse = lax.rsqrt(intensity)
-            modulus = intensity * inverse
-            amplitude = measured[0, pl.ds(odd_row * HALF + i, CHUNK), :]
-            factor = 1.0 - amplitude * inverse
-            misfit = (modulus - amplitude) ** 2
-            strength = amplitude**2
-            error = error + fold8(misfit[:, :HALF]) + fold8(misfit[:, HALF:])
-            energy = energy + fold8(strength[:, :HALF]) + fold8(strength[:, HALF:])
+                        zs[m, odd_row, pl.ds(at, CHUNK), :] = high
+                        zs[m, odd_row, pl.ds(SIZE + at, CHUNK), :] = high
+                        zs[m, odd_row, pl.ds(2 * SIZE + at, CHUNK), :] = low
+        sums[0] += error
+        sums[1] += energy
+
+    def rows_back(n):
+        zs, fs = slots[n][1], slots[n][3]
+        for odd_row in range(2):
             for m in range(modes):
+                fs[m, odd_row] = dot(left(odd_row, 0), zs[m, odd_row])
+
+    def rows_join(n):
+        xs, fs = slots[n][0], slots[n][3]
+        for m in range(modes):
+            for i in range(0, HALF, CHUNK):
                 for p in range(2):
-                    high, low = split2(parts[m][p] * factor)
-                    at = p * HALF + i
-                    gs[m, odd_row, pl.ds(at, CHUNK), :] = high
-                    gs[m, odd_row, pl.ds(SIZE + at, CHUNK), :] = high
-                    gs[m, odd_row, pl.ds(2 * SIZE + at, CHUNK), :] = low
-    sums[0] += error
-    sums[1] += energy
-
-    for m in range(modes):
-        even = dot(left(0, 0), gs[m, 0])
-        odds = dot(left(1, 0), gs[m, 1])
-        for i in range(0, HALF, CHUNK):
+                    a, b = [fs[m, odd_row, pl.ds(p * HALF + i, CHUNK), :] for odd_row in range(2)]
+                    for bottom in range(2):
+                        high, low = split2(a - b if bottom else a + b)
+                        at = pl.ds(m * SIZE + bottom * HALF + i, CHUNK)
+                        for odd in range(2):
+                            span = slice(odd * HALF, (odd + 1) * HALF)
+                            xs[odd, at, p * HALF : (p + 1) * HALF] = high[:, span]
+                            xs[odd, at, SIZE + p * HALF : SIZE + (p + 1) * HALF] = low[:, span]
+                            xs[odd, at, 2 * SIZE + p * HALF : 2 * SIZE + (p + 1) * HALF] = high[:, span]
+
+    def lanes_back(n):
+        xs, ys = slots[n][0], slots[n][2]
+        for odd in range(2):
+            ys[odd] = dot(xs[odd], right(odd, 1))
+
+    def leave(n):
+        ys, patch = slots[n][2], slots[n][4]
+        row, base, shift = position(n)
+        first, last = lanes == 0, lanes == HALF - 1
+        sums_of = [jnp.zeros((8, HALF), F32) for _ in range(4)]
+        for i in range(0, SIZE, CHUNK):
+            part = pl.ds(i, CHUNK)
+            where = pl.ds(row + i, CHUNK)
+            obj = [[patch[p, b, pl.ds(8 + i, CHUNK), :] for b in range(2)] for p in range(2)]
+            grads = [[0.0, 0.0], [0.0, 0.0]]
+            for b in range(2):
+                re, im = obj[0][b], obj[1][b]
+                span = slice(b * HALF, (b + 1) * HALF)
+                for m in range(modes):
+                    at = pl.ds(m * SIZE + i, CHUNK)
+                    evens = [ys[0, at, p * HALF : (p + 1) * HALF] for p in range(2)]
+                    odds = [ys[1, at, p * HALF : (p + 1) * HALF] for p in range(2)]
+                    br, bi = [x - y if b else x + y for x, y in zip(evens, odds)]
+                    pr, pi = probe[m, 0, part, span], probe[m, 1, part, span]
+                    grads[0][b] = grads[0][b] + (pr * br + pi * bi)
+                    grads[1][b] = grads[1][b] + (pr * bi - pi * br)
+                    totals[b, 2 * m, part, :] += re * br + im * bi
+                    totals[b, 2 * m + 1, part, :] += re * bi - im * br
+                totals[b, 4, part, :] += re**2 + im**2
             for p in range(2):
-                a, b = even[p * HALF + i : p * HALF + i + CHUNK], odds[p * HALF + i : p * HALF + i + CHUNK]
-                for bottom in range(2):
-                    high, low = split2(a - b if bottom else a + b)
-                    at = pl.ds(m * SIZE + bottom * HALF + i, CHUNK)
-                    for odd in range(2):
-                        span = slice(odd * HALF, (odd + 1) * HALF)
-                        xs[odd, at, p * HALF : (p + 1) * HALF] = high[:, span]
-                        xs[odd, at, SIZE + p * HALF : SIZE + (p + 1) * HALF] = low[:, span]
-                        xs[odd, at, 2 * SIZE + p * HALF : 2 * SIZE + (p + 1) * HALF] = high[:, span]
-
-    for odd in range(2):
-        back[odd] = dot(xs[odd], right(odd, 1))
-
-    for i in range(0, SIZE, CHUNK):
-        part = pl.ds(i, CHUNK)
-        for b in range(2):
-            re, im = patch[0, 0, b, part, :], patch[0, 1, b, part, :]
-            span = slice(b * HALF, (b + 1) * HALF)
-            grad_re, grad_im = 0.0, 0.0
-            for m in range(modes):
-                at = pl.ds(m * SIZE + i, CHUNK)
-                even = [back[0, at, p * HALF : (p + 1) * HALF] for p in range(2)]
-                odds = [back[1, at, p * HALF : (p + 1) * HALF] for p in range(2)]
-                br, bi = [x - y if b else x + y for x, y in zip(even, odds)]
-                pr, pi = probe[m, 0, part, span], probe[m, 1, part, span]
-                grad_re = grad_re + (pr * br + pi * bi)
-                grad_im = grad_im + (pr * bi - pi * br)
-                totals[b, 2 * m, part, :] += re * br + im * bi
-                totals[b, 2 * m + 1, part, :] += re * bi - im * br
-            object_part[0, 0, b, part, :] = grad_re
-            object_part[0, 1, b, part, :] = grad_im
-            totals[b, 4, part, :] += re**2 + im**2
+                moved = spread(grads[p][0], grads[p][1], shift, lanes)
+                for b in range(3):
+                    accum[p, base + b, where, :] += moved[b]
+            columns = []
+            for p in range(2):
+                before = [pltpu.roll(x, 1, 1) for x in obj[p]]
+                after = [pltpu.roll(x, HALF - 1, 1) for x in obj[p]]
+                columns.append(
+                    (
+                        jnp.where(last, after[1], after[0]) - jnp.where(first, 0.0, before[0]),
+                        jnp.where(last, 0.0, after[1]) - jnp.where(first, before[0], before[1]),
+                    )
+                )
+            for b in range(2):
+                strength = power[part, b * HALF : (b + 1) * HALF]
+                rows = [patch[p, b, pl.ds(9 + i, CHUNK), :] - patch[p, b, pl.ds(7 + i, CHUNK), :] for p in range(2)]
+                for d, slope in enumerate((rows, [columns[0][b], columns[1][b]])):
+                    sums_of[2 * d] = sums_of[2 * d] + fold8(grads[0][b] * slope[0] + grads[1][b] * slope[1])
+                    sums_of[2 * d + 1] = sums_of[2 * d + 1] + fold8(strength * (slope[0] ** 2 + slope[1] ** 2))
+        for d in range(2):
+            numerator = 0.5 * jnp.sum(sums_of[2 * d], keepdims=True)
+            denominator = 0.25 * jnp.sum(sums_of[2 * d + 1], keepdims=True) + small_value
+            at = pl.ds(2 * (width * step + n) + d, 1)
+            steps[at, :] = jnp.broadcast_to(-numerator / denominator, (1, HALF))
+
+    stages = [enter, lanes_forward, rows_split, rows_forward, scale, rows_back, rows_join, lanes_back, leave]
+    for at in range(len(stages) + width - 1):
+        for n in range(width):
+            if 0 <= at - n < len(stages):
+                stages[at - n](n)
 
     @pl.when(step == pl.num_programs(0) - 1)
     def _():
@@ -307,66 +371,6 @@
             for c in range(5):
                 out[:, 16 * c : 16 * c + 16, :] = totals[block, c].reshape(16, 16, HALF)
             out[:, 80:88, :] = jnp.broadcast_to(scalar, (16, 8, HALF))
-
-
-def place_kernel(
-    starts, object_part, patch, probe,
-    center, even, odd, cross, same, cross_corner, same_corner, steps,
-    padded, power, accum,
-):
-    step = pl.program_id(0)
-    lanes = lane_index(CHUNK)
-
-    @pl.when(step == 0)
-    def _():
-        accum[...] = jnp.zeros_like(accum)
-        padded[:, :, 0:8, :] = jnp.zeros((2, 2, 8, HALF), F32)
-        padded[:, :, 264:272, :] = jnp.zeros((2, 2, 8, HALF), F32)
-        for i in range(0, SIZE, CHUNK):
-            part = pl.ds(i, CHUNK)
-            power[part] = probe_power(probe, part)
-
-    row, col = starts[0, step], starts[1, step]
-    base, shift = col // HALF, lax.rem(col, HALF)
-    for p in range(2):
-        for b in range(2):
-            padded[p, b, 8:264] = patch[0, p, b]
-
-    first, last = lanes == 0, lanes == HALF - 1
-    parts = [jnp.zeros((8, HALF), F32) for _ in range(4)]
-    for i in range(0, SIZE, CHUNK):
-        part = pl.ds(i, CHUNK)
-        where = pl.ds(row + i, CHUNK)
-        grads = [[object_part[0, p, b, part, :] for b in range(2)] for p in range(2)]
-        strength = [power[part, :HALF], power[part, HALF:]]
-        for p, pair in enumerate(grads):
-            moved = spread(pair[0], pair[1], shift, lanes)
-            for b in range(3):
-                accum[p, base + b, where, :] += moved[b]
-        columns = []
-        for p in range(2):
-            obj = [patch[0, p, b, part, :] for b in range(2)]
-            before = [pltpu.roll(x, 1, 1) for x in obj]
-            after = [pltpu.roll(x, HALF - 1, 1) for x in obj]
-            columns.append(
-                (
-                    jnp.where(last, after[1], after[0]) - jnp.where(first, 0.0, before[0]),
-                    jnp.where(last, 0.0, after[1]) - jnp.where(first, before[0], before[1]),
-                )
-            )
-        for b in range(2):
-            rows = [padded[p, b, pl.ds(9 + i, CHUNK), :] - padded[p, b, pl.ds(7 + i, CHUNK), :] for p in range(2)]
-            for d, slope in enumerate((rows, [columns[0][b], columns[1][b]])):
-                parts[2 * d] = parts[2 * d] + fold8(grads[0][b] * slope[0] + grads[1][b] * slope[1])
-                parts[2 * d + 1] = parts[2 * d + 1] + fold8(strength[b] * (slope[0] ** 2 + slope[1] ** 2))
-
-    for d in range(2):
-        numerator = 0.5 * jnp.sum(parts[2 * d], keepdims=True)
-        denominator = 0.25 * jnp.sum(parts[2 * d + 1], keepdims=True) + small_value
-        steps[pl.ds(2 * step + d, 1), :] = jnp.broadcast_to(-numerator / denominator, (1, HALF))
-
-    @pl.when(step == pl.num_programs(0) - 1)
-    def _():
         even_rows, odd_rows, cross_block, same_block = sides()
         for p in range(2):
             for b in range(2):
@@ -374,10 +378,8 @@
                 center[p, :, span] = accum[p, 1 + b, 128:384]
                 even[p, :, span] = accum[p, 1 + b, even_rows]
                 odd[p, :, span] = accum[p, 1 + b, odd_rows]
-            for block, strip, corner in ((cross_block, cross, cross_corner), (same_block, same, same_corner)):
-                strip[p] = accum[p, block, 128:384]
-                corner[0, p] = accum[p, block, even_rows]
-                corner[1, p] = accum[p, block, odd_rows]
+            cross_out[p] = accum[p, cross_block]
+            same_out[p] = accum[p, same_block]
 
 
 def probe_power(probe, part):
@@ -453,6 +455,16 @@
     ratio[...] = jnp.broadcast_to(total[80:81, 0:1] / total[80:81, 1:2], (8, HALF))
 
 
+def fold_kernel(even, odd, cross, same, even_out, odd_out):
+    even_rows, odd_rows, _, _ = sides()
+    swapped = place_of()[1] == 1
+    for p in range(2):
+        for strip, rows, out in ((even, even_rows, even_out), (odd, odd_rows, odd_out)):
+            a, b = cross[p, rows], same[p, rows]
+            out[p, :, :HALF] = strip[p, :, :HALF] + jnp.where(swapped, b, a)
+            out[p, :, HALF:] = strip[p, :, HALF:] + jnp.where(swapped, a, b)
+
+
 def update_kernel(center, even, odd, cross, same, light, out, total):
     for p in range(2):
         total[p] = center[p]
@@ -467,7 +479,7 @@
         part = pl.ds(i, CHUNK)
         scale = 1.0 / (light[part] + object_damping)
         for p in range(2):
-            a, b = cross[p, part], same[p, part]
+            a, b = cross[p, pl.ds(HALF + i, CHUNK)], same[p, pl.ds(HALF + i, CHUNK)]
             out[p, part, :HALF] = (total[p, part, :HALF] + jnp.where(swapped, b, a)) * scale[:, :HALF]
             out[p, part, HALF:] = (total[p, part, HALF:] + jnp.where(swapped, a, b)) * scale[:, HALF:]
 
@@ -495,10 +507,6 @@
 
 
 ANY = pl.BlockSpec(memory_space=pl.ANY)
-
-
-def stepped(*shape):
-    return pl.BlockSpec((1, *shape), lambda i, *_: (i,) + (0,) * len(shape))
 
 
 def shaped(shapes):
@@ -555,63 +563,49 @@
     return simple(prepare_kernel, [], arrays, measured.shape, [], 1 << 30, 3 << 20)
 
 
+def stepped(width, *shape):
+    return pl.BlockSpec((width, *shape), lambda i, *_: (i,) + (0,) * len(shape))
+
+
 def transforms(starts, own, halo, probe, measured):
     mats = jnp.asarray(constants())
     arrays = [own, *halo, probe, mats]
     count = measured.shape[0]
+    width = WIDTH
     halves = (16, 88, HALF)
-    fields = (2, 2, SIZE, HALF)
+    rows, columns = (2, HALF, SIZE), (2, 2 * SIZE, HALF)
+    shapes = [(2, SIZE, SIZE), rows, rows, columns, columns, (2 * count, HALF)]
+    slot = [
+        pltpu.VMEM((2, 2 * SIZE, 3 * SIZE), BF),
+        pltpu.VMEM((2, 2, 3 * SIZE, SIZE), BF),
+        pltpu.VMEM((2, 2 * SIZE, SIZE), F32),
+        pltpu.VMEM((2, 2, SIZE, SIZE), F32),
+        pltpu.VMEM((2, 2, SIZE + 16, HALF), F32),
+    ]
     return pl.pallas_call(
         transform_kernel,
-        out_shape=shaped([halves, halves, (count, *fields), (count, *fields)])
-        + [jax.ShapeDtypeStruct((8, HALF), jnp.int32)],
+        out_shape=shaped([halves, halves]) + [jax.ShapeDtypeStruct((8, HALF), jnp.int32)] + shaped(shapes),
         grid_spec=pltpu.PrefetchScalarGridSpec(
             num_scalar_prefetch=1,
-            grid=(count,),
-            in_specs=[ANY] * len(arrays) + [stepped(SIZE, SIZE)],
-            out_specs=[whole(*halves), whole(*halves), stepped(*fields), stepped(*fields), whole(8, HALF)],
+            grid=(count // width,),
+            in_specs=[ANY] * len(arrays) + [stepped(width, SIZE, SIZE)],
+            out_specs=[whole(*x) for x in [halves, halves, (8, HALF), *shapes]],
             scratch_shapes=[
                 pltpu.VMEM((2, 5, 2 * SIZE, HALF), F32),
                 pltpu.VMEM(probe.shape, F32),
                 pltpu.VMEM(mats.shape, BF),
                 pltpu.VMEM((8, 8, HALF), F32),
                 pltpu.VMEM((2, 5, SIZE, HALF), F32),
-                pltpu.VMEM((2, 2 * SIZE, 3 * SIZE), BF),
-                pltpu.VMEM((2, 2, 3 * SIZE, SIZE), BF),
-                pltpu.VMEM((2, 2, 3 * SIZE, SIZE), BF),
-                pltpu.VMEM((2, 2 * SIZE, SIZE), F32),
-                pltpu.VMEM((2, 2 * SIZE, SIZE), F32),
                 pltpu.VMEM((2, 8, HALF), F32),
+                pltpu.VMEM((2, 5, 2 * SIZE, HALF), F32),
+                pltpu.VMEM((SIZE, SIZE), F32),
                 pltpu.SemaphoreType.DMA((24,)),
-            ],
+            ]
+            + slot * width,
         ),
         compiler_params=params(),
         cost_estimate=cost(13 << 30, 12 << 20),
     )(starts, *arrays, measured)
-
-
-def place_parts(starts, object_part, patch, probe):
-    count = patch.shape[0]
-    fields = (2, 2, SIZE, HALF)
-    rows, columns, corners = (2, HALF, SIZE), (2, SIZE, HALF), (2, 2, HALF, HALF)
-    shapes = [(2, SIZE, SIZE), rows, rows, columns, columns, corners, corners, (2 * count, HALF)]
-    return pl.pallas_call(
-        place_kernel,
-        out_shape=shaped(shapes),
-        grid_spec=pltpu.PrefetchScalarGridSpec(
-            num_scalar_prefetch=1,
-            grid=(count,),
-            in_specs=[stepped(*fields), stepped(*fields), whole(*probe.shape)],
-            out_specs=[whole(*s) for s in shapes],
-            scratch_shapes=[
-                pltpu.VMEM((2, 2, SIZE + 16, HALF), F32),
-                pltpu.VMEM((SIZE, SIZE), F32),
-                pltpu.VMEM((2, 5, 2 * SIZE, HALF), F32),
-            ],
-        ),
-        compiler_params=params(),
-        cost_estimate=cost(5 << 30, 8 << 20),
-    )(starts, object_part, patch, probe)
 
 
 def illuminate(starts, around, probe):
@@ -685,25 +679,20 @@
         same_corner = swap_columns(half_lanes(rows, core == 1), 0)
 
     halo = [odd, even, cross, same, cross_corner, same_corner]
-    keep, send, object_part, patch, around = transforms(starts, object_tile, halo, probe, permuted)
-
-    parts = place_parts(starts, object_part, patch, probe)
-    with jax.named_scope("probe_reduce"):
-        chunk, parts, around = lax.optimization_barrier((keep + swap_columns(send, 0), parts, around))
-        chunk = lax.all_to_all(chunk, AXES, 0, 0, axis_index_groups=groups, tiled=True)
-    center, even, odd, cross, same, cross_corner, same_corner, steps = parts
-
-    with jax.named_scope("gradient_corners"):
-        cross_corner = swap_columns(cross_corner, 1)
-        same_corner = swap_columns(same_corner, 0)
+    keep, send, around, *parts = transforms(starts, object_tile, halo, probe, permuted)
+
+    center, even, odd, cross, same, steps = parts
+    with jax.named_scope("gradient_columns"):
         cross = swap_columns(cross, 1)
         same = swap_columns(same, 0)
+
+    with jax.named_scope("probe_reduce"):
+        chunk, around = lax.optimization_barrier((keep + swap_columns(send, 0), around))
+        chunk = lax.all_to_all(chunk, AXES, 0, 0, axis_index_groups=groups, tiled=True)
+
     with jax.named_scope("gradient_rows"):
-        first = jnp.where(core == 0, cross_corner, same_corner)
-        second = jnp.where(core == 0, same_corner, cross_corner)
-        added = jnp.concatenate([first, second], -1)
-        odd, even = odd + added[1], even + added[0]
         light = illuminate(starts, around, probe)
+        even, odd = simple(fold_kernel, [], [even, odd, cross, same], [even.shape] * 2, [], 1 << 20, 1 << 20)
         chunk, light, odd, even = lax.optimization_barrier((chunk, light, odd, even))
         odd = swap_rows(odd, 1)
         even = swap_rows(even, 0)
@@ -716,7 +705,7 @@
 
     with jax.named_scope("probe_gather"):
         gathered = lax.all_to_all(spread_out, AXES, 0, 0, axis_index_groups=groups, tiled=True)
-        gathered, odd, even, cross, same = lax.optimization_barrier((gathered, odd, even, cross, same))
+        gathered, odd, even = lax.optimization_barrier((gathered, odd, even))
         probe_update = assemble(gathered, swap_columns(gathered, 0)).reshape(probe.shape)
 
     object_update = update([center, even, odd, cross, same, light])

time: 112 us -> 106 us (0.946)
  starting transfers between devices: 46.1 us -> 41.6 us
  Pallas kernels: 26.2 us -> 23 us
  waiting for transfers between devices: 28.3 us -> 30.9 us
    pallas_call x2 -> x1, Pallas kernels: 18.5 us -> 14.2 us  [transforms(): pl.pallas_call(transform_kernel, out_shape=shaped([halves, halves]) + [ja...]
    ppermute x10 -> x8, starting transfers between devices: 18.6 us -> 14.8 us  [swap_columns(): return lax.ppermute(value, 'col', pairs_from(first, lax.axis_size('col')))]
    ppermute x10 -> x8, waiting for transfers between devices: 8.4 us -> 10.8 us  [swap_columns(): return lax.ppermute(value, 'col', pairs_from(first, lax.axis_size('col')))]
    ppermute x4, waiting for transfers between devices: 8.92 us -> 11.2 us  [swap_rows(): return lax.ppermute(value, 'row', pairs_from(first, lax.axis_size('row')))]
    all_to_all x1, waiting for transfers between devices: 7.03 us -> 4.92 us  [local(): lax.all_to_all(chunk, AXES, 0, 0, axis_index_groups=groups, tiled=True)]
    pallas_call x6 -> x7, Pallas kernels: 6.98 us -> 8.03 us  [simple(): return call(*scalars, *arrays)]
    unnamed x21 -> x27, local copies, waits for them, and re-layouts: 6.81 us -> 6.96 us
  transfers between devices with their start and end apart: 19 -> 17, of which waited for: 8 -> 8; matrix products, arithmetic and copies ran while one was open for 1% -> 2% of each run, Pallas kernels for 8% -> 6%
where the time goes in v9:
time: 106 us; the launch traced here: 105 us
  starting transfers between devices  41.6 us (39%)
  waiting for transfers between devices  30.9 us (29%)
  Pallas kernels  23 us (22%)
  local copies, waits for them, and re-layouts  7.67 us (7%)
    ppermute x8, starting transfers between devices, swap_columns(): return lax.ppermute(value, 'col', pairs_from(first, lax.axis_size('col')))  14.8 us
    pallas_call x1, Pallas kernels, transforms(): pl.pallas_call(transform_kernel, out_shape=shaped([halves, halves]) + [ja...  14.2 us
    ppermute x4, waiting for transfers between devices, swap_rows(): return lax.ppermute(value, 'row', pairs_from(first, lax.axis_size('row')))  11.2 us
    ppermute x8, waiting for transfers between devices, swap_columns(): return lax.ppermute(value, 'col', pairs_from(first, lax.axis_size('col')))  10.8 us
    all_to_all x1, starting transfers between devices, local(): lax.all_to_all(chunk, AXES, 0, 0, axis_index_groups=groups, tiled=True)  9.26 us
    ppermute x4, starting transfers between devices, swap_rows(): return lax.ppermute(value, 'row', pairs_from(first, lax.axis_size('row')))  8.73 us
    pallas_call x7, Pallas kernels, simple(): return call(*scalars, *arrays)  8.03 us
    unnamed x27, local copies, waits for them, and re-layouts  6.96 us
  transfers between devices with their start and end apart: 17, of which 8 were waited for; matrix products, arithmetic and copies ran while one was open for 2% of the time, Pallas kernels for 6%

profile of v9, /device:TPU:25, one launch (start us, length us, event | category | flops | bytes accessed | tf_op | source)
XLA Modules:
  0.0 105.0 jit_solution(4267857556540026279)
XLA Ops:
  0.6 0.0 copy-start.4
  0.6 0.7 copy-done.4
  1.3 0.0 copy-start
  1.3 1.0 copy-done
  2.4 0.8 object_halo.1
  3.1 5.2 %collective-permute-start = (f32[2,136,256]{2,1,0:T(8,128)S(1)}, f32[2,136,256]{2,1,0:T(8,128)S(1)}, u32[]{:S(2)}, u32[]{:S(2)}) collective-permute-start(f32[2,136,256]{2,1,0:T(8,128)S(1)} %get-tuple-element.35), channel_id=1, source_target_pairs={{16,32},{32,16},{48,64},{64,48},{80,96},{96,80},{17,33},{33,17},{4... | collective-permute-start | bytes 835592 | tf_op jit(solution)/shard_map/object_halo/ppermute | solution.py:633
  8.3 0.1 collective-permute-start.1
  8.4 3.5 %collective-permute-start.2 = (f32[2,264,128]{2,1,0:T(8,128)S(1)}, f32[2,264,128]{2,1,0:T(8,128)S(1)}, u32[]{:S(2)}, u32[]{:S(2)}) collective-permute-start(f32[2,264,128]{2,1,0:T(8,128)S(1)} %get-tuple-element.37), channel_id=1, source_target_pairs={{1,2},{2,1},{3,4},{4,3},{5,6},{6,5},{7,8},{8,7},{9,10},{10,9},{11,... | collective-permute-start | bytes 811016 | tf_op jit(solution)/shard_map/object_halo/ppermute | solution.py:637
  11.9 0.1 collective-permute-start.3
  12.0 0.0 copy-done.11
  12.0 0.0 copy-start.5
  12.0 1.2 %copy-done.5 = f32[1,1,4,256,256]{4,3,2,1,0:T(8,128)S(1)} copy-done((f32[1,1,4,256,256]{4,3,2,1,0:T(8,128)S(1)}, f32[1,1,4,256,256]{4,3,2,1,0:T(8,128)}, u32[]{:S(2)}) %copy-start.5) | copy-done | bytes 1048600
  13.2 1.0 copy-done.12
  14.2 1.3 %shard_map.102.measured = f32[4,256,256]{2,1,0:T(8,128)S(1)} custom-call(f32[4,256,256]{2,1,0:T(8,128)S(1)} %bitcast.13, bf16[768,256]{1,0:T(8,128)(2,1)S(1)} %copy-done.12, bf16[256,768]{1,0:T(8,128)(2,1)S(1)} %copy-done.11), custom_call_target="tpu_custom_call" | custom-call | flops 1073741824 | bytes 3145728 | tf_op jit(solution)/shard_map/pallas_call | solution.py:540
  15.5 2.6 %collective-permute-done.2.cross = f32[2,264,128]{2,1,0:T(8,128)S(1)} collective-permute-done((f32[2,264,128]{2,1,0:T(8,128)S(1)}, f32[2,264,128]{2,1,0:T(8,128)S(1)}, u32[]{:S(2)}, u32[]{:S(2)}) %collective-permute-start.2) | collective-permute-done | bytes 270368 | tf_op jit(solution)/shard_map/object_halo/ppermute | solution.py:637
  18.2 0.0 collective-permute-done.3.same
  18.2 0.0 collective-permute-done.odd_strip
  18.2 0.0 collective-permute-done.1.even_strip
  18.2 0.0 copy-start.1
  18.2 1.2 %collective-permute-start.5 = (f32[2,2,136,128]{3,2,1,0:T(8,128)S(1)}, f32[2,2,136,128]{3,2,1,0:T(8,128)S(1)}, u32[]{:S(2)}, u32[]{:S(2)}) collective-permute-start(f32[2,2,136,128]{3,2,1,0:T(8,128)S(1)} %get-tuple-element.74), channel_id=1, source_target_pairs={{0,1},{1,0},{2,3},{3,2},{4,5},{5,4},{6,7},{7,6},{8,9},{9,8},{10,11... | collective-permute-start | bytes 835592 | tf_op jit(solution)/shard_map/object_corners/ppermute | solution.py:637
  19.4 3.3 %collective-permute-start.4 = (f32[2,2,136,128]{3,2,1,0:T(8,128)S(1)}, f32[2,2,136,128]{3,2,1,0:T(8,128)S(1)}, u32[]{:S(2)}, u32[]{:S(2)}) collective-permute-start(f32[2,2,136,128]{3,2,1,0:T(8,128)S(1)} %get-tuple-element.75), channel_id=1, source_target_pairs={{1,2},{2,1},{3,4},{4,3},{5,6},{6,5},{7,8},{8,7},{9,10},{10,9},{11,... | collective-permute-start | bytes 835592 | tf_op jit(solution)/shard_map/object_corners/ppermute | solution.py:637
  22.7 0.0 collective-permute-done.5.same_corner
  22.7 6.4 %collective-permute-done.4.cross_corner = f32[2,2,136,128]{3,2,1,0:T(8,128)S(1)} collective-permute-done((f32[2,2,136,128]{3,2,1,0:T(8,128)S(1)}, f32[2,2,136,128]{3,2,1,0:T(8,128)S(1)}, u32[]{:S(2)}, u32[]{:S(2)}) %collective-permute-start.4) | collective-permute-done | bytes 278560 | tf_op jit(solution)/shard_map/object_corners/ppermute | solution.py:637
  29.2 0.0 copy-done.6
  29.2 0.0 copy-done.10
  29.2 0.0 copy-done.1
  29.2 14.2 %shard_map.103 = (f32[16,88,128]{2,1,0:T(8,128)S(1)}, f32[16,88,128]{2,1,0:T(8,128)S(1)}, s32[8,128]{1,0:T(8,128)S(1)}, f32[2,256,256]{2,1,0:T(8,128)S(1)}, f32[...) custom-call(s32[2,4]{1,0:T(2,128)S(1)} %bitcast.11, ...), custom_call_target="tpu_custom_call" | custom-call | flops 13958643712 | bytes 12582912 | tf_op jit(solution)/shard_map/pallas_call | solution.py:585
  43.4 0.1 collective-permute-start.6
  43.5 4.4 %collective-permute-start.7 = (f32[2,512,128]{2,1,0:T(8,128)}, f32[2,512,128]{2,1,0:T(8,128)S(1)}, u32[]{:S(2)}, u32[]{:S(2)}) collective-permute-start(f32[2,512,128]{2,1,0:T(8,128)} %get-tuple-element.52), channel_id=1, source_target_pairs={{1,2},{2,1},{3,4},{4,3},{5,6},{6,5},{7,8},{8,7},{9,10},{10,9},{11,... | collective-permute-start | bytes 1572872 | tf_op jit(solution)/shard_map/gradient_columns/ppermute | solution.py:637
  47.9 0.1 collective-permute-start.8
  48.0 0.0 collective-permute-done.6
  48.0 0.9 add.3
  49.0 9.3 %all-to-all-start = ((f32[16,88,128]{2,1,0:T(8,128)}), f32[16,88,128]{2,1,0:T(8,128)S(1)}, u32[]{:S(2)}, u32[]{:S(2)}) async-start(f32[16,88,128]{2,1,0:T(8,128)} %add.3), calls=%async_computation | async-start | bytes 1441792 | tf_op jit(solution)/shard_map/probe_reduce/all_to_all | solution.py:691
  58.2 1.7 %collective-permute-done.7.cross = f32[2,512,128]{2,1,0:T(8,128)S(1)} collective-permute-done((f32[2,512,128]{2,1,0:T(8,128)}, f32[2,512,128]{2,1,0:T(8,128)S(1)}, u32[]{:S(2)}, u32[]{:S(2)}) %collective-permute-start.7) | collective-permute-done | bytes 524320 | tf_op jit(solution)/shard_map/gradient_columns/ppermute | solution.py:637
  60.0 0.0 collective-permute-done.8.same
  60.0 0.7 gradient_rows.3
  60.7 0.7 copy-done.8
  61.4 0.0 copy-done.7
  61.4 3.0 %gradient_rows.2.light = f32[256,256]{1,0:T(8,128)S(1)} custom-call(s32[2,4]{1,0:T(2,128)S(1)} %bitcast.12, s32[8,128]{1,0:T(8,128)S(1)} %get-tuple-element.49.around, f32[2,2,256,256]{3,2,1,0:T(8,128)S(1)} %copy-done.7), custom_call_target="tpu_custom_call" | custom-call | flops 2147483648 | bytes 4194304 | tf_op jit(solution)/shard_map/gradient_rows/pallas_call | solution.py:540
  64.5 4.9 %all-to-all-done.chunk = f32[16,88,128]{2,1,0:T(8,128)S(1)} async-done(((f32[16,88,128]{2,1,0:T(8,128)}), f32[16,88,128]{2,1,0:T(8,128)S(1)}, u32[]{:S(2)}, u32[]{:S(2)}) %all-to-all-start) | async-done | bytes 720928 | tf_op jit(solution)/shard_map/probe_reduce/all_to_all | solution.py:691
  69.4 2.4 %collective-permute-start.11 = (f32[88,128]{1,0:T(8,128)S(1)}, f32[88,128]{1,0:T(8,128)S(1)}, u32[]{:S(2)}, u32[]{:S(2)}) collective-permute-start(f32[88,128]{1,0:T(8,128)S(1)} %probe_sum.2.own), channel_id=1, source_target_pairs={{0,66},{1,67},{2,0},{3,1},{4,70},{5,71},{6,4},{7,5},{8,74},{9,75},... | collective-permute-start | bytes 135176 | tf_op jit(solution)/shard_map/probe_sum/ppermute | solution.py:647
  71.9 0.0 collective-permute-start.10
  71.9 0.7 collective-permute-start.9
  72.5 0.5 collective-permute-done.11.third
  73.0 3.4 %collective-permute-done.10.second = f32[88,128]{1,0:T(8,128)S(1)} collective-permute-done((f32[88,128]{1,0:T(8,128)S(1)}, f32[88,128]{1,0:T(8,128)S(1)}, u32[]{:S(2)}, u32[]{:S(2)}) %collective-permute-start.10) | collective-permute-done | bytes 45088 | tf_op jit(solution)/shard_map/probe_sum/ppermute | solution.py:647
  76.4 0.1 collective-permute-done.9.first
  76.5 0.9 probe_sum.3
  77.3 5.8 %all-to-all-start.1 = ((f32[16,64,128]{2,1,0:T(8,128)}), f32[16,64,128]{2,1,0:T(8,128)S(1)}, u32[]{:S(2)}, u32[]{:S(2)}) async-start(f32[16,64,128]{2,1,0:T(8,128)} %get-tuple-element.57), calls=%async_computation.1 | async-start | bytes 1048576 | tf_op jit(solution)/shard_map/probe_gather/all_to_all | solution.py:707
  83.1 3.4 %collective-permute-start.12 = (f32[2,128,256]{2,1,0:T(8,128)}, f32[2,128,256]{2,1,0:T(8,128)S(1)}, u32[]{:S(2)}, u32[]{:S(2)}) collective-permute-start(f32[2,128,256]{2,1,0:T(8,128)} %get-tuple-element.58), channel_id=1, source_target_pairs={{16,32},{32,16},{48,64},{64,48},{80,96},{96,80},{17,33},{33,17},{4... | collective-permute-start | bytes 786440 | tf_op jit(solution)/shard_map/gradient_rows/ppermute | solution.py:633
  86.5 0.0 copy-done.9
  86.5 0.1 collective-permute-start.13
  86.6 11.2 %collective-permute-done.12.odd = f32[2,128,256]{2,1,0:T(8,128)S(1)} collective-permute-done((f32[2,128,256]{2,1,0:T(8,128)}, f32[2,128,256]{2,1,0:T(8,128)S(1)}, u32[]{:S(2)}, u32[]{:S(2)}) %collective-permute-start.12) | collective-permute-done | bytes 262176 | tf_op jit(solution)/shard_map/gradient_rows/ppermute | solution.py:633
  97.8 0.0 collective-permute-done.13.even
  97.8 0.7 copy-done.2
  98.5 0.0 all-to-all-done.1.mine
  98.5 2.1 %collective-permute-start.14 = (f32[16,64,128]{2,1,0:T(8,128)S(1)}, f32[16,64,128]{2,1,0:T(8,128)S(1)}, u32[]{:S(2)}, u32[]{:S(2)}) collective-permute-start(f32[16,64,128]{2,1,0:T(8,128)S(1)} %all-to-all-done.1.mine), channel_id=1, source_target_pairs={{0,1},{1,0},{2,3},{3,2},{4,5},{5,4},{6,7},{7,6},{8,9},{9,8},{10,11... | collective-permute-start | bytes 1572872 | tf_op jit(solution)/shard_map/probe_gather/ppermute | solution.py:637
  100.6 0.1 slice_reduce_fusion
  100.7 0.1 reshape_squeeze.3
  100.8 0.7 copy.12
  101.5 0.5 slice.17
  102.0 0.9 copy-done.3
  102.9 1.0 shard_map.104
  103.9 0.0 collective-permute-done.14.other
  103.9 1.1 %probe_gather.1 = f32[4,256,256]{2,1,0:T(8,128)} custom-call(f32[16,64,128]{2,1,0:T(8,128)S(1)} %all-to-all-done.1.mine, f32[16,64,128]{2,1,0:T(8,128)S(1)} %collective-permute-done.14.other), custom_call_target="tpu_custom_call" | custom-call | flops 1048576 | bytes 2097152 | tf_op jit(solution)/shard_map/probe_gather/pallas_call | solution.py:540
  (11 shorter events, 0.1 us)
Async XLA Ops:
  0.6 0.7 copy-start.4
  1.3 1.0 copy-start
  2.4 9.6 %copy-start.11 = (bf16[256,768]{1,0:T(8,128)(2,1)S(1)}, bf16[256,768]{1,0:T(8,128)(2,1)}, u32[]{:S(2)}) copy-start(bf16[256,768]{1,0:T(8,128)(2,1)} %constant.18.clone.rows) | copy-start | bytes 1179652
  3.1 15.0 %collective-permute-start = (f32[2,136,256]{2,1,0:T(8,128)S(1)}, f32[2,136,256]{2,1,0:T(8,128)S(1)}, u32[]{:S(2)}, u32[]{:S(2)}) collective-permute-start(f32[2,136,256]{2,1,0:T(8,128)S(1)} %get-tuple-element.35), channel_id=1, source_target_pairs={{16,32},{32,16},{48,64},{64,48},{80,96},{96,80},{17,33},{33,17},{4... | collective-permute-start | bytes 835592 | tf_op jit(solution)/shard_map/object_halo/ppermute | solution.py:633
  8.3 9.9 %collective-permute-start.1 = (f32[2,136,256]{2,1,0:T(8,128)S(1)}, f32[2,136,256]{2,1,0:T(8,128)S(1)}, u32[]{:S(2)}, u32[]{:S(2)}) collective-permute-start(f32[2,136,256]{2,1,0:T(8,128)S(1)} %get-tuple-element.36), channel_id=1, source_target_pairs={{0,16},{16,0},{32,48},{48,32},{64,80},{80,64},{96,112},{112,96},{1... | collective-permute-start | bytes 835592 | tf_op jit(solution)/shard_map/object_halo/ppermute | solution.py:633
  8.4 9.8 %collective-permute-start.2 = (f32[2,264,128]{2,1,0:T(8,128)S(1)}, f32[2,264,128]{2,1,0:T(8,128)S(1)}, u32[]{:S(2)}, u32[]{:S(2)}) collective-permute-start(f32[2,264,128]{2,1,0:T(8,128)S(1)} %get-tuple-element.37), channel_id=1, source_target_pairs={{1,2},{2,1},{3,4},{4,3},{5,6},{6,5},{7,8},{8,7},{9,10},{10,9},{11,... | collective-permute-start | bytes 811016 | tf_op jit(solution)/shard_map/object_halo/ppermute | solution.py:637
  11.9 6.3 %collective-permute-start.3 = (f32[2,264,128]{2,1,0:T(8,128)S(1)}, f32[2,264,128]{2,1,0:T(8,128)S(1)}, u32[]{:S(2)}, u32[]{:S(2)}) collective-permute-start(f32[2,264,128]{2,1,0:T(8,128)S(1)} %get-tuple-element.38), channel_id=1, source_target_pairs={{0,1},{1,0},{2,3},{3,2},{4,5},{5,4},{6,7},{7,6},{8,9},{9,8},{10,11... | collective-permute-start | bytes 811016 | tf_op jit(solution)/shard_map/object_halo/ppermute | solution.py:637
  12.0 1.2 %copy-start.5 = (f32[1,1,4,256,256]{4,3,2,1,0:T(8,128)S(1)}, f32[1,1,4,256,256]{4,3,2,1,0:T(8,128)}, u32[]{:S(2)}) copy-start(f32[1,1,4,256,256]{4,3,2,1,0:T(8,128)} %param.9) | copy-start | bytes 3145732
  13.2 1.0 copy-start.12
  14.2 15.0 %copy-start.6 = (f32[2,2,256,256]{3,2,1,0:T(8,128)S(1)}, f32[2,2,256,256]{3,2,1,0:T(8,128)}, u32[]{:S(2)}) copy-start(f32[2,2,256,256]{3,2,1,0:T(8,128)} %probe.1) | copy-start | bytes 3145732
  14.2 15.0 %copy-start.10 = (bf16[2,2,2,256,256]{4,3,2,1,0:T(8,128)(2,1)S(1)}, bf16[2,2,2,256,256]{4,3,2,1,0:T(8,128)(2,1)}, u32[]{:S(2)}) copy-start(bf16[2,2,2,256,256]{4,3,2,1,0:T(8,128)(2,1)} %constant.19.clone.matrices) | copy-start | bytes 3145732
  18.2 11.0 %copy-start.1 = (f32[2,256,256]{2,1,0:T(8,128)S(1)}, f32[2,256,256]{2,1,0:T(8,128)}, u32[]{:S(2)}) copy-start(f32[2,256,256]{2,1,0:T(8,128)} %own.3) | copy-start | bytes 1572868
  18.2 4.5 %collective-permute-start.5 = (f32[2,2,136,128]{3,2,1,0:T(8,128)S(1)}, f32[2,2,136,128]{3,2,1,0:T(8,128)S(1)}, u32[]{:S(2)}, u32[]{:S(2)}) collective-permute-start(f32[2,2,136,128]{3,2,1,0:T(8,128)S(1)} %get-tuple-element.74), channel_id=1, source_target_pairs={{0,1},{1,0},{2,3},{3,2},{4,5},{5,4},{6,7},{7,6},{8,9},{9,8},{10,11... | collective-permute-start | bytes 835592 | tf_op jit(solution)/shard_map/object_corners/ppermute | solution.py:637
  19.4 9.8 %collective-permute-start.4 = (f32[2,2,136,128]{3,2,1,0:T(8,128)S(1)}, f32[2,2,136,128]{3,2,1,0:T(8,128)S(1)}, u32[]{:S(2)}, u32[]{:S(2)}) collective-permute-start(f32[2,2,136,128]{3,2,1,0:T(8,128)S(1)} %get-tuple-element.75), channel_id=1, source_target_pairs={{1,2},{2,1},{3,4},{4,3},{5,6},{6,5},{7,8},{8,7},{9,10},{10,9},{11,... | collective-permute-start | bytes 835592 | tf_op jit(solution)/shard_map/object_corners/ppermute | solution.py:637
  43.4 4.6 %collective-permute-start.6 = (f32[16,88,128]{2,1,0:T(8,128)S(1)}, f32[16,88,128]{2,1,0:T(8,128)S(1)}, u32[]{:S(2)}, u32[]{:S(2)}) collective-permute-start(f32[16,88,128]{2,1,0:T(8,128)S(1)} %get-tuple-element.46), channel_id=1, source_target_pairs={{0,1},{1,0},{2,3},{3,2},{4,5},{5,4},{6,7},{7,6},{8,9},{9,8},{10,11... | collective-permute-start | bytes 2162696 | tf_op jit(solution)/shard_map/probe_reduce/ppermute | solution.py:637
  43.5 16.5 %collective-permute-start.7 = (f32[2,512,128]{2,1,0:T(8,128)}, f32[2,512,128]{2,1,0:T(8,128)S(1)}, u32[]{:S(2)}, u32[]{:S(2)}) collective-permute-start(f32[2,512,128]{2,1,0:T(8,128)} %get-tuple-element.52), channel_id=1, source_target_pairs={{1,2},{2,1},{3,4},{4,3},{5,6},{6,5},{7,8},{8,7},{9,10},{10,9},{11,... | collective-permute-start | bytes 1572872 | tf_op jit(solution)/shard_map/gradient_columns/ppermute | solution.py:637
  47.9 12.0 %collective-permute-start.8 = (f32[2,512,128]{2,1,0:T(8,128)}, f32[2,512,128]{2,1,0:T(8,128)S(1)}, u32[]{:S(2)}, u32[]{:S(2)}) collective-permute-start(f32[2,512,128]{2,1,0:T(8,128)} %get-tuple-element.53), channel_id=1, source_target_pairs={{0,1},{1,0},{2,3},{3,2},{4,5},{5,4},{6,7},{7,6},{8,9},{9,8},{10,11... | collective-permute-start | bytes 1572872 | tf_op jit(solution)/shard_map/gradient_columns/ppermute | solution.py:637
  49.0 20.4 %all-to-all-start = ((f32[16,88,128]{2,1,0:T(8,128)}), f32[16,88,128]{2,1,0:T(8,128)S(1)}, u32[]{:S(2)}, u32[]{:S(2)}) async-start(f32[16,88,128]{2,1,0:T(8,128)} %add.3), calls=%async_computation | async-start | bytes 1441792 | tf_op jit(solution)/shard_map/probe_reduce/all_to_all | solution.py:691
  58.2 3.2 %copy-start.7 = (f32[2,2,256,256]{3,2,1,0:T(8,128)S(1)}, f32[2,2,256,256]{3,2,1,0:T(8,128)}, u32[]{:S(2)}) copy-start(f32[2,2,256,256]{3,2,1,0:T(8,128)} %probe.1) | copy-start | bytes 3145732
  60.7 0.7 copy-start.8
  69.4 3.6 %collective-permute-start.11 = (f32[88,128]{1,0:T(8,128)S(1)}, f32[88,128]{1,0:T(8,128)S(1)}, u32[]{:S(2)}, u32[]{:S(2)}) collective-permute-start(f32[88,128]{1,0:T(8,128)S(1)} %probe_sum.2.own), channel_id=1, source_target_pairs={{0,66},{1,67},{2,0},{3,1},{4,70},{5,71},{6,4},{7,5},{8,74},{9,75},... | collective-permute-start | bytes 135176 | tf_op jit(solution)/shard_map/probe_sum/ppermute | solution.py:647
  71.9 4.5 %collective-permute-start.10 = (f32[88,128]{1,0:T(8,128)S(1)}, f32[88,128]{1,0:T(8,128)S(1)}, u32[]{:S(2)}, u32[]{:S(2)}) collective-permute-start(f32[88,128]{1,0:T(8,128)S(1)} %probe_sum.2.own), channel_id=1, source_target_pairs={{0,64},{1,65},{2,66},{3,67},{4,68},{5,69},{6,70},{7,71},{8,72},{9,... | collective-permute-start | bytes 135176 | tf_op jit(solution)/shard_map/probe_sum/ppermute | solution.py:647
  71.9 4.6 %collective-permute-start.9 = (f32[88,128]{1,0:T(8,128)S(1)}, f32[88,128]{1,0:T(8,128)S(1)}, u32[]{:S(2)}, u32[]{:S(2)}) collective-permute-start(f32[88,128]{1,0:T(8,128)S(1)} %probe_sum.2.own), channel_id=1, source_target_pairs={{0,2},{1,3},{2,64},{3,65},{4,6},{5,7},{6,68},{7,69},{8,10},{9,11},... | collective-permute-start | bytes 135176 | tf_op jit(solution)/shard_map/probe_sum/ppermute | solution.py:647
  77.3 9.2 %copy-start.9 = (f32[2,128,256]{2,1,0:T(8,128)S(1)}, f32[2,128,256]{2,1,0:T(8,128)}, u32[]{:S(2)}) copy-start(f32[2,128,256]{2,1,0:T(8,128)} %copy-done.8) | copy-start | bytes 786436
  77.3 21.2 %all-to-all-start.1 = ((f32[16,64,128]{2,1,0:T(8,128)}), f32[16,64,128]{2,1,0:T(8,128)S(1)}, u32[]{:S(2)}, u32[]{:S(2)}) async-start(f32[16,64,128]{2,1,0:T(8,128)} %get-tuple-element.57), calls=%async_computation.1 | async-start | bytes 1048576 | tf_op jit(solution)/shard_map/probe_gather/all_to_all | solution.py:707
  83.1 14.7 %collective-permute-start.12 = (f32[2,128,256]{2,1,0:T(8,128)}, f32[2,128,256]{2,1,0:T(8,128)S(1)}, u32[]{:S(2)}, u32[]{:S(2)}) collective-permute-start(f32[2,128,256]{2,1,0:T(8,128)} %get-tuple-element.58), channel_id=1, source_target_pairs={{16,32},{32,16},{48,64},{64,48},{80,96},{96,80},{17,33},{33,17},{4... | collective-permute-start | bytes 786440 | tf_op jit(solution)/shard_map/gradient_rows/ppermute | solution.py:633
  86.5 11.3 %collective-permute-start.13 = (f32[2,128,256]{2,1,0:T(8,128)S(1)}, f32[2,128,256]{2,1,0:T(8,128)S(1)}, u32[]{:S(2)}, u32[]{:S(2)}) collective-permute-start(f32[2,128,256]{2,1,0:T(8,128)S(1)} %copy-done.9), channel_id=1, source_target_pairs={{0,16},{16,0},{32,48},{48,32},{64,80},{80,64},{96,112},{112,96},{1... | collective-permute-start | bytes 786440 | tf_op jit(solution)/shard_map/gradient_rows/ppermute | solution.py:633
  97.8 0.7 copy-start.2
  98.5 5.4 %collective-permute-start.14 = (f32[16,64,128]{2,1,0:T(8,128)S(1)}, f32[16,64,128]{2,1,0:T(8,128)S(1)}, u32[]{:S(2)}, u32[]{:S(2)}) collective-permute-start(f32[16,64,128]{2,1,0:T(8,128)S(1)} %all-to-all-done.1.mine), channel_id=1, source_target_pairs={{0,1},{1,0},{2,3},{3,2},{4,5},{5,4},{6,7},{7,6},{8,9},{9,8},{10,11... | collective-permute-start | bytes 1572872 | tf_op jit(solution)/shard_map/probe_gather/ppermute | solution.py:637
  102.0 0.9 copy-start.3

commit v10 on v9

--- a/solution.py
+++ b/solution.py
@@ -667,13 +667,13 @@
 
     with jax.named_scope("object_halo"):
         even, odd, cross, same = pack(starts, object_tile)
+        cross = swap_columns(cross, 1)
         odd = swap_rows(odd, 1)
         even = swap_rows(even, 0)
-        cross = swap_columns(cross, 1)
         same = swap_columns(same, 0)
     permuted = prepare(measured)
     with jax.named_scope("object_corners"):
-        odd, even, cross, same, permuted = lax.optimization_barrier((odd, even, cross, same, permuted))
+        cross, odd, even, same, permuted = lax.optimization_barrier((cross, odd, even, same, permuted))
         rows = jnp.stack([odd, even])
         cross_corner = swap_columns(half_lanes(rows, core == 0), 1)
         same_corner = swap_columns(half_lanes(rows, core == 1), 0)
@@ -702,13 +702,14 @@
         parts = [total] + [along_z(total, d) for d in (1, 2, 3)]
         shapes = [(16, 64, HALF), (8, HALF)]
         spread_out, ratio = simple(quotient_kernel, [], parts, shapes, [(4, 88, HALF)], 1 << 20, 2 << 20)
+        spread_out, odd, even = lax.optimization_barrier((spread_out, odd, even))
+        object_update = update([center, even, odd, cross, same, light])
 
     with jax.named_scope("probe_gather"):
         gathered = lax.all_to_all(spread_out, AXES, 0, 0, axis_index_groups=groups, tiled=True)
-        gathered, odd, even = lax.optimization_barrier((gathered, odd, even))
+        gathered, object_update = lax.optimization_barrier((gathered, object_update))
         probe_update = assemble(gathered, swap_columns(gathered, 0)).reshape(probe.shape)
 
-    object_update = update([center, even, odd, cross, same, light])
     relative_error = ratio[0, :1]
     position_step = steps[:, 0].reshape(1, 1, -1, 2)
     return (object_update, probe_update, position_step, relative_error)

time: 106 us -> 108 us (1.019)
  the two profiles are of different devices: /device:TPU:25 before, /device:TPU:1 now
where the time goes in v10:
time: 108 us
  waiting for transfers between devices  39.7 us (37%)
  starting transfers between devices  38.4 us (36%)
  Pallas kernels  21.8 us (20%)
  local copies, waits for them, and re-layouts  6.01 us (6%)
    ppermute x8, waiting for transfers between devices, swap_columns(): return lax.ppermute(value, 'col', pairs_from(first, lax.axis_size('col')))  20 us
    ppermute x8, starting transfers between devices, swap_columns(): return lax.ppermute(value, 'col', pairs_from(first, lax.axis_size('col')))  16 us
    pallas_call x1, Pallas kernels, transforms(): pl.pallas_call(transform_kernel, out_shape=shaped([halves, halves]) + [ja...  14.2 us
    all_to_all x1, waiting for transfers between devices, local(): lax.all_to_all(spread_out, AXES, 0, 0, axis_index_groups=groups, tiled=True)  9.34 us
    ppermute x4, starting transfers between devices, swap_rows(): return lax.ppermute(value, 'row', pairs_from(first, lax.axis_size('row')))  7.64 us
    ppermute x3, waiting for transfers between devices, along_z(): return lax.ppermute(value, AXES, pairs)  6.86 us
    pallas_call x7, Pallas kernels, simple(): return call(*scalars, *arrays)  6.79 us
    all_to_all x1, starting transfers between devices, local(): lax.all_to_all(spread_out, AXES, 0, 0, axis_index_groups=groups, tiled=True)  6.18 us
  transfers between devices with their start and end apart: 17, of which 8 were waited for; matrix products, arithmetic and copies ran while one was open for 2% of the time, Pallas kernels for 5%

profile of v10, /device:TPU:1, one launch (start us, length us, event | category | flops | bytes accessed | tf_op | source)
XLA Modules:
  0.0 107.7 jit_solution(6420539998589051772)
XLA Ops:
  0.6 0.0 copy-start.2
  0.6 0.7 copy-done.2
  1.3 0.0 copy-start
  1.3 1.0 copy-done
  2.4 0.0 copy-start.8
  2.4 0.8 object_halo.1
  3.1 0.7 collective-permute-start.1
  3.8 4.7 %collective-permute-start.2 = (f32[2,136,256]{2,1,0:T(8,128)S(1)}, f32[2,136,256]{2,1,0:T(8,128)S(1)}, u32[]{:S(2)}, u32[]{:S(2)}) collective-permute-start(f32[2,136,256]{2,1,0:T(8,128)S(1)} %get-tuple-element.39), channel_id=1, source_target_pairs={{0,16},{16,0},{32,48},{48,32},{64,80},{80,64},{96,112},{112,96},{1... | collective-permute-start | bytes 835592 | tf_op jit(solution)/shard_map/object_halo/ppermute | solution.py:633
  8.5 4.7 %collective-permute-start = (f32[2,264,128]{2,1,0:T(8,128)S(1)}, f32[2,264,128]{2,1,0:T(8,128)S(1)}, u32[]{:S(2)}, u32[]{:S(2)}) collective-permute-start(f32[2,264,128]{2,1,0:T(8,128)S(1)} %get-tuple-element.37), channel_id=1, source_target_pairs={{1,2},{2,1},{3,4},{4,3},{5,6},{6,5},{7,8},{8,7},{9,10},{10,9},{11,... | collective-permute-start | bytes 811016 | tf_op jit(solution)/shard_map/object_halo/ppermute | solution.py:637
  13.2 0.1 collective-permute-start.3
  13.3 0.0 copy-done.8
  13.3 0.0 copy-start.3
  13.3 1.2 %copy-done.3 = f32[1,1,4,256,256]{4,3,2,1,0:T(8,128)S(1)} copy-done((f32[1,1,4,256,256]{4,3,2,1,0:T(8,128)S(1)}, f32[1,1,4,256,256]{4,3,2,1,0:T(8,128)}, u32[]{:S(2)}) %copy-start.3) | copy-done | bytes 1048600
  14.5 1.0 copy-done.9
  15.5 1.3 %shard_map.102.measured = f32[4,256,256]{2,1,0:T(8,128)S(1)} custom-call(f32[4,256,256]{2,1,0:T(8,128)S(1)} %bitcast.13, bf16[768,256]{1,0:T(8,128)(2,1)S(1)} %copy-done.9, bf16[256,768]{1,0:T(8,128)(2,1)S(1)} %copy-done.8), custom_call_target="tpu_custom_call" | custom-call | flops 1073741824 | bytes 3145728 | tf_op jit(solution)/shard_map/pallas_call | solution.py:540
  16.9 6.9 %collective-permute-done.cross = f32[2,264,128]{2,1,0:T(8,128)S(1)} collective-permute-done((f32[2,264,128]{2,1,0:T(8,128)S(1)}, f32[2,264,128]{2,1,0:T(8,128)S(1)}, u32[]{:S(2)}, u32[]{:S(2)}) %collective-permute-start) | collective-permute-done | bytes 270368 | tf_op jit(solution)/shard_map/object_halo/ppermute | solution.py:637
  23.8 0.0 collective-permute-done.3.same
  23.8 0.0 collective-permute-done.1.odd_strip
  23.8 0.0 collective-permute-done.2.even_strip
  23.8 0.0 copy-start.1
  23.9 0.1 collective-permute-start.5
  24.0 4.4 %collective-permute-start.4 = (f32[2,2,136,128]{3,2,1,0:T(8,128)S(1)}, f32[2,2,136,128]{3,2,1,0:T(8,128)S(1)}, u32[]{:S(2)}, u32[]{:S(2)}) collective-permute-start(f32[2,2,136,128]{3,2,1,0:T(8,128)S(1)} %get-tuple-element.79), channel_id=1, source_target_pairs={{1,2},{2,1},{3,4},{4,3},{5,6},{6,5},{7,8},{8,7},{9,10},{10,9},{11,... | collective-permute-start | bytes 835592 | tf_op jit(solution)/shard_map/object_corners/ppermute | solution.py:637
  28.4 0.0 collective-permute-done.5.same_corner
  28.4 6.4 %collective-permute-done.4.cross_corner = f32[2,2,136,128]{3,2,1,0:T(8,128)S(1)} collective-permute-done((f32[2,2,136,128]{3,2,1,0:T(8,128)S(1)}, f32[2,2,136,128]{3,2,1,0:T(8,128)S(1)}, u32[]{:S(2)}, u32[]{:S(2)}) %collective-permute-start.4) | collective-permute-done | bytes 278560 | tf_op jit(solution)/shard_map/object_corners/ppermute | solution.py:637
  34.8 0.0 copy-done.4
  34.8 0.0 copy-done.7
  34.9 0.0 copy-done.1
  34.9 14.2 %shard_map.103 = (f32[16,88,128]{2,1,0:T(8,128)S(1)}, f32[16,88,128]{2,1,0:T(8,128)S(1)}, s32[8,128]{1,0:T(8,128)S(1)}, f32[2,256,256]{2,1,0:T(8,128)S(1)}, f32[...) custom-call(s32[2,4]{1,0:T(2,128)S(1)} %bitcast.11, ...), custom_call_target="tpu_custom_call" | custom-call | flops 13958643712 | bytes 12582912 | tf_op jit(solution)/shard_map/pallas_call | solution.py:585
  49.1 0.1 collective-permute-start.6
  49.2 4.4 %collective-permute-start.7 = (f32[2,512,128]{2,1,0:T(8,128)}, f32[2,512,128]{2,1,0:T(8,128)S(1)}, u32[]{:S(2)}, u32[]{:S(2)}) collective-permute-start(f32[2,512,128]{2,1,0:T(8,128)} %get-tuple-element.53), channel_id=1, source_target_pairs={{1,2},{2,1},{3,4},{4,3},{5,6},{6,5},{7,8},{8,7},{9,10},{10,9},{11,... | collective-permute-start | bytes 1572872 | tf_op jit(solution)/shard_map/gradient_columns/ppermute | solution.py:637
  53.6 0.1 collective-permute-start.8
  53.7 0.0 collective-permute-done.6
  53.7 0.9 add.3
  54.6 4.6 %all-to-all-start = ((f32[16,88,128]{2,1,0:T(8,128)}), f32[16,88,128]{2,1,0:T(8,128)S(1)}, u32[]{:S(2)}, u32[]{:S(2)}) async-start(f32[16,88,128]{2,1,0:T(8,128)} %add.3), calls=%async_computation | async-start | bytes 1441792 | tf_op jit(solution)/shard_map/probe_reduce/all_to_all | solution.py:691
  59.2 0.0 copy-start.5
  59.2 6.4 %collective-permute-done.7.cross = f32[2,512,128]{2,1,0:T(8,128)S(1)} collective-permute-done((f32[2,512,128]{2,1,0:T(8,128)}, f32[2,512,128]{2,1,0:T(8,128)S(1)}, u32[]{:S(2)}, u32[]{:S(2)}) %collective-permute-start.7) | collective-permute-done | bytes 524320 | tf_op jit(solution)/shard_map/gradient_columns/ppermute | solution.py:637
  65.6 0.0 collective-permute-done.8.same
  65.6 0.1 gradient_rows.3
  65.7 0.0 copy-start.6
  65.7 0.7 copy-done.6
  66.4 0.0 copy-done.5
  66.4 2.4 %gradient_rows.2.light = f32[256,256]{1,0:T(8,128)S(1)} custom-call(s32[2,4]{1,0:T(2,128)S(1)} %bitcast.12, s32[8,128]{1,0:T(8,128)S(1)} %get-tuple-element.50.around, f32[2,2,256,256]{3,2,1,0:T(8,128)S(1)} %copy-done.5), custom_call_target="tpu_custom_call" | custom-call | flops 2147483648 | bytes 4194304 | tf_op jit(solution)/shard_map/gradient_rows/pallas_call | solution.py:540
  68.9 3.5 %all-to-all-done.chunk = f32[16,88,128]{2,1,0:T(8,128)S(1)} async-done(((f32[16,88,128]{2,1,0:T(8,128)}), f32[16,88,128]{2,1,0:T(8,128)S(1)}, u32[]{:S(2)}, u32[]{:S(2)}) %all-to-all-start) | async-done | bytes 720928 | tf_op jit(solution)/shard_map/probe_reduce/all_to_all | solution.py:691
  72.4 0.7 collective-permute-start.12
  73.1 1.6 %collective-permute-start.13 = (f32[2,128,256]{2,1,0:T(8,128)S(1)}, f32[2,128,256]{2,1,0:T(8,128)S(1)}, u32[]{:S(2)}, u32[]{:S(2)}) collective-permute-start(f32[2,128,256]{2,1,0:T(8,128)S(1)} %get-tuple-element.60), channel_id=1, source_target_pairs={{0,16},{16,0},{32,48},{48,32},{64,80},{80,64},{96,112},{112,96},{1... | collective-permute-start | bytes 786440 | tf_op jit(solution)/shard_map/gradient_rows/ppermute | solution.py:633
  74.7 2.7 %collective-permute-start.11 = (f32[88,128]{1,0:T(8,128)S(1)}, f32[88,128]{1,0:T(8,128)S(1)}, u32[]{:S(2)}, u32[]{:S(2)}) collective-permute-start(f32[88,128]{1,0:T(8,128)S(1)} %probe_sum.3.own), channel_id=1, source_target_pairs={{0,66},{1,67},{2,0},{3,1},{4,70},{5,71},{6,4},{7,5},{8,74},{9,75},... | collective-permute-start | bytes 135176 | tf_op jit(solution)/shard_map/probe_sum/ppermute | solution.py:647
  77.4 0.5 collective-permute-start.10
  77.9 0.8 collective-permute-start.9
  78.6 0.0 collective-permute-done.11.third
  78.6 3.2 %collective-permute-done.10.second = f32[88,128]{1,0:T(8,128)S(1)} collective-permute-done((f32[88,128]{1,0:T(8,128)S(1)}, f32[88,128]{1,0:T(8,128)S(1)}, u32[]{:S(2)}, u32[]{:S(2)}) %collective-permute-start.10) | collective-permute-done | bytes 45088 | tf_op jit(solution)/shard_map/probe_sum/ppermute | solution.py:647
  81.8 3.7 %collective-permute-done.9.first = f32[88,128]{1,0:T(8,128)S(1)} collective-permute-done((f32[88,128]{1,0:T(8,128)S(1)}, f32[88,128]{1,0:T(8,128)S(1)}, u32[]{:S(2)}, u32[]{:S(2)}) %collective-permute-start.9) | collective-permute-done | bytes 45088 | tf_op jit(solution)/shard_map/probe_sum/ppermute | solution.py:647
  85.5 0.9 probe_sum.4
  86.4 0.0 collective-permute-done.12.odd
  86.4 0.0 collective-permute-done.13.even
  86.4 6.2 %all-to-all-start.1 = ((f32[16,64,128]{2,1,0:T(8,128)}), f32[16,64,128]{2,1,0:T(8,128)S(1)}, u32[]{:S(2)}, u32[]{:S(2)}) async-start(f32[16,64,128]{2,1,0:T(8,128)} %get-tuple-element.61), calls=%async_computation.1 | async-start | bytes 1048576 | tf_op jit(solution)/shard_map/probe_gather/all_to_all | solution.py:709
  92.6 1.0 probe_sum.5
  93.5 9.3 %all-to-all-done.1.mine = f32[16,64,128]{2,1,0:T(8,128)S(1)} async-done(((f32[16,64,128]{2,1,0:T(8,128)}), f32[16,64,128]{2,1,0:T(8,128)S(1)}, u32[]{:S(2)}, u32[]{:S(2)}) %all-to-all-start.1) | async-done | bytes 524320 | tf_op jit(solution)/shard_map/probe_gather/all_to_all | solution.py:709
  102.9 2.2 %collective-permute-start.14 = (f32[16,64,128]{2,1,0:T(8,128)S(1)}, f32[16,64,128]{2,1,0:T(8,128)S(1)}, u32[]{:S(2)}, u32[]{:S(2)}) collective-permute-start(f32[16,64,128]{2,1,0:T(8,128)S(1)} %all-to-all-done.1.mine), channel_id=1, source_target_pairs={{0,1},{1,0},{2,3},{3,2},{4,5},{5,4},{6,7},{7,6},{8,9},{9,8},{10,11... | collective-permute-start | bytes 1572872 | tf_op jit(solution)/shard_map/probe_gather/ppermute | solution.py:637
  105.1 0.1 slice_reduce_fusion
  105.2 0.1 reshape_squeeze.3
  105.3 0.7 copy.12
  105.9 0.5 slice.17
  106.4 0.2 collective-permute-done.14.other
  106.6 1.1 probe_gather.1
  (5 shorter events, 0.1 us)
Async XLA Ops:
  0.6 0.7 copy-start.2
  1.3 1.0 copy-start
  2.4 11.0 %copy-start.8 = (bf16[256,768]{1,0:T(8,128)(2,1)S(1)}, bf16[256,768]{1,0:T(8,128)(2,1)}, u32[]{:S(2)}) copy-start(bf16[256,768]{1,0:T(8,128)(2,1)} %constant.18.clone.rows) | copy-start | bytes 1179652
  3.1 20.7 %collective-permute-start.1 = (f32[2,136,256]{2,1,0:T(8,128)S(1)}, f32[2,136,256]{2,1,0:T(8,128)S(1)}, u32[]{:S(2)}, u32[]{:S(2)}) collective-permute-start(f32[2,136,256]{2,1,0:T(8,128)S(1)} %get-tuple-element.38), channel_id=1, source_target_pairs={{16,32},{32,16},{48,64},{64,48},{80,96},{96,80},{17,33},{33,17},{4... | collective-permute-start | bytes 835592 | tf_op jit(solution)/shard_map/object_halo/ppermute | solution.py:633
  3.8 20.0 %collective-permute-start.2 = (f32[2,136,256]{2,1,0:T(8,128)S(1)}, f32[2,136,256]{2,1,0:T(8,128)S(1)}, u32[]{:S(2)}, u32[]{:S(2)}) collective-permute-start(f32[2,136,256]{2,1,0:T(8,128)S(1)} %get-tuple-element.39), channel_id=1, source_target_pairs={{0,16},{16,0},{32,48},{48,32},{64,80},{80,64},{96,112},{112,96},{1... | collective-permute-start | bytes 835592 | tf_op jit(solution)/shard_map/object_halo/ppermute | solution.py:633
  8.5 15.3 %collective-permute-start = (f32[2,264,128]{2,1,0:T(8,128)S(1)}, f32[2,264,128]{2,1,0:T(8,128)S(1)}, u32[]{:S(2)}, u32[]{:S(2)}) collective-permute-start(f32[2,264,128]{2,1,0:T(8,128)S(1)} %get-tuple-element.37), channel_id=1, source_target_pairs={{1,2},{2,1},{3,4},{4,3},{5,6},{6,5},{7,8},{8,7},{9,10},{10,9},{11,... | collective-permute-start | bytes 811016 | tf_op jit(solution)/shard_map/object_halo/ppermute | solution.py:637
  13.2 10.6 %collective-permute-start.3 = (f32[2,264,128]{2,1,0:T(8,128)S(1)}, f32[2,264,128]{2,1,0:T(8,128)S(1)}, u32[]{:S(2)}, u32[]{:S(2)}) collective-permute-start(f32[2,264,128]{2,1,0:T(8,128)S(1)} %get-tuple-element.40), channel_id=1, source_target_pairs={{0,1},{1,0},{2,3},{3,2},{4,5},{5,4},{6,7},{7,6},{8,9},{9,8},{10,11... | collective-permute-start | bytes 811016 | tf_op jit(solution)/shard_map/object_halo/ppermute | solution.py:637
  13.3 1.2 %copy-start.3 = (f32[1,1,4,256,256]{4,3,2,1,0:T(8,128)S(1)}, f32[1,1,4,256,256]{4,3,2,1,0:T(8,128)}, u32[]{:S(2)}) copy-start(f32[1,1,4,256,256]{4,3,2,1,0:T(8,128)} %param.9) | copy-start | bytes 3145732
  14.5 1.0 copy-start.9
  15.5 19.3 %copy-start.4 = (f32[2,2,256,256]{3,2,1,0:T(8,128)S(1)}, f32[2,2,256,256]{3,2,1,0:T(8,128)}, u32[]{:S(2)}) copy-start(f32[2,2,256,256]{3,2,1,0:T(8,128)} %probe.1) | copy-start | bytes 3145732
  15.5 19.3 %copy-start.7 = (bf16[2,2,2,256,256]{4,3,2,1,0:T(8,128)(2,1)S(1)}, bf16[2,2,2,256,256]{4,3,2,1,0:T(8,128)(2,1)}, u32[]{:S(2)}) copy-start(bf16[2,2,2,256,256]{4,3,2,1,0:T(8,128)(2,1)} %constant.19.clone.matrices) | copy-start | bytes 3145732
  23.8 11.0 %copy-start.1 = (f32[2,256,256]{2,1,0:T(8,128)S(1)}, f32[2,256,256]{2,1,0:T(8,128)}, u32[]{:S(2)}) copy-start(f32[2,256,256]{2,1,0:T(8,128)} %own.3) | copy-start | bytes 1572868
  23.9 4.5 %collective-permute-start.5 = (f32[2,2,136,128]{3,2,1,0:T(8,128)S(1)}, f32[2,2,136,128]{3,2,1,0:T(8,128)S(1)}, u32[]{:S(2)}, u32[]{:S(2)}) collective-permute-start(f32[2,2,136,128]{3,2,1,0:T(8,128)S(1)} %get-tuple-element.78), channel_id=1, source_target_pairs={{0,1},{1,0},{2,3},{3,2},{4,5},{5,4},{6,7},{7,6},{8,9},{9,8},{10,11... | collective-permute-start | bytes 835592 | tf_op jit(solution)/shard_map/object_corners/ppermute | solution.py:637
  24.0 10.9 %collective-permute-start.4 = (f32[2,2,136,128]{3,2,1,0:T(8,128)S(1)}, f32[2,2,136,128]{3,2,1,0:T(8,128)S(1)}, u32[]{:S(2)}, u32[]{:S(2)}) collective-permute-start(f32[2,2,136,128]{3,2,1,0:T(8,128)S(1)} %get-tuple-element.79), channel_id=1, source_target_pairs={{1,2},{2,1},{3,4},{4,3},{5,6},{6,5},{7,8},{8,7},{9,10},{10,9},{11,... | collective-permute-start | bytes 835592 | tf_op jit(solution)/shard_map/object_corners/ppermute | solution.py:637
  49.1 4.6 %collective-permute-start.6 = (f32[16,88,128]{2,1,0:T(8,128)S(1)}, f32[16,88,128]{2,1,0:T(8,128)S(1)}, u32[]{:S(2)}, u32[]{:S(2)}) collective-permute-start(f32[16,88,128]{2,1,0:T(8,128)S(1)} %get-tuple-element.47), channel_id=1, source_target_pairs={{0,1},{1,0},{2,3},{3,2},{4,5},{5,4},{6,7},{7,6},{8,9},{9,8},{10,11... | collective-permute-start | bytes 2162696 | tf_op jit(solution)/shard_map/probe_reduce/ppermute | solution.py:637
  49.2 16.5 %collective-permute-start.7 = (f32[2,512,128]{2,1,0:T(8,128)}, f32[2,512,128]{2,1,0:T(8,128)S(1)}, u32[]{:S(2)}, u32[]{:S(2)}) collective-permute-start(f32[2,512,128]{2,1,0:T(8,128)} %get-tuple-element.53), channel_id=1, source_target_pairs={{1,2},{2,1},{3,4},{4,3},{5,6},{6,5},{7,8},{8,7},{9,10},{10,9},{11,... | collective-permute-start | bytes 1572872 | tf_op jit(solution)/shard_map/gradient_columns/ppermute | solution.py:637
  53.6 12.0 %collective-permute-start.8 = (f32[2,512,128]{2,1,0:T(8,128)}, f32[2,512,128]{2,1,0:T(8,128)S(1)}, u32[]{:S(2)}, u32[]{:S(2)}) collective-permute-start(f32[2,512,128]{2,1,0:T(8,128)} %get-tuple-element.54), channel_id=1, source_target_pairs={{0,1},{1,0},{2,3},{3,2},{4,5},{5,4},{6,7},{7,6},{8,9},{9,8},{10,11... | collective-permute-start | bytes 1572872 | tf_op jit(solution)/shard_map/gradient_columns/ppermute | solution.py:637
  54.6 17.8 %all-to-all-start = ((f32[16,88,128]{2,1,0:T(8,128)}), f32[16,88,128]{2,1,0:T(8,128)S(1)}, u32[]{:S(2)}, u32[]{:S(2)}) async-start(f32[16,88,128]{2,1,0:T(8,128)} %add.3), calls=%async_computation | async-start | bytes 1441792 | tf_op jit(solution)/shard_map/probe_reduce/all_to_all | solution.py:691
  59.2 7.2 %copy-start.5 = (f32[2,2,256,256]{3,2,1,0:T(8,128)S(1)}, f32[2,2,256,256]{3,2,1,0:T(8,128)}, u32[]{:S(2)}) copy-start(f32[2,2,256,256]{3,2,1,0:T(8,128)} %probe.1) | copy-start | bytes 3145732
  65.7 0.7 copy-start.6
  72.4 14.0 %collective-permute-start.12 = (f32[2,128,256]{2,1,0:T(8,128)}, f32[2,128,256]{2,1,0:T(8,128)S(1)}, u32[]{:S(2)}, u32[]{:S(2)}) collective-permute-start(f32[2,128,256]{2,1,0:T(8,128)} %copy-done.6), channel_id=1, source_target_pairs={{16,32},{32,16},{48,64},{64,48},{80,96},{96,80},{17,33},{33,17},{4... | collective-permute-start | bytes 786440 | tf_op jit(solution)/shard_map/gradient_rows/ppermute | solution.py:633
  73.1 13.3 %collective-permute-start.13 = (f32[2,128,256]{2,1,0:T(8,128)S(1)}, f32[2,128,256]{2,1,0:T(8,128)S(1)}, u32[]{:S(2)}, u32[]{:S(2)}) collective-permute-start(f32[2,128,256]{2,1,0:T(8,128)S(1)} %get-tuple-element.60), channel_id=1, source_target_pairs={{0,16},{16,0},{32,48},{48,32},{64,80},{80,64},{96,112},{112,96},{1... | collective-permute-start | bytes 786440 | tf_op jit(solution)/shard_map/gradient_rows/ppermute | solution.py:633
  74.7 4.0 %collective-permute-start.11 = (f32[88,128]{1,0:T(8,128)S(1)}, f32[88,128]{1,0:T(8,128)S(1)}, u32[]{:S(2)}, u32[]{:S(2)}) collective-permute-start(f32[88,128]{1,0:T(8,128)S(1)} %probe_sum.3.own), channel_id=1, source_target_pairs={{0,66},{1,67},{2,0},{3,1},{4,70},{5,71},{6,4},{7,5},{8,74},{9,75},... | collective-permute-start | bytes 135176 | tf_op jit(solution)/shard_map/probe_sum/ppermute | solution.py:647
  77.4 4.4 %collective-permute-start.10 = (f32[88,128]{1,0:T(8,128)S(1)}, f32[88,128]{1,0:T(8,128)S(1)}, u32[]{:S(2)}, u32[]{:S(2)}) collective-permute-start(f32[88,128]{1,0:T(8,128)S(1)} %probe_sum.3.own), channel_id=1, source_target_pairs={{0,64},{1,65},{2,66},{3,67},{4,68},{5,69},{6,70},{7,71},{8,72},{9,... | collective-permute-start | bytes 135176 | tf_op jit(solution)/shard_map/probe_sum/ppermute | solution.py:647
  77.9 7.6 %collective-permute-start.9 = (f32[88,128]{1,0:T(8,128)S(1)}, f32[88,128]{1,0:T(8,128)S(1)}, u32[]{:S(2)}, u32[]{:S(2)}) collective-permute-start(f32[88,128]{1,0:T(8,128)S(1)} %probe_sum.3.own), channel_id=1, source_target_pairs={{0,2},{1,3},{2,64},{3,65},{4,6},{5,7},{6,68},{7,69},{8,10},{9,11},... | collective-permute-start | bytes 135176 | tf_op jit(solution)/shard_map/probe_sum/ppermute | solution.py:647
  86.4 16.5 %all-to-all-start.1 = ((f32[16,64,128]{2,1,0:T(8,128)}), f32[16,64,128]{2,1,0:T(8,128)S(1)}, u32[]{:S(2)}, u32[]{:S(2)}) async-start(f32[16,64,128]{2,1,0:T(8,128)} %get-tuple-element.61), calls=%async_computation.1 | async-start | bytes 1048576 | tf_op jit(solution)/shard_map/probe_gather/all_to_all | solution.py:709
  102.9 3.7 %collective-permute-start.14 = (f32[16,64,128]{2,1,0:T(8,128)S(1)}, f32[16,64,128]{2,1,0:T(8,128)S(1)}, u32[]{:S(2)}, u32[]{:S(2)}) collective-permute-start(f32[16,64,128]{2,1,0:T(8,128)S(1)} %all-to-all-done.1.mine), channel_id=1, source_target_pairs={{0,1},{1,0},{2,3},{3,2},{4,5},{5,4},{6,7},{7,6},{8,9},{9,8},{10,11... | collective-permute-start | bytes 1572872 | tf_op jit(solution)/shard_map/probe_gather/ppermute | solution.py:637

commit v11 on v9

--- a/solution.py
+++ b/solution.py
@@ -513,8 +513,8 @@
     return [jax.ShapeDtypeStruct(s, F32) for s in shapes]
 
 
-def params():
-    return pltpu.CompilerParams(vmem_limit_bytes=VMEM_LIMIT)
+def params(limit=VMEM_LIMIT):
+    return pltpu.CompilerParams(vmem_limit_bytes=limit)
 
 
 def cost(flops, size):
@@ -552,7 +552,7 @@
             out_specs=[ANY] * 4,
             scratch_shapes=[pltpu.VMEM((2, 8, SIZE), F32), pltpu.SemaphoreType.DMA((8,))],
         ),
-        compiler_params=params(),
+        compiler_params=params(60 * 2**20),
         cost_estimate=cost(1 << 10, 2 << 20),
     )(starts, own)
 
@@ -705,12 +705,13 @@
 
     with jax.named_scope("probe_gather"):
         gathered = lax.all_to_all(spread_out, AXES, 0, 0, axis_index_groups=groups, tiled=True)
-        gathered, odd, even = lax.optimization_barrier((gathered, odd, even))
+        relative_error = ratio[0, :1]
+        position_step = steps[:, 0].reshape(1, 1, -1, 2)
+        tied = (gathered, odd, even, relative_error, position_step)
+        gathered, odd, even, relative_error, position_step = lax.optimization_barrier(tied)
         probe_update = assemble(gathered, swap_columns(gathered, 0)).reshape(probe.shape)
 
     object_update = update([center, even, odd, cross, same, light])
-    relative_error = ratio[0, :1]
-    position_step = steps[:, 0].reshape(1, 1, -1, 2)
     return (object_update, probe_update, position_step, relative_error)
 
 

time: 106 us -> 137 us (1.29)
  Pallas kernels: 23 us -> 55.8 us
  local copies, waits for them, and re-layouts: 7.67 us -> 5.96 us
    pallas_call x1, Pallas kernels: 0.76 us -> 33.8 us  [pack(): pl.pallas_call(pack_kernel, out_shape=shaped([rows, rows, columns, column...]
    unnamed x27 -> x25, local copies, waits for them, and re-layouts: 6.96 us -> 5.25 us
  transfers between devices with their start and end apart: 17 -> 17, of which waited for: 8 -> 8; matrix products, arithmetic and copies ran while one was open for 2% -> 2% of each run, Pallas kernels for 6% -> 4%
where the time goes in v11:
time: 137 us; the launch traced here: 136 us
  Pallas kernels  55.8 us (41%)
  starting transfers between devices  41.5 us (30%)
  waiting for transfers between devices  30.7 us (22%)
  local copies, waits for them, and re-layouts  5.96 us (4%)
    pallas_call x1, Pallas kernels, pack(): pl.pallas_call(pack_kernel, out_shape=shaped([rows, rows, columns, column...  33.8 us
    ppermute x8, starting transfers between devices, swap_columns(): return lax.ppermute(value, 'col', pairs_from(first, lax.axis_size('col')))  14.6 us
    pallas_call x1, Pallas kernels, transforms(): pl.pallas_call(transform_kernel, out_shape=shaped([halves, halves]) + [ja...  14.2 us
    ppermute x8, waiting for transfers between devices, swap_columns(): return lax.ppermute(value, 'col', pairs_from(first, lax.axis_size('col')))  11.2 us
    ppermute x4, waiting for transfers between devices, swap_rows(): return lax.ppermute(value, 'row', pairs_from(first, lax.axis_size('row')))  10.5 us
    all_to_all x1, starting transfers between devices, local(): lax.all_to_all(chunk, AXES, 0, 0, axis_index_groups=groups, tiled=True)  9.27 us
    ppermute x4, starting transfers between devices, swap_rows(): return lax.ppermute(value, 'row', pairs_from(first, lax.axis_size('row')))  8.73 us
    pallas_call x7, Pallas kernels, simple(): return call(*scalars, *arrays)  7.84 us
  transfers between devices with their start and end apart: 17, of which 8 were waited for; matrix products, arithmetic and copies ran while one was open for 2% of the time, Pallas kernels for 4%

profile of v11, /device:TPU:25, one launch (start us, length us, event | category | flops | bytes accessed | tf_op | source)
XLA Modules:
  0.0 135.7 jit_solution(2908385208536212421)
XLA Ops:
  0.6 0.0 copy-start.10
  0.6 33.8 %object_halo.1 = (f32[2,136,256]{2,1,0:T(8,128)}, f32[2,136,256]{2,1,0:T(8,128)}, f32[2,264,128]{2,1,0:T(8,128)}, f32[2,264,128]{2,1,0:T(8,128)}) custom-call(s32[2,4]{1,0:T(2,128)} %bitcast.10, f32[2,256,256]{2,1,0:T(8,128)} %own.3), custom_call_target="tpu_custom_call" | custom-call | flops 1024 | bytes 2097152 | tf_op jit(solution)/shard_map/object_halo/pallas_call | solution.py:545
  34.4 5.2 %collective-permute-start = (f32[2,136,256]{2,1,0:T(8,128)}, f32[2,136,256]{2,1,0:T(8,128)S(1)}, u32[]{:S(2)}, u32[]{:S(2)}) collective-permute-start(f32[2,136,256]{2,1,0:T(8,128)} %get-tuple-element.37), channel_id=1, source_target_pairs={{16,32},{32,16},{48,64},{64,48},{80,96},{96,80},{17,33},{33,17},{4... | collective-permute-start | bytes 835592 | tf_op jit(solution)/shard_map/object_halo/ppermute | solution.py:633
  39.6 0.1 collective-permute-start.1
  39.7 3.5 %collective-permute-start.2 = (f32[2,264,128]{2,1,0:T(8,128)}, f32[2,264,128]{2,1,0:T(8,128)S(1)}, u32[]{:S(2)}, u32[]{:S(2)}) collective-permute-start(f32[2,264,128]{2,1,0:T(8,128)} %get-tuple-element.39), channel_id=1, source_target_pairs={{1,2},{2,1},{3,4},{4,3},{5,6},{6,5},{7,8},{8,7},{9,10},{10,9},{11,... | collective-permute-start | bytes 811016 | tf_op jit(solution)/shard_map/object_halo/ppermute | solution.py:637
  43.2 0.1 collective-permute-start.3
  43.3 0.0 copy-done.10
  43.3 0.0 copy-start.4
  43.3 1.2 copy-done.4
  44.5 0.0 copy-start.11
  44.5 1.0 copy-done.11
  45.5 1.3 shard_map.102.measured
  46.8 3.0 %collective-permute-done.2.cross = f32[2,264,128]{2,1,0:T(8,128)S(1)} collective-permute-done((f32[2,264,128]{2,1,0:T(8,128)}, f32[2,264,128]{2,1,0:T(8,128)S(1)}, u32[]{:S(2)}, u32[]{:S(2)}) %collective-permute-start.2) | collective-permute-done | bytes 270368 | tf_op jit(solution)/shard_map/object_halo/ppermute | solution.py:637
  49.8 0.0 collective-permute-done.3.same
  49.8 0.0 collective-permute-done.odd_strip
  49.8 0.0 collective-permute-done.1.even_strip
  49.8 0.0 copy-start
  49.9 0.0 copy-start.3
  49.9 1.1 collective-permute-start.5
  50.9 3.3 %collective-permute-start.4 = (f32[2,2,136,128]{3,2,1,0:T(8,128)S(1)}, f32[2,2,136,128]{3,2,1,0:T(8,128)S(1)}, u32[]{:S(2)}, u32[]{:S(2)}) collective-permute-start(f32[2,2,136,128]{3,2,1,0:T(8,128)S(1)} %get-tuple-element.79), channel_id=1, source_target_pairs={{1,2},{2,1},{3,4},{4,3},{5,6},{6,5},{7,8},{8,7},{9,10},{10,9},{11,... | collective-permute-start | bytes 835592 | tf_op jit(solution)/shard_map/object_corners/ppermute | solution.py:637
  54.3 0.0 collective-permute-done.5.same_corner
  54.3 6.4 %collective-permute-done.4.cross_corner = f32[2,2,136,128]{3,2,1,0:T(8,128)S(1)} collective-permute-done((f32[2,2,136,128]{3,2,1,0:T(8,128)S(1)}, f32[2,2,136,128]{3,2,1,0:T(8,128)S(1)}, u32[]{:S(2)}, u32[]{:S(2)}) %collective-permute-start.4) | collective-permute-done | bytes 278560 | tf_op jit(solution)/shard_map/object_corners/ppermute | solution.py:637
  60.7 0.0 copy-done.5
  60.7 0.0 copy-done.9
  60.7 0.0 copy-done
  60.7 0.0 copy-done.3
  60.7 14.2 %shard_map.103 = (f32[16,88,128]{2,1,0:T(8,128)S(1)}, f32[16,88,128]{2,1,0:T(8,128)S(1)}, s32[8,128]{1,0:T(8,128)S(1)}, f32[2,256,256]{2,1,0:T(8,128)S(1)}, f32[...) custom-call(s32[2,4]{1,0:T(2,128)S(1)} %bitcast.11, ...), custom_call_target="tpu_custom_call" | custom-call | flops 13958643712 | bytes 12582912 | tf_op jit(solution)/shard_map/pallas_call | solution.py:585
  74.9 0.1 collective-permute-start.6
  75.0 4.4 %collective-permute-start.7 = (f32[2,512,128]{2,1,0:T(8,128)}, f32[2,512,128]{2,1,0:T(8,128)S(1)}, u32[]{:S(2)}, u32[]{:S(2)}) collective-permute-start(f32[2,512,128]{2,1,0:T(8,128)} %get-tuple-element.54), channel_id=1, source_target_pairs={{1,2},{2,1},{3,4},{4,3},{5,6},{6,5},{7,8},{8,7},{9,10},{10,9},{11,... | collective-permute-start | bytes 1572872 | tf_op jit(solution)/shard_map/gradient_columns/ppermute | solution.py:637
  79.4 0.1 collective-permute-start.8
  79.5 0.0 collective-permute-done.6
  79.5 0.9 add.3
  80.5 9.3 %all-to-all-start = ((f32[16,88,128]{2,1,0:T(8,128)}), f32[16,88,128]{2,1,0:T(8,128)S(1)}, u32[]{:S(2)}, u32[]{:S(2)}) async-start(f32[16,88,128]{2,1,0:T(8,128)} %add.3), calls=%async_computation | async-start | bytes 1441792 | tf_op jit(solution)/shard_map/probe_reduce/all_to_all | solution.py:691
  89.7 1.7 %collective-permute-done.7.cross = f32[2,512,128]{2,1,0:T(8,128)S(1)} collective-permute-done((f32[2,512,128]{2,1,0:T(8,128)}, f32[2,512,128]{2,1,0:T(8,128)S(1)}, u32[]{:S(2)}, u32[]{:S(2)}) %collective-permute-start.7) | collective-permute-done | bytes 524320 | tf_op jit(solution)/shard_map/gradient_columns/ppermute | solution.py:637
  91.5 0.0 collective-permute-done.8.same
  91.5 0.8 gradient_rows.3
  92.2 0.7 copy-done.7
  92.9 0.0 copy-done.6
  92.9 2.9 %gradient_rows.2.light = f32[256,256]{1,0:T(8,128)S(1)} custom-call(s32[2,4]{1,0:T(2,128)S(1)} %bitcast.12, s32[8,128]{1,0:T(8,128)S(1)} %get-tuple-element.51.around, f32[2,2,256,256]{3,2,1,0:T(8,128)S(1)} %copy-done.6), custom_call_target="tpu_custom_call" | custom-call | flops 2147483648 | bytes 4194304 | tf_op jit(solution)/shard_map/gradient_rows/pallas_call | solution.py:540
  95.8 5.1 %all-to-all-done.chunk = f32[16,88,128]{2,1,0:T(8,128)S(1)} async-done(((f32[16,88,128]{2,1,0:T(8,128)}), f32[16,88,128]{2,1,0:T(8,128)S(1)}, u32[]{:S(2)}, u32[]{:S(2)}) %all-to-all-start) | async-done | bytes 720928 | tf_op jit(solution)/shard_map/probe_reduce/all_to_all | solution.py:691
  100.9 2.4 %collective-permute-start.11 = (f32[88,128]{1,0:T(8,128)S(1)}, f32[88,128]{1,0:T(8,128)S(1)}, u32[]{:S(2)}, u32[]{:S(2)}) collective-permute-start(f32[88,128]{1,0:T(8,128)S(1)} %probe_sum.2.own), channel_id=1, source_target_pairs={{0,66},{1,67},{2,0},{3,1},{4,70},{5,71},{6,4},{7,5},{8,74},{9,75},... | collective-permute-start | bytes 135176 | tf_op jit(solution)/shard_map/probe_sum/ppermute | solution.py:647
  103.4 0.0 collective-permute-start.10
  103.4 0.7 collective-permute-start.9
  104.0 0.5 collective-permute-done.11.third
  104.5 3.4 %collective-permute-done.10.second = f32[88,128]{1,0:T(8,128)S(1)} collective-permute-done((f32[88,128]{1,0:T(8,128)S(1)}, f32[88,128]{1,0:T(8,128)S(1)}, u32[]{:S(2)}, u32[]{:S(2)}) %collective-permute-start.10) | collective-permute-done | bytes 45088 | tf_op jit(solution)/shard_map/probe_sum/ppermute | solution.py:647
  107.9 0.1 collective-permute-done.9.first
  107.9 0.9 probe_sum.3
  108.8 5.8 %all-to-all-start.1 = ((f32[16,64,128]{2,1,0:T(8,128)}), f32[16,64,128]{2,1,0:T(8,128)S(1)}, u32[]{:S(2)}, u32[]{:S(2)}) async-start(f32[16,64,128]{2,1,0:T(8,128)} %get-tuple-element.59), calls=%async_computation.1 | async-start | bytes 1048576 | tf_op jit(solution)/shard_map/probe_gather/all_to_all | solution.py:707
  114.6 3.4 %collective-permute-start.12 = (f32[2,128,256]{2,1,0:T(8,128)}, f32[2,128,256]{2,1,0:T(8,128)S(1)}, u32[]{:S(2)}, u32[]{:S(2)}) collective-permute-start(f32[2,128,256]{2,1,0:T(8,128)} %get-tuple-element.60), channel_id=1, source_target_pairs={{16,32},{32,16},{48,64},{64,48},{80,96},{96,80},{17,33},{33,17},{4... | collective-permute-start | bytes 786440 | tf_op jit(solution)/shard_map/gradient_rows/ppermute | solution.py:633
  118.0 0.0 copy-done.8
  118.0 0.1 collective-permute-start.13
  118.1 0.1 slice_reduce_fusion
  118.2 0.1 squeeze.15
  118.3 0.5 slice.16
  118.8 10.5 %collective-permute-done.12.odd = f32[2,128,256]{2,1,0:T(8,128)S(1)} collective-permute-done((f32[2,128,256]{2,1,0:T(8,128)}, f32[2,128,256]{2,1,0:T(8,128)S(1)}, u32[]{:S(2)}, u32[]{:S(2)}) %collective-permute-start.12) | collective-permute-done | bytes 262176 | tf_op jit(solution)/shard_map/gradient_rows/ppermute | solution.py:633
  129.3 0.0 collective-permute-done.13.even
  129.3 0.7 copy-done.1
  130.0 0.0 all-to-all-done.1.mine
  130.0 2.1 %collective-permute-start.14 = (f32[16,64,128]{2,1,0:T(8,128)S(1)}, f32[16,64,128]{2,1,0:T(8,128)S(1)}, u32[]{:S(2)}, u32[]{:S(2)}) collective-permute-start(f32[16,64,128]{2,1,0:T(8,128)S(1)} %all-to-all-done.1.mine), channel_id=1, source_target_pairs={{0,1},{1,0},{2,3},{3,2},{4,5},{5,4},{6,7},{7,6},{8,9},{9,8},{10,11... | collective-permute-start | bytes 1572872 | tf_op jit(solution)/shard_map/probe_gather/ppermute | solution.py:637
  132.1 0.6 copy.12
  132.8 0.9 copy-done.2
  133.7 1.0 shard_map.104
  134.7 0.0 collective-permute-done.14.other
  134.7 1.1 probe_gather.1
  (9 shorter events, 0.1 us)
Async XLA Ops:
  0.6 42.7 %copy-start.10 = (bf16[256,768]{1,0:T(8,128)(2,1)S(1)}, bf16[256,768]{1,0:T(8,128)(2,1)}, u32[]{:S(2)}) copy-start(bf16[256,768]{1,0:T(8,128)(2,1)} %constant.18.clone.rows) | copy-start | bytes 1179652
  34.4 15.4 %collective-permute-start = (f32[2,136,256]{2,1,0:T(8,128)}, f32[2,136,256]{2,1,0:T(8,128)S(1)}, u32[]{:S(2)}, u32[]{:S(2)}) collective-permute-start(f32[2,136,256]{2,1,0:T(8,128)} %get-tuple-element.37), channel_id=1, source_target_pairs={{16,32},{32,16},{48,64},{64,48},{80,96},{96,80},{17,33},{33,17},{4... | collective-permute-start | bytes 835592 | tf_op jit(solution)/shard_map/object_halo/ppermute | solution.py:633
  39.6 10.2 %collective-permute-start.1 = (f32[2,136,256]{2,1,0:T(8,128)}, f32[2,136,256]{2,1,0:T(8,128)S(1)}, u32[]{:S(2)}, u32[]{:S(2)}) collective-permute-start(f32[2,136,256]{2,1,0:T(8,128)} %get-tuple-element.38), channel_id=1, source_target_pairs={{0,16},{16,0},{32,48},{48,32},{64,80},{80,64},{96,112},{112,96},{1... | collective-permute-start | bytes 835592 | tf_op jit(solution)/shard_map/object_halo/ppermute | solution.py:633
  39.7 10.1 %collective-permute-start.2 = (f32[2,264,128]{2,1,0:T(8,128)}, f32[2,264,128]{2,1,0:T(8,128)S(1)}, u32[]{:S(2)}, u32[]{:S(2)}) collective-permute-start(f32[2,264,128]{2,1,0:T(8,128)} %get-tuple-element.39), channel_id=1, source_target_pairs={{1,2},{2,1},{3,4},{4,3},{5,6},{6,5},{7,8},{8,7},{9,10},{10,9},{11,... | collective-permute-start | bytes 811016 | tf_op jit(solution)/shard_map/object_halo/ppermute | solution.py:637
  43.2 6.6 %collective-permute-start.3 = (f32[2,264,128]{2,1,0:T(8,128)}, f32[2,264,128]{2,1,0:T(8,128)S(1)}, u32[]{:S(2)}, u32[]{:S(2)}) collective-permute-start(f32[2,264,128]{2,1,0:T(8,128)} %get-tuple-element.40), channel_id=1, source_target_pairs={{0,1},{1,0},{2,3},{3,2},{4,5},{5,4},{6,7},{7,6},{8,9},{9,8},{10,11... | collective-permute-start | bytes 811016 | tf_op jit(solution)/shard_map/object_halo/ppermute | solution.py:637
  43.3 1.2 copy-start.4
  44.5 1.0 copy-start.11
  45.5 15.2 %copy-start.5 = (f32[2,2,256,256]{3,2,1,0:T(8,128)S(1)}, f32[2,2,256,256]{3,2,1,0:T(8,128)}, u32[]{:S(2)}) copy-start(f32[2,2,256,256]{3,2,1,0:T(8,128)} %probe.1) | copy-start | bytes 3145732
  45.5 15.2 %copy-start.9 = (bf16[2,2,2,256,256]{4,3,2,1,0:T(8,128)(2,1)S(1)}, bf16[2,2,2,256,256]{4,3,2,1,0:T(8,128)(2,1)}, u32[]{:S(2)}) copy-start(bf16[2,2,2,256,256]{4,3,2,1,0:T(8,128)(2,1)} %constant.19.clone.matrices) | copy-start | bytes 3145732
  49.8 10.9 %copy-start = (f32[2,256,256]{2,1,0:T(8,128)S(1)}, f32[2,256,256]{2,1,0:T(8,128)}, u32[]{:S(2)}) copy-start(f32[2,256,256]{2,1,0:T(8,128)} %own.3) | copy-start | bytes 1572868
  49.9 10.9 %copy-start.3 = (s32[1,1,4,2]{2,3,1,0:T(2,128)S(1)}, s32[1,1,4,2]{2,3,1,0:T(2,128)}, u32[]{:S(2)}) copy-start(s32[1,1,4,2]{2,3,1,0:T(2,128)} %param.10) | copy-start | bytes 100
  49.9 4.4 %collective-permute-start.5 = (f32[2,2,136,128]{3,2,1,0:T(8,128)S(1)}, f32[2,2,136,128]{3,2,1,0:T(8,128)S(1)}, u32[]{:S(2)}, u32[]{:S(2)}) collective-permute-start(f32[2,2,136,128]{3,2,1,0:T(8,128)S(1)} %get-tuple-element.78), channel_id=1, source_target_pairs={{0,1},{1,0},{2,3},{3,2},{4,5},{5,4},{6,7},{7,6},{8,9},{9,8},{10,11... | collective-permute-start | bytes 835592 | tf_op jit(solution)/shard_map/object_corners/ppermute | solution.py:637
  50.9 9.8 %collective-permute-start.4 = (f32[2,2,136,128]{3,2,1,0:T(8,128)S(1)}, f32[2,2,136,128]{3,2,1,0:T(8,128)S(1)}, u32[]{:S(2)}, u32[]{:S(2)}) collective-permute-start(f32[2,2,136,128]{3,2,1,0:T(8,128)S(1)} %get-tuple-element.79), channel_id=1, source_target_pairs={{1,2},{2,1},{3,4},{4,3},{5,6},{6,5},{7,8},{8,7},{9,10},{10,9},{11,... | collective-permute-start | bytes 835592 | tf_op jit(solution)/shard_map/object_corners/ppermute | solution.py:637
  74.9 4.6 %collective-permute-start.6 = (f32[16,88,128]{2,1,0:T(8,128)S(1)}, f32[16,88,128]{2,1,0:T(8,128)S(1)}, u32[]{:S(2)}, u32[]{:S(2)}) collective-permute-start(f32[16,88,128]{2,1,0:T(8,128)S(1)} %get-tuple-element.48), channel_id=1, source_target_pairs={{0,1},{1,0},{2,3},{3,2},{4,5},{5,4},{6,7},{7,6},{8,9},{9,8},{10,11... | collective-permute-start | bytes 2162696 | tf_op jit(solution)/shard_map/probe_reduce/ppermute | solution.py:637
  75.0 16.4 %collective-permute-start.7 = (f32[2,512,128]{2,1,0:T(8,128)}, f32[2,512,128]{2,1,0:T(8,128)S(1)}, u32[]{:S(2)}, u32[]{:S(2)}) collective-permute-start(f32[2,512,128]{2,1,0:T(8,128)} %get-tuple-element.54), channel_id=1, source_target_pairs={{1,2},{2,1},{3,4},{4,3},{5,6},{6,5},{7,8},{8,7},{9,10},{10,9},{11,... | collective-permute-start | bytes 1572872 | tf_op jit(solution)/shard_map/gradient_columns/ppermute | solution.py:637
  79.4 12.0 %collective-permute-start.8 = (f32[2,512,128]{2,1,0:T(8,128)}, f32[2,512,128]{2,1,0:T(8,128)S(1)}, u32[]{:S(2)}, u32[]{:S(2)}) collective-permute-start(f32[2,512,128]{2,1,0:T(8,128)} %get-tuple-element.55), channel_id=1, source_target_pairs={{0,1},{1,0},{2,3},{3,2},{4,5},{5,4},{6,7},{7,6},{8,9},{9,8},{10,11... | collective-permute-start | bytes 1572872 | tf_op jit(solution)/shard_map/gradient_columns/ppermute | solution.py:637
  80.5 20.4 %all-to-all-start = ((f32[16,88,128]{2,1,0:T(8,128)}), f32[16,88,128]{2,1,0:T(8,128)S(1)}, u32[]{:S(2)}, u32[]{:S(2)}) async-start(f32[16,88,128]{2,1,0:T(8,128)} %add.3), calls=%async_computation | async-start | bytes 1441792 | tf_op jit(solution)/shard_map/probe_reduce/all_to_all | solution.py:691
  89.7 3.2 %copy-start.6 = (f32[2,2,256,256]{3,2,1,0:T(8,128)S(1)}, f32[2,2,256,256]{3,2,1,0:T(8,128)}, u32[]{:S(2)}) copy-start(f32[2,2,256,256]{3,2,1,0:T(8,128)} %probe.1) | copy-start | bytes 3145732
  92.2 0.7 copy-start.7
  100.9 3.6 %collective-permute-start.11 = (f32[88,128]{1,0:T(8,128)S(1)}, f32[88,128]{1,0:T(8,128)S(1)}, u32[]{:S(2)}, u32[]{:S(2)}) collective-permute-start(f32[88,128]{1,0:T(8,128)S(1)} %probe_sum.2.own), channel_id=1, source_target_pairs={{0,66},{1,67},{2,0},{3,1},{4,70},{5,71},{6,4},{7,5},{8,74},{9,75},... | collective-permute-start | bytes 135176 | tf_op jit(solution)/shard_map/probe_sum/ppermute | solution.py:647
  103.4 4.5 %collective-permute-start.10 = (f32[88,128]{1,0:T(8,128)S(1)}, f32[88,128]{1,0:T(8,128)S(1)}, u32[]{:S(2)}, u32[]{:S(2)}) collective-permute-start(f32[88,128]{1,0:T(8,128)S(1)} %probe_sum.2.own), channel_id=1, source_target_pairs={{0,64},{1,65},{2,66},{3,67},{4,68},{5,69},{6,70},{7,71},{8,72},{9,... | collective-permute-start | bytes 135176 | tf_op jit(solution)/shard_map/probe_sum/ppermute | solution.py:647
  103.4 4.6 %collective-permute-start.9 = (f32[88,128]{1,0:T(8,128)S(1)}, f32[88,128]{1,0:T(8,128)S(1)}, u32[]{:S(2)}, u32[]{:S(2)}) collective-permute-start(f32[88,128]{1,0:T(8,128)S(1)} %probe_sum.2.own), channel_id=1, source_target_pairs={{0,2},{1,3},{2,64},{3,65},{4,6},{5,7},{6,68},{7,69},{8,10},{9,11},... | collective-permute-start | bytes 135176 | tf_op jit(solution)/shard_map/probe_sum/ppermute | solution.py:647
  108.8 9.2 %copy-start.8 = (f32[2,128,256]{2,1,0:T(8,128)S(1)}, f32[2,128,256]{2,1,0:T(8,128)}, u32[]{:S(2)}) copy-start(f32[2,128,256]{2,1,0:T(8,128)} %copy-done.7) | copy-start | bytes 786436
  108.8 21.2 %all-to-all-start.1 = ((f32[16,64,128]{2,1,0:T(8,128)}), f32[16,64,128]{2,1,0:T(8,128)S(1)}, u32[]{:S(2)}, u32[]{:S(2)}) async-start(f32[16,64,128]{2,1,0:T(8,128)} %get-tuple-element.59), calls=%async_computation.1 | async-start | bytes 1048576 | tf_op jit(solution)/shard_map/probe_gather/all_to_all | solution.py:707
  114.6 14.7 %collective-permute-start.12 = (f32[2,128,256]{2,1,0:T(8,128)}, f32[2,128,256]{2,1,0:T(8,128)S(1)}, u32[]{:S(2)}, u32[]{:S(2)}) collective-permute-start(f32[2,128,256]{2,1,0:T(8,128)} %get-tuple-element.60), channel_id=1, source_target_pairs={{16,32},{32,16},{48,64},{64,48},{80,96},{96,80},{17,33},{33,17},{4... | collective-permute-start | bytes 786440 | tf_op jit(solution)/shard_map/gradient_rows/ppermute | solution.py:633
  118.0 11.3 %collective-permute-start.13 = (f32[2,128,256]{2,1,0:T(8,128)S(1)}, f32[2,128,256]{2,1,0:T(8,128)S(1)}, u32[]{:S(2)}, u32[]{:S(2)}) collective-permute-start(f32[2,128,256]{2,1,0:T(8,128)S(1)} %copy-done.8), channel_id=1, source_target_pairs={{0,16},{16,0},{32,48},{48,32},{64,80},{80,64},{96,112},{112,96},{1... | collective-permute-start | bytes 786440 | tf_op jit(solution)/shard_map/gradient_rows/ppermute | solution.py:633
  129.3 0.7 copy-start.1
  130.0 4.7 %collective-permute-start.14 = (f32[16,64,128]{2,1,0:T(8,128)S(1)}, f32[16,64,128]{2,1,0:T(8,128)S(1)}, u32[]{:S(2)}, u32[]{:S(2)}) collective-permute-start(f32[16,64,128]{2,1,0:T(8,128)S(1)} %all-to-all-done.1.mine), channel_id=1, source_target_pairs={{0,1},{1,0},{2,3},{3,2},{4,5},{5,4},{6,7},{7,6},{8,9},{9,8},{10,11... | collective-permute-start | bytes 1572872 | tf_op jit(solution)/shard_map/probe_gather/ppermute | solution.py:637
  132.8 0.9 copy-start.2

commit v12 on v9

--- a/solution.py
+++ b/solution.py
@@ -615,7 +615,7 @@
 
 def update(arrays):
     shape = arrays[0].shape
-    return simple(update_kernel, [], arrays, shape, [shape], 1 << 20, 3 << 20)
+    return simple(update_kernel, [], arrays, shape, [shape], 16 << 30, 3 << 20)
 
 
 def assemble(mine, other):
@@ -705,12 +705,13 @@
 
     with jax.named_scope("probe_gather"):
         gathered = lax.all_to_all(spread_out, AXES, 0, 0, axis_index_groups=groups, tiled=True)
-        gathered, odd, even = lax.optimization_barrier((gathered, odd, even))
+        object_update = update([center, even, odd, cross, same, light])
+        relative_error = ratio[0, :1]
+        position_step = steps[:, 0].reshape(1, 1, -1, 2)
+        tied = (gathered, object_update, relative_error, position_step)
+        gathered, object_update, relative_error, position_step = lax.optimization_barrier(tied)
         probe_update = assemble(gathered, swap_columns(gathered, 0)).reshape(probe.shape)
 
-    object_update = update([center, even, odd, cross, same, light])
-    relative_error = ratio[0, :1]
-    position_step = steps[:, 0].reshape(1, 1, -1, 2)
     return (object_update, probe_update, position_step, relative_error)
 
 

time: 106 us -> 109 us (1.028)
  the two profiles are of different devices: /device:TPU:25 before, /device:TPU:1 now
where the time goes in v12:
time: 109 us
  starting transfers between devices  38.8 us (36%)
  waiting for transfers between devices  38.3 us (35%)
  Pallas kernels  21.3 us (20%)
  local copies, waits for them, and re-layouts  8.41 us (8%)
    ppermute x8, waiting for transfers between devices, swap_columns(): return lax.ppermute(value, 'col', pairs_from(first, lax.axis_size('col')))  19.8 us
    ppermute x8, starting transfers between devices, swap_columns(): return lax.ppermute(value, 'col', pairs_from(first, lax.axis_size('col')))  15.7 us
    pallas_call x1, Pallas kernels, transforms(): pl.pallas_call(transform_kernel, out_shape=shaped([halves, halves]) + [ja...  14.2 us
    all_to_all x1, waiting for transfers between devices, local(): lax.all_to_all(spread_out, AXES, 0, 0, axis_index_groups=groups, tiled=True)  9.57 us
    unnamed x29, local copies, waits for them, and re-layouts  7.7 us
    all_to_all x1, starting transfers between devices, local(): lax.all_to_all(spread_out, AXES, 0, 0, axis_index_groups=groups, tiled=True)  6.79 us
    ppermute x3, waiting for transfers between devices, along_z(): return lax.ppermute(value, AXES, pairs)  6.47 us
    pallas_call x7, Pallas kernels, simple(): return call(*scalars, *arrays)  6.39 us
  transfers between devices with their start and end apart: 17, of which 8 were waited for; matrix products, arithmetic and copies ran while one was open for 2% of the time, Pallas kernels for 5%

profile of v12, /device:TPU:1, one launch (start us, length us, event | category | flops | bytes accessed | tf_op | source)
XLA Modules:
  0.0 108.7 jit_solution(13634741072788296631)
XLA Ops:
  0.6 0.0 copy-start.2
  0.6 0.7 copy-done.2
  1.3 1.0 copy-done
  2.4 0.8 object_halo.1
  3.1 0.7 collective-permute-start
  3.8 4.7 %collective-permute-start.1 = (f32[2,136,256]{2,1,0:T(8,128)S(1)}, f32[2,136,256]{2,1,0:T(8,128)S(1)}, u32[]{:S(2)}, u32[]{:S(2)}) collective-permute-start(f32[2,136,256]{2,1,0:T(8,128)S(1)} %get-tuple-element.37), channel_id=1, source_target_pairs={{0,16},{16,0},{32,48},{48,32},{64,80},{80,64},{96,112},{112,96},{1... | collective-permute-start | bytes 835592 | tf_op jit(solution)/shard_map/object_halo/ppermute | solution.py:633
  8.5 4.7 %collective-permute-start.2 = (f32[2,264,128]{2,1,0:T(8,128)S(1)}, f32[2,264,128]{2,1,0:T(8,128)S(1)}, u32[]{:S(2)}, u32[]{:S(2)}) collective-permute-start(f32[2,264,128]{2,1,0:T(8,128)S(1)} %get-tuple-element.38), channel_id=1, source_target_pairs={{1,2},{2,1},{3,4},{4,3},{5,6},{6,5},{7,8},{8,7},{9,10},{10,9},{11,... | collective-permute-start | bytes 811016 | tf_op jit(solution)/shard_map/object_halo/ppermute | solution.py:637
  13.2 0.1 collective-permute-start.3
  13.3 0.0 copy-start.3
  13.3 1.2 %copy-done.3 = f32[1,1,4,256,256]{4,3,2,1,0:T(8,128)S(1)} copy-done((f32[1,1,4,256,256]{4,3,2,1,0:T(8,128)S(1)}, f32[1,1,4,256,256]{4,3,2,1,0:T(8,128)}, u32[]{:S(2)}) %copy-start.3) | copy-done | bytes 1048600
  14.5 1.0 copy-done.8
  15.5 1.0 copy-done.9
  16.5 1.3 %shard_map.102.measured = f32[4,256,256]{2,1,0:T(8,128)S(1)} custom-call(f32[4,256,256]{2,1,0:T(8,128)S(1)} %bitcast.13, bf16[768,256]{1,0:T(8,128)(2,1)S(1)} %copy-done.9, bf16[256,768]{1,0:T(8,128)(2,1)S(1)} %copy-done.8), custom_call_target="tpu_custom_call" | custom-call | flops 1073741824 | bytes 3145728 | tf_op jit(solution)/shard_map/pallas_call | solution.py:540
  17.8 6.0 %collective-permute-done.2.cross = f32[2,264,128]{2,1,0:T(8,128)S(1)} collective-permute-done((f32[2,264,128]{2,1,0:T(8,128)S(1)}, f32[2,264,128]{2,1,0:T(8,128)S(1)}, u32[]{:S(2)}, u32[]{:S(2)}) %collective-permute-start.2) | collective-permute-done | bytes 270368 | tf_op jit(solution)/shard_map/object_halo/ppermute | solution.py:637
  23.8 0.0 collective-permute-done.3.same
  23.8 0.0 collective-permute-done.odd_strip
  23.8 0.0 collective-permute-done.1.even_strip
  23.8 0.0 copy-start.1
  23.9 0.1 collective-permute-start.5
  24.0 4.4 %collective-permute-start.4 = (f32[2,2,136,128]{3,2,1,0:T(8,128)S(1)}, f32[2,2,136,128]{3,2,1,0:T(8,128)S(1)}, u32[]{:S(2)}, u32[]{:S(2)}) collective-permute-start(f32[2,2,136,128]{3,2,1,0:T(8,128)S(1)} %get-tuple-element.77), channel_id=1, source_target_pairs={{1,2},{2,1},{3,4},{4,3},{5,6},{6,5},{7,8},{8,7},{9,10},{10,9},{11,... | collective-permute-start | bytes 835592 | tf_op jit(solution)/shard_map/object_corners/ppermute | solution.py:637
  28.4 0.0 collective-permute-done.5.same_corner
  28.4 6.4 %collective-permute-done.4.cross_corner = f32[2,2,136,128]{3,2,1,0:T(8,128)S(1)} collective-permute-done((f32[2,2,136,128]{3,2,1,0:T(8,128)S(1)}, f32[2,2,136,128]{3,2,1,0:T(8,128)S(1)}, u32[]{:S(2)}, u32[]{:S(2)}) %collective-permute-start.4) | collective-permute-done | bytes 278560 | tf_op jit(solution)/shard_map/object_corners/ppermute | solution.py:637
  34.8 0.0 copy-done.4
  34.8 0.0 copy-done.7
  34.8 0.0 copy-done.1
  34.9 14.2 %shard_map.103 = (f32[16,88,128]{2,1,0:T(8,128)S(1)}, f32[16,88,128]{2,1,0:T(8,128)S(1)}, s32[8,128]{1,0:T(8,128)S(1)}, f32[2,256,256]{2,1,0:T(8,128)S(1)}, f32[...) custom-call(s32[2,4]{1,0:T(2,128)S(1)} %bitcast.11, ...), custom_call_target="tpu_custom_call" | custom-call | flops 13958643712 | bytes 12582912 | tf_op jit(solution)/shard_map/pallas_call | solution.py:585
  49.0 0.0 copy-start.12
  49.0 0.1 collective-permute-start.6
  49.1 4.4 %collective-permute-start.7 = (f32[2,512,128]{2,1,0:T(8,128)}, f32[2,512,128]{2,1,0:T(8,128)S(1)}, u32[]{:S(2)}, u32[]{:S(2)}) collective-permute-start(f32[2,512,128]{2,1,0:T(8,128)} %get-tuple-element.52), channel_id=1, source_target_pairs={{1,2},{2,1},{3,4},{4,3},{5,6},{6,5},{7,8},{8,7},{9,10},{10,9},{11,... | collective-permute-start | bytes 1572872 | tf_op jit(solution)/shard_map/gradient_columns/ppermute | solution.py:637
  53.6 0.1 collective-permute-start.8
  53.7 0.0 collective-permute-done.6
  53.7 0.9 add.3
  54.6 0.0 copy-done.12
  54.6 4.5 %all-to-all-start = ((f32[16,88,128]{2,1,0:T(8,128)}), f32[16,88,128]{2,1,0:T(8,128)S(1)}, u32[]{:S(2)}, u32[]{:S(2)}) async-start(f32[16,88,128]{2,1,0:T(8,128)} %add.3), calls=%async_computation | async-start | bytes 1441792 | tf_op jit(solution)/shard_map/probe_reduce/all_to_all | solution.py:691
  59.2 6.4 %collective-permute-done.7.cross = f32[2,512,128]{2,1,0:T(8,128)S(1)} collective-permute-done((f32[2,512,128]{2,1,0:T(8,128)}, f32[2,512,128]{2,1,0:T(8,128)S(1)}, u32[]{:S(2)}, u32[]{:S(2)}) %collective-permute-start.7) | collective-permute-done | bytes 524320 | tf_op jit(solution)/shard_map/gradient_columns/ppermute | solution.py:637
  65.6 0.0 collective-permute-done.8.same
  65.6 0.1 gradient_rows.3
  65.7 0.0 copy-start.5
  65.7 0.7 copy-done.5
  66.4 0.7 copy-done.6
  67.1 2.1 %gradient_rows.2.light = f32[256,256]{1,0:T(8,128)S(1)} custom-call(s32[2,4]{1,0:T(2,128)S(1)} %bitcast.12, s32[8,128]{1,0:T(8,128)S(1)} %get-tuple-element.49.around, f32[2,2,256,256]{3,2,1,0:T(8,128)S(1)} %copy-done.4), custom_call_target="tpu_custom_call" | custom-call | flops 2147483648 | bytes 4194304 | tf_op jit(solution)/shard_map/gradient_rows/pallas_call | solution.py:540
  69.2 0.7 copy-done.10
  69.9 2.4 %all-to-all-done.chunk = f32[16,88,128]{2,1,0:T(8,128)S(1)} async-done(((f32[16,88,128]{2,1,0:T(8,128)}), f32[16,88,128]{2,1,0:T(8,128)S(1)}, u32[]{:S(2)}, u32[]{:S(2)}) %all-to-all-start) | async-done | bytes 720928 | tf_op jit(solution)/shard_map/probe_reduce/all_to_all | solution.py:691
  72.4 0.0 collective-permute-start.12
  72.4 0.7 collective-permute-start.13
  73.1 4.7 %collective-permute-start.11 = (f32[88,128]{1,0:T(8,128)S(1)}, f32[88,128]{1,0:T(8,128)S(1)}, u32[]{:S(2)}, u32[]{:S(2)}) collective-permute-start(f32[88,128]{1,0:T(8,128)S(1)} %probe_sum.2.own), channel_id=1, source_target_pairs={{0,66},{1,67},{2,0},{3,1},{4,70},{5,71},{6,4},{7,5},{8,74},{9,75},... | collective-permute-start | bytes 135176 | tf_op jit(solution)/shard_map/probe_sum/ppermute | solution.py:647
  77.8 0.2 collective-permute-start.10
  78.0 0.8 collective-permute-start.9
  78.8 0.1 slice_reduce_fusion
  78.9 0.1 squeeze.15
  79.0 0.0 collective-permute-done.11.third
  79.0 3.3 %collective-permute-done.10.second = f32[88,128]{1,0:T(8,128)S(1)} collective-permute-done((f32[88,128]{1,0:T(8,128)S(1)}, f32[88,128]{1,0:T(8,128)S(1)}, u32[]{:S(2)}, u32[]{:S(2)}) %collective-permute-start.10) | collective-permute-done | bytes 45088 | tf_op jit(solution)/shard_map/probe_sum/ppermute | solution.py:647
  82.3 3.1 %collective-permute-done.9.first = f32[88,128]{1,0:T(8,128)S(1)} collective-permute-done((f32[88,128]{1,0:T(8,128)S(1)}, f32[88,128]{1,0:T(8,128)S(1)}, u32[]{:S(2)}, u32[]{:S(2)}) %collective-permute-start.9) | collective-permute-done | bytes 45088 | tf_op jit(solution)/shard_map/probe_sum/ppermute | solution.py:647
  85.5 0.9 probe_sum.3
  86.3 0.5 slice.16
  86.9 6.8 %all-to-all-start.1 = ((f32[16,64,128]{2,1,0:T(8,128)}), f32[16,64,128]{2,1,0:T(8,128)S(1)}, u32[]{:S(2)}, u32[]{:S(2)}) async-start(f32[16,64,128]{2,1,0:T(8,128)} %get-tuple-element.57), calls=%async_computation.1 | async-start | bytes 1048576 | tf_op jit(solution)/shard_map/probe_gather/all_to_all | solution.py:707
  93.7 0.0 collective-permute-done.12.even
  93.7 0.0 collective-permute-done.13.odd
  93.7 1.0 probe_gather.2
  94.7 9.6 %all-to-all-done.1.mine = f32[16,64,128]{2,1,0:T(8,128)S(1)} async-done(((f32[16,64,128]{2,1,0:T(8,128)}), f32[16,64,128]{2,1,0:T(8,128)S(1)}, u32[]{:S(2)}, u32[]{:S(2)}) %all-to-all-start.1) | async-done | bytes 524320 | tf_op jit(solution)/shard_map/probe_gather/all_to_all | solution.py:707
  104.2 1.9 %collective-permute-start.14 = (f32[16,64,128]{2,1,0:T(8,128)S(1)}, f32[16,64,128]{2,1,0:T(8,128)S(1)}, u32[]{:S(2)}, u32[]{:S(2)}) collective-permute-start(f32[16,64,128]{2,1,0:T(8,128)S(1)} %all-to-all-done.1.mine), channel_id=1, source_target_pairs={{0,1},{1,0},{2,3},{3,2},{4,5},{5,4},{6,7},{7,6},{8,9},{9,8},{10,11... | collective-permute-start | bytes 1572872 | tf_op jit(solution)/shard_map/probe_gather/ppermute | solution.py:637
  106.1 0.6 copy.12
  106.8 0.9 collective-permute-done.14.other
  107.7 1.1 probe_gather.3
  (13 shorter events, 0.1 us)
Async XLA Ops:
  0.6 0.7 copy-start.2
  1.3 1.0 copy-start
  3.1 20.7 %collective-permute-start = (f32[2,136,256]{2,1,0:T(8,128)S(1)}, f32[2,136,256]{2,1,0:T(8,128)S(1)}, u32[]{:S(2)}, u32[]{:S(2)}) collective-permute-start(f32[2,136,256]{2,1,0:T(8,128)S(1)} %get-tuple-element.36), channel_id=1, source_target_pairs={{16,32},{32,16},{48,64},{64,48},{80,96},{96,80},{17,33},{33,17},{4... | collective-permute-start | bytes 835592 | tf_op jit(solution)/shard_map/object_halo/ppermute | solution.py:633
  3.8 20.0 %collective-permute-start.1 = (f32[2,136,256]{2,1,0:T(8,128)S(1)}, f32[2,136,256]{2,1,0:T(8,128)S(1)}, u32[]{:S(2)}, u32[]{:S(2)}) collective-permute-start(f32[2,136,256]{2,1,0:T(8,128)S(1)} %get-tuple-element.37), channel_id=1, source_target_pairs={{0,16},{16,0},{32,48},{48,32},{64,80},{80,64},{96,112},{112,96},{1... | collective-permute-start | bytes 835592 | tf_op jit(solution)/shard_map/object_halo/ppermute | solution.py:633
  8.5 15.3 %collective-permute-start.2 = (f32[2,264,128]{2,1,0:T(8,128)S(1)}, f32[2,264,128]{2,1,0:T(8,128)S(1)}, u32[]{:S(2)}, u32[]{:S(2)}) collective-permute-start(f32[2,264,128]{2,1,0:T(8,128)S(1)} %get-tuple-element.38), channel_id=1, source_target_pairs={{1,2},{2,1},{3,4},{4,3},{5,6},{6,5},{7,8},{8,7},{9,10},{10,9},{11,... | collective-permute-start | bytes 811016 | tf_op jit(solution)/shard_map/object_halo/ppermute | solution.py:637
  13.2 10.6 %collective-permute-start.3 = (f32[2,264,128]{2,1,0:T(8,128)S(1)}, f32[2,264,128]{2,1,0:T(8,128)S(1)}, u32[]{:S(2)}, u32[]{:S(2)}) collective-permute-start(f32[2,264,128]{2,1,0:T(8,128)S(1)} %get-tuple-element.39), channel_id=1, source_target_pairs={{0,1},{1,0},{2,3},{3,2},{4,5},{5,4},{6,7},{7,6},{8,9},{9,8},{10,11... | collective-permute-start | bytes 811016 | tf_op jit(solution)/shard_map/object_halo/ppermute | solution.py:637
  13.3 1.2 %copy-start.3 = (f32[1,1,4,256,256]{4,3,2,1,0:T(8,128)S(1)}, f32[1,1,4,256,256]{4,3,2,1,0:T(8,128)}, u32[]{:S(2)}) copy-start(f32[1,1,4,256,256]{4,3,2,1,0:T(8,128)} %param.9) | copy-start | bytes 3145732
  14.5 1.0 copy-start.8
  15.5 1.0 copy-start.9
  16.5 18.3 %copy-start.4 = (f32[2,2,256,256]{3,2,1,0:T(8,128)S(1)}, f32[2,2,256,256]{3,2,1,0:T(8,128)}, u32[]{:S(2)}) copy-start(f32[2,2,256,256]{3,2,1,0:T(8,128)} %probe.1) | copy-start | bytes 3145732
  16.5 18.3 %copy-start.7 = (bf16[2,2,2,256,256]{4,3,2,1,0:T(8,128)(2,1)S(1)}, bf16[2,2,2,256,256]{4,3,2,1,0:T(8,128)(2,1)}, u32[]{:S(2)}) copy-start(bf16[2,2,2,256,256]{4,3,2,1,0:T(8,128)(2,1)} %constant.19.clone.matrices) | copy-start | bytes 3145732
  23.8 11.0 %copy-start.1 = (f32[2,256,256]{2,1,0:T(8,128)S(1)}, f32[2,256,256]{2,1,0:T(8,128)}, u32[]{:S(2)}) copy-start(f32[2,256,256]{2,1,0:T(8,128)} %own.3) | copy-start | bytes 1572868
  23.9 4.5 %collective-permute-start.5 = (f32[2,2,136,128]{3,2,1,0:T(8,128)S(1)}, f32[2,2,136,128]{3,2,1,0:T(8,128)S(1)}, u32[]{:S(2)}, u32[]{:S(2)}) collective-permute-start(f32[2,2,136,128]{3,2,1,0:T(8,128)S(1)} %get-tuple-element.76), channel_id=1, source_target_pairs={{0,1},{1,0},{2,3},{3,2},{4,5},{5,4},{6,7},{7,6},{8,9},{9,8},{10,11... | collective-permute-start | bytes 835592 | tf_op jit(solution)/shard_map/object_corners/ppermute | solution.py:637
  24.0 10.9 %collective-permute-start.4 = (f32[2,2,136,128]{3,2,1,0:T(8,128)S(1)}, f32[2,2,136,128]{3,2,1,0:T(8,128)S(1)}, u32[]{:S(2)}, u32[]{:S(2)}) collective-permute-start(f32[2,2,136,128]{3,2,1,0:T(8,128)S(1)} %get-tuple-element.77), channel_id=1, source_target_pairs={{1,2},{2,1},{3,4},{4,3},{5,6},{6,5},{7,8},{8,7},{9,10},{10,9},{11,... | collective-permute-start | bytes 835592 | tf_op jit(solution)/shard_map/object_corners/ppermute | solution.py:637
  49.0 5.6 %copy-start.12 = (f32[2,256,256]{2,1,0:T(8,128)}, f32[2,256,256]{2,1,0:T(8,128)S(1)}, u32[]{:S(2)}) copy-start(f32[2,256,256]{2,1,0:T(8,128)S(1)} %get-tuple-element.58.center) | copy-start | bytes 1572868
  49.0 4.6 %collective-permute-start.6 = (f32[16,88,128]{2,1,0:T(8,128)S(1)}, f32[16,88,128]{2,1,0:T(8,128)S(1)}, u32[]{:S(2)}, u32[]{:S(2)}) collective-permute-start(f32[16,88,128]{2,1,0:T(8,128)S(1)} %get-tuple-element.46), channel_id=1, source_target_pairs={{0,1},{1,0},{2,3},{3,2},{4,5},{5,4},{6,7},{7,6},{8,9},{9,8},{10,11... | collective-permute-start | bytes 2162696 | tf_op jit(solution)/shard_map/probe_reduce/ppermute | solution.py:637
  49.1 16.5 %collective-permute-start.7 = (f32[2,512,128]{2,1,0:T(8,128)}, f32[2,512,128]{2,1,0:T(8,128)S(1)}, u32[]{:S(2)}, u32[]{:S(2)}) collective-permute-start(f32[2,512,128]{2,1,0:T(8,128)} %get-tuple-element.52), channel_id=1, source_target_pairs={{1,2},{2,1},{3,4},{4,3},{5,6},{6,5},{7,8},{8,7},{9,10},{10,9},{11,... | collective-permute-start | bytes 1572872 | tf_op jit(solution)/shard_map/gradient_columns/ppermute | solution.py:637
  53.6 12.0 %collective-permute-start.8 = (f32[2,512,128]{2,1,0:T(8,128)}, f32[2,512,128]{2,1,0:T(8,128)S(1)}, u32[]{:S(2)}, u32[]{:S(2)}) collective-permute-start(f32[2,512,128]{2,1,0:T(8,128)} %get-tuple-element.53), channel_id=1, source_target_pairs={{0,1},{1,0},{2,3},{3,2},{4,5},{5,4},{6,7},{7,6},{8,9},{9,8},{10,11... | collective-permute-start | bytes 1572872 | tf_op jit(solution)/shard_map/gradient_columns/ppermute | solution.py:637
  54.6 17.7 %all-to-all-start = ((f32[16,88,128]{2,1,0:T(8,128)}), f32[16,88,128]{2,1,0:T(8,128)S(1)}, u32[]{:S(2)}, u32[]{:S(2)}) async-start(f32[16,88,128]{2,1,0:T(8,128)} %add.3), calls=%async_computation | async-start | bytes 1441792 | tf_op jit(solution)/shard_map/probe_reduce/all_to_all | solution.py:691
  65.7 0.7 copy-start.5
  66.4 0.7 copy-start.6
  69.2 0.7 copy-start.10
  72.4 21.3 %collective-permute-start.12 = (f32[2,128,256]{2,1,0:T(8,128)}, f32[2,128,256]{2,1,0:T(8,128)S(1)}, u32[]{:S(2)}, u32[]{:S(2)}) collective-permute-start(f32[2,128,256]{2,1,0:T(8,128)} %copy-done.6), channel_id=1, source_target_pairs={{0,16},{16,0},{32,48},{48,32},{64,80},{80,64},{96,112},{112,96},{1... | collective-permute-start | bytes 786440 | tf_op jit(solution)/shard_map/gradient_rows/ppermute | solution.py:633
  72.4 21.3 %collective-permute-start.13 = (f32[2,128,256]{2,1,0:T(8,128)}, f32[2,128,256]{2,1,0:T(8,128)S(1)}, u32[]{:S(2)}, u32[]{:S(2)}) collective-permute-start(f32[2,128,256]{2,1,0:T(8,128)} %copy-done.5), channel_id=1, source_target_pairs={{16,32},{32,16},{48,64},{64,48},{80,96},{96,80},{17,33},{33,17},{4... | collective-permute-start | bytes 786440 | tf_op jit(solution)/shard_map/gradient_rows/ppermute | solution.py:633
  73.1 5.9 %collective-permute-start.11 = (f32[88,128]{1,0:T(8,128)S(1)}, f32[88,128]{1,0:T(8,128)S(1)}, u32[]{:S(2)}, u32[]{:S(2)}) collective-permute-start(f32[88,128]{1,0:T(8,128)S(1)} %probe_sum.2.own), channel_id=1, source_target_pairs={{0,66},{1,67},{2,0},{3,1},{4,70},{5,71},{6,4},{7,5},{8,74},{9,75},... | collective-permute-start | bytes 135176 | tf_op jit(solution)/shard_map/probe_sum/ppermute | solution.py:647
  77.8 4.5 %collective-permute-start.10 = (f32[88,128]{1,0:T(8,128)S(1)}, f32[88,128]{1,0:T(8,128)S(1)}, u32[]{:S(2)}, u32[]{:S(2)}) collective-permute-start(f32[88,128]{1,0:T(8,128)S(1)} %probe_sum.2.own), channel_id=1, source_target_pairs={{0,64},{1,65},{2,66},{3,67},{4,68},{5,69},{6,70},{7,71},{8,72},{9,... | collective-permute-start | bytes 135176 | tf_op jit(solution)/shard_map/probe_sum/ppermute | solution.py:647
  78.0 7.4 %collective-permute-start.9 = (f32[88,128]{1,0:T(8,128)S(1)}, f32[88,128]{1,0:T(8,128)S(1)}, u32[]{:S(2)}, u32[]{:S(2)}) collective-permute-start(f32[88,128]{1,0:T(8,128)S(1)} %probe_sum.2.own), channel_id=1, source_target_pairs={{0,2},{1,3},{2,64},{3,65},{4,6},{5,7},{6,68},{7,69},{8,10},{9,11},... | collective-permute-start | bytes 135176 | tf_op jit(solution)/shard_map/probe_sum/ppermute | solution.py:647
  86.9 6.8 %copy-start.11 = (f32[256,256]{1,0:T(8,128)S(1)}, f32[256,256]{1,0:T(8,128)}, u32[]{:S(2)}) copy-start(f32[256,256]{1,0:T(8,128)} %copy-done.10) | copy-start | bytes 786436
  86.9 6.8 %copy-start.13 = (f32[2,256,256]{2,1,0:T(8,128)S(1)}, f32[2,256,256]{2,1,0:T(8,128)}, u32[]{:S(2)}) copy-start(f32[2,256,256]{2,1,0:T(8,128)} %copy-done.12) | copy-start | bytes 1572868
  86.9 17.4 %all-to-all-start.1 = ((f32[16,64,128]{2,1,0:T(8,128)}), f32[16,64,128]{2,1,0:T(8,128)S(1)}, u32[]{:S(2)}, u32[]{:S(2)}) async-start(f32[16,64,128]{2,1,0:T(8,128)} %get-tuple-element.57), calls=%async_computation.1 | async-start | bytes 1048576 | tf_op jit(solution)/shard_map/probe_gather/all_to_all | solution.py:707
  104.2 3.4 %collective-permute-start.14 = (f32[16,64,128]{2,1,0:T(8,128)S(1)}, f32[16,64,128]{2,1,0:T(8,128)S(1)}, u32[]{:S(2)}, u32[]{:S(2)}) collective-permute-start(f32[16,64,128]{2,1,0:T(8,128)S(1)} %all-to-all-done.1.mine), channel_id=1, source_target_pairs={{0,1},{1,0},{2,3},{3,2},{4,5},{5,4},{6,7},{7,6},{8,9},{9,8},{10,11... | collective-permute-start | bytes 1572872 | tf_op jit(solution)/shard_map/probe_gather/ppermute | solution.py:637

commit v13 on v12

--- a/solution.py
+++ b/solution.py
@@ -127,7 +127,7 @@
         (own.at[:, :, far], same.at[:, :SIZE, :]),
         (offsets, odd.at[:, HALF:, :]),
         (offsets, even.at[:, HALF:, :]),
-        (offsets.at[:, :, :HALF], cross.at[:, SIZE:, :]),
+        (offsets.at[:, :, :HALF], cross.at[:, SIZE : SIZE + 8, :]),
         (offsets.at[:, :, :HALF], same.at[:, SIZE:, :]),
     ]
     run_all([pltpu.make_async_copy(x, y, sems.at[n]) for n, (x, y) in enumerate(moves)])
@@ -166,10 +166,10 @@
             moves.append((own.at[:, :, span], tile.at[:, 1 + b, middle, :]))
             moves.append((even_strip.at[:, :HALF, span], tile.at[:, 1 + b, even_rows, :]))
             moves.append((odd_strip.at[:, :HALF, span], tile.at[:, 1 + b, odd_rows, :]))
-        strips = [x.at[0] for x in (odd_strip, even_strip, cross, same)]
-        strips += [x.at[n, 0] for x in (cross_corner, same_corner) for n in range(2)]
-        for n, strip in enumerate(strips):
-            moves.append((strip.at[pl.ds(strip.shape[0] - 8, 8), pl.ds(0, HALF)], offsets.at[n]))
+        strips = [(odd_strip.at[0], HALF), (even_strip.at[0], HALF), (cross.at[0], SIZE), (same.at[0], SIZE)]
+        strips += [(x.at[n, 0], HALF) for x in (cross_corner, same_corner) for n in range(2)]
+        for n, (strip, at) in enumerate(strips):
+            moves.append((strip.at[pl.ds(at, 8), pl.ds(0, HALF)], offsets.at[n]))
         copies = [pltpu.make_async_copy(x, y, sems.at[n]) for n, (x, y) in enumerate(moves)]
         for copy in copies:
             copy.start()
@@ -541,10 +541,10 @@
 
 
 def pack(starts, own):
-    rows, columns = (2, HALF + 8, SIZE), (2, SIZE + 8, HALF)
+    rows, crossing, columns = (2, HALF + 8, SIZE), (2, SIZE + 24, HALF), (2, SIZE + 8, HALF)
     return pl.pallas_call(
         pack_kernel,
-        out_shape=shaped([rows, rows, columns, columns]),
+        out_shape=shaped([rows, rows, crossing, columns]),
         grid_spec=pltpu.PrefetchScalarGridSpec(
             num_scalar_prefetch=1,
             grid=(),
@@ -615,7 +615,7 @@
 
 def update(arrays):
     shape = arrays[0].shape
-    return simple(update_kernel, [], arrays, shape, [shape], 16 << 30, 3 << 20)
+    return simple(update_kernel, [], arrays, shape, [shape], 1 << 20, 3 << 20)
 
 
 def assemble(mine, other):
@@ -694,14 +694,15 @@
         light = illuminate(starts, around, probe)
         even, odd = simple(fold_kernel, [], [even, odd, cross, same], [even.shape] * 2, [], 1 << 20, 1 << 20)
         chunk, light, odd, even = lax.optimization_barrier((chunk, light, odd, even))
-        odd = swap_rows(odd, 1)
-        even = swap_rows(even, 0)
 
     with jax.named_scope("probe_sum"):
         total = simple(sum_kernel, [], [chunk], (88, HALF), [], 1 << 20, 1 << 20)
         parts = [total] + [along_z(total, d) for d in (1, 2, 3)]
         shapes = [(16, 64, HALF), (8, HALF)]
         spread_out, ratio = simple(quotient_kernel, [], parts, shapes, [(4, 88, HALF)], 1 << 20, 2 << 20)
+        spread_out, odd, even = lax.optimization_barrier((spread_out, odd, even))
+        odd = swap_rows(odd, 1)
+        even = swap_rows(even, 0)
 
     with jax.named_scope("probe_gather"):
         gathered = lax.all_to_all(spread_out, AXES, 0, 0, axis_index_groups=groups, tiled=True)

time: 109 us -> 104 us (0.954)
  the two profiles are of different devices: /device:TPU:1 before, /device:TPU:25 now
where the time goes in v13:
time: 104 us; the launch traced here: 103 us
  starting transfers between devices  39.8 us (38%)
  waiting for transfers between devices  33.5 us (32%)
  Pallas kernels  22.6 us (22%)
  local copies, waits for them, and re-layouts  5.31 us (5%)
    ppermute x4, waiting for transfers between devices, swap_rows(): return lax.ppermute(value, 'row', pairs_from(first, lax.axis_size('row')))  14.9 us
    pallas_call x1, Pallas kernels, transforms(): pl.pallas_call(transform_kernel, out_shape=shaped([halves, halves]) + [ja...  14.2 us
    ppermute x8, starting transfers between devices, swap_columns(): return lax.ppermute(value, 'col', pairs_from(first, lax.axis_size('col')))  14.1 us
    ppermute x8, waiting for transfers between devices, swap_columns(): return lax.ppermute(value, 'col', pairs_from(first, lax.axis_size('col')))  11.4 us
    ppermute x4, starting transfers between devices, swap_rows(): return lax.ppermute(value, 'row', pairs_from(first, lax.axis_size('row')))  8.47 us
    pallas_call x7, Pallas kernels, simple(): return call(*scalars, *arrays)  7.56 us
    all_to_all x1, starting transfers between devices, local(): lax.all_to_all(chunk, AXES, 0, 0, axis_index_groups=groups, tiled=True)  6.95 us
    all_to_all x1, starting transfers between devices, local(): lax.all_to_all(spread_out, AXES, 0, 0, axis_index_groups=groups, tiled=True)  5.93 us
  transfers between devices with their start and end apart: 17, of which 9 were waited for; matrix products, arithmetic and copies ran while one was open for 2% of the time, Pallas kernels for 5%

profile of v13, /device:TPU:25, one launch (start us, length us, event | category | flops | bytes accessed | tf_op | source)
XLA Modules:
  0.0 103.0 jit_solution(3940856436205409693)
XLA Ops:
  0.6 0.0 copy-start.2
  0.6 0.7 copy-done.2
  1.3 0.0 copy-start
  1.3 1.0 %copy-done = f32[2,256,256]{2,1,0:T(8,128)S(1)} copy-done((f32[2,256,256]{2,1,0:T(8,128)S(1)}, f32[2,256,256]{2,1,0:T(8,128)}, u32[]{:S(2)}) %copy-start) | copy-done | bytes 524312
  2.4 0.0 copy-start.7
  2.4 0.8 object_halo.1
  3.1 4.1 %collective-permute-start.2 = (f32[2,280,128]{2,1,0:T(8,128)S(1)}, f32[2,280,128]{2,1,0:T(8,128)S(1)}, u32[]{:S(2)}, u32[]{:S(2)}) collective-permute-start(f32[2,280,128]{2,1,0:T(8,128)S(1)} %get-tuple-element.41), channel_id=1, source_target_pairs={{1,2},{2,1},{3,4},{4,3},{5,6},{6,5},{7,8},{8,7},{9,10},{10,9},{11,... | collective-permute-start | bytes 860168 | tf_op jit(solution)/shard_map/object_halo/ppermute | solution.py:637
  7.2 4.9 %collective-permute-start = (f32[2,136,256]{2,1,0:T(8,128)S(1)}, f32[2,136,256]{2,1,0:T(8,128)S(1)}, u32[]{:S(2)}, u32[]{:S(2)}) collective-permute-start(f32[2,136,256]{2,1,0:T(8,128)S(1)} %get-tuple-element.39), channel_id=1, source_target_pairs={{16,32},{32,16},{48,64},{64,48},{80,96},{96,80},{17,33},{33,17},{4... | collective-permute-start | bytes 835592 | tf_op jit(solution)/shard_map/object_halo/ppermute | solution.py:633
  12.1 0.1 collective-permute-start.1
  12.2 0.1 collective-permute-start.3
  12.3 0.0 copy-done.7
  12.3 0.0 copy-start.3
  12.3 1.2 %copy-done.3 = f32[1,1,4,256,256]{4,3,2,1,0:T(8,128)S(1)} copy-done((f32[1,1,4,256,256]{4,3,2,1,0:T(8,128)S(1)}, f32[1,1,4,256,256]{4,3,2,1,0:T(8,128)}, u32[]{:S(2)}) %copy-start.3) | copy-done | bytes 1048600
  13.5 0.0 copy-start.8
  13.5 1.0 copy-done.8
  14.5 0.0 copy-start.4
  14.5 1.3 %shard_map.102.measured = f32[4,256,256]{2,1,0:T(8,128)S(1)} custom-call(f32[4,256,256]{2,1,0:T(8,128)S(1)} %bitcast.13, bf16[768,256]{1,0:T(8,128)(2,1)S(1)} %copy-done.8, bf16[256,768]{1,0:T(8,128)(2,1)S(1)} %copy-done.7), custom_call_target="tpu_custom_call" | custom-call | flops 1073741824 | bytes 3145728 | tf_op jit(solution)/shard_map/pallas_call | solution.py:540
  15.9 0.0 collective-permute-done.3.same
  15.9 5.6 %collective-permute-done.odd_strip = f32[2,136,256]{2,1,0:T(8,128)S(1)} collective-permute-done((f32[2,136,256]{2,1,0:T(8,128)S(1)}, f32[2,136,256]{2,1,0:T(8,128)S(1)}, u32[]{:S(2)}, u32[]{:S(2)}) %collective-permute-start) | collective-permute-done | bytes 278560 | tf_op jit(solution)/shard_map/object_halo/ppermute | solution.py:633
  21.5 0.0 collective-permute-done.1.even_strip
  21.5 0.0 collective-permute-done.2.cross
  21.5 0.0 copy-start.1
  21.6 0.1 collective-permute-start.5
  21.7 2.6 %collective-permute-start.4 = (f32[2,2,136,128]{3,2,1,0:T(8,128)S(1)}, f32[2,2,136,128]{3,2,1,0:T(8,128)S(1)}, u32[]{:S(2)}, u32[]{:S(2)}) collective-permute-start(f32[2,2,136,128]{3,2,1,0:T(8,128)S(1)} %get-tuple-element.83), channel_id=1, source_target_pairs={{1,2},{2,1},{3,4},{4,3},{5,6},{6,5},{7,8},{8,7},{9,10},{10,9},{11,... | collective-permute-start | bytes 835592 | tf_op jit(solution)/shard_map/object_corners/ppermute | solution.py:637
  24.3 0.0 collective-permute-done.5.same_corner
  24.3 6.4 %collective-permute-done.4.cross_corner = f32[2,2,136,128]{3,2,1,0:T(8,128)S(1)} collective-permute-done((f32[2,2,136,128]{3,2,1,0:T(8,128)S(1)}, f32[2,2,136,128]{3,2,1,0:T(8,128)S(1)}, u32[]{:S(2)}, u32[]{:S(2)}) %collective-permute-start.4) | collective-permute-done | bytes 278560 | tf_op jit(solution)/shard_map/object_corners/ppermute | solution.py:637
  30.7 0.0 copy-done.4
  30.7 0.0 copy-done.6
  30.7 0.0 copy-done.1
  30.7 14.2 %shard_map.103 = (f32[16,88,128]{2,1,0:T(8,128)S(1)}, f32[16,88,128]{2,1,0:T(8,128)S(1)}, s32[8,128]{1,0:T(8,128)S(1)}, f32[2,256,256]{2,1,0:T(8,128)S(1)}, f32[...) custom-call(s32[2,4]{1,0:T(2,128)S(1)} %bitcast.11, ...), custom_call_target="tpu_custom_call" | custom-call | flops 13958643712 | bytes 12582912 | tf_op jit(solution)/shard_map/pallas_call | solution.py:585
  45.0 0.1 collective-permute-start.6
  45.1 4.4 %collective-permute-start.7 = (f32[2,512,128]{2,1,0:T(8,128)}, f32[2,512,128]{2,1,0:T(8,128)S(1)}, u32[]{:S(2)}, u32[]{:S(2)}) collective-permute-start(f32[2,512,128]{2,1,0:T(8,128)} %get-tuple-element.55), channel_id=1, source_target_pairs={{1,2},{2,1},{3,4},{4,3},{5,6},{6,5},{7,8},{8,7},{9,10},{10,9},{11,... | collective-permute-start | bytes 1572872 | tf_op jit(solution)/shard_map/gradient_columns/ppermute | solution.py:637
  49.5 0.1 collective-permute-start.8
  49.6 0.0 collective-permute-done.6
  49.6 0.9 add.3
  50.6 6.9 %all-to-all-start = ((f32[16,88,128]{2,1,0:T(8,128)}), f32[16,88,128]{2,1,0:T(8,128)S(1)}, u32[]{:S(2)}, u32[]{:S(2)}) async-start(f32[16,88,128]{2,1,0:T(8,128)} %add.3), calls=%async_computation | async-start | bytes 1441792 | tf_op jit(solution)/shard_map/probe_reduce/all_to_all | solution.py:691
  57.5 0.0 copy-start.5
  57.5 4.0 %collective-permute-done.7.cross = f32[2,512,128]{2,1,0:T(8,128)S(1)} collective-permute-done((f32[2,512,128]{2,1,0:T(8,128)}, f32[2,512,128]{2,1,0:T(8,128)S(1)}, u32[]{:S(2)}, u32[]{:S(2)}) %collective-permute-start.7) | collective-permute-done | bytes 524320 | tf_op jit(solution)/shard_map/gradient_columns/ppermute | solution.py:637
  61.6 0.0 collective-permute-done.8.same
  61.6 0.8 gradient_rows.3
  62.3 0.0 copy-done.5
  62.3 2.5 %gradient_rows.2.light = f32[256,256]{1,0:T(8,128)S(1)} custom-call(s32[2,4]{1,0:T(2,128)S(1)} %bitcast.12, s32[8,128]{1,0:T(8,128)S(1)} %get-tuple-element.52.around, f32[2,2,256,256]{3,2,1,0:T(8,128)S(1)} %copy-done.5), custom_call_target="tpu_custom_call" | custom-call | flops 2147483648 | bytes 4194304 | tf_op jit(solution)/shard_map/gradient_rows/pallas_call | solution.py:540
  64.9 3.8 %all-to-all-done.chunk = f32[16,88,128]{2,1,0:T(8,128)S(1)} async-done(((f32[16,88,128]{2,1,0:T(8,128)}), f32[16,88,128]{2,1,0:T(8,128)S(1)}, u32[]{:S(2)}, u32[]{:S(2)}) %all-to-all-start) | async-done | bytes 720928 | tf_op jit(solution)/shard_map/probe_reduce/all_to_all | solution.py:691
  68.7 2.1 %collective-permute-start.11 = (f32[88,128]{1,0:T(8,128)S(1)}, f32[88,128]{1,0:T(8,128)S(1)}, u32[]{:S(2)}, u32[]{:S(2)}) collective-permute-start(f32[88,128]{1,0:T(8,128)S(1)} %probe_sum.2.own), channel_id=1, source_target_pairs={{0,66},{1,67},{2,0},{3,1},{4,70},{5,71},{6,4},{7,5},{8,74},{9,75},... | collective-permute-start | bytes 135176 | tf_op jit(solution)/shard_map/probe_sum/ppermute | solution.py:647
  70.8 1.5 %collective-permute-start.10 = (f32[88,128]{1,0:T(8,128)S(1)}, f32[88,128]{1,0:T(8,128)S(1)}, u32[]{:S(2)}, u32[]{:S(2)}) collective-permute-start(f32[88,128]{1,0:T(8,128)S(1)} %probe_sum.2.own), channel_id=1, source_target_pairs={{0,64},{1,65},{2,66},{3,67},{4,68},{5,69},{6,70},{7,71},{8,72},{9,... | collective-permute-start | bytes 135176 | tf_op jit(solution)/shard_map/probe_sum/ppermute | solution.py:647
  72.3 0.8 collective-permute-start.9
  73.1 0.0 collective-permute-done.11.third
  73.1 2.1 %collective-permute-done.10.second = f32[88,128]{1,0:T(8,128)S(1)} collective-permute-done((f32[88,128]{1,0:T(8,128)S(1)}, f32[88,128]{1,0:T(8,128)S(1)}, u32[]{:S(2)}, u32[]{:S(2)}) %collective-permute-start.10) | collective-permute-done | bytes 45088 | tf_op jit(solution)/shard_map/probe_sum/ppermute | solution.py:647
  75.2 1.2 %collective-permute-done.9.first = f32[88,128]{1,0:T(8,128)S(1)} collective-permute-done((f32[88,128]{1,0:T(8,128)S(1)}, f32[88,128]{1,0:T(8,128)S(1)}, u32[]{:S(2)}, u32[]{:S(2)}) %collective-permute-start.9) | collective-permute-done | bytes 45088 | tf_op jit(solution)/shard_map/probe_sum/ppermute | solution.py:647
  76.4 0.9 probe_sum.3
  77.3 5.9 %all-to-all-start.1 = ((f32[16,64,128]{2,1,0:T(8,128)}), f32[16,64,128]{2,1,0:T(8,128)S(1)}, u32[]{:S(2)}, u32[]{:S(2)}) async-start(f32[16,64,128]{2,1,0:T(8,128)} %get-tuple-element.63), calls=%async_computation.1 | async-start | bytes 1048576 | tf_op jit(solution)/shard_map/probe_gather/all_to_all | solution.py:708
  83.2 0.6 collective-permute-start.12
  83.8 2.9 %collective-permute-start.13 = (f32[2,128,256]{2,1,0:T(8,128)S(1)}, f32[2,128,256]{2,1,0:T(8,128)S(1)}, u32[]{:S(2)}, u32[]{:S(2)}) collective-permute-start(f32[2,128,256]{2,1,0:T(8,128)S(1)} %get-tuple-element.66), channel_id=1, source_target_pairs={{16,32},{32,16},{48,64},{64,48},{80,96},{96,80},{17,33},{33,17},{4... | collective-permute-start | bytes 786440 | tf_op jit(solution)/shard_map/probe_sum/ppermute | solution.py:633
  86.8 0.1 slice_reduce_fusion
  86.9 0.1 squeeze.15
  87.0 0.5 slice.16
  87.5 7.2 %collective-permute-done.12.even = f32[2,128,256]{2,1,0:T(8,128)S(1)} collective-permute-done((f32[2,128,256]{2,1,0:T(8,128)}, f32[2,128,256]{2,1,0:T(8,128)S(1)}, u32[]{:S(2)}, u32[]{:S(2)}) %collective-permute-start.12) | collective-permute-done | bytes 262176 | tf_op jit(solution)/shard_map/probe_sum/ppermute | solution.py:633
  94.7 2.0 %collective-permute-done.13.odd = f32[2,128,256]{2,1,0:T(8,128)S(1)} collective-permute-done((f32[2,128,256]{2,1,0:T(8,128)S(1)}, f32[2,128,256]{2,1,0:T(8,128)S(1)}, u32[]{:S(2)}, u32[]{:S(2)}) %collective-permute-start.13) | collective-permute-done | bytes 262176 | tf_op jit(solution)/shard_map/probe_sum/ppermute | solution.py:633
  96.8 1.0 probe_gather.2
  97.7 0.0 all-to-all-done.1.mine
  97.7 2.6 %collective-permute-start.14 = (f32[16,64,128]{2,1,0:T(8,128)S(1)}, f32[16,64,128]{2,1,0:T(8,128)S(1)}, u32[]{:S(2)}, u32[]{:S(2)}) collective-permute-start(f32[16,64,128]{2,1,0:T(8,128)S(1)} %all-to-all-done.1.mine), channel_id=1, source_target_pairs={{0,1},{1,0},{2,3},{3,2},{4,5},{5,4},{6,7},{7,6},{8,9},{9,8},{10,11... | collective-permute-start | bytes 1572872 | tf_op jit(solution)/shard_map/probe_gather/ppermute | solution.py:637
  100.4 0.6 copy.12
  101.0 0.9 collective-permute-done.14.other
  101.9 1.1 %probe_gather.3 = f32[4,256,256]{2,1,0:T(8,128)} custom-call(f32[16,64,128]{2,1,0:T(8,128)S(1)} %all-to-all-done.1.mine, f32[16,64,128]{2,1,0:T(8,128)S(1)} %collective-permute-done.14.other), custom_call_target="tpu_custom_call" | custom-call | flops 1048576 | bytes 2097152 | tf_op jit(solution)/shard_map/probe_gather/pallas_call | solution.py:540
  (3 shorter events, 0.1 us)
Async XLA Ops:
  0.6 0.7 copy-start.2
  1.3 1.0 %copy-start = (f32[2,256,256]{2,1,0:T(8,128)S(1)}, f32[2,256,256]{2,1,0:T(8,128)}, u32[]{:S(2)}) copy-start(f32[2,256,256]{2,1,0:T(8,128)} %own.3) | copy-start | bytes 1572868
  2.4 10.0 %copy-start.7 = (bf16[256,768]{1,0:T(8,128)(2,1)S(1)}, bf16[256,768]{1,0:T(8,128)(2,1)}, u32[]{:S(2)}) copy-start(bf16[256,768]{1,0:T(8,128)(2,1)} %constant.18.clone.rows) | copy-start | bytes 1179652
  3.1 18.4 %collective-permute-start.2 = (f32[2,280,128]{2,1,0:T(8,128)S(1)}, f32[2,280,128]{2,1,0:T(8,128)S(1)}, u32[]{:S(2)}, u32[]{:S(2)}) collective-permute-start(f32[2,280,128]{2,1,0:T(8,128)S(1)} %get-tuple-element.41), channel_id=1, source_target_pairs={{1,2},{2,1},{3,4},{4,3},{5,6},{6,5},{7,8},{8,7},{9,10},{10,9},{11,... | collective-permute-start | bytes 860168 | tf_op jit(solution)/shard_map/object_halo/ppermute | solution.py:637
  7.2 14.3 %collective-permute-start = (f32[2,136,256]{2,1,0:T(8,128)S(1)}, f32[2,136,256]{2,1,0:T(8,128)S(1)}, u32[]{:S(2)}, u32[]{:S(2)}) collective-permute-start(f32[2,136,256]{2,1,0:T(8,128)S(1)} %get-tuple-element.39), channel_id=1, source_target_pairs={{16,32},{32,16},{48,64},{64,48},{80,96},{96,80},{17,33},{33,17},{4... | collective-permute-start | bytes 835592 | tf_op jit(solution)/shard_map/object_halo/ppermute | solution.py:633
  12.1 9.4 %collective-permute-start.1 = (f32[2,136,256]{2,1,0:T(8,128)S(1)}, f32[2,136,256]{2,1,0:T(8,128)S(1)}, u32[]{:S(2)}, u32[]{:S(2)}) collective-permute-start(f32[2,136,256]{2,1,0:T(8,128)S(1)} %get-tuple-element.40), channel_id=1, source_target_pairs={{0,16},{16,0},{32,48},{48,32},{64,80},{80,64},{96,112},{112,96},{1... | collective-permute-start | bytes 835592 | tf_op jit(solution)/shard_map/object_halo/ppermute | solution.py:633
  12.2 3.7 %collective-permute-start.3 = (f32[2,264,128]{2,1,0:T(8,128)S(1)}, f32[2,264,128]{2,1,0:T(8,128)S(1)}, u32[]{:S(2)}, u32[]{:S(2)}) collective-permute-start(f32[2,264,128]{2,1,0:T(8,128)S(1)} %get-tuple-element.42), channel_id=1, source_target_pairs={{0,1},{1,0},{2,3},{3,2},{4,5},{5,4},{6,7},{7,6},{8,9},{9,8},{10,11... | collective-permute-start | bytes 811016 | tf_op jit(solution)/shard_map/object_halo/ppermute | solution.py:637
  12.3 1.2 %copy-start.3 = (f32[1,1,4,256,256]{4,3,2,1,0:T(8,128)S(1)}, f32[1,1,4,256,256]{4,3,2,1,0:T(8,128)}, u32[]{:S(2)}) copy-start(f32[1,1,4,256,256]{4,3,2,1,0:T(8,128)} %param.9) | copy-start | bytes 3145732
  13.5 1.0 copy-start.8
  14.5 16.2 %copy-start.4 = (f32[2,2,256,256]{3,2,1,0:T(8,128)S(1)}, f32[2,2,256,256]{3,2,1,0:T(8,128)}, u32[]{:S(2)}) copy-start(f32[2,2,256,256]{3,2,1,0:T(8,128)} %probe.1) | copy-start | bytes 3145732
  14.5 16.2 %copy-start.6 = (bf16[2,2,2,256,256]{4,3,2,1,0:T(8,128)(2,1)S(1)}, bf16[2,2,2,256,256]{4,3,2,1,0:T(8,128)(2,1)}, u32[]{:S(2)}) copy-start(bf16[2,2,2,256,256]{4,3,2,1,0:T(8,128)(2,1)} %constant.19.clone.matrices) | copy-start | bytes 3145732
  21.5 9.2 %copy-start.1 = (f32[2,256,256]{2,1,0:T(8,128)S(1)}, f32[2,256,256]{2,1,0:T(8,128)}, u32[]{:S(2)}) copy-start(f32[2,256,256]{2,1,0:T(8,128)} %own.3) | copy-start | bytes 1572868
  21.6 2.7 %collective-permute-start.5 = (f32[2,2,136,128]{3,2,1,0:T(8,128)S(1)}, f32[2,2,136,128]{3,2,1,0:T(8,128)S(1)}, u32[]{:S(2)}, u32[]{:S(2)}) collective-permute-start(f32[2,2,136,128]{3,2,1,0:T(8,128)S(1)} %get-tuple-element.82), channel_id=1, source_target_pairs={{0,1},{1,0},{2,3},{3,2},{4,5},{5,4},{6,7},{7,6},{8,9},{9,8},{10,11... | collective-permute-start | bytes 835592 | tf_op jit(solution)/shard_map/object_corners/ppermute | solution.py:637
  21.7 9.1 %collective-permute-start.4 = (f32[2,2,136,128]{3,2,1,0:T(8,128)S(1)}, f32[2,2,136,128]{3,2,1,0:T(8,128)S(1)}, u32[]{:S(2)}, u32[]{:S(2)}) collective-permute-start(f32[2,2,136,128]{3,2,1,0:T(8,128)S(1)} %get-tuple-element.83), channel_id=1, source_target_pairs={{1,2},{2,1},{3,4},{4,3},{5,6},{6,5},{7,8},{8,7},{9,10},{10,9},{11,... | collective-permute-start | bytes 835592 | tf_op jit(solution)/shard_map/object_corners/ppermute | solution.py:637
  45.0 4.6 %collective-permute-start.6 = (f32[16,88,128]{2,1,0:T(8,128)S(1)}, f32[16,88,128]{2,1,0:T(8,128)S(1)}, u32[]{:S(2)}, u32[]{:S(2)}) collective-permute-start(f32[16,88,128]{2,1,0:T(8,128)S(1)} %get-tuple-element.49), channel_id=1, source_target_pairs={{0,1},{1,0},{2,3},{3,2},{4,5},{5,4},{6,7},{7,6},{8,9},{9,8},{10,11... | collective-permute-start | bytes 2162696 | tf_op jit(solution)/shard_map/probe_reduce/ppermute | solution.py:637
  45.1 16.5 %collective-permute-start.7 = (f32[2,512,128]{2,1,0:T(8,128)}, f32[2,512,128]{2,1,0:T(8,128)S(1)}, u32[]{:S(2)}, u32[]{:S(2)}) collective-permute-start(f32[2,512,128]{2,1,0:T(8,128)} %get-tuple-element.55), channel_id=1, source_target_pairs={{1,2},{2,1},{3,4},{4,3},{5,6},{6,5},{7,8},{8,7},{9,10},{10,9},{11,... | collective-permute-start | bytes 1572872 | tf_op jit(solution)/shard_map/gradient_columns/ppermute | solution.py:637
  49.5 12.0 %collective-permute-start.8 = (f32[2,512,128]{2,1,0:T(8,128)}, f32[2,512,128]{2,1,0:T(8,128)S(1)}, u32[]{:S(2)}, u32[]{:S(2)}) collective-permute-start(f32[2,512,128]{2,1,0:T(8,128)} %get-tuple-element.56), channel_id=1, source_target_pairs={{0,1},{1,0},{2,3},{3,2},{4,5},{5,4},{6,7},{7,6},{8,9},{9,8},{10,11... | collective-permute-start | bytes 1572872 | tf_op jit(solution)/shard_map/gradient_columns/ppermute | solution.py:637
  50.6 18.1 %all-to-all-start = ((f32[16,88,128]{2,1,0:T(8,128)}), f32[16,88,128]{2,1,0:T(8,128)S(1)}, u32[]{:S(2)}, u32[]{:S(2)}) async-start(f32[16,88,128]{2,1,0:T(8,128)} %add.3), calls=%async_computation | async-start | bytes 1441792 | tf_op jit(solution)/shard_map/probe_reduce/all_to_all | solution.py:691
  57.5 4.8 %copy-start.5 = (f32[2,2,256,256]{3,2,1,0:T(8,128)S(1)}, f32[2,2,256,256]{3,2,1,0:T(8,128)}, u32[]{:S(2)}) copy-start(f32[2,2,256,256]{3,2,1,0:T(8,128)} %probe.1) | copy-start | bytes 3145732
  68.7 4.4 %collective-permute-start.11 = (f32[88,128]{1,0:T(8,128)S(1)}, f32[88,128]{1,0:T(8,128)S(1)}, u32[]{:S(2)}, u32[]{:S(2)}) collective-permute-start(f32[88,128]{1,0:T(8,128)S(1)} %probe_sum.2.own), channel_id=1, source_target_pairs={{0,66},{1,67},{2,0},{3,1},{4,70},{5,71},{6,4},{7,5},{8,74},{9,75},... | collective-permute-start | bytes 135176 | tf_op jit(solution)/shard_map/probe_sum/ppermute | solution.py:647
  70.8 4.4 %collective-permute-start.10 = (f32[88,128]{1,0:T(8,128)S(1)}, f32[88,128]{1,0:T(8,128)S(1)}, u32[]{:S(2)}, u32[]{:S(2)}) collective-permute-start(f32[88,128]{1,0:T(8,128)S(1)} %probe_sum.2.own), channel_id=1, source_target_pairs={{0,64},{1,65},{2,66},{3,67},{4,68},{5,69},{6,70},{7,71},{8,72},{9,... | collective-permute-start | bytes 135176 | tf_op jit(solution)/shard_map/probe_sum/ppermute | solution.py:647
  72.3 4.1 %collective-permute-start.9 = (f32[88,128]{1,0:T(8,128)S(1)}, f32[88,128]{1,0:T(8,128)S(1)}, u32[]{:S(2)}, u32[]{:S(2)}) collective-permute-start(f32[88,128]{1,0:T(8,128)S(1)} %probe_sum.2.own), channel_id=1, source_target_pairs={{0,2},{1,3},{2,64},{3,65},{4,6},{5,7},{6,68},{7,69},{8,10},{9,11},... | collective-permute-start | bytes 135176 | tf_op jit(solution)/shard_map/probe_sum/ppermute | solution.py:647
  77.3 20.4 %all-to-all-start.1 = ((f32[16,64,128]{2,1,0:T(8,128)}), f32[16,64,128]{2,1,0:T(8,128)S(1)}, u32[]{:S(2)}, u32[]{:S(2)}) async-start(f32[16,64,128]{2,1,0:T(8,128)} %get-tuple-element.63), calls=%async_computation.1 | async-start | bytes 1048576 | tf_op jit(solution)/shard_map/probe_gather/all_to_all | solution.py:708
  83.2 11.5 %collective-permute-start.12 = (f32[2,128,256]{2,1,0:T(8,128)}, f32[2,128,256]{2,1,0:T(8,128)S(1)}, u32[]{:S(2)}, u32[]{:S(2)}) collective-permute-start(f32[2,128,256]{2,1,0:T(8,128)} %get-tuple-element.65), channel_id=1, source_target_pairs={{0,16},{16,0},{32,48},{48,32},{64,80},{80,64},{96,112},{112,96},{1... | collective-permute-start | bytes 786440 | tf_op jit(solution)/shard_map/probe_sum/ppermute | solution.py:633
  83.8 12.9 %collective-permute-start.13 = (f32[2,128,256]{2,1,0:T(8,128)S(1)}, f32[2,128,256]{2,1,0:T(8,128)S(1)}, u32[]{:S(2)}, u32[]{:S(2)}) collective-permute-start(f32[2,128,256]{2,1,0:T(8,128)S(1)} %get-tuple-element.66), channel_id=1, source_target_pairs={{16,32},{32,16},{48,64},{64,48},{80,96},{96,80},{17,33},{33,17},{4... | collective-permute-start | bytes 786440 | tf_op jit(solution)/shard_map/probe_sum/ppermute | solution.py:633
  97.7 4.2 %collective-permute-start.14 = (f32[16,64,128]{2,1,0:T(8,128)S(1)}, f32[16,64,128]{2,1,0:T(8,128)S(1)}, u32[]{:S(2)}, u32[]{:S(2)}) collective-permute-start(f32[16,64,128]{2,1,0:T(8,128)S(1)} %all-to-all-done.1.mine), channel_id=1, source_target_pairs={{0,1},{1,0},{2,3},{3,2},{4,5},{5,4},{6,7},{7,6},{8,9},{9,8},{10,11... | collective-permute-start | bytes 1572872 | tf_op jit(solution)/shard_map/probe_gather/ppermute | solution.py:637

commit v14 on v13

--- a/solution.py
+++ b/solution.py
@@ -461,8 +461,9 @@
     for p in range(2):
         for strip, rows, out in ((even, even_rows, even_out), (odd, odd_rows, odd_out)):
             a, b = cross[p, rows], same[p, rows]
-            out[p, :, :HALF] = strip[p, :, :HALF] + jnp.where(swapped, b, a)
-            out[p, :, HALF:] = strip[p, :, HALF:] + jnp.where(swapped, a, b)
+            out[p, :HALF, :HALF] = strip[p, :, :HALF] + jnp.where(swapped, b, a)
+            out[p, :HALF, HALF:] = strip[p, :, HALF:] + jnp.where(swapped, a, b)
+    odd_out[:, HALF:, :] = jnp.zeros((2, 8, SIZE), F32)
 
 
 def update_kernel(center, even, odd, cross, same, light, out, total):
@@ -473,7 +474,7 @@
     odd_half = pl.ds(pl.multiple_of(HALF * row_odd, HALF), HALF)
     for p in range(2):
         total[p, even_half, :] += even[p]
-        total[p, odd_half, :] += odd[p]
+        total[p, odd_half, :] += odd[p, :HALF]
     swapped = core == 1
     for i in range(0, SIZE, CHUNK):
         part = pl.ds(i, CHUNK)
@@ -692,7 +693,7 @@
 
     with jax.named_scope("gradient_rows"):
         light = illuminate(starts, around, probe)
-        even, odd = simple(fold_kernel, [], [even, odd, cross, same], [even.shape] * 2, [], 1 << 20, 1 << 20)
+        even, odd = simple(fold_kernel, [], [even, odd, cross, same], [even.shape, (2, HALF + 8, SIZE)], [], 1 << 20, 1 << 20)
         chunk, light, odd, even = lax.optimization_barrier((chunk, light, odd, even))
 
     with jax.named_scope("probe_sum"):
@@ -706,13 +707,14 @@
 
     with jax.named_scope("probe_gather"):
         gathered = lax.all_to_all(spread_out, AXES, 0, 0, axis_index_groups=groups, tiled=True)
-        object_update = update([center, even, odd, cross, same, light])
         relative_error = ratio[0, :1]
         position_step = steps[:, 0].reshape(1, 1, -1, 2)
-        tied = (gathered, object_update, relative_error, position_step)
-        gathered, object_update, relative_error, position_step = lax.optimization_barrier(tied)
+        tied = (gathered, relative_error, position_step)
+        gathered, relative_error, position_step = lax.optimization_barrier(tied)
         probe_update = assemble(gathered, swap_columns(gathered, 0)).reshape(probe.shape)
 
+    probe_update, odd, even = lax.optimization_barrier((probe_update, odd, even))
+    object_update = update([center, even, odd, cross, same, light])
     return (object_update, probe_update, position_step, relative_error)
 
 

time: 104 us -> 110 us (1.058)
  waiting for transfers between devices: 33.5 us -> 36.8 us
  starting transfers between devices: 39.8 us -> 42.3 us
    all_to_all x1, waiting for transfers between devices: 0.01 us -> 6.27 us  [local(): lax.all_to_all(spread_out, AXES, 0, 0, axis_index_groups=groups, tiled=True)]
    ppermute x4, waiting for transfers between devices: 14.9 us -> 12.9 us  [swap_rows(): return lax.ppermute(value, 'row', pairs_from(first, lax.axis_size('row')))]
    ppermute x8, starting transfers between devices: 14.1 us -> 15.5 us  [swap_columns(): return lax.ppermute(value, 'col', pairs_from(first, lax.axis_size('col')))]
    ppermute x4, starting transfers between devices: 8.47 us -> 9.73 us  [swap_rows(): return lax.ppermute(value, 'row', pairs_from(first, lax.axis_size('row')))]
    unnamed x19 -> x25, local copies, waits for them, and re-layouts: 4.59 us -> 5.3 us
where the time goes in v14:
time: 110 us
  starting transfers between devices  42.3 us (38%)
  waiting for transfers between devices  36.8 us (33%)
  Pallas kernels  22.6 us (21%)
  local copies, waits for them, and re-layouts  6.01 us (5%)
    ppermute x8, starting transfers between devices, swap_columns(): return lax.ppermute(value, 'col', pairs_from(first, lax.axis_size('col')))  15.5 us
    pallas_call x1, Pallas kernels, transforms(): pl.pallas_call(transform_kernel, out_shape=shaped([halves, halves]) + [ja...  14 us
    ppermute x4, waiting for transfers between devices, swap_rows(): return lax.ppermute(value, 'row', pairs_from(first, lax.axis_size('row')))  12.9 us
    ppermute x8, waiting for transfers between devices, swap_columns(): return lax.ppermute(value, 'col', pairs_from(first, lax.axis_size('col')))  10.5 us
    ppermute x4, starting transfers between devices, swap_rows(): return lax.ppermute(value, 'row', pairs_from(first, lax.axis_size('row')))  9.73 us
    pallas_call x7, Pallas kernels, simple(): return call(*scalars, *arrays)  7.8 us
    all_to_all x1, starting transfers between devices, local(): lax.all_to_all(chunk, AXES, 0, 0, axis_index_groups=groups, tiled=True)  6.95 us
    all_to_all x1, waiting for transfers between devices, local(): lax.all_to_all(spread_out, AXES, 0, 0, axis_index_groups=groups, tiled=True)  6.27 us
  transfers between devices with their start and end apart: 17, of which 9 were waited for; matrix products, arithmetic and copies ran while one was open for 2% of the time, Pallas kernels for 5%

profile of v14, /device:TPU:25, one launch (start us, length us, event | category | flops | bytes accessed | tf_op | source)
XLA Modules:
  0.0 109.6 jit_solution(17494155667185241627)
XLA Ops:
  0.6 0.0 copy-start.2
  0.6 0.7 copy-done.2
  1.3 0.0 copy-start
  1.3 1.0 copy-done
  2.4 0.0 copy-start.10
  2.4 0.8 object_halo.1
  3.1 4.1 %collective-permute-start.2 = (f32[2,280,128]{2,1,0:T(8,128)S(1)}, f32[2,280,128]{2,1,0:T(8,128)S(1)}, u32[]{:S(2)}, u32[]{:S(2)}) collective-permute-start(f32[2,280,128]{2,1,0:T(8,128)S(1)} %get-tuple-element.43), channel_id=1, source_target_pairs={{1,2},{2,1},{3,4},{4,3},{5,6},{6,5},{7,8},{8,7},{9,10},{10,9},{11,... | collective-permute-start | bytes 860168 | tf_op jit(solution)/shard_map/object_halo/ppermute | solution.py:638
  7.2 4.9 %collective-permute-start = (f32[2,136,256]{2,1,0:T(8,128)S(1)}, f32[2,136,256]{2,1,0:T(8,128)S(1)}, u32[]{:S(2)}, u32[]{:S(2)}) collective-permute-start(f32[2,136,256]{2,1,0:T(8,128)S(1)} %get-tuple-element.41), channel_id=1, source_target_pairs={{16,32},{32,16},{48,64},{64,48},{80,96},{96,80},{17,33},{33,17},{4... | collective-permute-start | bytes 835592 | tf_op jit(solution)/shard_map/object_halo/ppermute | solution.py:634
  12.1 0.1 collective-permute-start.1
  12.2 0.1 collective-permute-start.3
  12.3 0.0 copy-done.10
  12.3 0.0 copy-start.3
  12.3 1.2 %copy-done.3 = f32[1,1,4,256,256]{4,3,2,1,0:T(8,128)S(1)} copy-done((f32[1,1,4,256,256]{4,3,2,1,0:T(8,128)S(1)}, f32[1,1,4,256,256]{4,3,2,1,0:T(8,128)}, u32[]{:S(2)}) %copy-start.3) | copy-done | bytes 1048600
  13.5 1.0 copy-done.11
  14.5 1.3 %shard_map.102.measured = f32[4,256,256]{2,1,0:T(8,128)S(1)} custom-call(f32[4,256,256]{2,1,0:T(8,128)S(1)} %bitcast.13, bf16[768,256]{1,0:T(8,128)(2,1)S(1)} %copy-done.11, bf16[256,768]{1,0:T(8,128)(2,1)S(1)} %copy-done.10), custom_call_target="tpu_custom_call" | custom-call | flops 1073741824 | bytes 3145728 | tf_op jit(solution)/shard_map/pallas_call | solution.py:541
  15.9 0.0 collective-permute-done.3.same
  15.9 5.7 %collective-permute-done.odd_strip = f32[2,136,256]{2,1,0:T(8,128)S(1)} collective-permute-done((f32[2,136,256]{2,1,0:T(8,128)S(1)}, f32[2,136,256]{2,1,0:T(8,128)S(1)}, u32[]{:S(2)}, u32[]{:S(2)}) %collective-permute-start) | collective-permute-done | bytes 278560 | tf_op jit(solution)/shard_map/object_halo/ppermute | solution.py:634
  21.5 0.0 collective-permute-done.1.even_strip
  21.5 0.0 collective-permute-done.2.cross
  21.6 0.1 collective-permute-start.5
  21.7 2.6 %collective-permute-start.4 = (f32[2,2,136,128]{3,2,1,0:T(8,128)S(1)}, f32[2,2,136,128]{3,2,1,0:T(8,128)S(1)}, u32[]{:S(2)}, u32[]{:S(2)}) collective-permute-start(f32[2,2,136,128]{3,2,1,0:T(8,128)S(1)} %get-tuple-element.87), channel_id=1, source_target_pairs={{1,2},{2,1},{3,4},{4,3},{5,6},{6,5},{7,8},{8,7},{9,10},{10,9},{11,... | collective-permute-start | bytes 835592 | tf_op jit(solution)/shard_map/object_corners/ppermute | solution.py:638
  24.3 0.0 collective-permute-done.5.same_corner
  24.3 6.4 %collective-permute-done.4.cross_corner = f32[2,2,136,128]{3,2,1,0:T(8,128)S(1)} collective-permute-done((f32[2,2,136,128]{3,2,1,0:T(8,128)S(1)}, f32[2,2,136,128]{3,2,1,0:T(8,128)S(1)}, u32[]{:S(2)}, u32[]{:S(2)}) %collective-permute-start.4) | collective-permute-done | bytes 278560 | tf_op jit(solution)/shard_map/object_corners/ppermute | solution.py:638
  30.7 0.0 copy-done.4
  30.7 0.0 copy-done.9
  30.7 0.0 copy-done.1
  30.7 14.0 %shard_map.103 = (f32[16,88,128]{2,1,0:T(8,128)S(1)}, f32[16,88,128]{2,1,0:T(8,128)S(1)}, s32[8,128]{1,0:T(8,128)S(1)}, f32[2,256,256]{2,1,0:T(8,128)S(1)}, f32[...) custom-call(s32[2,4]{1,0:T(2,128)S(1)} %bitcast.11, ...), custom_call_target="tpu_custom_call" | custom-call | flops 13958643712 | bytes 12582912 | tf_op jit(solution)/shard_map/pallas_call | solution.py:586
  44.8 0.1 collective-permute-start.6
  44.9 4.4 %collective-permute-start.7 = (f32[2,512,128]{2,1,0:T(8,128)}, f32[2,512,128]{2,1,0:T(8,128)S(1)}, u32[]{:S(2)}, u32[]{:S(2)}) collective-permute-start(f32[2,512,128]{2,1,0:T(8,128)} %get-tuple-element.58), channel_id=1, source_target_pairs={{1,2},{2,1},{3,4},{4,3},{5,6},{6,5},{7,8},{8,7},{9,10},{10,9},{11,... | collective-permute-start | bytes 1572872 | tf_op jit(solution)/shard_map/gradient_columns/ppermute | solution.py:638
  49.3 0.1 collective-permute-start.8
  49.4 0.0 collective-permute-done.6
  49.4 0.9 add.3
  50.3 6.9 %all-to-all-start = ((f32[16,88,128]{2,1,0:T(8,128)}), f32[16,88,128]{2,1,0:T(8,128)S(1)}, u32[]{:S(2)}, u32[]{:S(2)}) async-start(f32[16,88,128]{2,1,0:T(8,128)} %add.3), calls=%async_computation | async-start | bytes 1441792 | tf_op jit(solution)/shard_map/probe_reduce/all_to_all | solution.py:692
  57.3 4.0 %collective-permute-done.7.cross = f32[2,512,128]{2,1,0:T(8,128)S(1)} collective-permute-done((f32[2,512,128]{2,1,0:T(8,128)}, f32[2,512,128]{2,1,0:T(8,128)S(1)}, u32[]{:S(2)}, u32[]{:S(2)}) %collective-permute-start.7) | collective-permute-done | bytes 524320 | tf_op jit(solution)/shard_map/gradient_columns/ppermute | solution.py:638
  61.3 0.0 collective-permute-done.8.same
  61.3 0.1 gradient_rows.3
  61.4 0.0 copy-start.8
  61.4 0.7 copy-done.8
  62.1 0.0 copy-done.5
  62.1 2.5 %gradient_rows.2.light = f32[256,256]{1,0:T(8,128)S(1)} custom-call(s32[2,4]{1,0:T(2,128)S(1)} %bitcast.12, s32[8,128]{1,0:T(8,128)S(1)} %get-tuple-element.55.around, f32[2,2,256,256]{3,2,1,0:T(8,128)S(1)} %copy-done.5), custom_call_target="tpu_custom_call" | custom-call | flops 2147483648 | bytes 4194304 | tf_op jit(solution)/shard_map/gradient_rows/pallas_call | solution.py:541
  64.6 0.0 copy-done.6
  64.7 3.8 %all-to-all-done.chunk = f32[16,88,128]{2,1,0:T(8,128)S(1)} async-done(((f32[16,88,128]{2,1,0:T(8,128)}), f32[16,88,128]{2,1,0:T(8,128)S(1)}, u32[]{:S(2)}, u32[]{:S(2)}) %all-to-all-start) | async-done | bytes 720928 | tf_op jit(solution)/shard_map/probe_reduce/all_to_all | solution.py:692
  68.5 2.1 %collective-permute-start.11 = (f32[88,128]{1,0:T(8,128)S(1)}, f32[88,128]{1,0:T(8,128)S(1)}, u32[]{:S(2)}, u32[]{:S(2)}) collective-permute-start(f32[88,128]{1,0:T(8,128)S(1)} %probe_sum.2.own), channel_id=1, source_target_pairs={{0,66},{1,67},{2,0},{3,1},{4,70},{5,71},{6,4},{7,5},{8,74},{9,75},... | collective-permute-start | bytes 135176 | tf_op jit(solution)/shard_map/probe_sum/ppermute | solution.py:648
  70.6 1.5 %collective-permute-start.10 = (f32[88,128]{1,0:T(8,128)S(1)}, f32[88,128]{1,0:T(8,128)S(1)}, u32[]{:S(2)}, u32[]{:S(2)}) collective-permute-start(f32[88,128]{1,0:T(8,128)S(1)} %probe_sum.2.own), channel_id=1, source_target_pairs={{0,64},{1,65},{2,66},{3,67},{4,68},{5,69},{6,70},{7,71},{8,72},{9,... | collective-permute-start | bytes 135176 | tf_op jit(solution)/shard_map/probe_sum/ppermute | solution.py:648
  72.1 0.8 collective-permute-start.9
  72.9 0.0 collective-permute-done.11.third
  72.9 2.1 %collective-permute-done.10.second = f32[88,128]{1,0:T(8,128)S(1)} collective-permute-done((f32[88,128]{1,0:T(8,128)S(1)}, f32[88,128]{1,0:T(8,128)S(1)}, u32[]{:S(2)}, u32[]{:S(2)}) %collective-permute-start.10) | collective-permute-done | bytes 45088 | tf_op jit(solution)/shard_map/probe_sum/ppermute | solution.py:648
  75.0 1.2 %collective-permute-done.9.first = f32[88,128]{1,0:T(8,128)S(1)} collective-permute-done((f32[88,128]{1,0:T(8,128)S(1)}, f32[88,128]{1,0:T(8,128)S(1)}, u32[]{:S(2)}, u32[]{:S(2)}) %collective-permute-start.9) | collective-permute-done | bytes 45088 | tf_op jit(solution)/shard_map/probe_sum/ppermute | solution.py:648
  76.2 0.9 probe_sum.3
  77.1 5.8 %all-to-all-start.1 = ((f32[16,64,128]{2,1,0:T(8,128)}), f32[16,64,128]{2,1,0:T(8,128)S(1)}, u32[]{:S(2)}, u32[]{:S(2)}) async-start(f32[16,64,128]{2,1,0:T(8,128)} %get-tuple-element.66), calls=%async_computation.1 | async-start | bytes 1048576 | tf_op jit(solution)/shard_map/probe_gather/all_to_all | solution.py:709
  82.9 0.1 slice_reduce_fusion
  83.0 0.1 squeeze.15
  83.1 0.5 slice.16
  83.6 6.3 %all-to-all-done.1.mine = f32[16,64,128]{2,1,0:T(8,128)S(1)} async-done(((f32[16,64,128]{2,1,0:T(8,128)}), f32[16,64,128]{2,1,0:T(8,128)S(1)}, u32[]{:S(2)}, u32[]{:S(2)}) %all-to-all-start.1) | async-done | bytes 524320 | tf_op jit(solution)/shard_map/probe_gather/all_to_all | solution.py:709
  89.9 4.0 %collective-permute-start.12 = (f32[16,64,128]{2,1,0:T(8,128)S(1)}, f32[16,64,128]{2,1,0:T(8,128)S(1)}, u32[]{:S(2)}, u32[]{:S(2)}) collective-permute-start(f32[16,64,128]{2,1,0:T(8,128)S(1)} %all-to-all-done.1.mine), channel_id=1, source_target_pairs={{0,1},{1,0},{2,3},{3,2},{4,5},{5,4},{6,7},{7,6},{8,9},{9,8},{10,11... | collective-permute-start | bytes 1572872 | tf_op jit(solution)/shard_map/probe_gather/ppermute | solution.py:638
  93.9 0.0 copy-done.7
  93.9 4.7 %collective-permute-start.13 = (f32[2,136,256]{2,1,0:T(8,128)S(1)}, f32[2,136,256]{2,1,0:T(8,128)S(1)}, u32[]{:S(2)}, u32[]{:S(2)}) collective-permute-start(f32[2,136,256]{2,1,0:T(8,128)S(1)} %copy-done.7), channel_id=1, source_target_pairs={{16,32},{32,16},{48,64},{64,48},{80,96},{96,80},{17,33},{33,17},{4... | collective-permute-start | bytes 835592 | tf_op jit(solution)/shard_map/probe_sum/ppermute | solution.py:634
  98.6 0.1 collective-permute-start.14
  98.7 0.6 copy.12
  99.3 0.0 collective-permute-done.12.other
  99.3 1.1 probe_gather.1
  100.4 6.2 %collective-permute-done.14.even = f32[2,128,256]{2,1,0:T(8,128)} collective-permute-done((f32[2,128,256]{2,1,0:T(8,128)}, f32[2,128,256]{2,1,0:T(8,128)}, u32[]{:S(2)}, u32[]{:S(2)}) %collective-permute-start.14) | collective-permute-done | bytes 262176 | tf_op jit(solution)/shard_map/probe_sum/ppermute | solution.py:634
  106.6 1.1 collective-permute-done.13.odd
  107.7 1.9 %shard_map.104 = f32[2,256,256]{2,1,0:T(8,128)} custom-call(f32[2,256,256]{2,1,0:T(8,128)S(1)} %get-tuple-element.50.center, f32[2,128,256]{2,1,0:T(8,128)} %collective-permute-done.14.even, f32[2,136,256]{2,1,0:T(8,128)S(1)} %collective-permute-done.13.odd, f32[2,512,128]{2,1,0:T(8,128)S(1)} %collective-permute-done.7.cross, ...), custom_call_target="tpu_custom_call" | custom-call | flops 1048576 | bytes 3145728 | tf_op jit(solution)/shard_map/pallas_call | solution.py:541
  (9 shorter events, 0.1 us)
Async XLA Ops:
  0.6 0.7 copy-start.2
  1.3 1.0 copy-start
  2.4 10.0 %copy-start.10 = (bf16[256,768]{1,0:T(8,128)(2,1)S(1)}, bf16[256,768]{1,0:T(8,128)(2,1)}, u32[]{:S(2)}) copy-start(bf16[256,768]{1,0:T(8,128)(2,1)} %constant.18.clone.rows) | copy-start | bytes 1179652
  3.1 18.4 %collective-permute-start.2 = (f32[2,280,128]{2,1,0:T(8,128)S(1)}, f32[2,280,128]{2,1,0:T(8,128)S(1)}, u32[]{:S(2)}, u32[]{:S(2)}) collective-permute-start(f32[2,280,128]{2,1,0:T(8,128)S(1)} %get-tuple-element.43), channel_id=1, source_target_pairs={{1,2},{2,1},{3,4},{4,3},{5,6},{6,5},{7,8},{8,7},{9,10},{10,9},{11,... | collective-permute-start | bytes 860168 | tf_op jit(solution)/shard_map/object_halo/ppermute | solution.py:638
  7.2 14.3 %collective-permute-start = (f32[2,136,256]{2,1,0:T(8,128)S(1)}, f32[2,136,256]{2,1,0:T(8,128)S(1)}, u32[]{:S(2)}, u32[]{:S(2)}) collective-permute-start(f32[2,136,256]{2,1,0:T(8,128)S(1)} %get-tuple-element.41), channel_id=1, source_target_pairs={{16,32},{32,16},{48,64},{64,48},{80,96},{96,80},{17,33},{33,17},{4... | collective-permute-start | bytes 835592 | tf_op jit(solution)/shard_map/object_halo/ppermute | solution.py:634
  12.1 9.4 %collective-permute-start.1 = (f32[2,136,256]{2,1,0:T(8,128)S(1)}, f32[2,136,256]{2,1,0:T(8,128)S(1)}, u32[]{:S(2)}, u32[]{:S(2)}) collective-permute-start(f32[2,136,256]{2,1,0:T(8,128)S(1)} %get-tuple-element.42), channel_id=1, source_target_pairs={{0,16},{16,0},{32,48},{48,32},{64,80},{80,64},{96,112},{112,96},{1... | collective-permute-start | bytes 835592 | tf_op jit(solution)/shard_map/object_halo/ppermute | solution.py:634
  12.2 3.7 %collective-permute-start.3 = (f32[2,264,128]{2,1,0:T(8,128)S(1)}, f32[2,264,128]{2,1,0:T(8,128)S(1)}, u32[]{:S(2)}, u32[]{:S(2)}) collective-permute-start(f32[2,264,128]{2,1,0:T(8,128)S(1)} %get-tuple-element.44), channel_id=1, source_target_pairs={{0,1},{1,0},{2,3},{3,2},{4,5},{5,4},{6,7},{7,6},{8,9},{9,8},{10,11... | collective-permute-start | bytes 811016 | tf_op jit(solution)/shard_map/object_halo/ppermute | solution.py:638
  12.3 1.2 %copy-start.3 = (f32[1,1,4,256,256]{4,3,2,1,0:T(8,128)S(1)}, f32[1,1,4,256,256]{4,3,2,1,0:T(8,128)}, u32[]{:S(2)}) copy-start(f32[1,1,4,256,256]{4,3,2,1,0:T(8,128)} %param.9) | copy-start | bytes 3145732
  13.5 1.0 copy-start.11
  14.5 16.2 %copy-start.4 = (f32[2,2,256,256]{3,2,1,0:T(8,128)S(1)}, f32[2,2,256,256]{3,2,1,0:T(8,128)}, u32[]{:S(2)}) copy-start(f32[2,2,256,256]{3,2,1,0:T(8,128)} %probe.1) | copy-start | bytes 3145732
  14.5 16.2 %copy-start.9 = (bf16[2,2,2,256,256]{4,3,2,1,0:T(8,128)(2,1)S(1)}, bf16[2,2,2,256,256]{4,3,2,1,0:T(8,128)(2,1)}, u32[]{:S(2)}) copy-start(bf16[2,2,2,256,256]{4,3,2,1,0:T(8,128)(2,1)} %constant.19.clone.matrices) | copy-start | bytes 3145732
  21.5 9.2 %copy-start.1 = (f32[2,256,256]{2,1,0:T(8,128)S(1)}, f32[2,256,256]{2,1,0:T(8,128)}, u32[]{:S(2)}) copy-start(f32[2,256,256]{2,1,0:T(8,128)} %own.3) | copy-start | bytes 1572868
  21.6 2.7 %collective-permute-start.5 = (f32[2,2,136,128]{3,2,1,0:T(8,128)S(1)}, f32[2,2,136,128]{3,2,1,0:T(8,128)S(1)}, u32[]{:S(2)}, u32[]{:S(2)}) collective-permute-start(f32[2,2,136,128]{3,2,1,0:T(8,128)S(1)} %get-tuple-element.86), channel_id=1, source_target_pairs={{0,1},{1,0},{2,3},{3,2},{4,5},{5,4},{6,7},{7,6},{8,9},{9,8},{10,11... | collective-permute-start | bytes 835592 | tf_op jit(solution)/shard_map/object_corners/ppermute | solution.py:638
  21.7 9.1 %collective-permute-start.4 = (f32[2,2,136,128]{3,2,1,0:T(8,128)S(1)}, f32[2,2,136,128]{3,2,1,0:T(8,128)S(1)}, u32[]{:S(2)}, u32[]{:S(2)}) collective-permute-start(f32[2,2,136,128]{3,2,1,0:T(8,128)S(1)} %get-tuple-element.87), channel_id=1, source_target_pairs={{1,2},{2,1},{3,4},{4,3},{5,6},{6,5},{7,8},{8,7},{9,10},{10,9},{11,... | collective-permute-start | bytes 835592 | tf_op jit(solution)/shard_map/object_corners/ppermute | solution.py:638
  44.8 4.6 %collective-permute-start.6 = (f32[16,88,128]{2,1,0:T(8,128)S(1)}, f32[16,88,128]{2,1,0:T(8,128)S(1)}, u32[]{:S(2)}, u32[]{:S(2)}) collective-permute-start(f32[16,88,128]{2,1,0:T(8,128)S(1)} %get-tuple-element.52), channel_id=1, source_target_pairs={{0,1},{1,0},{2,3},{3,2},{4,5},{5,4},{6,7},{7,6},{8,9},{9,8},{10,11... | collective-permute-start | bytes 2162696 | tf_op jit(solution)/shard_map/probe_reduce/ppermute | solution.py:638
  44.9 16.5 %collective-permute-start.7 = (f32[2,512,128]{2,1,0:T(8,128)}, f32[2,512,128]{2,1,0:T(8,128)S(1)}, u32[]{:S(2)}, u32[]{:S(2)}) collective-permute-start(f32[2,512,128]{2,1,0:T(8,128)} %get-tuple-element.58), channel_id=1, source_target_pairs={{1,2},{2,1},{3,4},{4,3},{5,6},{6,5},{7,8},{8,7},{9,10},{10,9},{11,... | collective-permute-start | bytes 1572872 | tf_op jit(solution)/shard_map/gradient_columns/ppermute | solution.py:638
  49.3 12.0 %collective-permute-start.8 = (f32[2,512,128]{2,1,0:T(8,128)S(1)}, f32[2,512,128]{2,1,0:T(8,128)S(1)}, u32[]{:S(2)}, u32[]{:S(2)}) collective-permute-start(f32[2,512,128]{2,1,0:T(8,128)S(1)} %get-tuple-element.59), channel_id=1, source_target_pairs={{0,1},{1,0},{2,3},{3,2},{4,5},{5,4},{6,7},{7,6},{8,9},{9,8},{10,11... | collective-permute-start | bytes 1572872 | tf_op jit(solution)/shard_map/gradient_columns/ppermute | solution.py:638
  50.3 18.1 %all-to-all-start = ((f32[16,88,128]{2,1,0:T(8,128)}), f32[16,88,128]{2,1,0:T(8,128)S(1)}, u32[]{:S(2)}, u32[]{:S(2)}) async-start(f32[16,88,128]{2,1,0:T(8,128)} %add.3), calls=%async_computation | async-start | bytes 1441792 | tf_op jit(solution)/shard_map/probe_reduce/all_to_all | solution.py:692
  57.3 4.8 %copy-start.5 = (f32[2,2,256,256]{3,2,1,0:T(8,128)S(1)}, f32[2,2,256,256]{3,2,1,0:T(8,128)}, u32[]{:S(2)}) copy-start(f32[2,2,256,256]{3,2,1,0:T(8,128)} %probe.1) | copy-start | bytes 3145732
  61.4 0.7 copy-start.8
  62.1 2.5 %copy-start.6 = (f32[2,136,256]{2,1,0:T(8,128)}, f32[2,136,256]{2,1,0:T(8,128)S(1)}, u32[]{:S(2)}) copy-start(f32[2,136,256]{2,1,0:T(8,128)S(1)} %get-tuple-element.70) | copy-start | bytes 835588
  68.5 4.4 %collective-permute-start.11 = (f32[88,128]{1,0:T(8,128)S(1)}, f32[88,128]{1,0:T(8,128)S(1)}, u32[]{:S(2)}, u32[]{:S(2)}) collective-permute-start(f32[88,128]{1,0:T(8,128)S(1)} %probe_sum.2.own), channel_id=1, source_target_pairs={{0,66},{1,67},{2,0},{3,1},{4,70},{5,71},{6,4},{7,5},{8,74},{9,75},... | collective-permute-start | bytes 135176 | tf_op jit(solution)/shard_map/probe_sum/ppermute | solution.py:648
  70.6 4.4 %collective-permute-start.10 = (f32[88,128]{1,0:T(8,128)S(1)}, f32[88,128]{1,0:T(8,128)S(1)}, u32[]{:S(2)}, u32[]{:S(2)}) collective-permute-start(f32[88,128]{1,0:T(8,128)S(1)} %probe_sum.2.own), channel_id=1, source_target_pairs={{0,64},{1,65},{2,66},{3,67},{4,68},{5,69},{6,70},{7,71},{8,72},{9,... | collective-permute-start | bytes 135176 | tf_op jit(solution)/shard_map/probe_sum/ppermute | solution.py:648
  72.1 4.1 %collective-permute-start.9 = (f32[88,128]{1,0:T(8,128)S(1)}, f32[88,128]{1,0:T(8,128)S(1)}, u32[]{:S(2)}, u32[]{:S(2)}) collective-permute-start(f32[88,128]{1,0:T(8,128)S(1)} %probe_sum.2.own), channel_id=1, source_target_pairs={{0,2},{1,3},{2,64},{3,65},{4,6},{5,7},{6,68},{7,69},{8,10},{9,11},... | collective-permute-start | bytes 135176 | tf_op jit(solution)/shard_map/probe_sum/ppermute | solution.py:648
  77.1 16.8 %copy-start.7 = (f32[2,136,256]{2,1,0:T(8,128)S(1)}, f32[2,136,256]{2,1,0:T(8,128)}, u32[]{:S(2)}) copy-start(f32[2,136,256]{2,1,0:T(8,128)} %copy-done.6) | copy-start | bytes 835588
  77.1 12.7 %all-to-all-start.1 = ((f32[16,64,128]{2,1,0:T(8,128)}), f32[16,64,128]{2,1,0:T(8,128)S(1)}, u32[]{:S(2)}, u32[]{:S(2)}) async-start(f32[16,64,128]{2,1,0:T(8,128)} %get-tuple-element.66), calls=%async_computation.1 | async-start | bytes 1048576 | tf_op jit(solution)/shard_map/probe_gather/all_to_all | solution.py:709
  89.9 9.4 %collective-permute-start.12 = (f32[16,64,128]{2,1,0:T(8,128)S(1)}, f32[16,64,128]{2,1,0:T(8,128)S(1)}, u32[]{:S(2)}, u32[]{:S(2)}) collective-permute-start(f32[16,64,128]{2,1,0:T(8,128)S(1)} %all-to-all-done.1.mine), channel_id=1, source_target_pairs={{0,1},{1,0},{2,3},{3,2},{4,5},{5,4},{6,7},{7,6},{8,9},{9,8},{10,11... | collective-permute-start | bytes 1572872 | tf_op jit(solution)/shard_map/probe_gather/ppermute | solution.py:638
  93.9 13.8 %collective-permute-start.13 = (f32[2,136,256]{2,1,0:T(8,128)S(1)}, f32[2,136,256]{2,1,0:T(8,128)S(1)}, u32[]{:S(2)}, u32[]{:S(2)}) collective-permute-start(f32[2,136,256]{2,1,0:T(8,128)S(1)} %copy-done.7), channel_id=1, source_target_pairs={{16,32},{32,16},{48,64},{64,48},{80,96},{96,80},{17,33},{33,17},{4... | collective-permute-start | bytes 835592 | tf_op jit(solution)/shard_map/probe_sum/ppermute | solution.py:634
  98.6 8.0 %collective-permute-start.14 = (f32[2,128,256]{2,1,0:T(8,128)}, f32[2,128,256]{2,1,0:T(8,128)}, u32[]{:S(2)}, u32[]{:S(2)}) collective-permute-start(f32[2,128,256]{2,1,0:T(8,128)} %copy-done.8), channel_id=1, source_target_pairs={{0,16},{16,0},{32,48},{48,32},{64,80},{80,64},{96,112},{112,96},{1... | collective-permute-start | bytes 786440 | tf_op jit(solution)/shard_map/probe_sum/ppermute | solution.py:634

commit v15 on v14

--- a/solution.py
+++ b/solution.py
@@ -707,14 +707,13 @@
 
     with jax.named_scope("probe_gather"):
         gathered = lax.all_to_all(spread_out, AXES, 0, 0, axis_index_groups=groups, tiled=True)
+        object_update = update([center, even, odd, cross, same, light])
         relative_error = ratio[0, :1]
         position_step = steps[:, 0].reshape(1, 1, -1, 2)
-        tied = (gathered, relative_error, position_step)
-        gathered, relative_error, position_step = lax.optimization_barrier(tied)
+        tied = (gathered, object_update, relative_error, position_step)
+        gathered, object_update, relative_error, position_step = lax.optimization_barrier(tied)
         probe_update = assemble(gathered, swap_columns(gathered, 0)).reshape(probe.shape)
 
-    probe_update, odd, even = lax.optimization_barrier((probe_update, odd, even))
-    object_update = update([center, even, odd, cross, same, light])
     return (object_update, probe_update, position_step, relative_error)
 
 

time: 110 us -> 104 us (0.945)
  starting transfers between devices: 42.3 us -> 38.2 us
  waiting for transfers between devices: 36.8 us -> 35.2 us
    all_to_all x1, waiting for transfers between devices: 6.27 us -> 0.01 us  [local(): lax.all_to_all(spread_out, AXES, 0, 0, axis_index_groups=groups, tiled=True)]
    ppermute x4, waiting for transfers between devices: 12.9 us -> 16.9 us  [swap_rows(): return lax.ppermute(value, 'row', pairs_from(first, lax.axis_size('row')))]
    ppermute x8, starting transfers between devices: 15.5 us -> 13.3 us  [swap_columns(): return lax.ppermute(value, 'col', pairs_from(first, lax.axis_size('col')))]
    ppermute x4, starting transfers between devices: 9.73 us -> 7.79 us  [swap_rows(): return lax.ppermute(value, 'row', pairs_from(first, lax.axis_size('row')))]
    unnamed x25 -> x23, local copies, waits for them, and re-layouts: 5.3 us -> 5.29 us
where the time goes in v15:
time: 104 us; the launch traced here: 103 us
  starting transfers between devices  38.2 us (37%)
  waiting for transfers between devices  35.2 us (34%)
  Pallas kernels  22 us (21%)
  local copies, waits for them, and re-layouts  6.01 us (6%)
    ppermute x4, waiting for transfers between devices, swap_rows(): return lax.ppermute(value, 'row', pairs_from(first, lax.axis_size('row')))  16.9 us
    pallas_call x1, Pallas kernels, transforms(): pl.pallas_call(transform_kernel, out_shape=shaped([halves, halves]) + [ja...  14.2 us
    ppermute x8, starting transfers between devices, swap_columns(): return lax.ppermute(value, 'col', pairs_from(first, lax.axis_size('col')))  13.3 us
    ppermute x8, waiting for transfers between devices, swap_columns(): return lax.ppermute(value, 'col', pairs_from(first, lax.axis_size('col')))  11.4 us
    ppermute x4, starting transfers between devices, swap_rows(): return lax.ppermute(value, 'row', pairs_from(first, lax.axis_size('row')))  7.79 us
    pallas_call x7, Pallas kernels, simple(): return call(*scalars, *arrays)  7.03 us
    all_to_all x1, starting transfers between devices, local(): lax.all_to_all(chunk, AXES, 0, 0, axis_index_groups=groups, tiled=True)  6.97 us
    all_to_all x1, starting transfers between devices, local(): lax.all_to_all(spread_out, AXES, 0, 0, axis_index_groups=groups, tiled=True)  5.76 us
  transfers between devices with their start and end apart: 17, of which 9 were waited for; matrix products, arithmetic and copies ran while one was open for 2% of the time, Pallas kernels for 5%

profile of v15, /device:TPU:25, one launch (start us, length us, event | category | flops | bytes accessed | tf_op | source)
XLA Modules:
  0.0 103.3 jit_solution(7070795247804551714)
XLA Ops:
  0.6 0.0 copy-start.2
  0.6 0.7 copy-done.2
  1.3 0.0 copy-start
  1.3 1.0 %copy-done = f32[2,256,256]{2,1,0:T(8,128)S(1)} copy-done((f32[2,256,256]{2,1,0:T(8,128)S(1)}, f32[2,256,256]{2,1,0:T(8,128)}, u32[]{:S(2)}) %copy-start) | copy-done | bytes 524312
  2.4 0.0 copy-start.9
  2.4 0.8 object_halo.1
  3.1 4.1 %collective-permute-start.2 = (f32[2,280,128]{2,1,0:T(8,128)S(1)}, f32[2,280,128]{2,1,0:T(8,128)S(1)}, u32[]{:S(2)}, u32[]{:S(2)}) collective-permute-start(f32[2,280,128]{2,1,0:T(8,128)S(1)} %get-tuple-element.41), channel_id=1, source_target_pairs={{1,2},{2,1},{3,4},{4,3},{5,6},{6,5},{7,8},{8,7},{9,10},{10,9},{11,... | collective-permute-start | bytes 860168 | tf_op jit(solution)/shard_map/object_halo/ppermute | solution.py:638
  7.2 4.9 %collective-permute-start = (f32[2,136,256]{2,1,0:T(8,128)S(1)}, f32[2,136,256]{2,1,0:T(8,128)S(1)}, u32[]{:S(2)}, u32[]{:S(2)}) collective-permute-start(f32[2,136,256]{2,1,0:T(8,128)S(1)} %get-tuple-element.39), channel_id=1, source_target_pairs={{16,32},{32,16},{48,64},{64,48},{80,96},{96,80},{17,33},{33,17},{4... | collective-permute-start | bytes 835592 | tf_op jit(solution)/shard_map/object_halo/ppermute | solution.py:634
  12.1 0.1 collective-permute-start.1
  12.2 0.1 collective-permute-start.3
  12.3 0.0 copy-done.9
  12.3 0.0 copy-start.3
  12.3 1.2 %copy-done.3 = f32[1,1,4,256,256]{4,3,2,1,0:T(8,128)S(1)} copy-done((f32[1,1,4,256,256]{4,3,2,1,0:T(8,128)S(1)}, f32[1,1,4,256,256]{4,3,2,1,0:T(8,128)}, u32[]{:S(2)}) %copy-start.3) | copy-done | bytes 1048600
  13.5 0.0 copy-start.10
  13.5 1.0 copy-done.10
  14.5 1.3 %shard_map.102.measured = f32[4,256,256]{2,1,0:T(8,128)S(1)} custom-call(f32[4,256,256]{2,1,0:T(8,128)S(1)} %bitcast.13, bf16[768,256]{1,0:T(8,128)(2,1)S(1)} %copy-done.10, bf16[256,768]{1,0:T(8,128)(2,1)S(1)} %copy-done.9), custom_call_target="tpu_custom_call" | custom-call | flops 1073741824 | bytes 3145728 | tf_op jit(solution)/shard_map/pallas_call | solution.py:541
  15.9 0.0 collective-permute-done.3.same
  15.9 5.6 %collective-permute-done.odd_strip = f32[2,136,256]{2,1,0:T(8,128)S(1)} collective-permute-done((f32[2,136,256]{2,1,0:T(8,128)S(1)}, f32[2,136,256]{2,1,0:T(8,128)S(1)}, u32[]{:S(2)}, u32[]{:S(2)}) %collective-permute-start) | collective-permute-done | bytes 278560 | tf_op jit(solution)/shard_map/object_halo/ppermute | solution.py:634
  21.5 0.0 collective-permute-done.1.even_strip
  21.5 0.0 collective-permute-done.2.cross
  21.6 0.1 collective-permute-start.5
  21.7 2.6 %collective-permute-start.4 = (f32[2,2,136,128]{3,2,1,0:T(8,128)S(1)}, f32[2,2,136,128]{3,2,1,0:T(8,128)S(1)}, u32[]{:S(2)}, u32[]{:S(2)}) collective-permute-start(f32[2,2,136,128]{3,2,1,0:T(8,128)S(1)} %get-tuple-element.83), channel_id=1, source_target_pairs={{1,2},{2,1},{3,4},{4,3},{5,6},{6,5},{7,8},{8,7},{9,10},{10,9},{11,... | collective-permute-start | bytes 835592 | tf_op jit(solution)/shard_map/object_corners/ppermute | solution.py:638
  24.3 0.0 collective-permute-done.5.same_corner
  24.3 6.4 %collective-permute-done.4.cross_corner = f32[2,2,136,128]{3,2,1,0:T(8,128)S(1)} collective-permute-done((f32[2,2,136,128]{3,2,1,0:T(8,128)S(1)}, f32[2,2,136,128]{3,2,1,0:T(8,128)S(1)}, u32[]{:S(2)}, u32[]{:S(2)}) %collective-permute-start.4) | collective-permute-done | bytes 278560 | tf_op jit(solution)/shard_map/object_corners/ppermute | solution.py:638
  30.7 0.0 copy-done.4
  30.7 0.0 copy-done.8
  30.7 0.0 copy-done.1
  30.7 14.2 %shard_map.103 = (f32[16,88,128]{2,1,0:T(8,128)S(1)}, f32[16,88,128]{2,1,0:T(8,128)S(1)}, s32[8,128]{1,0:T(8,128)S(1)}, f32[2,256,256]{2,1,0:T(8,128)S(1)}, f32[...) custom-call(s32[2,4]{1,0:T(2,128)S(1)} %bitcast.11, ...), custom_call_target="tpu_custom_call" | custom-call | flops 13958643712 | bytes 12582912 | tf_op jit(solution)/shard_map/pallas_call | solution.py:586
  45.0 0.1 collective-permute-start.6
  45.1 4.4 %collective-permute-start.7 = (f32[2,512,128]{2,1,0:T(8,128)}, f32[2,512,128]{2,1,0:T(8,128)S(1)}, u32[]{:S(2)}, u32[]{:S(2)}) collective-permute-start(f32[2,512,128]{2,1,0:T(8,128)} %get-tuple-element.55), channel_id=1, source_target_pairs={{1,2},{2,1},{3,4},{4,3},{5,6},{6,5},{7,8},{8,7},{9,10},{10,9},{11,... | collective-permute-start | bytes 1572872 | tf_op jit(solution)/shard_map/gradient_columns/ppermute | solution.py:638
  49.5 0.1 collective-permute-start.8
  49.5 0.0 collective-permute-done.6
  49.6 0.9 add.3
  50.5 7.0 %all-to-all-start = ((f32[16,88,128]{2,1,0:T(8,128)}), f32[16,88,128]{2,1,0:T(8,128)S(1)}, u32[]{:S(2)}, u32[]{:S(2)}) async-start(f32[16,88,128]{2,1,0:T(8,128)} %add.3), calls=%async_computation | async-start | bytes 1441792 | tf_op jit(solution)/shard_map/probe_reduce/all_to_all | solution.py:692
  57.5 4.0 %collective-permute-done.7.cross = f32[2,512,128]{2,1,0:T(8,128)S(1)} collective-permute-done((f32[2,512,128]{2,1,0:T(8,128)}, f32[2,512,128]{2,1,0:T(8,128)S(1)}, u32[]{:S(2)}, u32[]{:S(2)}) %collective-permute-start.7) | collective-permute-done | bytes 524320 | tf_op jit(solution)/shard_map/gradient_columns/ppermute | solution.py:638
  61.5 0.0 collective-permute-done.8.same
  61.5 0.1 gradient_rows.3
  61.6 0.0 copy-start.6
  61.6 0.7 copy-done.6
  62.3 0.0 copy-done.5
  62.3 2.7 %gradient_rows.2.light = f32[256,256]{1,0:T(8,128)S(1)} custom-call(s32[2,4]{1,0:T(2,128)S(1)} %bitcast.12, s32[8,128]{1,0:T(8,128)S(1)} %get-tuple-element.52.around, f32[2,2,256,256]{3,2,1,0:T(8,128)S(1)} %copy-done.5), custom_call_target="tpu_custom_call" | custom-call | flops 2147483648 | bytes 4194304 | tf_op jit(solution)/shard_map/gradient_rows/pallas_call | solution.py:541
  65.0 3.7 %all-to-all-done.chunk = f32[16,88,128]{2,1,0:T(8,128)S(1)} async-done(((f32[16,88,128]{2,1,0:T(8,128)}), f32[16,88,128]{2,1,0:T(8,128)S(1)}, u32[]{:S(2)}, u32[]{:S(2)}) %all-to-all-start) | async-done | bytes 720928 | tf_op jit(solution)/shard_map/probe_reduce/all_to_all | solution.py:692
  68.7 2.2 %collective-permute-start.11 = (f32[88,128]{1,0:T(8,128)S(1)}, f32[88,128]{1,0:T(8,128)S(1)}, u32[]{:S(2)}, u32[]{:S(2)}) collective-permute-start(f32[88,128]{1,0:T(8,128)S(1)} %probe_sum.2.own), channel_id=1, source_target_pairs={{0,66},{1,67},{2,0},{3,1},{4,70},{5,71},{6,4},{7,5},{8,74},{9,75},... | collective-permute-start | bytes 135176 | tf_op jit(solution)/shard_map/probe_sum/ppermute | solution.py:648
  70.8 1.5 %collective-permute-start.10 = (f32[88,128]{1,0:T(8,128)S(1)}, f32[88,128]{1,0:T(8,128)S(1)}, u32[]{:S(2)}, u32[]{:S(2)}) collective-permute-start(f32[88,128]{1,0:T(8,128)S(1)} %probe_sum.2.own), channel_id=1, source_target_pairs={{0,64},{1,65},{2,66},{3,67},{4,68},{5,69},{6,70},{7,71},{8,72},{9,... | collective-permute-start | bytes 135176 | tf_op jit(solution)/shard_map/probe_sum/ppermute | solution.py:648
  72.3 0.8 collective-permute-start.9
  73.1 0.0 collective-permute-done.11.third
  73.1 2.1 %collective-permute-done.10.second = f32[88,128]{1,0:T(8,128)S(1)} collective-permute-done((f32[88,128]{1,0:T(8,128)S(1)}, f32[88,128]{1,0:T(8,128)S(1)}, u32[]{:S(2)}, u32[]{:S(2)}) %collective-permute-start.10) | collective-permute-done | bytes 45088 | tf_op jit(solution)/shard_map/probe_sum/ppermute | solution.py:648
  75.2 1.2 %collective-permute-done.9.first = f32[88,128]{1,0:T(8,128)S(1)} collective-permute-done((f32[88,128]{1,0:T(8,128)S(1)}, f32[88,128]{1,0:T(8,128)S(1)}, u32[]{:S(2)}, u32[]{:S(2)}) %collective-permute-start.9) | collective-permute-done | bytes 45088 | tf_op jit(solution)/shard_map/probe_sum/ppermute | solution.py:648
  76.4 0.9 probe_sum.3
  77.3 5.8 %all-to-all-start.1 = ((f32[16,64,128]{2,1,0:T(8,128)}), f32[16,64,128]{2,1,0:T(8,128)S(1)}, u32[]{:S(2)}, u32[]{:S(2)}) async-start(f32[16,64,128]{2,1,0:T(8,128)} %get-tuple-element.63), calls=%async_computation.1 | async-start | bytes 1048576 | tf_op jit(solution)/shard_map/probe_gather/all_to_all | solution.py:709
  83.1 2.6 %collective-permute-start.13 = (f32[2,136,256]{2,1,0:T(8,128)S(1)}, f32[2,136,256]{2,1,0:T(8,128)S(1)}, u32[]{:S(2)}, u32[]{:S(2)}) collective-permute-start(f32[2,136,256]{2,1,0:T(8,128)S(1)} %get-tuple-element.66), channel_id=1, source_target_pairs={{16,32},{32,16},{48,64},{64,48},{80,96},{96,80},{17,33},{33,17},{4... | collective-permute-start | bytes 835592 | tf_op jit(solution)/shard_map/probe_sum/ppermute | solution.py:634
  85.6 0.0 copy-done.7
  85.7 0.3 collective-permute-start.12
  85.9 0.1 slice_reduce_fusion
  86.1 0.1 squeeze.15
  86.1 0.5 slice.16
  86.7 10.3 %collective-permute-done.12.even = f32[2,128,256]{2,1,0:T(8,128)S(1)} collective-permute-done((f32[2,128,256]{2,1,0:T(8,128)S(1)}, f32[2,128,256]{2,1,0:T(8,128)S(1)}, u32[]{:S(2)}, u32[]{:S(2)}) %collective-permute-start.12) | collective-permute-done | bytes 262176 | tf_op jit(solution)/shard_map/probe_sum/ppermute | solution.py:634
  96.9 1.0 collective-permute-done.13.odd
  97.9 1.0 probe_gather.2
  98.9 0.0 all-to-all-done.1.mine
  98.9 1.9 %collective-permute-start.14 = (f32[16,64,128]{2,1,0:T(8,128)S(1)}, f32[16,64,128]{2,1,0:T(8,128)S(1)}, u32[]{:S(2)}, u32[]{:S(2)}) collective-permute-start(f32[16,64,128]{2,1,0:T(8,128)S(1)} %all-to-all-done.1.mine), channel_id=1, source_target_pairs={{0,1},{1,0},{2,3},{3,2},{4,5},{5,4},{6,7},{7,6},{8,9},{9,8},{10,11... | collective-permute-start | bytes 1572872 | tf_op jit(solution)/shard_map/probe_gather/ppermute | solution.py:638
  100.7 0.6 copy.12
  101.4 0.9 collective-permute-done.14.other
  102.3 1.1 %probe_gather.3 = f32[4,256,256]{2,1,0:T(8,128)} custom-call(f32[16,64,128]{2,1,0:T(8,128)S(1)} %all-to-all-done.1.mine, f32[16,64,128]{2,1,0:T(8,128)S(1)} %collective-permute-done.14.other), custom_call_target="tpu_custom_call" | custom-call | flops 1048576 | bytes 2097152 | tf_op jit(solution)/shard_map/probe_gather/pallas_call | solution.py:541
  (7 shorter events, 0.1 us)
Async XLA Ops:
  0.6 0.7 copy-start.2
  1.3 1.0 %copy-start = (f32[2,256,256]{2,1,0:T(8,128)S(1)}, f32[2,256,256]{2,1,0:T(8,128)}, u32[]{:S(2)}) copy-start(f32[2,256,256]{2,1,0:T(8,128)} %own.3) | copy-start | bytes 1572868
  2.4 10.0 %copy-start.9 = (bf16[256,768]{1,0:T(8,128)(2,1)S(1)}, bf16[256,768]{1,0:T(8,128)(2,1)}, u32[]{:S(2)}) copy-start(bf16[256,768]{1,0:T(8,128)(2,1)} %constant.18.clone.rows) | copy-start | bytes 1179652
  3.1 18.4 %collective-permute-start.2 = (f32[2,280,128]{2,1,0:T(8,128)S(1)}, f32[2,280,128]{2,1,0:T(8,128)S(1)}, u32[]{:S(2)}, u32[]{:S(2)}) collective-permute-start(f32[2,280,128]{2,1,0:T(8,128)S(1)} %get-tuple-element.41), channel_id=1, source_target_pairs={{1,2},{2,1},{3,4},{4,3},{5,6},{6,5},{7,8},{8,7},{9,10},{10,9},{11,... | collective-permute-start | bytes 860168 | tf_op jit(solution)/shard_map/object_halo/ppermute | solution.py:638
  7.2 14.3 %collective-permute-start = (f32[2,136,256]{2,1,0:T(8,128)S(1)}, f32[2,136,256]{2,1,0:T(8,128)S(1)}, u32[]{:S(2)}, u32[]{:S(2)}) collective-permute-start(f32[2,136,256]{2,1,0:T(8,128)S(1)} %get-tuple-element.39), channel_id=1, source_target_pairs={{16,32},{32,16},{48,64},{64,48},{80,96},{96,80},{17,33},{33,17},{4... | collective-permute-start | bytes 835592 | tf_op jit(solution)/shard_map/object_halo/ppermute | solution.py:634
  12.1 9.4 %collective-permute-start.1 = (f32[2,136,256]{2,1,0:T(8,128)S(1)}, f32[2,136,256]{2,1,0:T(8,128)S(1)}, u32[]{:S(2)}, u32[]{:S(2)}) collective-permute-start(f32[2,136,256]{2,1,0:T(8,128)S(1)} %get-tuple-element.40), channel_id=1, source_target_pairs={{0,16},{16,0},{32,48},{48,32},{64,80},{80,64},{96,112},{112,96},{1... | collective-permute-start | bytes 835592 | tf_op jit(solution)/shard_map/object_halo/ppermute | solution.py:634
  12.2 3.7 %collective-permute-start.3 = (f32[2,264,128]{2,1,0:T(8,128)S(1)}, f32[2,264,128]{2,1,0:T(8,128)S(1)}, u32[]{:S(2)}, u32[]{:S(2)}) collective-permute-start(f32[2,264,128]{2,1,0:T(8,128)S(1)} %get-tuple-element.42), channel_id=1, source_target_pairs={{0,1},{1,0},{2,3},{3,2},{4,5},{5,4},{6,7},{7,6},{8,9},{9,8},{10,11... | collective-permute-start | bytes 811016 | tf_op jit(solution)/shard_map/object_halo/ppermute | solution.py:638
  12.3 1.2 %copy-start.3 = (f32[1,1,4,256,256]{4,3,2,1,0:T(8,128)S(1)}, f32[1,1,4,256,256]{4,3,2,1,0:T(8,128)}, u32[]{:S(2)}) copy-start(f32[1,1,4,256,256]{4,3,2,1,0:T(8,128)} %param.9) | copy-start | bytes 3145732
  13.5 1.0 copy-start.10
  14.5 16.2 %copy-start.4 = (f32[2,2,256,256]{3,2,1,0:T(8,128)S(1)}, f32[2,2,256,256]{3,2,1,0:T(8,128)}, u32[]{:S(2)}) copy-start(f32[2,2,256,256]{3,2,1,0:T(8,128)} %probe.1) | copy-start | bytes 3145732
  14.5 16.2 %copy-start.8 = (bf16[2,2,2,256,256]{4,3,2,1,0:T(8,128)(2,1)S(1)}, bf16[2,2,2,256,256]{4,3,2,1,0:T(8,128)(2,1)}, u32[]{:S(2)}) copy-start(bf16[2,2,2,256,256]{4,3,2,1,0:T(8,128)(2,1)} %constant.19.clone.matrices) | copy-start | bytes 3145732
  21.5 9.2 %copy-start.1 = (f32[2,256,256]{2,1,0:T(8,128)S(1)}, f32[2,256,256]{2,1,0:T(8,128)}, u32[]{:S(2)}) copy-start(f32[2,256,256]{2,1,0:T(8,128)} %own.3) | copy-start | bytes 1572868
  21.6 2.7 %collective-permute-start.5 = (f32[2,2,136,128]{3,2,1,0:T(8,128)S(1)}, f32[2,2,136,128]{3,2,1,0:T(8,128)S(1)}, u32[]{:S(2)}, u32[]{:S(2)}) collective-permute-start(f32[2,2,136,128]{3,2,1,0:T(8,128)S(1)} %get-tuple-element.82), channel_id=1, source_target_pairs={{0,1},{1,0},{2,3},{3,2},{4,5},{5,4},{6,7},{7,6},{8,9},{9,8},{10,11... | collective-permute-start | bytes 835592 | tf_op jit(solution)/shard_map/object_corners/ppermute | solution.py:638
  21.7 9.1 %collective-permute-start.4 = (f32[2,2,136,128]{3,2,1,0:T(8,128)S(1)}, f32[2,2,136,128]{3,2,1,0:T(8,128)S(1)}, u32[]{:S(2)}, u32[]{:S(2)}) collective-permute-start(f32[2,2,136,128]{3,2,1,0:T(8,128)S(1)} %get-tuple-element.83), channel_id=1, source_target_pairs={{1,2},{2,1},{3,4},{4,3},{5,6},{6,5},{7,8},{8,7},{9,10},{10,9},{11,... | collective-permute-start | bytes 835592 | tf_op jit(solution)/shard_map/object_corners/ppermute | solution.py:638
  45.0 4.6 %collective-permute-start.6 = (f32[16,88,128]{2,1,0:T(8,128)S(1)}, f32[16,88,128]{2,1,0:T(8,128)S(1)}, u32[]{:S(2)}, u32[]{:S(2)}) collective-permute-start(f32[16,88,128]{2,1,0:T(8,128)S(1)} %get-tuple-element.49), channel_id=1, source_target_pairs={{0,1},{1,0},{2,3},{3,2},{4,5},{5,4},{6,7},{7,6},{8,9},{9,8},{10,11... | collective-permute-start | bytes 2162696 | tf_op jit(solution)/shard_map/probe_reduce/ppermute | solution.py:638
  45.1 16.4 %collective-permute-start.7 = (f32[2,512,128]{2,1,0:T(8,128)}, f32[2,512,128]{2,1,0:T(8,128)S(1)}, u32[]{:S(2)}, u32[]{:S(2)}) collective-permute-start(f32[2,512,128]{2,1,0:T(8,128)} %get-tuple-element.55), channel_id=1, source_target_pairs={{1,2},{2,1},{3,4},{4,3},{5,6},{6,5},{7,8},{8,7},{9,10},{10,9},{11,... | collective-permute-start | bytes 1572872 | tf_op jit(solution)/shard_map/gradient_columns/ppermute | solution.py:638
  49.5 12.0 %collective-permute-start.8 = (f32[2,512,128]{2,1,0:T(8,128)}, f32[2,512,128]{2,1,0:T(8,128)S(1)}, u32[]{:S(2)}, u32[]{:S(2)}) collective-permute-start(f32[2,512,128]{2,1,0:T(8,128)} %get-tuple-element.56), channel_id=1, source_target_pairs={{0,1},{1,0},{2,3},{3,2},{4,5},{5,4},{6,7},{7,6},{8,9},{9,8},{10,11... | collective-permute-start | bytes 1572872 | tf_op jit(solution)/shard_map/gradient_columns/ppermute | solution.py:638
  50.5 18.1 %all-to-all-start = ((f32[16,88,128]{2,1,0:T(8,128)}), f32[16,88,128]{2,1,0:T(8,128)S(1)}, u32[]{:S(2)}, u32[]{:S(2)}) async-start(f32[16,88,128]{2,1,0:T(8,128)} %add.3), calls=%async_computation | async-start | bytes 1441792 | tf_op jit(solution)/shard_map/probe_reduce/all_to_all | solution.py:692
  57.5 4.8 %copy-start.5 = (f32[2,2,256,256]{3,2,1,0:T(8,128)S(1)}, f32[2,2,256,256]{3,2,1,0:T(8,128)}, u32[]{:S(2)}) copy-start(f32[2,2,256,256]{3,2,1,0:T(8,128)} %probe.1) | copy-start | bytes 3145732
  61.6 0.7 copy-start.6
  68.7 4.4 %collective-permute-start.11 = (f32[88,128]{1,0:T(8,128)S(1)}, f32[88,128]{1,0:T(8,128)S(1)}, u32[]{:S(2)}, u32[]{:S(2)}) collective-permute-start(f32[88,128]{1,0:T(8,128)S(1)} %probe_sum.2.own), channel_id=1, source_target_pairs={{0,66},{1,67},{2,0},{3,1},{4,70},{5,71},{6,4},{7,5},{8,74},{9,75},... | collective-permute-start | bytes 135176 | tf_op jit(solution)/shard_map/probe_sum/ppermute | solution.py:648
  70.8 4.4 %collective-permute-start.10 = (f32[88,128]{1,0:T(8,128)S(1)}, f32[88,128]{1,0:T(8,128)S(1)}, u32[]{:S(2)}, u32[]{:S(2)}) collective-permute-start(f32[88,128]{1,0:T(8,128)S(1)} %probe_sum.2.own), channel_id=1, source_target_pairs={{0,64},{1,65},{2,66},{3,67},{4,68},{5,69},{6,70},{7,71},{8,72},{9,... | collective-permute-start | bytes 135176 | tf_op jit(solution)/shard_map/probe_sum/ppermute | solution.py:648
  72.3 4.1 %collective-permute-start.9 = (f32[88,128]{1,0:T(8,128)S(1)}, f32[88,128]{1,0:T(8,128)S(1)}, u32[]{:S(2)}, u32[]{:S(2)}) collective-permute-start(f32[88,128]{1,0:T(8,128)S(1)} %probe_sum.2.own), channel_id=1, source_target_pairs={{0,2},{1,3},{2,64},{3,65},{4,6},{5,7},{6,68},{7,69},{8,10},{9,11},... | collective-permute-start | bytes 135176 | tf_op jit(solution)/shard_map/probe_sum/ppermute | solution.py:648
  77.3 8.3 %copy-start.7 = (f32[2,128,256]{2,1,0:T(8,128)S(1)}, f32[2,128,256]{2,1,0:T(8,128)}, u32[]{:S(2)}) copy-start(f32[2,128,256]{2,1,0:T(8,128)} %copy-done.6) | copy-start | bytes 786436
  77.3 21.5 %all-to-all-start.1 = ((f32[16,64,128]{2,1,0:T(8,128)}), f32[16,64,128]{2,1,0:T(8,128)S(1)}, u32[]{:S(2)}, u32[]{:S(2)}) async-start(f32[16,64,128]{2,1,0:T(8,128)} %get-tuple-element.63), calls=%async_computation.1 | async-start | bytes 1048576 | tf_op jit(solution)/shard_map/probe_gather/all_to_all | solution.py:709
  83.1 14.8 %collective-permute-start.13 = (f32[2,136,256]{2,1,0:T(8,128)S(1)}, f32[2,136,256]{2,1,0:T(8,128)S(1)}, u32[]{:S(2)}, u32[]{:S(2)}) collective-permute-start(f32[2,136,256]{2,1,0:T(8,128)S(1)} %get-tuple-element.66), channel_id=1, source_target_pairs={{16,32},{32,16},{48,64},{64,48},{80,96},{96,80},{17,33},{33,17},{4... | collective-permute-start | bytes 835592 | tf_op jit(solution)/shard_map/probe_sum/ppermute | solution.py:634
  85.7 11.3 %collective-permute-start.12 = (f32[2,128,256]{2,1,0:T(8,128)S(1)}, f32[2,128,256]{2,1,0:T(8,128)S(1)}, u32[]{:S(2)}, u32[]{:S(2)}) collective-permute-start(f32[2,128,256]{2,1,0:T(8,128)S(1)} %copy-done.7), channel_id=1, source_target_pairs={{0,16},{16,0},{32,48},{48,32},{64,80},{80,64},{96,112},{112,96},{1... | collective-permute-start | bytes 786440 | tf_op jit(solution)/shard_map/probe_sum/ppermute | solution.py:634
  98.9 3.4 %collective-permute-start.14 = (f32[16,64,128]{2,1,0:T(8,128)S(1)}, f32[16,64,128]{2,1,0:T(8,128)S(1)}, u32[]{:S(2)}, u32[]{:S(2)}) collective-permute-start(f32[16,64,128]{2,1,0:T(8,128)S(1)} %all-to-all-done.1.mine), channel_id=1, source_target_pairs={{0,1},{1,0},{2,3},{3,2},{4,5},{5,4},{6,7},{7,6},{8,9},{9,8},{10,11... | collective-permute-start | bytes 1572872 | tf_op jit(solution)/shard_map/probe_gather/ppermute | solution.py:638

commit v16 on v13

--- a/solution.py
+++ b/solution.py
@@ -14,7 +14,7 @@
 SIZE = 256
 HALF = 128
 CHUNK = 32
-WIDTH = 2
+WIDTH = 4
 BF = jnp.bfloat16
 F32 = jnp.float32
 AXES = ("row", "col")
@@ -603,7 +603,7 @@
             ]
             + slot * width,
         ),
-        compiler_params=params(),
+        compiler_params=pltpu.CompilerParams(vmem_limit_bytes=42 * 2**20),
         cost_estimate=cost(13 << 30, 12 << 20),
     )(starts, *arrays, measured)
 

time: 104 us -> 104 us (level)
  no operation moved by 1% of the time
where the time goes in v16:
time: 104 us; the launch traced here: 103 us
  starting transfers between devices  40 us (38%)
  waiting for transfers between devices  33.7 us (32%)
  Pallas kernels  22.1 us (21%)
  local copies, waits for them, and re-layouts  5.31 us (5%)
    ppermute x4, waiting for transfers between devices, swap_rows(): return lax.ppermute(value, 'row', pairs_from(first, lax.axis_size('row')))  14.9 us
    ppermute x8, starting transfers between devices, swap_columns(): return lax.ppermute(value, 'col', pairs_from(first, lax.axis_size('col')))  14.2 us
    pallas_call x1, Pallas kernels, transforms(): pl.pallas_call(transform_kernel, out_shape=shaped([halves, halves]) + [ja...  14.2 us
    ppermute x8, waiting for transfers between devices, swap_columns(): return lax.ppermute(value, 'col', pairs_from(first, lax.axis_size('col')))  11.2 us
    ppermute x4, starting transfers between devices, swap_rows(): return lax.ppermute(value, 'row', pairs_from(first, lax.axis_size('row')))  8.76 us
    pallas_call x7, Pallas kernels, simple(): return call(*scalars, *arrays)  7.18 us
    all_to_all x1, starting transfers between devices, local(): lax.all_to_all(chunk, AXES, 0, 0, axis_index_groups=groups, tiled=True)  6.95 us
    all_to_all x1, starting transfers between devices, local(): lax.all_to_all(spread_out, AXES, 0, 0, axis_index_groups=groups, tiled=True)  5.63 us
  transfers between devices with their start and end apart: 17, of which 9 were waited for; matrix products, arithmetic and copies ran while one was open for 2% of the time, Pallas kernels for 5%

profile of v16, /device:TPU:25, one launch (start us, length us, event | category | flops | bytes accessed | tf_op | source)
XLA Modules:
  0.0 102.9 jit_solution(3425937800451912684)
XLA Ops:
  0.6 0.0 copy-start.2
  0.6 0.7 copy-done.2
  1.3 0.0 copy-start
  1.3 1.0 %copy-done = f32[2,256,256]{2,1,0:T(8,128)S(1)} copy-done((f32[2,256,256]{2,1,0:T(8,128)S(1)}, f32[2,256,256]{2,1,0:T(8,128)}, u32[]{:S(2)}) %copy-start) | copy-done | bytes 524312
  2.4 0.0 copy-start.7
  2.4 0.8 object_halo.1
  3.1 4.1 %collective-permute-start.2 = (f32[2,280,128]{2,1,0:T(8,128)S(1)}, f32[2,280,128]{2,1,0:T(8,128)S(1)}, u32[]{:S(2)}, u32[]{:S(2)}) collective-permute-start(f32[2,280,128]{2,1,0:T(8,128)S(1)} %get-tuple-element.41), channel_id=1, source_target_pairs={{1,2},{2,1},{3,4},{4,3},{5,6},{6,5},{7,8},{8,7},{9,10},{10,9},{11,... | collective-permute-start | bytes 860168 | tf_op jit(solution)/shard_map/object_halo/ppermute | solution.py:637
  7.2 4.9 %collective-permute-start = (f32[2,136,256]{2,1,0:T(8,128)S(1)}, f32[2,136,256]{2,1,0:T(8,128)S(1)}, u32[]{:S(2)}, u32[]{:S(2)}) collective-permute-start(f32[2,136,256]{2,1,0:T(8,128)S(1)} %get-tuple-element.39), channel_id=1, source_target_pairs={{16,32},{32,16},{48,64},{64,48},{80,96},{96,80},{17,33},{33,17},{4... | collective-permute-start | bytes 835592 | tf_op jit(solution)/shard_map/object_halo/ppermute | solution.py:633
  12.1 0.1 collective-permute-start.1
  12.2 0.1 collective-permute-start.3
  12.3 0.0 copy-done.7
  12.3 0.0 copy-start.3
  12.3 1.2 %copy-done.3 = f32[1,1,4,256,256]{4,3,2,1,0:T(8,128)S(1)} copy-done((f32[1,1,4,256,256]{4,3,2,1,0:T(8,128)S(1)}, f32[1,1,4,256,256]{4,3,2,1,0:T(8,128)}, u32[]{:S(2)}) %copy-start.3) | copy-done | bytes 1048600
  13.5 0.0 copy-start.8
  13.5 1.0 copy-done.8
  14.5 0.0 copy-start.4
  14.5 0.0 copy-start.6
  14.5 1.3 %shard_map.102.measured = f32[4,256,256]{2,1,0:T(8,128)S(1)} custom-call(f32[4,256,256]{2,1,0:T(8,128)S(1)} %bitcast.13, bf16[768,256]{1,0:T(8,128)(2,1)S(1)} %copy-done.8, bf16[256,768]{1,0:T(8,128)(2,1)S(1)} %copy-done.7), custom_call_target="tpu_custom_call" | custom-call | flops 1073741824 | bytes 3145728 | tf_op jit(solution)/shard_map/pallas_call | solution.py:540
  15.9 0.0 collective-permute-done.3.same
  15.9 5.6 %collective-permute-done.odd_strip = f32[2,136,256]{2,1,0:T(8,128)S(1)} collective-permute-done((f32[2,136,256]{2,1,0:T(8,128)S(1)}, f32[2,136,256]{2,1,0:T(8,128)S(1)}, u32[]{:S(2)}, u32[]{:S(2)}) %collective-permute-start) | collective-permute-done | bytes 278560 | tf_op jit(solution)/shard_map/object_halo/ppermute | solution.py:633
  21.5 0.0 collective-permute-done.1.even_strip
  21.5 0.0 collective-permute-done.2.cross
  21.5 0.0 copy-start.1
  21.6 0.1 collective-permute-start.5
  21.7 2.8 %collective-permute-start.4 = (f32[2,2,136,128]{3,2,1,0:T(8,128)S(1)}, f32[2,2,136,128]{3,2,1,0:T(8,128)S(1)}, u32[]{:S(2)}, u32[]{:S(2)}) collective-permute-start(f32[2,2,136,128]{3,2,1,0:T(8,128)S(1)} %get-tuple-element.83), channel_id=1, source_target_pairs={{1,2},{2,1},{3,4},{4,3},{5,6},{6,5},{7,8},{8,7},{9,10},{10,9},{11,... | collective-permute-start | bytes 835592 | tf_op jit(solution)/shard_map/object_corners/ppermute | solution.py:637
  24.5 0.0 collective-permute-done.5.same_corner
  24.5 6.3 %collective-permute-done.4.cross_corner = f32[2,2,136,128]{3,2,1,0:T(8,128)S(1)} collective-permute-done((f32[2,2,136,128]{3,2,1,0:T(8,128)S(1)}, f32[2,2,136,128]{3,2,1,0:T(8,128)S(1)}, u32[]{:S(2)}, u32[]{:S(2)}) %collective-permute-start.4) | collective-permute-done | bytes 278560 | tf_op jit(solution)/shard_map/object_corners/ppermute | solution.py:637
  30.7 0.0 copy-done.4
  30.7 0.0 copy-done.6
  30.7 0.0 copy-done.1
  30.7 14.2 %shard_map.103 = (f32[16,88,128]{2,1,0:T(8,128)S(1)}, f32[16,88,128]{2,1,0:T(8,128)S(1)}, s32[8,128]{1,0:T(8,128)S(1)}, f32[2,256,256]{2,1,0:T(8,128)S(1)}, f32[...) custom-call(s32[2,4]{1,0:T(2,128)S(1)} %bitcast.11, ...), custom_call_target="tpu_custom_call" | custom-call | flops 13958643712 | bytes 12582912 | tf_op jit(solution)/shard_map/pallas_call | solution.py:585
  44.9 0.1 collective-permute-start.6
  45.0 4.4 %collective-permute-start.7 = (f32[2,512,128]{2,1,0:T(8,128)}, f32[2,512,128]{2,1,0:T(8,128)S(1)}, u32[]{:S(2)}, u32[]{:S(2)}) collective-permute-start(f32[2,512,128]{2,1,0:T(8,128)} %get-tuple-element.55), channel_id=1, source_target_pairs={{1,2},{2,1},{3,4},{4,3},{5,6},{6,5},{7,8},{8,7},{9,10},{10,9},{11,... | collective-permute-start | bytes 1572872 | tf_op jit(solution)/shard_map/gradient_columns/ppermute | solution.py:637
  49.4 0.1 collective-permute-start.8
  49.5 0.0 collective-permute-done.6
  49.5 0.9 add.3
  50.4 6.9 %all-to-all-start = ((f32[16,88,128]{2,1,0:T(8,128)}), f32[16,88,128]{2,1,0:T(8,128)S(1)}, u32[]{:S(2)}, u32[]{:S(2)}) async-start(f32[16,88,128]{2,1,0:T(8,128)} %add.3), calls=%async_computation | async-start | bytes 1441792 | tf_op jit(solution)/shard_map/probe_reduce/all_to_all | solution.py:691
  57.4 4.0 %collective-permute-done.7.cross = f32[2,512,128]{2,1,0:T(8,128)S(1)} collective-permute-done((f32[2,512,128]{2,1,0:T(8,128)}, f32[2,512,128]{2,1,0:T(8,128)S(1)}, u32[]{:S(2)}, u32[]{:S(2)}) %collective-permute-start.7) | collective-permute-done | bytes 524320 | tf_op jit(solution)/shard_map/gradient_columns/ppermute | solution.py:637
  61.4 0.0 collective-permute-done.8.same
  61.4 0.8 gradient_rows.3
  62.2 0.0 copy-done.5
  62.2 2.1 %gradient_rows.2.light = f32[256,256]{1,0:T(8,128)S(1)} custom-call(s32[2,4]{1,0:T(2,128)S(1)} %bitcast.12, s32[8,128]{1,0:T(8,128)S(1)} %get-tuple-element.52.around, f32[2,2,256,256]{3,2,1,0:T(8,128)S(1)} %copy-done.5), custom_call_target="tpu_custom_call" | custom-call | flops 2147483648 | bytes 4194304 | tf_op jit(solution)/shard_map/gradient_rows/pallas_call | solution.py:540
  64.3 4.2 %all-to-all-done.chunk = f32[16,88,128]{2,1,0:T(8,128)S(1)} async-done(((f32[16,88,128]{2,1,0:T(8,128)}), f32[16,88,128]{2,1,0:T(8,128)S(1)}, u32[]{:S(2)}, u32[]{:S(2)}) %all-to-all-start) | async-done | bytes 720928 | tf_op jit(solution)/shard_map/probe_reduce/all_to_all | solution.py:691
  68.6 2.1 %collective-permute-start.11 = (f32[88,128]{1,0:T(8,128)S(1)}, f32[88,128]{1,0:T(8,128)S(1)}, u32[]{:S(2)}, u32[]{:S(2)}) collective-permute-start(f32[88,128]{1,0:T(8,128)S(1)} %probe_sum.2.own), channel_id=1, source_target_pairs={{0,66},{1,67},{2,0},{3,1},{4,70},{5,71},{6,4},{7,5},{8,74},{9,75},... | collective-permute-start | bytes 135176 | tf_op jit(solution)/shard_map/probe_sum/ppermute | solution.py:647
  70.7 1.5 %collective-permute-start.10 = (f32[88,128]{1,0:T(8,128)S(1)}, f32[88,128]{1,0:T(8,128)S(1)}, u32[]{:S(2)}, u32[]{:S(2)}) collective-permute-start(f32[88,128]{1,0:T(8,128)S(1)} %probe_sum.2.own), channel_id=1, source_target_pairs={{0,64},{1,65},{2,66},{3,67},{4,68},{5,69},{6,70},{7,71},{8,72},{9,... | collective-permute-start | bytes 135176 | tf_op jit(solution)/shard_map/probe_sum/ppermute | solution.py:647
  72.2 0.8 collective-permute-start.9
  73.0 0.0 collective-permute-done.11.third
  73.0 2.1 %collective-permute-done.10.second = f32[88,128]{1,0:T(8,128)S(1)} collective-permute-done((f32[88,128]{1,0:T(8,128)S(1)}, f32[88,128]{1,0:T(8,128)S(1)}, u32[]{:S(2)}, u32[]{:S(2)}) %collective-permute-start.10) | collective-permute-done | bytes 45088 | tf_op jit(solution)/shard_map/probe_sum/ppermute | solution.py:647
  75.1 1.2 %collective-permute-done.9.first = f32[88,128]{1,0:T(8,128)S(1)} collective-permute-done((f32[88,128]{1,0:T(8,128)S(1)}, f32[88,128]{1,0:T(8,128)S(1)}, u32[]{:S(2)}, u32[]{:S(2)}) %collective-permute-start.9) | collective-permute-done | bytes 45088 | tf_op jit(solution)/shard_map/probe_sum/ppermute | solution.py:647
  76.3 0.9 probe_sum.3
  77.2 5.6 %all-to-all-start.1 = ((f32[16,64,128]{2,1,0:T(8,128)}), f32[16,64,128]{2,1,0:T(8,128)S(1)}, u32[]{:S(2)}, u32[]{:S(2)}) async-start(f32[16,64,128]{2,1,0:T(8,128)} %get-tuple-element.63), calls=%async_computation.1 | async-start | bytes 1048576 | tf_op jit(solution)/shard_map/probe_gather/all_to_all | solution.py:708
  82.8 0.6 collective-permute-start.12
  83.4 3.2 %collective-permute-start.13 = (f32[2,128,256]{2,1,0:T(8,128)S(1)}, f32[2,128,256]{2,1,0:T(8,128)S(1)}, u32[]{:S(2)}, u32[]{:S(2)}) collective-permute-start(f32[2,128,256]{2,1,0:T(8,128)S(1)} %get-tuple-element.66), channel_id=1, source_target_pairs={{16,32},{32,16},{48,64},{64,48},{80,96},{96,80},{17,33},{33,17},{4... | collective-permute-start | bytes 786440 | tf_op jit(solution)/shard_map/probe_sum/ppermute | solution.py:633
  86.6 0.1 slice_reduce_fusion
  86.8 0.1 squeeze.15
  86.8 0.5 slice.16
  87.4 7.0 %collective-permute-done.12.even = f32[2,128,256]{2,1,0:T(8,128)S(1)} collective-permute-done((f32[2,128,256]{2,1,0:T(8,128)}, f32[2,128,256]{2,1,0:T(8,128)S(1)}, u32[]{:S(2)}, u32[]{:S(2)}) %collective-permute-start.12) | collective-permute-done | bytes 262176 | tf_op jit(solution)/shard_map/probe_sum/ppermute | solution.py:633
  94.3 2.3 %collective-permute-done.13.odd = f32[2,128,256]{2,1,0:T(8,128)S(1)} collective-permute-done((f32[2,128,256]{2,1,0:T(8,128)S(1)}, f32[2,128,256]{2,1,0:T(8,128)S(1)}, u32[]{:S(2)}, u32[]{:S(2)}) %collective-permute-start.13) | collective-permute-done | bytes 262176 | tf_op jit(solution)/shard_map/probe_sum/ppermute | solution.py:633
  96.7 1.0 probe_gather.2
  97.6 0.0 all-to-all-done.1.mine
  97.6 2.6 %collective-permute-start.14 = (f32[16,64,128]{2,1,0:T(8,128)S(1)}, f32[16,64,128]{2,1,0:T(8,128)S(1)}, u32[]{:S(2)}, u32[]{:S(2)}) collective-permute-start(f32[16,64,128]{2,1,0:T(8,128)S(1)} %all-to-all-done.1.mine), channel_id=1, source_target_pairs={{0,1},{1,0},{2,3},{3,2},{4,5},{5,4},{6,7},{7,6},{8,9},{9,8},{10,11... | collective-permute-start | bytes 1572872 | tf_op jit(solution)/shard_map/probe_gather/ppermute | solution.py:637
  100.3 0.6 copy.12
  100.9 0.9 collective-permute-done.14.other
  101.8 1.1 %probe_gather.3 = f32[4,256,256]{2,1,0:T(8,128)} custom-call(f32[16,64,128]{2,1,0:T(8,128)S(1)} %all-to-all-done.1.mine, f32[16,64,128]{2,1,0:T(8,128)S(1)} %collective-permute-done.14.other), custom_call_target="tpu_custom_call" | custom-call | flops 1048576 | bytes 2097152 | tf_op jit(solution)/shard_map/probe_gather/pallas_call | solution.py:540
  (3 shorter events, 0.1 us)
Async XLA Ops:
  0.6 0.7 copy-start.2
  1.3 1.0 %copy-start = (f32[2,256,256]{2,1,0:T(8,128)S(1)}, f32[2,256,256]{2,1,0:T(8,128)}, u32[]{:S(2)}) copy-start(f32[2,256,256]{2,1,0:T(8,128)} %own.3) | copy-start | bytes 1572868
  2.4 10.0 %copy-start.7 = (bf16[256,768]{1,0:T(8,128)(2,1)S(1)}, bf16[256,768]{1,0:T(8,128)(2,1)}, u32[]{:S(2)}) copy-start(bf16[256,768]{1,0:T(8,128)(2,1)} %constant.18.clone.rows) | copy-start | bytes 1179652
  3.1 18.4 %collective-permute-start.2 = (f32[2,280,128]{2,1,0:T(8,128)S(1)}, f32[2,280,128]{2,1,0:T(8,128)S(1)}, u32[]{:S(2)}, u32[]{:S(2)}) collective-permute-start(f32[2,280,128]{2,1,0:T(8,128)S(1)} %get-tuple-element.41), channel_id=1, source_target_pairs={{1,2},{2,1},{3,4},{4,3},{5,6},{6,5},{7,8},{8,7},{9,10},{10,9},{11,... | collective-permute-start | bytes 860168 | tf_op jit(solution)/shard_map/object_halo/ppermute | solution.py:637
  7.2 14.3 %collective-permute-start = (f32[2,136,256]{2,1,0:T(8,128)S(1)}, f32[2,136,256]{2,1,0:T(8,128)S(1)}, u32[]{:S(2)}, u32[]{:S(2)}) collective-permute-start(f32[2,136,256]{2,1,0:T(8,128)S(1)} %get-tuple-element.39), channel_id=1, source_target_pairs={{16,32},{32,16},{48,64},{64,48},{80,96},{96,80},{17,33},{33,17},{4... | collective-permute-start | bytes 835592 | tf_op jit(solution)/shard_map/object_halo/ppermute | solution.py:633
  12.1 9.4 %collective-permute-start.1 = (f32[2,136,256]{2,1,0:T(8,128)S(1)}, f32[2,136,256]{2,1,0:T(8,128)S(1)}, u32[]{:S(2)}, u32[]{:S(2)}) collective-permute-start(f32[2,136,256]{2,1,0:T(8,128)S(1)} %get-tuple-element.40), channel_id=1, source_target_pairs={{0,16},{16,0},{32,48},{48,32},{64,80},{80,64},{96,112},{112,96},{1... | collective-permute-start | bytes 835592 | tf_op jit(solution)/shard_map/object_halo/ppermute | solution.py:633
  12.2 3.7 %collective-permute-start.3 = (f32[2,264,128]{2,1,0:T(8,128)S(1)}, f32[2,264,128]{2,1,0:T(8,128)S(1)}, u32[]{:S(2)}, u32[]{:S(2)}) collective-permute-start(f32[2,264,128]{2,1,0:T(8,128)S(1)} %get-tuple-element.42), channel_id=1, source_target_pairs={{0,1},{1,0},{2,3},{3,2},{4,5},{5,4},{6,7},{7,6},{8,9},{9,8},{10,11... | collective-permute-start | bytes 811016 | tf_op jit(solution)/shard_map/object_halo/ppermute | solution.py:637
  12.3 1.2 %copy-start.3 = (f32[1,1,4,256,256]{4,3,2,1,0:T(8,128)S(1)}, f32[1,1,4,256,256]{4,3,2,1,0:T(8,128)}, u32[]{:S(2)}) copy-start(f32[1,1,4,256,256]{4,3,2,1,0:T(8,128)} %param.9) | copy-start | bytes 3145732
  13.5 1.0 copy-start.8
  14.5 16.2 %copy-start.4 = (f32[2,2,256,256]{3,2,1,0:T(8,128)S(1)}, f32[2,2,256,256]{3,2,1,0:T(8,128)}, u32[]{:S(2)}) copy-start(f32[2,2,256,256]{3,2,1,0:T(8,128)} %probe.1) | copy-start | bytes 3145732
  14.5 16.2 %copy-start.6 = (bf16[2,2,2,256,256]{4,3,2,1,0:T(8,128)(2,1)S(1)}, bf16[2,2,2,256,256]{4,3,2,1,0:T(8,128)(2,1)}, u32[]{:S(2)}) copy-start(bf16[2,2,2,256,256]{4,3,2,1,0:T(8,128)(2,1)} %constant.19.clone.matrices) | copy-start | bytes 3145732
  21.5 9.2 %copy-start.1 = (f32[2,256,256]{2,1,0:T(8,128)S(1)}, f32[2,256,256]{2,1,0:T(8,128)}, u32[]{:S(2)}) copy-start(f32[2,256,256]{2,1,0:T(8,128)} %own.3) | copy-start | bytes 1572868
  21.6 2.9 %collective-permute-start.5 = (f32[2,2,136,128]{3,2,1,0:T(8,128)S(1)}, f32[2,2,136,128]{3,2,1,0:T(8,128)S(1)}, u32[]{:S(2)}, u32[]{:S(2)}) collective-permute-start(f32[2,2,136,128]{3,2,1,0:T(8,128)S(1)} %get-tuple-element.82), channel_id=1, source_target_pairs={{0,1},{1,0},{2,3},{3,2},{4,5},{5,4},{6,7},{7,6},{8,9},{9,8},{10,11... | collective-permute-start | bytes 835592 | tf_op jit(solution)/shard_map/object_corners/ppermute | solution.py:637
  21.7 9.1 %collective-permute-start.4 = (f32[2,2,136,128]{3,2,1,0:T(8,128)S(1)}, f32[2,2,136,128]{3,2,1,0:T(8,128)S(1)}, u32[]{:S(2)}, u32[]{:S(2)}) collective-permute-start(f32[2,2,136,128]{3,2,1,0:T(8,128)S(1)} %get-tuple-element.83), channel_id=1, source_target_pairs={{1,2},{2,1},{3,4},{4,3},{5,6},{6,5},{7,8},{8,7},{9,10},{10,9},{11,... | collective-permute-start | bytes 835592 | tf_op jit(solution)/shard_map/object_corners/ppermute | solution.py:637
  44.9 4.6 %collective-permute-start.6 = (f32[16,88,128]{2,1,0:T(8,128)S(1)}, f32[16,88,128]{2,1,0:T(8,128)S(1)}, u32[]{:S(2)}, u32[]{:S(2)}) collective-permute-start(f32[16,88,128]{2,1,0:T(8,128)S(1)} %get-tuple-element.49), channel_id=1, source_target_pairs={{0,1},{1,0},{2,3},{3,2},{4,5},{5,4},{6,7},{7,6},{8,9},{9,8},{10,11... | collective-permute-start | bytes 2162696 | tf_op jit(solution)/shard_map/probe_reduce/ppermute | solution.py:637
  45.0 16.4 %collective-permute-start.7 = (f32[2,512,128]{2,1,0:T(8,128)}, f32[2,512,128]{2,1,0:T(8,128)S(1)}, u32[]{:S(2)}, u32[]{:S(2)}) collective-permute-start(f32[2,512,128]{2,1,0:T(8,128)} %get-tuple-element.55), channel_id=1, source_target_pairs={{1,2},{2,1},{3,4},{4,3},{5,6},{6,5},{7,8},{8,7},{9,10},{10,9},{11,... | collective-permute-start | bytes 1572872 | tf_op jit(solution)/shard_map/gradient_columns/ppermute | solution.py:637
  49.4 12.0 %collective-permute-start.8 = (f32[2,512,128]{2,1,0:T(8,128)}, f32[2,512,128]{2,1,0:T(8,128)S(1)}, u32[]{:S(2)}, u32[]{:S(2)}) collective-permute-start(f32[2,512,128]{2,1,0:T(8,128)} %get-tuple-element.56), channel_id=1, source_target_pairs={{0,1},{1,0},{2,3},{3,2},{4,5},{5,4},{6,7},{7,6},{8,9},{9,8},{10,11... | collective-permute-start | bytes 1572872 | tf_op jit(solution)/shard_map/gradient_columns/ppermute | solution.py:637
  50.4 18.1 %all-to-all-start = ((f32[16,88,128]{2,1,0:T(8,128)}), f32[16,88,128]{2,1,0:T(8,128)S(1)}, u32[]{:S(2)}, u32[]{:S(2)}) async-start(f32[16,88,128]{2,1,0:T(8,128)} %add.3), calls=%async_computation | async-start | bytes 1441792 | tf_op jit(solution)/shard_map/probe_reduce/all_to_all | solution.py:691
  57.4 4.8 %copy-start.5 = (f32[2,2,256,256]{3,2,1,0:T(8,128)S(1)}, f32[2,2,256,256]{3,2,1,0:T(8,128)}, u32[]{:S(2)}) copy-start(f32[2,2,256,256]{3,2,1,0:T(8,128)} %probe.1) | copy-start | bytes 3145732
  68.6 4.4 %collective-permute-start.11 = (f32[88,128]{1,0:T(8,128)S(1)}, f32[88,128]{1,0:T(8,128)S(1)}, u32[]{:S(2)}, u32[]{:S(2)}) collective-permute-start(f32[88,128]{1,0:T(8,128)S(1)} %probe_sum.2.own), channel_id=1, source_target_pairs={{0,66},{1,67},{2,0},{3,1},{4,70},{5,71},{6,4},{7,5},{8,74},{9,75},... | collective-permute-start | bytes 135176 | tf_op jit(solution)/shard_map/probe_sum/ppermute | solution.py:647
  70.7 4.4 %collective-permute-start.10 = (f32[88,128]{1,0:T(8,128)S(1)}, f32[88,128]{1,0:T(8,128)S(1)}, u32[]{:S(2)}, u32[]{:S(2)}) collective-permute-start(f32[88,128]{1,0:T(8,128)S(1)} %probe_sum.2.own), channel_id=1, source_target_pairs={{0,64},{1,65},{2,66},{3,67},{4,68},{5,69},{6,70},{7,71},{8,72},{9,... | collective-permute-start | bytes 135176 | tf_op jit(solution)/shard_map/probe_sum/ppermute | solution.py:647
  72.2 4.1 %collective-permute-start.9 = (f32[88,128]{1,0:T(8,128)S(1)}, f32[88,128]{1,0:T(8,128)S(1)}, u32[]{:S(2)}, u32[]{:S(2)}) collective-permute-start(f32[88,128]{1,0:T(8,128)S(1)} %probe_sum.2.own), channel_id=1, source_target_pairs={{0,2},{1,3},{2,64},{3,65},{4,6},{5,7},{6,68},{7,69},{8,10},{9,11},... | collective-permute-start | bytes 135176 | tf_op jit(solution)/shard_map/probe_sum/ppermute | solution.py:647
  77.2 20.4 %all-to-all-start.1 = ((f32[16,64,128]{2,1,0:T(8,128)}), f32[16,64,128]{2,1,0:T(8,128)S(1)}, u32[]{:S(2)}, u32[]{:S(2)}) async-start(f32[16,64,128]{2,1,0:T(8,128)} %get-tuple-element.63), calls=%async_computation.1 | async-start | bytes 1048576 | tf_op jit(solution)/shard_map/probe_gather/all_to_all | solution.py:708
  82.8 11.5 %collective-permute-start.12 = (f32[2,128,256]{2,1,0:T(8,128)}, f32[2,128,256]{2,1,0:T(8,128)S(1)}, u32[]{:S(2)}, u32[]{:S(2)}) collective-permute-start(f32[2,128,256]{2,1,0:T(8,128)} %get-tuple-element.65), channel_id=1, source_target_pairs={{0,16},{16,0},{32,48},{48,32},{64,80},{80,64},{96,112},{112,96},{1... | collective-permute-start | bytes 786440 | tf_op jit(solution)/shard_map/probe_sum/ppermute | solution.py:633
  83.4 13.2 %collective-permute-start.13 = (f32[2,128,256]{2,1,0:T(8,128)S(1)}, f32[2,128,256]{2,1,0:T(8,128)S(1)}, u32[]{:S(2)}, u32[]{:S(2)}) collective-permute-start(f32[2,128,256]{2,1,0:T(8,128)S(1)} %get-tuple-element.66), channel_id=1, source_target_pairs={{16,32},{32,16},{48,64},{64,48},{80,96},{96,80},{17,33},{33,17},{4... | collective-permute-start | bytes 786440 | tf_op jit(solution)/shard_map/probe_sum/ppermute | solution.py:633
  97.6 4.2 %collective-permute-start.14 = (f32[16,64,128]{2,1,0:T(8,128)S(1)}, f32[16,64,128]{2,1,0:T(8,128)S(1)}, u32[]{:S(2)}, u32[]{:S(2)}) collective-permute-start(f32[16,64,128]{2,1,0:T(8,128)S(1)} %all-to-all-done.1.mine), channel_id=1, source_target_pairs={{0,1},{1,0},{2,3},{3,2},{4,5},{5,4},{6,7},{7,6},{8,9},{9,8},{10,11... | collective-permute-start | bytes 1572872 | tf_op jit(solution)/shard_map/probe_gather/ppermute | solution.py:637
